TPU v7x, 32 devices: a whole 2x2x4 slice. The times are simulated.
32 devices in a mesh: parts: 2 (over x), tm: 8 (over z, y), stn: 2 (over core).
Axes of the slice: x: 2, y: 2, z: 4, core: 2. Of those that a mesh axis runs over, the one named last changes fastest.
Arguments:
- voltages: bfloat16 [256, 2, 32, 2, 2048], P(('parts', 'stn'), None, 'tm'), parts along dimension 0, may hold values from -6 to 6
- filter_taps: float32 [16, 2048], replicated, may hold values from -1.5 to 1.5
- use_mask: int32 [512, 8], P('parts'), parts along dimension 0, may hold values 0 or 1
- block_index: int32 [512, 8], P('parts'), parts along dimension 0, may hold values from 0 to 127
- weight_blocks: bfloat16 [128, 512], P('tm'), may hold values from -0.5 to 0.5
Outputs:
- power: float32 [2048, 32, 512], P('stn', 'tm', 'parts'), parts along dimension 2
There are 2 independent parts, one for each index of `parts`. A program takes and returns all parts, laid end to end along the dimension named above; an argument that names none is the same for every part. Nothing has to cross between parts.
All inputs are finite; a program needn't handle non-finite values.
Results may differ from a plain program's by a relative error of at most 0.008.
Values may be sent and summed in bfloat16 or wider, within the bound.
No kernel may reach another device: no remote copies, remote signals or barrier semaphores. Data moves between devices by JAX's collectives and lax.ppermute only.
A program may use at most 192 MiB of HBM per device.

v0:
```python
import math

import jax
import jax.numpy as jnp
from jax import lax
from jax.sharding import PartitionSpec as P

P_SIZE = 64
SB = 16
G = 16


def from_behind(block, axis, distance):
    devices = range(lax.axis_size(axis))
    route = [(i - distance, i) for i in devices if i - distance in devices]
    return lax.ppermute(block, axis, route)


def transform_tables(first_size, second_size):
    full_size = first_size * second_size
    first_range = jnp.arange(first_size, dtype=jnp.int32)
    second_range = jnp.arange(second_size, dtype=jnp.int32)
    first_angle = (first_range[:, None] * first_range[None, :] % first_size).astype(jnp.float32) * (
        2.0 * math.pi / first_size
    )
    cosine_first = jnp.cos(first_angle)
    sine_first = jnp.sin(first_angle)
    section_one = jnp.stack(
        [
            jnp.stack([cosine_first, -sine_first], axis=1),
            jnp.stack([sine_first, cosine_first], axis=1),
        ],
        axis=0,
    )
    second_angle = (second_range[:, None] * second_range[None, :] % second_size).astype(
        jnp.float32
    ) * (2.0 * math.pi / second_size)
    cosine_second = jnp.cos(second_angle)
    sine_second = jnp.sin(second_angle)
    section_two = jnp.stack(
        [
            jnp.stack([cosine_second, sine_second], axis=-1),
            jnp.stack([-sine_second, cosine_second], axis=-1),
        ],
        axis=1,
    )
    section_two = section_two.reshape(2 * second_size, 2 * second_size)
    twist_angle = (second_range[:, None] * first_range[None, :] % full_size).astype(jnp.float32) * (
        2.0 * math.pi / full_size
    )
    return (
        section_one.astype(jnp.bfloat16),
        jnp.cos(twist_angle),
        jnp.sin(twist_angle),
        section_two.astype(jnp.bfloat16),
    )


def filter_frames(window, filter_taps, frame_count):
    history = filter_taps.shape[0] - 1
    shape_out = window.shape[:2] + (frame_count,) + window.shape[3:]
    summed = jnp.zeros(shape_out, jnp.float32)
    for tap_index in range(filter_taps.shape[0]):
        sliced = lax.slice_in_dim(
            window, history - tap_index, history - tap_index + frame_count, axis=2
        )
        summed = summed + filter_taps[tap_index] * sliced.astype(jnp.float32)
    return summed.astype(jnp.bfloat16)


def channelize(filtered, tables):
    section_one, twist_cos, twist_sin, section_two = tables
    first_size = section_one.shape[1]
    second_size = twist_cos.shape[0]
    station_count, frame_count = (filtered.shape[0], filtered.shape[2])
    reshaped = filtered.reshape(station_count, 2, frame_count, 2, first_size, second_size)
    first_section = jnp.einsum(
        "spfrae,raob->spfeob", reshaped, section_one, preferred_element_type=jnp.float32
    )
    real_part = first_section[:, :, :, :, 0, :]
    imag_part = first_section[:, :, :, :, 1, :]
    norm_factor = 1.0 / math.sqrt(first_size * second_size)
    twist_real = (real_part * twist_cos + imag_part * twist_sin) * norm_factor
    twist_imag = (imag_part * twist_cos - real_part * twist_sin) * norm_factor
    twiddled = jnp.stack([twist_real, twist_imag], axis=-2).astype(jnp.bfloat16)
    twiddled = twiddled.reshape(station_count, 2, frame_count, 2 * second_size, first_size)
    spectra = jnp.einsum(
        "dk,spfkb->spfdb", section_two, twiddled, preferred_element_type=jnp.float32
    )
    return spectra.astype(jnp.bfloat16).reshape(
        station_count, 2, frame_count, second_size, 2, first_size
    )


def beam_matrix(use_rows, picked):
    beam_count, block_count = use_rows.shape
    shaped = (
        picked.reshape(beam_count, block_count, G, 2, SB)
        * use_rows.astype(jnp.bfloat16)[:, :, None, None, None]
    )
    real_part = shaped[:, :, :, 0, :].transpose(2, 1, 3, 0).reshape(G, block_count * SB, beam_count)
    imag_part = shaped[:, :, :, 1, :].transpose(2, 1, 3, 0).reshape(G, block_count * SB, beam_count)
    upper_rows = jnp.stack([real_part, imag_part], axis=2)
    lower_rows = jnp.stack([-imag_part, real_part], axis=2)
    return jnp.stack([upper_rows, lower_rows], axis=1)


def form_beams(row_block, weights):
    row_count = row_block.shape[0]
    group_count = weights.shape[0]
    reshaped = row_block.reshape(group_count, -1, row_block.shape[2])
    matrices = weights.reshape(group_count, row_block.shape[2], -1)
    product = jnp.einsum("gmk,gkn->gmn", reshaped, matrices, preferred_element_type=jnp.float32)
    return product.reshape(row_count, -1)


def detect(summed):
    shaped = summed.reshape(summed.shape[0], 4, -1)
    return jnp.sum(shaped * shaped, axis=1)


def body(voltages, filter_taps, use_mask, block_index, weight_blocks):
    stations = voltages.shape[0]
    frames = voltages.shape[2]
    channels = voltages.shape[4]
    history = filter_taps.shape[0] - 1
    reaches = -(-history // frames)
    earlier = []
    for distance in range(reaches, 0, -1):
        lowest = max(0, distance * frames - history)
        earlier.append(from_behind(voltages[:, :, lowest:], "tm", distance))
    window = jnp.concatenate(earlier + [voltages], axis=2)
    filtered = filter_frames(window, filter_taps, frames)
    spectra = channelize(filtered, transform_tables(P_SIZE, channels // P_SIZE))
    turned = spectra.transpose(2, 3, 5, 1, 4, 0).reshape(frames, channels, 2, 2 * stations)
    blocks_local = stations // SB
    row_width = weight_blocks.shape[1]
    block_start = lax.axis_index("stn") * blocks_local
    use_rows = lax.dynamic_slice_in_dim(use_mask, block_start, blocks_local, 1)
    index_rows = lax.dynamic_slice_in_dim(block_index, block_start, blocks_local, 1)
    flat_index = index_rows.reshape(-1)
    shard_rows = lax.all_gather(weight_blocks, "tm", axis=0, tiled=True)
    block_ids = jnp.arange(shard_rows.shape[0], dtype=jnp.int32)
    onehot = (flat_index[:, None] == block_ids[None, :]).astype(jnp.bfloat16)
    picked = jnp.dot(onehot, shard_rows, preferred_element_type=jnp.float32)
    picked = picked.astype(jnp.bfloat16).reshape(
        index_rows.shape[0], index_rows.shape[1], row_width
    )
    matrix = beam_matrix(use_rows, picked)

    def frame_power(running, frame_rows):
        partial_value = form_beams(frame_rows, matrix)
        summed = lax.psum_scatter(
            partial_value.astype(jnp.bfloat16).astype(jnp.float32).astype(jnp.bfloat16),
            "stn",
            scatter_dimension=0,
            tiled=True,
        ).astype(jnp.float32)
        return (running, detect(summed))

    unused, detected = lax.scan(frame_power, jnp.zeros((), jnp.float32), turned)
    return detected.transpose(1, 0, 2)


def solution(mesh):
    in_specs = (
        P(("parts", "stn"), None, "tm", None, None),
        P(),
        P("parts", None),
        P("parts", None),
        P("tm", None),
    )
    out_specs = P("stn", "tm", "parts")
    return jax.shard_map(body, mesh=mesh, in_specs=in_specs, out_specs=out_specs, check_vma=False)
```

profile of v0, /device:TPU:17, one launch (start us, length us, event | category | flops | bytes accessed | tf_op | source)
XLA Modules:
  0.0 1031.0 jit_solution(15683490791320955258)
XLA Ops:
  28.3 498.6 %all_gather.3 = bf16[128,512]{1,0:T(8,128)(2,1)S(1)} all-gather(bf16[16,512]{1,0:T(8,128)(2,1)S(1)} %copy-done.5), channel_id=1, replica_groups=mesh['parts'=2,'tm'=8,'stn'=2] {'tm'}, dimensions={0}, use_global_device_ids=true | all-gather | bytes 147456 | tf_op jit(solution)/shard_map/all_gather | solution.py:142
  527.4 8.2 reshape_reshape.3
  535.7 9.8 broadcast_multiply_fusion
  545.5 21.0 %fusion.38 = (bf16[256,4,16,1,16]{4,3,2,1,0:T(2,128)(2,1)}, bf16[256,4,16,1,16]{4,3,2,1,0:T(2,128)(2,1)}) fusion(bf16[256,4,16,2,16]{4,3,2,1,0:T(2,128)(2,1)S(1)} %broadcast_multiply_fusion), kind=kLoop, calls=%fused_computation.78 | loop fusion | bytes 2097152 | tf_op jit(solution)/shard_map/slice | solution.py:102
  566.6 17.6 %copy.117 = bf16[256,4,16,1,16]{0,4,1,2,3:T(8,128)(2,1)S(1)} copy(bf16[256,4,16,1,16]{4,3,2,1,0:T(2,128)(2,1)} %get-tuple-element.54) | data formatting | bytes 1048576 | tf_op jit(solution)/shard_map/transpose | solution.py:102
  584.2 17.6 %copy.116 = bf16[256,4,16,1,16]{0,4,1,2,3:T(8,128)(2,1)S(1)} copy(bf16[256,4,16,1,16]{4,3,2,1,0:T(2,128)(2,1)} %get-tuple-element.55) | data formatting | bytes 1048576 | tf_op jit(solution)/shard_map/transpose | solution.py:101
  633.3 25.6 %add_convert_fusion = bf16[64,2,4,2,2048]{4,0,3,2,1:T(8,128)(2,1)} fusion(bf16[64,2,4,2,2048]{4,0,3,2,1:T(8,128)(2,1)} %collective-permute-done.2, bf16[64,2,4,2,2048]{4,0,3,2,1:T(8,128)(2,1)} %collective-permute-done.1, bf16[64,2,4,2,2048]{4,0,3,2,1:T(8,128)(2,1)} %collective-permute-done, bf16[64,2,7,2,2048]{4,0,3,2,1:T(8,128)(2,1)S(1)} %get-tuple-element.61, ...), kind=kLoop, calls=%fused_computation.11 | loop fusion | flops 100663296 | bytes 71434240 | tf_op jit(solution)/shard_map/convert_element_type | solution.py:68
  658.9 8.4 copy.93
  667.3 8.9 fusion.6
  680.5 7.2 pad_maximum_fusion
  687.7 16.1 %convert_bitcast_fusion = bf16[64,2,4,64,64]{3,4,2,1,0:T(8,128)(2,1)} fusion(bf16[64,2,4,64,64]{4,0,3,2,1:T(8,128)(2,1)} %bitcast.84, bf16[64,64,1,1,1]{1,0,2,3,4:T(8,128)(2,1)S(1)} %reshape.261), kind=kOutput, calls=%fused_computation.8 | convolution fusion | flops 270532608 | bytes 8396800 | tf_op jit(solution)/shard_map/dk,spfkb->spfdb/dot_general | solution.py:87
  703.8 12.3 %copy.98 = bf16[64,2,4,64,64]{4,0,3,2,1:T(8,128)(2,1)} copy(bf16[64,2,4,64,64]{3,4,2,1,0:T(8,128)(2,1)} %convert_bitcast_fusion) | data formatting | bytes 8388608 | tf_op jit(solution)/shard_map/convert_element_type | solution.py:90
  716.1 21.1 %copy.115 = bf16[4,32,64,2,2,64]{5,4,3,2,1,0:T(2,128)(2,1)} copy(bf16[4,32,64,2,2,64]{2,5,4,1,0,3:T(8,128)(2,1)} %bitcast.85) | data formatting | bytes 8388608 | tf_op jit(solution)/shard_map/while | solution.py:161
  737.2 17.5 %reshape.263 = bf16[4,2048,2,128]{3,2,1,0:T(2,128)(2,1)} reshape(bf16[4,32,64,2,2,64]{5,4,3,2,1,0:T(2,128)(2,1)} %copy.115) | data formatting | bytes 8388608 | tf_op jit(solution)/shard_map/while | solution.py:161
  754.7 268.9 %while.11 = (s32[]{:T(128)}, f32[4,1024,256]{2,0,1:T(4,128)}, bf16[4,2048,2,128]{3,2,1,0:T(2,128)(2,1)}, bf16[16,2,64,2,256]{4,3,2,1,0:T(2,128)(2,1)}, bf16[16,1...) while((s32[]{:T(128)}, f32[4,1024,256]{2,0,1:T(4,128)}, ...), condition=%wide.wide.region_3.4_spmd, body=%wide.wide.region_0.3_spmd.sunk | while | flops 541851648 | bytes 60817552 | solution.py:161
  768.4 18.3 %reduce-scatter.2.cloned.1.call-done = bf16[1024,1024]{1,0:T(8,128)(2,1)} async-done(((bf16[2048,1024]{1,0:T(8,128)(2,1)}), bf16[1024,1024]{1,0:T(8,128)(2,1)}) %reduce-scatter.2.cloned.1.call-update) | async-done | bytes 2097168 | tf_op jit(solution)/shard_map/while/body/eval_jaxpr/reduce_scatter | solution.py:153
  802.4 23.2 %dynamic_update_slice.6 = f32[4,1024,256]{2,0,1:T(4,128)} dynamic-update-slice(f32[4,1024,256]{2,0,1:T(4,128)} %get-tuple-element.146, f32[1,1024,256]{2,0,1:T(1,128)S(1)} %copy.133, s32[]{:T(128)S(6)} %copy.141, s32[]{:T(128)} %constant.58.clone.1..sunk, s32[]{:T(128)} %constant.58.clone.1..sunk) | dynamic-update-slice | bytes 2097156 | tf_op jit(solution)/shard_map/while/body/jit(dynamic_update_index_in_dim)/dynamic_update_slice | solution.py:161
  832.1 7.1 convert_element_type.246
  839.3 13.5 %reduce-scatter.2.cloned.1.call-done = bf16[1024,1024]{1,0:T(8,128)(2,1)} async-done(((bf16[2048,1024]{1,0:T(8,128)(2,1)}), bf16[1024,1024]{1,0:T(8,128)(2,1)}) %reduce-scatter.2.cloned.1.call-update) | async-done | bytes 2097168 | tf_op jit(solution)/shard_map/while/body/eval_jaxpr/reduce_scatter | solution.py:153
  868.4 23.2 %dynamic_update_slice.6 = f32[4,1024,256]{2,0,1:T(4,128)} dynamic-update-slice(f32[4,1024,256]{2,0,1:T(4,128)} %get-tuple-element.146, f32[1,1024,256]{2,0,1:T(1,128)S(1)} %copy.133, s32[]{:T(128)S(6)} %copy.141, s32[]{:T(128)} %constant.58.clone.1..sunk, s32[]{:T(128)} %constant.58.clone.1..sunk) | dynamic-update-slice | bytes 2097156 | tf_op jit(solution)/shard_map/while/body/jit(dynamic_update_index_in_dim)/dynamic_update_slice | solution.py:161
  905.3 13.5 %reduce-scatter.2.cloned.1.call-done = bf16[1024,1024]{1,0:T(8,128)(2,1)} async-done(((bf16[2048,1024]{1,0:T(8,128)(2,1)}), bf16[1024,1024]{1,0:T(8,128)(2,1)}) %reduce-scatter.2.cloned.1.call-update) | async-done | bytes 2097168 | tf_op jit(solution)/shard_map/while/body/eval_jaxpr/reduce_scatter | solution.py:153
  934.4 23.2 %dynamic_update_slice.6 = f32[4,1024,256]{2,0,1:T(4,128)} dynamic-update-slice(f32[4,1024,256]{2,0,1:T(4,128)} %get-tuple-element.146, f32[1,1024,256]{2,0,1:T(1,128)S(1)} %copy.133, s32[]{:T(128)S(6)} %copy.141, s32[]{:T(128)} %constant.58.clone.1..sunk, s32[]{:T(128)} %constant.58.clone.1..sunk) | dynamic-update-slice | bytes 2097156 | tf_op jit(solution)/shard_map/while/body/jit(dynamic_update_index_in_dim)/dynamic_update_slice | solution.py:161
  971.3 13.5 %reduce-scatter.2.cloned.1.call-done = bf16[1024,1024]{1,0:T(8,128)(2,1)} async-done(((bf16[2048,1024]{1,0:T(8,128)(2,1)}), bf16[1024,1024]{1,0:T(8,128)(2,1)}) %reduce-scatter.2.cloned.1.call-update) | async-done | bytes 2097168 | tf_op jit(solution)/shard_map/while/body/eval_jaxpr/reduce_scatter | solution.py:153
  1000.4 23.2 %dynamic_update_slice.6 = f32[4,1024,256]{2,0,1:T(4,128)} dynamic-update-slice(f32[4,1024,256]{2,0,1:T(4,128)} %get-tuple-element.146, f32[1,1024,256]{2,0,1:T(1,128)S(1)} %copy.133, s32[]{:T(128)S(6)} %copy.141, s32[]{:T(128)} %constant.58.clone.1..sunk, s32[]{:T(128)} %constant.58.clone.1..sunk) | dynamic-update-slice | bytes 2097156 | tf_op jit(solution)/shard_map/while/body/jit(dynamic_update_index_in_dim)/dynamic_update_slice | solution.py:161
  (88 shorter events, 168.8 us)
Async XLA Ops:
  6.5 21.5 %copy-start = (s32[256,8]{0,1:T(8,128)S(1)}, s32[256,8]{0,1:T(8,128)}, u32[]{:S(2)}) copy-start(s32[256,8]{0,1:T(8,128)} %param.10) | copy-start | bytes 24580
  6.5 21.7 %copy-start.5 = (bf16[16,512]{1,0:T(8,128)(2,1)S(1)}, bf16[16,512]{1,0:T(8,128)(2,1)}, u32[]{:S(2)}) copy-start(bf16[16,512]{1,0:T(8,128)(2,1)} %param.11) | copy-start | bytes 49156
  13.0 522.5 %copy-start.6 = (s32[256,8]{0,1:T(8,128)S(1)}, s32[256,8]{0,1:T(8,128)}, u32[]{:S(2)}) copy-start(s32[256,8]{0,1:T(8,128)} %param.9) | copy-start | bytes 24580
  13.0 597.1 %collective-permute-start.2 = (bf16[64,2,4,2,2048]{4,0,3,2,1:T(8,128)(2,1)}, bf16[64,2,4,2,2048]{4,0,3,2,1:T(8,128)(2,1)}, u32[]{:S(2)}, u32[]{:S(2)}) collective-permute-start(bf16[64,2,4,2,2048]{4,0,3,2,1:T(8,128)(2,1)} %copy.87), channel_id=1, source_target_pairs={{0,6},{2,8},{4,10},{6,12},{8,14},{1,7},{3,9},{5,11},{7,13},{9,15},... | collective-permute-start | bytes 12582920 | tf_op jit(solution)/shard_map/ppermute | solution.py:16
  17.3 598.0 %collective-permute-start.1 = (bf16[64,2,4,2,2048]{4,0,3,2,1:T(8,128)(2,1)}, bf16[64,2,4,2,2048]{4,0,3,2,1:T(8,128)(2,1)}, u32[]{:S(2)}, u32[]{:S(2)}) collective-permute-start(bf16[64,2,4,2,2048]{4,0,3,2,1:T(8,128)(2,1)} %copy.87), channel_id=1, source_target_pairs={{0,4},{2,6},{4,8},{6,10},{8,12},{10,14},{1,5},{3,7},{5,9},{7,11},{... | collective-permute-start | bytes 12582920 | tf_op jit(solution)/shard_map/ppermute | solution.py:16
  19.3 602.9 %collective-permute-start = (bf16[64,2,4,2,2048]{4,0,3,2,1:T(8,128)(2,1)}, bf16[64,2,4,2,2048]{4,0,3,2,1:T(8,128)(2,1)}, u32[]{:S(2)}, u32[]{:S(2)}) collective-permute-start(bf16[64,2,4,2,2048]{4,0,3,2,1:T(8,128)(2,1)} %copy.87), channel_id=1, source_target_pairs={{0,2},{2,4},{4,6},{6,8},{8,10},{10,12},{12,14},{1,3},{3,5},{5,7},{... | collective-permute-start | bytes 12582920 | tf_op jit(solution)/shard_map/ppermute | solution.py:16
  25.1 582.8 %collective-permute-start.3 = (bf16[64,2,3,2,2048]{4,0,3,2,1:T(8,128)(2,1)}, bf16[64,2,3,2,2048]{4,0,3,2,1:T(8,128)(2,1)}, u32[]{:S(2)}, u32[]{:S(2)}) collective-permute-start(bf16[64,2,3,2,2048]{4,0,3,2,1:T(8,128)(2,1)} %slice.153), channel_id=1, source_target_pairs={{0,8},{2,10},{4,12},{6,14},{1,9},{3,11},{5,13},{7,15},{16,24},{18,... | collective-permute-start | bytes 9437192 | tf_op jit(solution)/shard_map/ppermute | solution.py:16
  601.9 6.0 copy-start.4
  604.5 10.8 %copy-start.3 = (bf16[16,2,64,2,256]{4,3,2,1,0:T(2,128)(2,1)}, bf16[16,2,64,2,256]{4,3,2,1,0:T(2,128)(2,1)S(1)}, u32[]{:S(2)}) copy-start(bf16[16,2,64,2,256]{4,3,2,1,0:T(2,128)(2,1)S(1)} %copy.107) | copy-start | bytes 6291460
  622.1 6.9 copy-start.2
  754.7 32.1 %reduce-scatter.2.cloned.1.call-start = ((), (), s32[]{:S(2)}) async-start(), calls=%async_computation.1 | async-start | bytes 6291456 | tf_op jit(solution)/shard_map/while/body/eval_jaxpr/reduce_scatter | solution.py:153
  825.5 27.3 %reduce-scatter.2.cloned.1.call-start = ((), (), s32[]{:S(2)}) async-start(), calls=%async_computation.1 | async-start | bytes 6291456 | tf_op jit(solution)/shard_map/while/body/eval_jaxpr/reduce_scatter | solution.py:153
  891.5 27.3 %reduce-scatter.2.cloned.1.call-start = ((), (), s32[]{:S(2)}) async-start(), calls=%async_computation.1 | async-start | bytes 6291456 | tf_op jit(solution)/shard_map/while/body/eval_jaxpr/reduce_scatter | solution.py:153
  957.6 27.3 %reduce-scatter.2.cloned.1.call-start = ((), (), s32[]{:S(2)}) async-start(), calls=%async_computation.1 | async-start | bytes 6291456 | tf_op jit(solution)/shard_map/while/body/eval_jaxpr/reduce_scatter | solution.py:153
  1023.6 0.7 copy-start.1
Sparse Core Ops, SparseCore 0:
  768.6 18.1 reduce-scatter.1
  839.4 13.3 reduce-scatter.1
  905.4 13.3 reduce-scatter.1
  971.4 13.3 reduce-scatter.1
where the time goes:
time: 1040 us; the launch traced here: 1030 us
  blocking collectives  499 us (48%)
  local copies, waits for them, and re-layouts  322 us (31%)
  other arithmetic  83.4 us (8%)
  waiting for transfers between devices  58.9 us (6%)
  matrix products  44.7 us (4%)
  between operations  13.5 us (1%)
    all_gather x1, blocking collectives, body(): shard_rows = lax.all_gather(weight_blocks, 'tm', axis=0, tiled=True)  499 us
    dynamic_update_slice x8, local copies, waits for them, and re-layouts, body(): unused, detected = lax.scan(frame_power, jnp.zeros((), jnp.float32), turned)  97 us
    reduce_scatter x4, waiting for transfers between devices, frame_power(): lax.psum_scatter(partial_value.astype(jnp.bfloat16).astype(jnp.float32).a...  58.8 us
    while x3, local copies, waits for them, and re-layouts, body(): unused, detected = lax.scan(frame_power, jnp.zeros((), jnp.float32), turned)  40.8 us
    convert_element_type x4, local copies, waits for them, and re-layouts, frame_power(): partial_value.astype(jnp.bfloat16).astype(jnp.float32).astype(jnp.bfloat16)  28.6 us
    unnamed x19, local copies, waits for them, and re-layouts  28.2 us
    convert_element_type x1, other arithmetic, filter_frames(): return summed.astype(jnp.bfloat16)  25.6 us
    mul x4, local copies, waits for them, and re-layouts, detect(): return jnp.sum(shaped * shaped, axis=1)  22.6 us
  transfers between devices with their start and end apart: 8, of which 4 were waited for; matrix products, arithmetic and copies ran while one was open for 10% of the time, Pallas kernels for 0%

commit v1 on v0

v1 whole, which is shorter than its diff:
```python
import functools
import math

import jax
import jax.numpy as jnp
import ml_dtypes
import numpy as np
from jax import lax
from jax.experimental import pallas as pl
from jax.experimental.pallas import tpu as pltpu
from jax.sharding import PartitionSpec as P

SB = 16
G = 16
RADIX = 16
LANES = 128
CORES = 2
VMEM_LIMIT = 56 * 1024 * 1024
F32 = jnp.float32
BF16 = jnp.bfloat16


def dft_tables(channels):
    per_half = channels // RADIX // CORES
    b = np.arange(RADIX)[None, :, None, None]
    e = np.arange(LANES)[None, None, None, :]
    d = np.arange(CORES * per_half).reshape(CORES, 1, per_half, 1)
    angle = (e * (RADIX * d + b) % channels) * (2.0 * math.pi / channels)
    cosine, sine = np.cos(angle), np.sin(angle)
    real_rows = np.concatenate([cosine, sine], axis=3)
    imag_rows = np.concatenate([-sine, cosine], axis=3)
    table = np.concatenate([real_rows, imag_rows], axis=2) / math.sqrt(channels)
    return table.astype(ml_dtypes.bfloat16)


def turned(value, step, size):
    re, im = value
    step %= size
    if step == 0:
        return re, im
    if 4 * step == size:
        return im, -re
    if 2 * step == size:
        return -re, -im
    if 4 * step == 3 * size:
        return -im, re
    cosine, sine = math.cos(2 * math.pi * step / size), math.sin(2 * math.pi * step / size)
    if 8 * step == size:
        return (re + im) * cosine, (im - re) * cosine
    if 8 * step == 3 * size:
        return (im - re) * sine, -(re + im) * sine
    return re * cosine + im * sine, im * cosine - re * sine


def four_points(values):
    (r0, i0), (r1, i1), (r2, i2), (r3, i3) = values
    sr, si, dr, di = r0 + r2, i0 + i2, r0 - r2, i0 - i2
    tr, ti, er, ei = r1 + r3, i1 + i3, r1 - r3, i1 - i3
    return [(sr + tr, si + ti), (dr + ei, di - er), (sr - tr, si - ti), (dr - ei, di + er)]


def sixteen_points(values):
    inner = [four_points([values[4 * a1 + a0] for a1 in range(4)]) for a0 in range(4)]
    result = [None] * 16
    for b0 in range(4):
        outer = four_points([turned(inner[a0][b0], a0 * b0, 16) for a0 in range(4)])
        for b1 in range(4):
            result[4 * b1 + b0] = outer[b1]
    return result


def filter_kernel(place, taps, own, other, own_back, other_back, far, keep, send):
    tap_count = taps.shape[0]
    history = tap_count - 1
    frames = own.shape[0]
    count = 2 * frames
    stations, samples = own.shape[2:]
    tiles = stations // SB

    def run(first, second, first_back, second_back, first_out, second_out):
        window = [(far, i) for i in range(far.shape[0])]
        for ref in (first_back, second_back, first, second):
            window += [(ref, i) for i in range(frames)]

        for low in range(0, samples, LANES):
            lanes = slice(low, low + LANES)
            tap_rows = [jnp.broadcast_to(taps[k : k + 1, lanes], (SB, LANES)) for k in range(tap_count)]

            def step(i, carry):
                part, rows = i // tiles, pl.ds(pl.multiple_of(i % tiles * SB, SB), SB)
                sums = [None] * count
                for j, (ref, index) in enumerate(window):
                    value = ref[index, part, rows, lanes].astype(F32)
                    for f in range(count):
                        k = f + history - j
                        if 0 <= k <= history:
                            term = tap_rows[k] * value
                            sums[f] = term if sums[f] is None else sums[f] + term
                for f in range(count):
                    out = first_out if f < frames else second_out
                    out[f % frames, part, rows, lanes] = sums[f].astype(BF16)
                return carry

            lax.fori_loop(0, 2 * tiles, step, 0)

    @pl.when(place[0] == 0)
    def _():
        run(own, other, own_back, other_back, keep, send)

    @pl.when(place[0] == 1)
    def _():
        run(other, own, other_back, own_back, send, keep)


def filter_frames(place, taps, own, other, own_back, other_back, far, low):
    frames, _, _, samples = own.shape
    stations = far.shape[2]
    block = 512
    where = low // stations

    def spec(depth, station_block):
        return pl.BlockSpec((depth, 2, stations, block), lambda i, place: (0, 0, station_block, i))

    shape = jax.ShapeDtypeStruct((frames, 2, stations, samples), BF16)
    return pl.pallas_call(
        filter_kernel,
        out_shape=(shape, shape),
        grid_spec=pltpu.PrefetchScalarGridSpec(
            num_scalar_prefetch=1,
            grid=(samples // block,),
            in_specs=[pl.BlockSpec((taps.shape[0], block), lambda i, place: (0, i))]
            + [spec(frames, where)] * 4
            + [spec(far.shape[0], 0)],
            out_specs=[spec(frames, 0)] * 2,
        ),
        compiler_params=pltpu.CompilerParams(vmem_limit_bytes=VMEM_LIMIT),
        cost_estimate=pl.CostEstimate(
            flops=2 * 2 * frames * 2 * stations * samples * taps.shape[0],
            bytes_accessed=2 * 2 * stations * samples * (6 * frames + far.shape[0]),
            transcendentals=0,
        ),
        name="filter",
    )(place, taps, own, other, own_back, other_back, far)


def onward_kernel(low, place, own_back, other_back, far, sems):
    frames = own_back.shape[0]
    stations = far.shape[2]
    drop = 2 * frames - far.shape[0]
    rows = pl.ds(low, stations)

    def run(first, second):
        copies = [
            pltpu.make_async_copy(first.at[drop:, :, rows], far.at[: frames - drop], sems.at[0]),
            pltpu.make_async_copy(second.at[:, :, rows], far.at[frames - drop :], sems.at[1]),
        ]
        for copy in copies:
            copy.start()
        for copy in copies:
            copy.wait()

    @pl.when(place[0] == 0)
    def _():
        run(own_back, other_back)

    @pl.when(place[0] == 1)
    def _():
        run(other_back, own_back)


def onward(place, own_back, other_back, low, stations, history):
    _, parts, _, samples = own_back.shape
    return pl.pallas_call(
        functools.partial(onward_kernel, low),
        out_shape=jax.ShapeDtypeStruct((history, parts, stations, samples), BF16),
        in_specs=[pl.BlockSpec(memory_space=pltpu.SMEM)] + [pl.BlockSpec(memory_space=pl.ANY)] * 2,
        out_specs=pl.BlockSpec(memory_space=pl.ANY),
        scratch_shapes=[pltpu.SemaphoreType.DMA((2,))],
        cost_estimate=pl.CostEstimate(
            flops=0, bytes_accessed=4 * history * parts * stations * samples, transcendentals=0
        ),
        name="onward",
    )(place, own_back, other_back)


def weight_kernel(table, index, mask, out):
    groups, depth, width = out.shape
    beams = width // 2
    half = depth // 2
    rows = lax.broadcasted_iota(jnp.int32, (table.shape[0], beams), 0)
    for q in range(index.shape[0]):
        hit = jnp.where((rows == index[q : q + 1, :]) & (mask[q : q + 1, :] != 0), 1.0, 0.0).astype(BF16)
        picked = lax.dot_general(table[...], hit, (((0,), (0,)), ((), ())), preferred_element_type=F32)
        picked = picked.reshape(groups, 2, SB, beams)
        low = q * SB
        re, im = picked[:, 0], picked[:, 1]
        out[:, low : low + SB, :beams] = re.astype(BF16)
        out[:, low : low + SB, beams:] = im.astype(BF16)
        out[:, half + low : half + low + SB, :beams] = (-im).astype(BF16)
        out[:, half + low : half + low + SB, beams:] = re.astype(BF16)


def beam_weights(table, index, mask):
    blocks, beams = index.shape
    groups = table.shape[1] // (2 * SB)
    shape = (groups, 2 * blocks * SB, 2 * beams)
    return pl.pallas_call(
        weight_kernel,
        out_shape=jax.ShapeDtypeStruct(shape, BF16),
        compiler_params=pltpu.CompilerParams(vmem_limit_bytes=VMEM_LIMIT),
        cost_estimate=pl.CostEstimate(
            flops=2 * table.shape[0] * table.shape[1] * blocks * beams,
            bytes_accessed=2 * math.prod(shape),
            transcendentals=0,
        ),
        name="weights",
    )(table, index, mask)


def beam_kernel(source_count, has_earlier, *refs):
    refs = list(refs)
    refs.pop(0)
    sources = [refs.pop(0) for _ in range(source_count)]
    table, weights = refs.pop(0), refs.pop(0)
    earlier = refs.pop(0) if has_earlier else None
    out, mixed, spectra = refs[:3]
    summed = refs[3] if has_earlier else out
    step = pl.program_id(0)
    pair = sources[0].shape[0]
    station_count = sum(ref.shape[2] for ref in sources)
    groups = weights.shape[0]
    beams = weights.shape[2] // 2
    rows_of = table.shape[2] // 2 // groups
    frames = pl.num_programs(0) * pair
    frame_count = out.shape[1] if has_earlier else 4
    lane_tiles = beams // LANES
    per_channel = lane_tiles * frame_count

    low = 0
    for ref in sources:
        tiles = ref.shape[2] // SB

        def radix(i, carry, ref=ref, low=low, tiles=tiles):
            f, rows = i // tiles, pl.ds(pl.multiple_of(i % tiles * SB, SB), SB)
            values = [
                tuple(ref[f, part, rows, a * LANES : (a + 1) * LANES].astype(F32) for part in range(2))
                for a in range(RADIX)
            ]
            target = pl.ds(pl.multiple_of(f * station_count + low + i % tiles * SB, SB), SB)
            for b, (re, im) in enumerate(sixteen_points(values)):
                mixed[b, target, :LANES] = re.astype(BF16)
                mixed[b, target, LANES:] = im.astype(BF16)
            return carry

        lax.fori_loop(0, pair * tiles, radix, 0)
        low += ref.shape[2]

    def transform(b, carry):
        product = lax.dot_general(
            table[0, b], mixed[b], (((1,), (1,)), ((), ())), preferred_element_type=F32
        )
        product = product.reshape(2, groups, rows_of, pair * station_count)
        for part in range(2):
            value = jnp.concatenate(
                [product[part, :, :, f * station_count : (f + 1) * station_count] for f in range(pair)], axis=1
            )
            spectra[:, b, :, part * station_count : (part + 1) * station_count] = value.astype(BF16)
        return carry

    lax.fori_loop(0, RADIX, transform, 0)

    def form(g, carry):
        rows = spectra[g].reshape(RADIX * pair * rows_of, 2 * station_count)
        beam = jnp.dot(rows, weights[g], preferred_element_type=F32)
        re, im = beam[:, :beams], beam[:, beams:]
        power = re * re + im * im
        for b in range(RADIX):
            for f in range(pair):
                at = (b * pair + f) * rows_of
                for t in range(lane_tiles):
                    start = (g * rows_of * RADIX + b) * per_channel + t * frame_count + step * pair + f
                    summed[pl.ds(start, rows_of, stride=RADIX * per_channel), :] = power[
                        at : at + rows_of, t * LANES : (t + 1) * LANES
                    ]
        return carry

    lax.fori_loop(0, groups, form, 0)

    if has_earlier:

        @pl.when(step == pl.num_programs(0) - 1)
        def _():
            def finish(i, carry):
                for k in range(8):
                    c = i * 8 + k
                    rows = pl.ds(pl.multiple_of(c * per_channel, per_channel), per_channel)
                    value = summed[rows, :] + earlier[rows, :]
                    for t in range(lane_tiles):
                        out[c, :, t * LANES : (t + 1) * LANES] = value[t * frame_count : (t + 1) * frame_count]
                return carry

            lax.fori_loop(0, out.shape[0] // 8, finish, 0)


def beam_power(place, sources, table, weights, earlier, channels):
    frames, _, _, samples = sources[0].shape
    groups, depth, width = weights.shape
    beams = width // 2
    pair = 2
    station_count = sum(s.shape[2] for s in sources)
    flat = (channels * frames * beams // LANES, LANES)
    flat_spec = pl.BlockSpec(flat, lambda i, place: (0, 0))
    in_specs = [pl.BlockSpec((pair, 2, s.shape[2], samples), lambda i, place: (i, 0, 0, 0)) for s in sources]
    in_specs += [
        pl.BlockSpec((1,) + table.shape[1:], lambda i, place: (place[1], 0, 0, 0)),
        pl.BlockSpec(weights.shape, lambda i, place: (0, 0, 0)),
    ]
    operands = list(sources) + [table, weights]
    scratch = [
        pltpu.VMEM((RADIX, pair * station_count, 2 * LANES), BF16),
        pltpu.VMEM((groups, RADIX, pair * channels // groups // RADIX, 2 * station_count), BF16),
    ]
    if earlier is None:
        out_shape = jax.ShapeDtypeStruct(flat, F32)
        out_spec = flat_spec
    else:
        out_shape = jax.ShapeDtypeStruct((channels, frames, beams), F32)
        out_spec = pl.BlockSpec(out_shape.shape, lambda i, place: (0, 0, 0))
        operands.append(earlier)
        in_specs.append(flat_spec)
        scratch.append(pltpu.VMEM(flat, F32))
    return pl.pallas_call(
        functools.partial(beam_kernel, len(sources), earlier is not None),
        out_shape=out_shape,
        grid_spec=pltpu.PrefetchScalarGridSpec(
            num_scalar_prefetch=1,
            grid=(frames // pair,),
            in_specs=in_specs,
            out_specs=out_spec,
            scratch_shapes=scratch,
        ),
        compiler_params=pltpu.CompilerParams(vmem_limit_bytes=VMEM_LIMIT),
        cost_estimate=pl.CostEstimate(
            flops=2 * channels * frames * depth * width + 8 * frames * station_count * LANES * channels,
            bytes_accessed=4 * math.prod(flat) + 4 * frames * station_count * samples + 2 * math.prod(weights.shape),
            transcendentals=0,
        ),
        name="beams",
    )(place, *operands)


def flipped(rows, bit):
    return jnp.where(bit == 1, rows[::-1], rows)


def body(voltages, filter_taps, use_mask, block_index, weight_blocks):
    stations, pols, frames, parts, samples = voltages.shape
    history = filter_taps.shape[0] - 1
    half = stations // 2
    time_devices = lax.axis_size("tm")
    side = lax.axis_index("tm") % 2
    core = lax.axis_index("stn")
    place = jnp.stack([side, core]).astype(jnp.int32)

    def pair(block):
        return lax.ppermute(block, "tm", [(i, i ^ 1) for i in range(time_devices)])

    def hop(block, skip=0):
        return lax.ppermute(block, "tm", [(i, i + 2) for i in range(skip, time_devices - 2)])

    def swap(block):
        return lax.ppermute(block, "stn", [(0, 1), (1, 0)])

    columns = weight_blocks.shape[1] // CORES
    shard = lax.dynamic_slice_in_dim(weight_blocks, core * columns, columns, 1)
    shard = lax.all_gather(shard, "tm", axis=0, tiled=True)
    voltages, shard = lax.optimization_barrier((voltages, shard))

    def some(pol, start):
        block = lax.dynamic_slice_in_dim(voltages, start, half, 0)[:, pol]
        return block.transpose(1, 2, 0, 3)

    own, other = [], []
    for pol in range(pols):
        other.append(pair(some(pol, half * (1 - side))))
        own.append(some(pol, half * side))
    own_back = [hop(block) for block in own]
    other_back = [hop(block) for block in other]

    def ordered(rows):
        rows = rows.T.reshape(2, 2, 2, -1)
        rows = flipped(rows, core)
        rows = flipped(rows.swapaxes(0, 1), side).swapaxes(0, 1)
        return rows.reshape(8, -1)

    weights = beam_weights(shard, ordered(block_index), ordered(use_mask))
    table = jnp.asarray(dft_tables(samples))

    power = None
    for pol in range(pols):
        chunks = [(0, half)] if pol == 0 else [(0, half // 2), (half // 2, half // 2)]
        keeps, sents = [], []
        for low, size in chunks:
            far = hop(onward(place, own_back[pol], other_back[pol], low, size, history - 2 * frames), 2)
            keep, send = filter_frames(
                place, filter_taps, own[pol], other[pol], own_back[pol], other_back[pol], far, low
            )
            keeps.append(keep)
            sents.append(pair(send))
        sources = keeps + sents + [swap(b) for b in keeps] + [swap(b) for b in sents]
        power = beam_power(place, sources, table, weights, power, samples // CORES)
    return power


def solution(mesh):
    in_specs = (
        P(("parts", "stn"), None, "tm", None, None),
        P(),
        P("parts", None),
        P("parts", None),
        P("tm", None),
    )
    out_specs = P("stn", "tm", "parts")
    return jax.shard_map(body, mesh=mesh, in_specs=in_specs, out_specs=out_specs, check_vma=False)
```

time: 1040 us -> 377 us (0.36)
  blocking collectives: 499 us -> 21.9 us
  local copies, waits for them, and re-layouts: 322 us -> 18.3 us
  Pallas kernels: 0 us -> 182 us
  other arithmetic: 83.4 us -> 0.64 us
  matrix products: 44.7 us -> 0 us
  starting transfers between devices: 9.41 us -> 53.6 us
  waiting for transfers between devices: 58.9 us -> 98.5 us
  between operations: 13.5 us -> 0.2 us
    all_gather x1, blocking collectives: 499 us -> 21.9 us  [body(): shard = lax.all_gather(shard, 'tm', axis=0, tiled=True)]
    pallas_call x0 -> x9, Pallas kernels: none -> 182 us  [the longest x3 117 us: onward(): pl.pallas_call(functools.partial(onward_kernel, low), out_shape=jax.Shape...]
    ppermute x4 -> x18, waiting for transfers between devices: 0.01 us -> 98.5 us  [the longest x7 84.2 us: hop(): lax.ppermute(block, 'tm', [(i, i + 2) for i in range(skip, time_devices -...]
    dynamic_update_slice x8 -> x0, local copies, waits for them, and re-layouts: 97 us -> none  [body(): unused, detected = lax.scan(frame_power, jnp.zeros((), jnp.float32), turned)]
    reduce_scatter x4 -> x0, waiting for transfers between devices: 58.8 us -> none  [frame_power(): lax.psum_scatter(partial_value.astype(jnp.bfloat16).astype(jnp.float32).a...]
    convert_element_type x8 -> x0, local copies, waits for them, and re-layouts: 50.3 us -> none  [the longest x4 28.6 us: frame_power(): partial_value.astype(jnp.bfloat16).astype(jnp.float32).astype(jnp.bfloat16)]
    dot_general x7 -> x0, matrix products: 44.7 us -> none  [the longest x4 19.2 us: form_beams(): jnp.einsum('gmk,gkn->gmn', reshaped, matrices, preferred_element_type=jnp...]
    ppermute x4 -> x18, starting transfers between devices: 9.4 us -> 53.6 us  [the longest x7 22.9 us: hop(): lax.ppermute(block, 'tm', [(i, i + 2) for i in range(skip, time_devices -...]
  transfers between devices with their start and end apart: 8 -> 18, of which waited for: 4 -> 6; matrix products, arithmetic and copies ran while one was open for 10% -> 1% of each run, Pallas kernels for 0% -> 43%
where the time goes in v1:
time: 377 us; the launch traced here: 375 us
  Pallas kernels  182 us (48%)
  waiting for transfers between devices  98.5 us (26%)
  starting transfers between devices  53.6 us (14%)
  blocking collectives  21.9 us (6%)
  local copies, waits for them, and re-layouts  18.3 us (5%)
    pallas_call x3, Pallas kernels, onward(): pl.pallas_call(functools.partial(onward_kernel, low), out_shape=jax.Shape...  117 us
    ppermute x7, waiting for transfers between devices, hop(): lax.ppermute(block, 'tm', [(i, i + 2) for i in range(skip, time_devices -...  84.2 us
    pallas_call x2, Pallas kernels, beam_power(): pl.pallas_call(functools.partial(beam_kernel, len(sources), earlier is no...  41.4 us
    ppermute x7, starting transfers between devices, hop(): lax.ppermute(block, 'tm', [(i, i + 2) for i in range(skip, time_devices -...  22.9 us
    ppermute x6, starting transfers between devices, swap(): return lax.ppermute(block, 'stn', [(0, 1), (1, 0)])  22.4 us
    all_gather x1, blocking collectives, body(): shard = lax.all_gather(shard, 'tm', axis=0, tiled=True)  21.9 us
    pallas_call x3, Pallas kernels, filter_frames(): pl.pallas_call(filter_kernel, out_shape=(shape, shape), grid_spec=pltpu.P...  20.9 us
    ppermute x5, waiting for transfers between devices, pair(): return lax.ppermute(block, 'tm', [(i, i ^ 1) for i in range(time_devices)])  14.4 us
  transfers between devices with their start and end apart: 18, of which 6 were waited for; matrix products, arithmetic and copies ran while one was open for 1% of the time, Pallas kernels for 43%

profile of v1, /device:TPU:17, one launch (start us, length us, event | category | flops | bytes accessed | tf_op | source)
XLA Modules:
  0.0 374.8 jit_solution(1154363095514622696)
XLA Ops:
  0.7 21.9 %all_gather.3.table = bf16[128,256]{1,0:T(8,128)(2,1)} all-gather(bf16[16,256]{1,0:T(8,128)(2,1)S(1)} %constant_dynamic-slice_fusion), channel_id=1, replica_groups=mesh['parts'=2,'tm'=8,'stn'=2] {'tm'}, dimensions={0}, use_global_device_ids=true | all-gather | bytes 73728 | tf_op jit(solution)/shard_map/all_gather | solution.py:376
  22.7 6.5 %copy.7 = bf16[64,2,4,2,2048]{4,0,3,2,1:T(8,128)(2,1)} copy(bf16[64,2,4,2,2048]{4,3,2,1,0:T(2,128)(2,1)} %param.6) | data formatting | bytes 8388608 | tf_op jit(solution)/shard_map/optimization_barrier | solution.py:377
  29.2 3.7 dynamic-slice_bitcast_fusion
  32.8 3.9 %collective-permute-start.11 = (bf16[4,2,32,2048]{3,2,1,0:T(8,128)(2,1)S(1)}, bf16[4,2,32,2048]{3,2,1,0:T(8,128)(2,1)S(1)}, u32[]{:S(2)}, u32[]{:S(2)}) collective-permute-start(bf16[4,2,32,2048]{3,2,1,0:T(8,128)(2,1)S(1)} %get-tuple-element.21), channel_id=1, source_target_pairs={{0,2},{2,0},{4,6},{6,4},{8,10},{10,8},{12,14},{14,12},{1,3},{3,1},... | collective-permute-start | bytes 3145736 | tf_op jit(solution)/shard_map/ppermute | solution.py:366
  36.7 4.6 %collective-permute-start.12 = (bf16[4,2,32,2048]{3,2,1,0:T(8,128)(2,1)S(1)}, bf16[4,2,32,2048]{3,2,1,0:T(8,128)(2,1)S(1)}, u32[]{:S(2)}, u32[]{:S(2)}) collective-permute-start(bf16[4,2,32,2048]{3,2,1,0:T(8,128)(2,1)S(1)} %get-tuple-element.24.own), channel_id=1, source_target_pairs={{0,4},{2,6},{4,8},{6,10},{8,12},{10,14},{1,5},{3,7},{5,9},{7,11},{... | collective-permute-start | bytes 3145736 | tf_op jit(solution)/shard_map/ppermute | solution.py:369
  41.4 12.0 %collective-permute-done.11.other = bf16[4,2,32,2048]{3,2,1,0:T(8,128)(2,1)S(1)} collective-permute-done((bf16[4,2,32,2048]{3,2,1,0:T(8,128)(2,1)S(1)}, bf16[4,2,32,2048]{3,2,1,0:T(8,128)(2,1)S(1)}, u32[]{:S(2)}, u32[]{:S(2)}) %collective-permute-start.11) | collective-permute-done | bytes 1048608 | tf_op jit(solution)/shard_map/ppermute | solution.py:366
  53.4 4.3 %collective-permute-start.13 = (bf16[4,2,32,2048]{3,2,1,0:T(8,128)(2,1)S(1)}, bf16[4,2,32,2048]{3,2,1,0:T(8,128)(2,1)S(1)}, u32[]{:S(2)}, u32[]{:S(2)}) collective-permute-start(bf16[4,2,32,2048]{3,2,1,0:T(8,128)(2,1)S(1)} %collective-permute-done.11.other), channel_id=1, source_target_pairs={{0,4},{2,6},{4,8},{6,10},{8,12},{10,14},{1,5},{3,7},{5,9},{7,11},{... | collective-permute-start | bytes 3145736 | tf_op jit(solution)/shard_map/ppermute | solution.py:369
  59.6 21.1 %collective-permute-done.13.other_back = bf16[4,2,32,2048]{3,2,1,0:T(8,128)(2,1)S(1)} collective-permute-done((bf16[4,2,32,2048]{3,2,1,0:T(8,128)(2,1)S(1)}, bf16[4,2,32,2048]{3,2,1,0:T(8,128)(2,1)S(1)}, u32[]{:S(2)}, u32[]{:S(2)}) %collective-permute-start.13) | collective-permute-done | bytes 1048608 | tf_op jit(solution)/shard_map/ppermute | solution.py:369
  81.8 57.4 %onward.5 = bf16[7,2,32,2048]{3,2,1,0:T(8,128)(2,1)} custom-call(s32[2]{0:T(128)} %pad_add_fusion.place.refs_0_, bf16[4,2,32,2048]{3,2,1,0:T(8,128)(2,1)} %copy-done.5, bf16[4,2,32,2048]{3,2,1,0:T(8,128)(2,1)} %copy-done.6), custom_call_target="tpu_custom_call" | custom-call | bytes 3670016 | tf_op jit(solution)/shard_map/onward/pallas_call | solution.py:173
  139.2 4.2 %collective-permute-start.14 = (bf16[7,2,32,2048]{3,2,1,0:T(8,128)(2,1)}, bf16[7,2,32,2048]{3,2,1,0:T(8,128)(2,1)S(1)}, u32[]{:S(2)}, u32[]{:S(2)}) collective-permute-start(bf16[7,2,32,2048]{3,2,1,0:T(8,128)(2,1)} %onward.5), channel_id=1, source_target_pairs={{4,8},{6,10},{8,12},{10,14},{5,9},{7,11},{9,13},{11,15},{20,24},{2... | collective-permute-start | bytes 5505032 | tf_op jit(solution)/shard_map/ppermute | solution.py:369
  147.3 29.4 %collective-permute-done.14.far = bf16[7,2,32,2048]{3,2,1,0:T(8,128)(2,1)S(1)} collective-permute-done((bf16[7,2,32,2048]{3,2,1,0:T(8,128)(2,1)}, bf16[7,2,32,2048]{3,2,1,0:T(8,128)(2,1)S(1)}, u32[]{:S(2)}, u32[]{:S(2)}) %collective-permute-start.14) | collective-permute-done | bytes 1835040 | tf_op jit(solution)/shard_map/ppermute | solution.py:369
  177.9 8.8 %filter.5 = (bf16[4,2,32,2048]{3,2,1,0:T(8,128)(2,1)}, bf16[4,2,32,2048]{3,2,1,0:T(8,128)(2,1)}) custom-call(s32[2]{0:T(128)} %pad_add_fusion.place.refs_0_, f32[16,2048]{1,0:T(8,128)} %taps.5, bf16[4,2,32,2048]{3,2,1,0:T(8,128)(2,1)} %copy-done.4, bf16[4,2,32,2048]{3,2,1,0:T(8,128)(2,1)} %copy-done.11, bf16[4,2,32,2048]{3,2,1,0:T(8,128)(2,1)} %copy-done.5, ...), custom_call_target="tpu_custom_call" | custom-call | flops 33554432 | bytes 8126464 | tf_op jit(solution)/shard_map/filter/pallas_call | solution.py:125
  187.9 11.1 %collective-permute-done.1.own_back = bf16[4,2,32,2048]{3,2,1,0:T(8,128)(2,1)S(1)} collective-permute-done((bf16[4,2,32,2048]{3,2,1,0:T(8,128)(2,1)S(1)}, bf16[4,2,32,2048]{3,2,1,0:T(8,128)(2,1)S(1)}, u32[]{:S(2)}, u32[]{:S(2)}) %collective-permute-start.1) | collective-permute-done | bytes 1048608 | tf_op jit(solution)/shard_map/ppermute | solution.py:369
  199.0 22.6 %collective-permute-done.2.other_back = bf16[4,2,32,2048]{3,2,1,0:T(8,128)(2,1)S(1)} collective-permute-done((bf16[4,2,32,2048]{3,2,1,0:T(8,128)(2,1)}, bf16[4,2,32,2048]{3,2,1,0:T(8,128)(2,1)S(1)}, u32[]{:S(2)}, u32[]{:S(2)}) %collective-permute-start.2) | collective-permute-done | bytes 1048608 | tf_op jit(solution)/shard_map/ppermute | solution.py:369
  222.6 29.6 %onward.3 = bf16[7,2,16,2048]{3,2,1,0:T(8,128)(2,1)} custom-call(s32[2]{0:T(128)} %pad_add_fusion.place.refs_0_, bf16[4,2,32,2048]{3,2,1,0:T(8,128)(2,1)} %copy-done.1, bf16[4,2,32,2048]{3,2,1,0:T(8,128)(2,1)} %copy-done.2), custom_call_target="tpu_custom_call" | custom-call | bytes 1835008 | tf_op jit(solution)/shard_map/onward/pallas_call | solution.py:173
  252.1 4.0 %collective-permute-start.3 = (bf16[7,2,16,2048]{3,2,1,0:T(8,128)(2,1)}, bf16[7,2,16,2048]{3,2,1,0:T(8,128)(2,1)}, u32[]{:S(2)}, u32[]{:S(2)}) collective-permute-start(bf16[7,2,16,2048]{3,2,1,0:T(8,128)(2,1)} %onward.3), channel_id=1, source_target_pairs={{4,8},{6,10},{8,12},{10,14},{5,9},{7,11},{9,13},{11,15},{20,24},{2... | collective-permute-start | bytes 2752520 | tf_op jit(solution)/shard_map/ppermute | solution.py:369
  256.2 29.6 %onward.4 = bf16[7,2,16,2048]{3,2,1,0:T(8,128)(2,1)} custom-call(s32[2]{0:T(128)} %pad_add_fusion.place.refs_0_, bf16[4,2,32,2048]{3,2,1,0:T(8,128)(2,1)} %copy-done.1, bf16[4,2,32,2048]{3,2,1,0:T(8,128)(2,1)} %copy-done.2), custom_call_target="tpu_custom_call" | custom-call | bytes 1835008 | tf_op jit(solution)/shard_map/onward/pallas_call | solution.py:173
  287.7 7.6 %collective-permute-start.16 = (bf16[4,2,32,2048]{3,2,1,0:T(8,128)(2,1)S(1)}, bf16[4,2,32,2048]{3,2,1,0:T(8,128)(2,1)S(1)}, u32[]{:S(2)}, u32[]{:S(2)}) collective-permute-start(bf16[4,2,32,2048]{3,2,1,0:T(8,128)(2,1)S(1)} %copy-done.8), channel_id=1, source_target_pairs={{0,1},{1,0},{2,3},{3,2},{4,5},{5,4},{6,7},{7,6},{8,9},{9,8},{10,11... | collective-permute-start | bytes 3145736 | tf_op jit(solution)/shard_map/ppermute | solution.py:372
  295.4 6.1 %filter.3 = (bf16[4,2,16,2048]{3,2,1,0:T(8,128)(2,1)}, bf16[4,2,16,2048]{3,2,1,0:T(8,128)(2,1)}) custom-call(s32[2]{0:T(128)} %pad_add_fusion.place.refs_0_, f32[16,2048]{1,0:T(8,128)} %taps.5, bf16[4,2,32,2048]{3,2,1,0:T(8,128)(2,1)} %copy-done.3, bf16[4,2,32,2048]{3,2,1,0:T(8,128)(2,1)} %collective-permute-done.other, bf16[4,2,32,2048]{3,2,1,0:T(8,128)(2,1)} %copy-done.1, ...), custom_call_target="tpu_custom_call" | custom-call | flops 16777216 | bytes 4063232 | tf_op jit(solution)/shard_map/filter/pallas_call | solution.py:125
  303.5 6.0 %filter.4 = (bf16[4,2,16,2048]{3,2,1,0:T(8,128)(2,1)}, bf16[4,2,16,2048]{3,2,1,0:T(8,128)(2,1)}) custom-call(s32[2]{0:T(128)} %pad_add_fusion.place.refs_0_, f32[16,2048]{1,0:T(8,128)} %taps.5, bf16[4,2,32,2048]{3,2,1,0:T(8,128)(2,1)} %copy-done.3, bf16[4,2,32,2048]{3,2,1,0:T(8,128)(2,1)} %collective-permute-done.other, bf16[4,2,32,2048]{3,2,1,0:T(8,128)(2,1)} %copy-done.1, ...), custom_call_target="tpu_custom_call" | custom-call | flops 16777216 | bytes 4063232 | tf_op jit(solution)/shard_map/filter/pallas_call | solution.py:125
  310.5 8.7 %collective-permute-start.7 = (bf16[4,2,16,2048]{3,2,1,0:T(8,128)(2,1)}, bf16[4,2,16,2048]{3,2,1,0:T(8,128)(2,1)}, u32[]{:S(2)}, u32[]{:S(2)}) collective-permute-start(bf16[4,2,16,2048]{3,2,1,0:T(8,128)(2,1)} %get-tuple-element.14.refs_1_), channel_id=1, source_target_pairs={{0,1},{1,0},{2,3},{3,2},{4,5},{5,4},{6,7},{7,6},{8,9},{9,8},{10,11... | collective-permute-start | bytes 1572872 | tf_op jit(solution)/shard_map/ppermute | solution.py:372
  321.6 5.8 %collective-permute-start.9 = (bf16[4,2,16,2048]{3,2,1,0:T(8,128)(2,1)}, bf16[4,2,16,2048]{3,2,1,0:T(8,128)(2,1)}, u32[]{:S(2)}, u32[]{:S(2)}) collective-permute-start(bf16[4,2,16,2048]{3,2,1,0:T(8,128)(2,1)} %collective-permute-done.5.refs_3_), channel_id=1, source_target_pairs={{0,1},{1,0},{2,3},{3,2},{4,5},{5,4},{6,7},{7,6},{8,9},{9,8},{10,11... | collective-permute-start | bytes 1572872 | tf_op jit(solution)/shard_map/ppermute | solution.py:372
  332.5 19.6 %beams.2.refs_11_ = f32[8192,128]{1,0:T(8,128)} custom-call(s32[2]{0:T(128)} %pad_add_fusion.place.refs_0_, bf16[4,2,32,2048]{3,2,1,0:T(8,128)(2,1)} %get-tuple-element.19.refs_1_, bf16[4,2,32,2048]{3,2,1,0:T(8,128)(2,1)} %collective-permute-done.15.refs_2_, bf16[4,2,32,2048]{3,2,1,0:T(8,128)(2,1)} %copy-done.9, bf16[4,2,32,2048]{3,2,1,0:T(8,128)(2,1)} %copy-done.10, ...), custom_call_target="tpu_custom_call" | custom-call | flops 1610612736 | bytes 10485760 | tf_op jit(solution)/shard_map/beams/pallas_call | solution.py:332
  353.0 21.8 %beams.3 = f32[1024,4,256]{2,1,0:T(4,128)} custom-call(s32[2]{0:T(128)} %pad_add_fusion.place.refs_0_, bf16[4,2,16,2048]{3,2,1,0:T(8,128)(2,1)} %get-tuple-element.14.refs_1_, bf16[4,2,16,2048]{3,2,1,0:T(8,128)(2,1)} %get-tuple-element.15.refs_2_, bf16[4,2,16,2048]{3,2,1,0:T(8,128)(2,1)} %collective-permute-done.5.refs_3_, ...), custom_call_target="tpu_custom_call" | custom-call | flops 1610612736 | bytes 10485760 | tf_op jit(solution)/shard_map/beams/pallas_call | solution.py:332
  (65 shorter events, 24.3 us)
Async XLA Ops:
  32.8 153.8 %copy-start.3 = (bf16[4,2,32,2048]{3,2,1,0:T(8,128)(2,1)}, bf16[4,2,32,2048]{3,2,1,0:T(8,128)(2,1)S(1)}, u32[]{:S(2)}) copy-start(bf16[4,2,32,2048]{3,2,1,0:T(8,128)(2,1)S(1)} %get-tuple-element.23.own) | copy-start | bytes 3145732
  32.8 20.5 %collective-permute-start.11 = (bf16[4,2,32,2048]{3,2,1,0:T(8,128)(2,1)S(1)}, bf16[4,2,32,2048]{3,2,1,0:T(8,128)(2,1)S(1)}, u32[]{:S(2)}, u32[]{:S(2)}) collective-permute-start(bf16[4,2,32,2048]{3,2,1,0:T(8,128)(2,1)S(1)} %get-tuple-element.21), channel_id=1, source_target_pairs={{0,2},{2,0},{4,6},{6,4},{8,10},{10,8},{12,14},{14,12},{1,3},{3,1},... | collective-permute-start | bytes 3145736 | tf_op jit(solution)/shard_map/ppermute | solution.py:366
  36.7 22.8 %collective-permute-start.12 = (bf16[4,2,32,2048]{3,2,1,0:T(8,128)(2,1)S(1)}, bf16[4,2,32,2048]{3,2,1,0:T(8,128)(2,1)S(1)}, u32[]{:S(2)}, u32[]{:S(2)}) collective-permute-start(bf16[4,2,32,2048]{3,2,1,0:T(8,128)(2,1)S(1)} %get-tuple-element.24.own), channel_id=1, source_target_pairs={{0,4},{2,6},{4,8},{6,10},{8,12},{10,14},{1,5},{3,7},{5,9},{7,11},{... | collective-permute-start | bytes 3145736 | tf_op jit(solution)/shard_map/ppermute | solution.py:369
  53.4 27.3 %collective-permute-start.13 = (bf16[4,2,32,2048]{3,2,1,0:T(8,128)(2,1)S(1)}, bf16[4,2,32,2048]{3,2,1,0:T(8,128)(2,1)S(1)}, u32[]{:S(2)}, u32[]{:S(2)}) collective-permute-start(bf16[4,2,32,2048]{3,2,1,0:T(8,128)(2,1)S(1)} %collective-permute-done.11.other), channel_id=1, source_target_pairs={{0,4},{2,6},{4,8},{6,10},{8,12},{10,14},{1,5},{3,7},{5,9},{7,11},{... | collective-permute-start | bytes 3145736 | tf_op jit(solution)/shard_map/ppermute | solution.py:369
  57.7 87.6 %collective-permute-start = (bf16[4,2,32,2048]{3,2,1,0:T(8,128)(2,1)}, bf16[4,2,32,2048]{3,2,1,0:T(8,128)(2,1)}, u32[]{:S(2)}, u32[]{:S(2)}) collective-permute-start(bf16[4,2,32,2048]{3,2,1,0:T(8,128)(2,1)} %get-tuple-element.22), channel_id=1, source_target_pairs={{0,2},{2,0},{4,6},{6,4},{8,10},{10,8},{12,14},{14,12},{1,3},{3,1},... | collective-permute-start | bytes 3145736 | tf_op jit(solution)/shard_map/ppermute | solution.py:366
  59.6 21.1 %copy-start.5 = (bf16[4,2,32,2048]{3,2,1,0:T(8,128)(2,1)}, bf16[4,2,32,2048]{3,2,1,0:T(8,128)(2,1)S(1)}, u32[]{:S(2)}) copy-start(bf16[4,2,32,2048]{3,2,1,0:T(8,128)(2,1)S(1)} %collective-permute-done.12.own_back) | copy-start | bytes 3145732
  139.2 37.5 %collective-permute-start.14 = (bf16[7,2,32,2048]{3,2,1,0:T(8,128)(2,1)}, bf16[7,2,32,2048]{3,2,1,0:T(8,128)(2,1)S(1)}, u32[]{:S(2)}, u32[]{:S(2)}) collective-permute-start(bf16[7,2,32,2048]{3,2,1,0:T(8,128)(2,1)} %onward.5), channel_id=1, source_target_pairs={{4,8},{6,10},{8,12},{10,14},{5,9},{7,11},{9,13},{11,15},{20,24},{2... | collective-permute-start | bytes 5505032 | tf_op jit(solution)/shard_map/ppermute | solution.py:369
  143.4 55.6 %collective-permute-start.1 = (bf16[4,2,32,2048]{3,2,1,0:T(8,128)(2,1)S(1)}, bf16[4,2,32,2048]{3,2,1,0:T(8,128)(2,1)S(1)}, u32[]{:S(2)}, u32[]{:S(2)}) collective-permute-start(bf16[4,2,32,2048]{3,2,1,0:T(8,128)(2,1)S(1)} %get-tuple-element.23.own), channel_id=1, source_target_pairs={{0,4},{2,6},{4,8},{6,10},{8,12},{10,14},{1,5},{3,7},{5,9},{7,11},{... | collective-permute-start | bytes 3145736 | tf_op jit(solution)/shard_map/ppermute | solution.py:369
  145.3 76.2 %collective-permute-start.2 = (bf16[4,2,32,2048]{3,2,1,0:T(8,128)(2,1)}, bf16[4,2,32,2048]{3,2,1,0:T(8,128)(2,1)S(1)}, u32[]{:S(2)}, u32[]{:S(2)}) collective-permute-start(bf16[4,2,32,2048]{3,2,1,0:T(8,128)(2,1)} %collective-permute-done.other), channel_id=1, source_target_pairs={{0,4},{2,6},{4,8},{6,10},{8,12},{10,14},{1,5},{3,7},{5,9},{7,11},{... | collective-permute-start | bytes 3145736 | tf_op jit(solution)/shard_map/ppermute | solution.py:369
  186.7 108.7 %collective-permute-start.15 = (bf16[4,2,32,2048]{3,2,1,0:T(8,128)(2,1)}, bf16[4,2,32,2048]{3,2,1,0:T(8,128)(2,1)}, u32[]{:S(2)}, u32[]{:S(2)}) collective-permute-start(bf16[4,2,32,2048]{3,2,1,0:T(8,128)(2,1)} %get-tuple-element.20), channel_id=1, source_target_pairs={{0,2},{2,0},{4,6},{6,4},{8,10},{10,8},{12,14},{14,12},{1,3},{3,1},... | collective-permute-start | bytes 3145736 | tf_op jit(solution)/shard_map/ppermute | solution.py:366
  199.0 22.6 %copy-start.1 = (bf16[4,2,32,2048]{3,2,1,0:T(8,128)(2,1)}, bf16[4,2,32,2048]{3,2,1,0:T(8,128)(2,1)S(1)}, u32[]{:S(2)}) copy-start(bf16[4,2,32,2048]{3,2,1,0:T(8,128)(2,1)S(1)} %collective-permute-done.1.own_back) | copy-start | bytes 3145732
  199.0 88.7 %copy-start.8 = (bf16[4,2,32,2048]{3,2,1,0:T(8,128)(2,1)S(1)}, bf16[4,2,32,2048]{3,2,1,0:T(8,128)(2,1)}, u32[]{:S(2)}) copy-start(bf16[4,2,32,2048]{3,2,1,0:T(8,128)(2,1)} %get-tuple-element.19.refs_1_) | copy-start | bytes 3145732
  252.1 43.3 %collective-permute-start.3 = (bf16[7,2,16,2048]{3,2,1,0:T(8,128)(2,1)}, bf16[7,2,16,2048]{3,2,1,0:T(8,128)(2,1)}, u32[]{:S(2)}, u32[]{:S(2)}) collective-permute-start(bf16[7,2,16,2048]{3,2,1,0:T(8,128)(2,1)} %onward.3), channel_id=1, source_target_pairs={{4,8},{6,10},{8,12},{10,14},{5,9},{7,11},{9,13},{11,15},{20,24},{2... | collective-permute-start | bytes 2752520 | tf_op jit(solution)/shard_map/ppermute | solution.py:369
  285.7 16.9 %collective-permute-start.4 = (bf16[7,2,16,2048]{3,2,1,0:T(8,128)(2,1)}, bf16[7,2,16,2048]{3,2,1,0:T(8,128)(2,1)S(1)}, u32[]{:S(2)}, u32[]{:S(2)}) collective-permute-start(bf16[7,2,16,2048]{3,2,1,0:T(8,128)(2,1)} %onward.4), channel_id=1, source_target_pairs={{4,8},{6,10},{8,12},{10,14},{5,9},{7,11},{9,13},{11,15},{20,24},{2... | collective-permute-start | bytes 2752520 | tf_op jit(solution)/shard_map/ppermute | solution.py:369
  287.7 22.7 %copy-start.14 = (s32[256,8]{0,1:T(8,128)S(1)}, s32[256,8]{0,1:T(8,128)}, u32[]{:S(2)}) copy-start(s32[256,8]{0,1:T(8,128)} %param.8) | copy-start | bytes 24580
  287.7 22.7 %copy-start.15 = (s32[256,8]{0,1:T(8,128)S(1)}, s32[256,8]{0,1:T(8,128)}, u32[]{:S(2)}) copy-start(s32[256,8]{0,1:T(8,128)} %param.9) | copy-start | bytes 24580
  287.7 39.7 %collective-permute-start.16 = (bf16[4,2,32,2048]{3,2,1,0:T(8,128)(2,1)S(1)}, bf16[4,2,32,2048]{3,2,1,0:T(8,128)(2,1)S(1)}, u32[]{:S(2)}, u32[]{:S(2)}) collective-permute-start(bf16[4,2,32,2048]{3,2,1,0:T(8,128)(2,1)S(1)} %copy-done.8), channel_id=1, source_target_pairs={{0,1},{1,0},{2,3},{3,2},{4,5},{5,4},{6,7},{7,6},{8,9},{9,8},{10,11... | collective-permute-start | bytes 3145736 | tf_op jit(solution)/shard_map/ppermute | solution.py:372
  295.3 36.2 %collective-permute-start.17 = (bf16[4,2,32,2048]{3,2,1,0:T(8,128)(2,1)}, bf16[4,2,32,2048]{3,2,1,0:T(8,128)(2,1)S(1)}, u32[]{:S(2)}, u32[]{:S(2)}) collective-permute-start(bf16[4,2,32,2048]{3,2,1,0:T(8,128)(2,1)} %collective-permute-done.15.refs_2_), channel_id=1, source_target_pairs={{0,1},{1,0},{2,3},{3,2},{4,5},{5,4},{6,7},{7,6},{8,9},{9,8},{10,11... | collective-permute-start | bytes 3145736 | tf_op jit(solution)/shard_map/ppermute | solution.py:372
  301.5 17.7 %collective-permute-start.5 = (bf16[4,2,16,2048]{3,2,1,0:T(8,128)(2,1)}, bf16[4,2,16,2048]{3,2,1,0:T(8,128)(2,1)}, u32[]{:S(2)}, u32[]{:S(2)}) collective-permute-start(bf16[4,2,16,2048]{3,2,1,0:T(8,128)(2,1)} %get-tuple-element.16), channel_id=1, source_target_pairs={{0,2},{2,0},{4,6},{6,4},{8,10},{10,8},{12,14},{14,12},{1,3},{3,1},... | collective-permute-start | bytes 1572872 | tf_op jit(solution)/shard_map/ppermute | solution.py:366
  309.6 12.1 %collective-permute-start.6 = (bf16[4,2,16,2048]{3,2,1,0:T(8,128)(2,1)}, bf16[4,2,16,2048]{3,2,1,0:T(8,128)(2,1)}, u32[]{:S(2)}, u32[]{:S(2)}) collective-permute-start(bf16[4,2,16,2048]{3,2,1,0:T(8,128)(2,1)} %get-tuple-element.17), channel_id=1, source_target_pairs={{0,2},{2,0},{4,6},{6,4},{8,10},{10,8},{12,14},{14,12},{1,3},{3,1},... | collective-permute-start | bytes 1572872 | tf_op jit(solution)/shard_map/ppermute | solution.py:366
  310.5 41.7 %collective-permute-start.7 = (bf16[4,2,16,2048]{3,2,1,0:T(8,128)(2,1)}, bf16[4,2,16,2048]{3,2,1,0:T(8,128)(2,1)}, u32[]{:S(2)}, u32[]{:S(2)}) collective-permute-start(bf16[4,2,16,2048]{3,2,1,0:T(8,128)(2,1)} %get-tuple-element.14.refs_1_), channel_id=1, source_target_pairs={{0,1},{1,0},{2,3},{3,2},{4,5},{5,4},{6,7},{7,6},{8,9},{9,8},{10,11... | collective-permute-start | bytes 1572872 | tf_op jit(solution)/shard_map/ppermute | solution.py:372
  319.2 33.0 %collective-permute-start.8 = (bf16[4,2,16,2048]{3,2,1,0:T(8,128)(2,1)}, bf16[4,2,16,2048]{3,2,1,0:T(8,128)(2,1)}, u32[]{:S(2)}, u32[]{:S(2)}) collective-permute-start(bf16[4,2,16,2048]{3,2,1,0:T(8,128)(2,1)} %get-tuple-element.15.refs_2_), channel_id=1, source_target_pairs={{0,1},{1,0},{2,3},{3,2},{4,5},{5,4},{6,7},{7,6},{8,9},{9,8},{10,11... | collective-permute-start | bytes 1572872 | tf_op jit(solution)/shard_map/ppermute | solution.py:372
  321.6 30.5 %collective-permute-start.9 = (bf16[4,2,16,2048]{3,2,1,0:T(8,128)(2,1)}, bf16[4,2,16,2048]{3,2,1,0:T(8,128)(2,1)}, u32[]{:S(2)}, u32[]{:S(2)}) collective-permute-start(bf16[4,2,16,2048]{3,2,1,0:T(8,128)(2,1)} %collective-permute-done.5.refs_3_), channel_id=1, source_target_pairs={{0,1},{1,0},{2,3},{3,2},{4,5},{5,4},{6,7},{7,6},{8,9},{9,8},{10,11... | collective-permute-start | bytes 1572872 | tf_op jit(solution)/shard_map/ppermute | solution.py:372
  327.4 24.8 %collective-permute-start.10 = (bf16[4,2,16,2048]{3,2,1,0:T(8,128)(2,1)}, bf16[4,2,16,2048]{3,2,1,0:T(8,128)(2,1)S(1)}, u32[]{:S(2)}, u32[]{:S(2)}) collective-permute-start(bf16[4,2,16,2048]{3,2,1,0:T(8,128)(2,1)} %collective-permute-done.6.refs_4_), channel_id=1, source_target_pairs={{0,1},{1,0},{2,3},{3,2},{4,5},{5,4},{6,7},{7,6},{8,9},{9,8},{10,11... | collective-permute-start | bytes 1572872 | tf_op jit(solution)/shard_map/ppermute | solution.py:372
  (10 other events, 21.0 us)

commit v2 on v1

v2 whole, which is shorter than its diff:
```python
import functools
import math

import jax
import jax.numpy as jnp
import ml_dtypes
import numpy as np
from jax import lax
from jax.experimental import pallas as pl
from jax.experimental.pallas import tpu as pltpu
from jax.sharding import PartitionSpec as P

SB = 16
G = 16
RADIX = 16
LANES = 128
CORES = 2
VMEM_LIMIT = 56 * 1024 * 1024
F32 = jnp.float32
BF16 = jnp.bfloat16


def cost(microseconds):
    return pl.CostEstimate(flops=0, bytes_accessed=int(microseconds * 3.3e6), transcendentals=0)


def dft_tables(channels):
    per_half = channels // RADIX // CORES
    b = np.arange(RADIX)[None, :, None, None]
    e = np.arange(LANES)[None, None, None, :]
    d = np.arange(CORES * per_half).reshape(CORES, 1, per_half, 1)
    angle = (e * (RADIX * d + b) % channels) * (2.0 * math.pi / channels)
    cosine, sine = np.cos(angle), np.sin(angle)
    real_rows = np.concatenate([cosine, sine], axis=3)
    imag_rows = np.concatenate([-sine, cosine], axis=3)
    table = np.concatenate([real_rows, imag_rows], axis=2) / math.sqrt(channels)
    return table.astype(ml_dtypes.bfloat16)


def turned(value, step, size):
    re, im = value
    step %= size
    if step == 0:
        return re, im
    if 4 * step == size:
        return im, -re
    if 2 * step == size:
        return -re, -im
    if 4 * step == 3 * size:
        return -im, re
    cosine, sine = math.cos(2 * math.pi * step / size), math.sin(2 * math.pi * step / size)
    if 8 * step == size:
        return (re + im) * cosine, (im - re) * cosine
    if 8 * step == 3 * size:
        return (im - re) * sine, -(re + im) * sine
    return re * cosine + im * sine, im * cosine - re * sine


def four_points(values):
    (r0, i0), (r1, i1), (r2, i2), (r3, i3) = values
    sr, si, dr, di = r0 + r2, i0 + i2, r0 - r2, i0 - i2
    tr, ti, er, ei = r1 + r3, i1 + i3, r1 - r3, i1 - i3
    return [(sr + tr, si + ti), (dr + ei, di - er), (sr - tr, si - ti), (dr - ei, di + er)]


def sixteen_points(values):
    inner = [four_points([values[4 * a1 + a0] for a1 in range(4)]) for a0 in range(4)]
    result = [None] * 16
    for b0 in range(4):
        outer = four_points([turned(inner[a0][b0], a0 * b0, 16) for a0 in range(4)])
        for b1 in range(4):
            result[4 * b1 + b0] = outer[b1]
    return result


def after(block, *earlier):
    return pl.pallas_call(
        lambda *refs: None,
        out_shape=jax.ShapeDtypeStruct(block.shape, block.dtype),
        in_specs=[pl.BlockSpec(memory_space=pl.ANY)] * (1 + len(earlier)),
        out_specs=pl.BlockSpec(memory_space=pl.ANY),
        input_output_aliases={0: 0},
        compiler_params=pltpu.CompilerParams(vmem_limit_bytes=VMEM_LIMIT),
        cost_estimate=cost(0),
        name="after",
    )(block, *earlier)


def filter_kernel(place, taps, own, other, own_back, other_back, far, *rest):
    keep, send = rest[-2:]
    tap_count = taps.shape[0]
    history = tap_count - 1
    frames = own.shape[0]
    count = 2 * frames
    stations, samples = own.shape[2:]
    tiles = stations // SB
    lane_tiles = samples // LANES

    def run(first, second, first_back, second_back, first_out, second_out):
        window = [(far, i) for i in range(far.shape[0])]
        for ref in (first_back, second_back, first, second):
            window += [(ref, i) for i in range(frames)]

        def step(i, carry):
            lanes = pl.ds(pl.multiple_of(i % lane_tiles * LANES, LANES), LANES)
            part = i // lane_tiles % 2
            rows = pl.ds(pl.multiple_of(i // (2 * lane_tiles) * SB, SB), SB)
            tap_rows = [jnp.broadcast_to(taps[k : k + 1, lanes], (SB, LANES)) for k in range(tap_count)]
            sums = [None] * count
            for j, (ref, index) in enumerate(window):
                value = ref[index, part, rows, lanes].astype(F32)
                for f in range(count):
                    k = f + history - j
                    if 0 <= k <= history:
                        term = tap_rows[k] * value
                        sums[f] = term if sums[f] is None else sums[f] + term
            for f in range(count):
                out = first_out if f < frames else second_out
                out[f % frames, part, rows, lanes] = sums[f].astype(BF16)
            return carry

        lax.fori_loop(0, 2 * tiles * lane_tiles, step, 0, unroll=2)

    @pl.when(place[0] == 0)
    def _():
        run(own, other, own_back, other_back, keep, send)

    @pl.when(place[0] == 1)
    def _():
        run(other, own, other_back, own_back, send, keep)


def filter_frames(place, taps, own, other, own_back, other_back, far, pol, low, earlier=()):
    frames, _, _, samples = other.shape
    stations = far.shape[2]
    block = 512
    where = low // stations

    def spec(depth, station_block):
        return pl.BlockSpec((depth, 2, stations, block), lambda i, place: (0, 0, station_block, i))

    both = pl.BlockSpec((None, frames, 2, stations, block), lambda i, place: (pol, 0, 0, where, i))
    one = spec(frames, where)
    shape = jax.ShapeDtypeStruct((frames, 2, stations, samples), BF16)
    return pl.pallas_call(
        filter_kernel,
        out_shape=(shape, shape),
        grid_spec=pltpu.PrefetchScalarGridSpec(
            num_scalar_prefetch=1,
            grid=(samples // block,),
            in_specs=[pl.BlockSpec((taps.shape[0], block), lambda i, place: (0, i))]
            + [both, one, both, one, spec(far.shape[0], 0)]
            + [pl.BlockSpec(memory_space=pl.ANY)] * len(earlier),
            out_specs=[spec(frames, 0)] * 2,
        ),
        compiler_params=pltpu.CompilerParams(vmem_limit_bytes=VMEM_LIMIT),
        cost_estimate=cost(8 * stations / 32),
        name="filter",
    )(place, taps, own, other, own_back, other_back, far, *earlier)


def onward_kernel(place, own_back, other_back, *rest):
    far = rest[-1]
    frames = own_back.shape[0]
    kept = far.shape[0] - frames

    def run(first, second):
        far[:kept] = first[frames - kept :]
        far[kept:] = second[...]

    @pl.when(place[0] == 0)
    def _():
        run(own_back, other_back)

    @pl.when(place[0] == 1)
    def _():
        run(other_back, own_back)


def onward(place, own_back, other_back, pol, low, stations, history, earlier=()):
    frames, parts, _, samples = other_back.shape
    where = low // stations
    return pl.pallas_call(
        onward_kernel,
        out_shape=jax.ShapeDtypeStruct((history, parts, stations, samples), BF16),
        grid_spec=pltpu.PrefetchScalarGridSpec(
            num_scalar_prefetch=1,
            grid=(parts,),
            in_specs=[
                pl.BlockSpec((None, frames, 1, stations, samples), lambda i, place: (pol, 0, i, where, 0)),
                pl.BlockSpec((frames, 1, stations, samples), lambda i, place: (0, i, where, 0)),
            ]
            + [pl.BlockSpec(memory_space=pl.ANY)] * len(earlier),
            out_specs=pl.BlockSpec((history, 1, stations, samples), lambda i, place: (0, i, 0, 0)),
        ),
        compiler_params=pltpu.CompilerParams(vmem_limit_bytes=VMEM_LIMIT),
        cost_estimate=cost(3 * stations / 32),
        name="onward",
    )(place, own_back, other_back, *earlier)


def weight_kernel(table, index, mask, out):
    groups, depth, width = out.shape
    beams = width // 2
    half = depth // 2
    rows = lax.broadcasted_iota(jnp.int32, (table.shape[0], beams), 0)
    for q in range(index.shape[0]):
        hit = jnp.where((rows == index[q : q + 1, :]) & (mask[q : q + 1, :] != 0), 1.0, 0.0).astype(BF16)
        picked = lax.dot_general(table[...], hit, (((0,), (0,)), ((), ())), preferred_element_type=F32)
        picked = picked.reshape(groups, 2, SB, beams)
        low = q * SB
        re, im = picked[:, 0], picked[:, 1]
        out[:, low : low + SB, :beams] = re.astype(BF16)
        out[:, low : low + SB, beams:] = im.astype(BF16)
        out[:, half + low : half + low + SB, :beams] = (-im).astype(BF16)
        out[:, half + low : half + low + SB, beams:] = re.astype(BF16)


def beam_weights(table, index, mask):
    blocks, beams = index.shape
    groups = table.shape[1] // (2 * SB)
    shape = (groups, 2 * blocks * SB, 2 * beams)
    return pl.pallas_call(
        weight_kernel,
        out_shape=jax.ShapeDtypeStruct(shape, BF16),
        compiler_params=pltpu.CompilerParams(vmem_limit_bytes=VMEM_LIMIT),
        cost_estimate=cost(4),
        name="weights",
    )(table, index, mask)


def beam_kernel(source_count, has_earlier, *refs):
    refs = list(refs)
    refs.pop(0)
    sources = [refs.pop(0) for _ in range(source_count)]
    table, weights = refs.pop(0), refs.pop(0)
    earlier = refs.pop(0) if has_earlier else None
    out, mixed, spectra = refs[:3]
    step = pl.program_id(0)
    frames = sources[0].shape[0]
    station_count = sum(ref.shape[2] for ref in sources)
    groups = spectra.shape[0]
    beams = weights.shape[2] // 2
    rows_of = table.shape[2] // 2 // groups
    pair = 2
    lane_tiles = beams // LANES
    per_channel = lane_tiles * frames

    @pl.when(step == 0)
    def _():
        low = 0
        for ref in sources:
            tiles = ref.shape[2] // SB

            def radix(i, carry, ref=ref, low=low, tiles=tiles):
                f, rows = i // tiles, pl.ds(pl.multiple_of(i % tiles * SB, SB), SB)
                values = [
                    tuple(ref[f, part, rows, a * LANES : (a + 1) * LANES].astype(F32) for part in range(2))
                    for a in range(RADIX)
                ]
                target = pl.ds(pl.multiple_of(f * station_count + low + i % tiles * SB, SB), SB)
                for b, (re, im) in enumerate(sixteen_points(values)):
                    mixed[b, target, :LANES] = re.astype(BF16)
                    mixed[b, target, LANES:] = im.astype(BF16)
                return carry

            lax.fori_loop(0, frames * tiles, radix, 0)
            low += ref.shape[2]

        def transform(b, carry):
            for start in range(0, frames, pair):
                product = lax.dot_general(
                    table[0, b],
                    mixed[b, start * station_count : (start + pair) * station_count],
                    (((1,), (1,)), ((), ())),
                    preferred_element_type=F32,
                )
                product = product.reshape(2, groups, rows_of, pair * station_count)
                rows = slice(start * rows_of, (start + pair) * rows_of)
                for part in range(2):
                    value = jnp.concatenate(
                        [product[part, :, :, f * station_count : (f + 1) * station_count] for f in range(pair)], axis=1
                    )
                    columns = slice(part * station_count, (part + 1) * station_count)
                    spectra[:, b, rows, columns] = value.astype(BF16)
            return carry

        lax.fori_loop(0, RADIX, transform, 0, unroll=4)

    for k in range(weights.shape[0]):
        rows = spectra[step * weights.shape[0] + k].reshape(RADIX * frames * rows_of, 2 * station_count)
        beam = jnp.dot(rows, weights[k], preferred_element_type=F32)
        re, im = beam[:, :beams], beam[:, beams:]
        power = re * re + im * im
        if not has_earlier:
            out[k] = power
            continue
        power = power + earlier[k]
        for b in range(RADIX):
            for f in range(frames):
                at = (b * frames + f) * rows_of
                for t in range(lane_tiles):
                    start = (k * rows_of * RADIX + b) * per_channel + t * frames + f
                    refs[3][pl.ds(start, rows_of, stride=RADIX * per_channel), :] = power[
                        at : at + rows_of, t * LANES : (t + 1) * LANES
                    ]

    if has_earlier:

        def finish(c, carry):
            value = refs[3][pl.ds(pl.multiple_of(c * per_channel, per_channel), per_channel), :]
            for t in range(lane_tiles):
                out[c, :, t * LANES : (t + 1) * LANES] = value[t * frames : (t + 1) * frames]
            return carry

        lax.fori_loop(0, out.shape[0], finish, 0, unroll=8)


def beam_power(place, sources, table, weights, earlier, channels):
    frames, _, _, samples = sources[0].shape
    groups, depth, width = weights.shape
    beams = width // 2
    station_count = sum(s.shape[2] for s in sources)
    at_once = 2
    flat = (groups, channels // groups * frames, beams)
    flat_spec = pl.BlockSpec((at_once,) + flat[1:], lambda i, place: (i, 0, 0))
    in_specs = [pl.BlockSpec(s.shape, lambda i, place: (0, 0, 0, 0)) for s in sources]
    in_specs += [
        pl.BlockSpec((1,) + table.shape[1:], lambda i, place: (place[1], 0, 0, 0)),
        pl.BlockSpec((at_once, depth, width), lambda i, place: (i, 0, 0)),
    ]
    operands = list(sources) + [table, weights]
    scratch = [
        pltpu.VMEM((RADIX, frames * station_count, 2 * LANES), BF16),
        pltpu.VMEM((groups, RADIX, frames * channels // groups // RADIX, 2 * station_count), BF16),
    ]
    if earlier is None:
        out_shape = jax.ShapeDtypeStruct(flat, F32)
        out_spec = flat_spec
    else:
        out_shape = jax.ShapeDtypeStruct((channels, frames, beams), F32)
        out_spec = pl.BlockSpec((channels // groups * at_once, frames, beams), lambda i, place: (i, 0, 0))
        operands.append(earlier)
        in_specs.append(flat_spec)
        scratch.append(pltpu.VMEM((math.prod(out_spec.block_shape) // LANES, LANES), F32))
    return pl.pallas_call(
        functools.partial(beam_kernel, len(sources), earlier is not None),
        out_shape=out_shape,
        grid_spec=pltpu.PrefetchScalarGridSpec(
            num_scalar_prefetch=1,
            grid=(groups // at_once,),
            in_specs=in_specs,
            out_specs=out_spec,
            scratch_shapes=scratch,
        ),
        compiler_params=pltpu.CompilerParams(vmem_limit_bytes=VMEM_LIMIT),
        cost_estimate=cost(0),
        name="beams",
    )(place, *operands)


def flipped(rows, bit):
    return jnp.where(bit == 1, rows[::-1], rows)


def body(voltages, filter_taps, use_mask, block_index, weight_blocks):
    stations, pols, frames, parts, samples = voltages.shape
    history = filter_taps.shape[0] - 1
    half = stations // 2
    time_devices = lax.axis_size("tm")
    side = lax.axis_index("tm") % 2
    core = lax.axis_index("stn")
    place = jnp.stack([side, core]).astype(jnp.int32)

    def pair(block):
        return lax.ppermute(block, "tm", [(i, i ^ 1) for i in range(time_devices)])

    def hop(block, skip=0):
        return lax.ppermute(block, "tm", [(i, i + 2) for i in range(skip, time_devices - 2)])

    def swap(block):
        return lax.ppermute(block, "stn", [(0, 1), (1, 0)])

    columns = weight_blocks.shape[1] // CORES
    shard = lax.dynamic_slice_in_dim(weight_blocks, core * columns, columns, 1)
    shard = jnp.concatenate([shard, pair(shard)])
    shards = [shard] + [
        lax.ppermute(shard, "tm", [(i, i ^ far) for i in range(time_devices)]) for far in range(2, time_devices, 2)
    ]

    other = [lax.dynamic_slice_in_dim(voltages, half * (1 - side), half, 0)[:, p].transpose(1, 2, 0, 3) for p in range(pols)]
    own = lax.dynamic_slice_in_dim(voltages, half * side, half, 0).transpose(1, 2, 3, 0, 4)
    other, own, shards = lax.optimization_barrier((other, own, shards))
    other = [pair(block) for block in other]
    own_back = hop(own)
    other_back = [hop(block) for block in other]

    def ordered(rows):
        rows = rows.T.reshape(2, 2, 2, -1)
        rows = flipped(rows, core)
        rows = flipped(rows.swapaxes(0, 1), side).swapaxes(0, 1)
        return rows.reshape(8, -1)

    index = block_index ^ (lax.axis_index("tm") * weight_blocks.shape[0])
    weights = beam_weights(jnp.concatenate(shards), ordered(index), ordered(use_mask))
    table = jnp.asarray(dft_tables(samples))

    chunks = [(pol, low, half // 2) for pol in range(pols) for low in (0, half // 2)]
    further = [
        onward(place, own_back, other_back[pol], pol, low, size, history - 2 * frames, other_back)
        for pol, low, size in chunks
    ]
    far = [hop(block, 2) for block in further]
    keeps, sends = [], []
    for (pol, low, _), block in zip(chunks, far):
        earlier = keeps[-1:] if keeps else further[1:] + [weights]
        keep, send = filter_frames(
            place, filter_taps, own, other[pol], own_back, other_back[pol], block, pol, low, earlier
        )
        keeps.append(keep)
        sends.append(send)
    sents = [pair(block) for block in sends]
    sents[:2] = [after(block, keeps[-1]) for block in sents[:2]]

    def power_of(pol, earlier):
        here = [i for i, chunk in enumerate(chunks) if chunk[0] == pol]
        sources = [keeps[i] for i in here] + [sents[i] for i in here]
        sources += [swap(block) for block in sources]
        return beam_power(place, sources, table, weights, earlier, samples // CORES)

    power = power_of(0, None)
    sents[-1] = after(sents[-1], power)
    return power_of(1, power)


def solution(mesh):
    in_specs = (
        P(("parts", "stn"), None, "tm", None, None),
        P(),
        P("parts", None),
        P("parts", None),
        P("tm", None),
    )
    out_specs = P("stn", "tm", "parts")
    return jax.shard_map(body, mesh=mesh, in_specs=in_specs, out_specs=out_specs, check_vma=False)
```

time: 377 us -> 241 us (0.64)
  Pallas kernels: 182 us -> 63.8 us
  blocking collectives: 21.9 us -> 0 us
    pallas_call x3 -> x7, Pallas kernels: 117 us -> 10.9 us  [the longest x4 10.9 us: onward(): pl.pallas_call(onward_kernel, out_shape=jax.ShapeDtypeStruct((history, pa...]
    all_gather x1 -> x0, blocking collectives: 21.9 us -> none  [body(): shard = lax.all_gather(shard, 'tm', axis=0, tiled=True)]
    ppermute x7, waiting for transfers between devices: 84.2 us -> 62.7 us  [hop(): lax.ppermute(block, 'tm', [(i, i + 2) for i in range(skip, time_devices -...]
    ppermute x5 -> x7, waiting for transfers between devices: 14.4 us -> 35.8 us  [pair(): return lax.ppermute(block, 'tm', [(i, i ^ 1) for i in range(time_devices)])]
    pallas_call x2, Pallas kernels: 41.4 us -> 25.7 us  [beam_power(): pl.pallas_call(functools.partial(beam_kernel, len(sources), earlier is no...]
    optimization_barrier x1 -> x0, local copies, waits for them, and re-layouts: 6.5 us -> none  [body(): voltages, shard = lax.optimization_barrier((voltages, shard))]
    unnamed x32 -> x51, local copies, waits for them, and re-layouts: 6.77 us -> 10.7 us
    pallas_call x3 -> x4, Pallas kernels: 20.9 us -> 24.5 us  [filter_frames(): pl.pallas_call(filter_kernel, out_shape=(shape, shape), grid_spec=pltpu.P...]
  transfers between devices with their start and end apart: 18 -> 25, of which waited for: 6 -> 8; matrix products, arithmetic and copies ran while one was open for 1% -> 6% of each run, Pallas kernels for 43% -> 20%
where the time goes in v2:
time: 241 us; the launch traced here: 239 us
  waiting for transfers between devices  100 us (41%)
  Pallas kernels  63.8 us (26%)
  starting transfers between devices  52.9 us (22%)
  local copies, waits for them, and re-layouts  20.8 us (9%)
    ppermute x7, waiting for transfers between devices, hop(): lax.ppermute(block, 'tm', [(i, i + 2) for i in range(skip, time_devices -...  62.7 us
    ppermute x7, waiting for transfers between devices, pair(): return lax.ppermute(block, 'tm', [(i, i ^ 1) for i in range(time_devices)])  35.8 us
    pallas_call x2, Pallas kernels, beam_power(): pl.pallas_call(functools.partial(beam_kernel, len(sources), earlier is no...  25.7 us
    pallas_call x4, Pallas kernels, filter_frames(): pl.pallas_call(filter_kernel, out_shape=(shape, shape), grid_spec=pltpu.P...  24.5 us
    ppermute x8, starting transfers between devices, swap(): return lax.ppermute(block, 'stn', [(0, 1), (1, 0)])  22.6 us
    ppermute x7, starting transfers between devices, hop(): lax.ppermute(block, 'tm', [(i, i + 2) for i in range(skip, time_devices -...  22.4 us
    pallas_call x4, Pallas kernels, onward(): pl.pallas_call(onward_kernel, out_shape=jax.ShapeDtypeStruct((history, pa...  10.9 us
    unnamed x51, local copies, waits for them, and re-layouts  10.7 us
  transfers between devices with their start and end apart: 25, of which 8 were waited for; matrix products, arithmetic and copies ran while one was open for 6% of the time, Pallas kernels for 20%

profile of v2, /device:TPU:17, one launch (start us, length us, event | category | flops | bytes accessed | tf_op | source)
XLA Modules:
  0.0 239.3 jit_solution(6465743620614082112)
XLA Ops:
  2.0 3.3 %constant_dynamic-slice_fusion.3 = (bf16[32,1,4,2,2048]{4,3,2,1,0:T(2,128)(2,1)S(1)}, bf16[32,1,4,2,2048]{4,3,2,1,0:T(2,128)(2,1)S(1)}) fusion(bf16[64,2,4,2,2048]{4,3,2,1,0:T(2,128)(2,1)} %param.6, s32[]{:T(128)S(6)} %select_n.40, s32[]{:T(128)S(6)} %add.19), kind=kLoop, calls=%fused_computation.17 | loop fusion | bytes 4194312 | tf_op jit(solution)/shard_map/slice | solution.py:391
  10.1 3.4 %constant_dynamic-slice_fusion.2 = bf16[32,2,4,2,2048]{4,3,2,1,0:T(2,128)(2,1)S(1)} fusion(bf16[64,2,4,2,2048]{4,3,2,1,0:T(2,128)(2,1)} %param.6, s32[]{:T(128)S(6)} %select_n.41), kind=kLoop, calls=%fused_computation.16 | loop fusion | bytes 4194308 | tf_op jit(solution)/shard_map/dynamic_slice | solution.py:392
  17.5 4.1 %collective-permute-start.5 = (bf16[2,4,2,32,2048]{4,3,2,1,0:T(8,128)(2,1)}, bf16[2,4,2,32,2048]{4,3,2,1,0:T(8,128)(2,1)S(1)}, u32[]{:S(2)}, u32[]{:S(2)}) collective-permute-start(bf16[2,4,2,32,2048]{4,3,2,1,0:T(8,128)(2,1)} %bitcast.23.own), channel_id=1, source_target_pairs={{0,4},{2,6},{4,8},{6,10},{8,12},{10,14},{1,5},{3,7},{5,9},{7,11},{... | collective-permute-start | bytes 6291464 | tf_op jit(solution)/shard_map/ppermute | solution.py:379
  21.6 17.4 %collective-permute-done.4.other = bf16[4,2,32,2048]{3,2,1,0:T(8,128)(2,1)} collective-permute-done((bf16[4,2,32,2048]{3,2,1,0:T(8,128)(2,1)S(1)}, bf16[4,2,32,2048]{3,2,1,0:T(8,128)(2,1)}, u32[]{:S(2)}, u32[]{:S(2)}) %collective-permute-start.4) | collective-permute-done | bytes 1048608 | tf_op jit(solution)/shard_map/ppermute | solution.py:376
  39.0 4.1 %collective-permute-start.6 = (bf16[4,2,32,2048]{3,2,1,0:T(8,128)(2,1)}, bf16[4,2,32,2048]{3,2,1,0:T(8,128)(2,1)S(1)}, u32[]{:S(2)}, u32[]{:S(2)}) collective-permute-start(bf16[4,2,32,2048]{3,2,1,0:T(8,128)(2,1)} %collective-permute-done.4.other), channel_id=1, source_target_pairs={{0,4},{2,6},{4,8},{6,10},{8,12},{10,14},{1,5},{3,7},{5,9},{7,11},{... | collective-permute-start | bytes 3145736 | tf_op jit(solution)/shard_map/ppermute | solution.py:379
  43.1 18.4 %collective-permute-done.7.other = bf16[4,2,32,2048]{3,2,1,0:T(8,128)(2,1)} collective-permute-done((bf16[4,2,32,2048]{3,2,1,0:T(8,128)(2,1)}, bf16[4,2,32,2048]{3,2,1,0:T(8,128)(2,1)}, u32[]{:S(2)}, u32[]{:S(2)}) %collective-permute-start.7) | collective-permute-done | bytes 1048608 | tf_op jit(solution)/shard_map/ppermute | solution.py:376
  61.5 4.1 %collective-permute-start.8 = (bf16[4,2,32,2048]{3,2,1,0:T(8,128)(2,1)}, bf16[4,2,32,2048]{3,2,1,0:T(8,128)(2,1)}, u32[]{:S(2)}, u32[]{:S(2)}) collective-permute-start(bf16[4,2,32,2048]{3,2,1,0:T(8,128)(2,1)} %collective-permute-done.7.other), channel_id=1, source_target_pairs={{0,4},{2,6},{4,8},{6,10},{8,12},{10,14},{1,5},{3,7},{5,9},{7,11},{... | collective-permute-start | bytes 3145736 | tf_op jit(solution)/shard_map/ppermute | solution.py:379
  66.2 20.8 %collective-permute-done.6.other_back.rest_1_ = bf16[4,2,32,2048]{3,2,1,0:T(8,128)(2,1)S(1)} collective-permute-done((bf16[4,2,32,2048]{3,2,1,0:T(8,128)(2,1)}, bf16[4,2,32,2048]{3,2,1,0:T(8,128)(2,1)S(1)}, u32[]{:S(2)}, u32[]{:S(2)}) %collective-permute-start.6) | collective-permute-done | bytes 1048608 | tf_op jit(solution)/shard_map/ppermute | solution.py:379
  87.0 22.5 %collective-permute-done.8.rest_0_.other_back = bf16[4,2,32,2048]{3,2,1,0:T(8,128)(2,1)} collective-permute-done((bf16[4,2,32,2048]{3,2,1,0:T(8,128)(2,1)}, bf16[4,2,32,2048]{3,2,1,0:T(8,128)(2,1)}, u32[]{:S(2)}, u32[]{:S(2)}) %collective-permute-start.8) | collective-permute-done | bytes 1048608 | tf_op jit(solution)/shard_map/ppermute | solution.py:379
  110.8 2.7 %onward.6 = bf16[7,2,16,2048]{3,2,1,0:T(8,128)(2,1)} custom-call(s32[2]{0:T(128)} %pad_add_fusion.place.refs_0_, bf16[2,4,2,32,2048]{4,3,2,1,0:T(8,128)(2,1)} %copy-done.1, bf16[4,2,32,2048]{3,2,1,0:T(8,128)(2,1)} %collective-permute-done.8.rest_0_.other_back, bf16[4,2,32,2048]{3,2,1,0:T(8,128)(2,1)} %collective-permute-done.8.rest_0_.other_back, ...), custom_call_target="tpu_custom_call" | custom-call | bytes 4950000 | tf_op jit(solution)/shard_map/onward/pallas_call | solution.py:183
  113.5 4.2 %collective-permute-start.11 = (bf16[7,2,16,2048]{3,2,1,0:T(8,128)(2,1)}, bf16[7,2,16,2048]{3,2,1,0:T(8,128)(2,1)S(1)}, u32[]{:S(2)}, u32[]{:S(2)}) collective-permute-start(bf16[7,2,16,2048]{3,2,1,0:T(8,128)(2,1)} %onward.6), channel_id=1, source_target_pairs={{4,8},{6,10},{8,12},{10,14},{5,9},{7,11},{9,13},{11,15},{20,24},{2... | collective-permute-start | bytes 2752520 | tf_op jit(solution)/shard_map/ppermute | solution.py:379
  117.8 2.8 %onward.5.rest_0_ = bf16[7,2,16,2048]{3,2,1,0:T(8,128)(2,1)} custom-call(s32[2]{0:T(128)} %pad_add_fusion.place.refs_0_, bf16[2,4,2,32,2048]{4,3,2,1,0:T(8,128)(2,1)} %copy-done.1, bf16[4,2,32,2048]{3,2,1,0:T(8,128)(2,1)} %collective-permute-done.8.rest_0_.other_back, bf16[4,2,32,2048]{3,2,1,0:T(8,128)(2,1)} %collective-permute-done.8.rest_0_.other_back, ...), custom_call_target="tpu_custom_call" | custom-call | bytes 4950000 | tf_op jit(solution)/shard_map/onward/pallas_call | solution.py:183
  137.5 6.1 %filter.4 = (bf16[4,2,16,2048]{3,2,1,0:T(8,128)(2,1)}, bf16[4,2,16,2048]{3,2,1,0:T(8,128)(2,1)}) custom-call(s32[2]{0:T(128)} %pad_add_fusion.place.refs_0_, f32[16,2048]{1,0:T(8,128)} %taps.7, bf16[2,4,2,32,2048]{4,3,2,1,0:T(8,128)(2,1)} %bitcast.23.own, bf16[4,2,32,2048]{3,2,1,0:T(8,128)(2,1)} %collective-permute-done.7.other, ...), custom_call_target="tpu_custom_call" | custom-call | bytes 13200000 | tf_op jit(solution)/shard_map/filter/pallas_call | solution.py:145
  143.6 10.5 %collective-permute-done.10.far = bf16[7,2,16,2048]{3,2,1,0:T(8,128)(2,1)} collective-permute-done((bf16[7,2,16,2048]{3,2,1,0:T(8,128)(2,1)}, bf16[7,2,16,2048]{3,2,1,0:T(8,128)(2,1)}, u32[]{:S(2)}, u32[]{:S(2)}) %collective-permute-start.10) | collective-permute-done | bytes 917536 | tf_op jit(solution)/shard_map/ppermute | solution.py:379
  154.1 6.2 %filter.5 = (bf16[4,2,16,2048]{3,2,1,0:T(8,128)(2,1)}, bf16[4,2,16,2048]{3,2,1,0:T(8,128)(2,1)}) custom-call(s32[2]{0:T(128)} %pad_add_fusion.place.refs_0_, f32[16,2048]{1,0:T(8,128)} %taps.7, bf16[2,4,2,32,2048]{4,3,2,1,0:T(8,128)(2,1)} %bitcast.23.own, bf16[4,2,32,2048]{3,2,1,0:T(8,128)(2,1)} %collective-permute-done.7.other, ...), custom_call_target="tpu_custom_call" | custom-call | bytes 13200000 | tf_op jit(solution)/shard_map/filter/pallas_call | solution.py:145
  161.8 8.6 %collective-permute-start.18 = (bf16[4,2,16,2048]{3,2,1,0:T(8,128)(2,1)}, bf16[4,2,16,2048]{3,2,1,0:T(8,128)(2,1)S(1)}, u32[]{:S(2)}, u32[]{:S(2)}) collective-permute-start(bf16[4,2,16,2048]{3,2,1,0:T(8,128)(2,1)} %get-tuple-element.28.rest_0_.refs_2_), channel_id=1, source_target_pairs={{0,1},{1,0},{2,3},{3,2},{4,5},{5,4},{6,7},{7,6},{8,9},{9,8},{10,11... | collective-permute-start | bytes 1572872 | tf_op jit(solution)/shard_map/ppermute | solution.py:382
  170.4 3.4 %collective-permute-done.9.far = bf16[7,2,16,2048]{3,2,1,0:T(8,128)(2,1)S(1)} collective-permute-done((bf16[7,2,16,2048]{3,2,1,0:T(8,128)(2,1)}, bf16[7,2,16,2048]{3,2,1,0:T(8,128)(2,1)S(1)}, u32[]{:S(2)}, u32[]{:S(2)}) %collective-permute-start.9) | collective-permute-done | bytes 917536 | tf_op jit(solution)/shard_map/ppermute | solution.py:379
  173.8 8.0 %collective-permute-start.17 = (bf16[4,2,16,2048]{3,2,1,0:T(8,128)(2,1)S(1)}, bf16[4,2,16,2048]{3,2,1,0:T(8,128)(2,1)S(1)}, u32[]{:S(2)}, u32[]{:S(2)}) collective-permute-start(bf16[4,2,16,2048]{3,2,1,0:T(8,128)(2,1)S(1)} %copy-done.4), channel_id=1, source_target_pairs={{0,1},{1,0},{2,3},{3,2},{4,5},{5,4},{6,7},{7,6},{8,9},{9,8},{10,11... | collective-permute-start | bytes 1572872 | tf_op jit(solution)/shard_map/ppermute | solution.py:382
  181.8 6.1 %filter.6 = (bf16[4,2,16,2048]{3,2,1,0:T(8,128)(2,1)}, bf16[4,2,16,2048]{3,2,1,0:T(8,128)(2,1)}) custom-call(s32[2]{0:T(128)} %pad_add_fusion.place.refs_0_, f32[16,2048]{1,0:T(8,128)} %taps.7, bf16[2,4,2,32,2048]{4,3,2,1,0:T(8,128)(2,1)} %bitcast.23.own, bf16[4,2,32,2048]{3,2,1,0:T(8,128)(2,1)} %collective-permute-done.4.other, ...), custom_call_target="tpu_custom_call" | custom-call | bytes 13200000 | tf_op jit(solution)/shard_map/filter/pallas_call | solution.py:145
  187.9 5.5 %collective-permute-done.12.far = bf16[7,2,16,2048]{3,2,1,0:T(8,128)(2,1)S(1)} collective-permute-done((bf16[7,2,16,2048]{3,2,1,0:T(8,128)(2,1)}, bf16[7,2,16,2048]{3,2,1,0:T(8,128)(2,1)S(1)}, u32[]{:S(2)}, u32[]{:S(2)}) %collective-permute-start.12) | collective-permute-done | bytes 917536 | tf_op jit(solution)/shard_map/ppermute | solution.py:379
  194.3 6.1 %filter.7 = (bf16[4,2,16,2048]{3,2,1,0:T(8,128)(2,1)}, bf16[4,2,16,2048]{3,2,1,0:T(8,128)(2,1)}) custom-call(s32[2]{0:T(128)} %pad_add_fusion.place.refs_0_, f32[16,2048]{1,0:T(8,128)} %taps.7, bf16[2,4,2,32,2048]{4,3,2,1,0:T(8,128)(2,1)} %bitcast.23.own, bf16[4,2,32,2048]{3,2,1,0:T(8,128)(2,1)} %collective-permute-done.4.other, ...), custom_call_target="tpu_custom_call" | custom-call | bytes 13200000 | tf_op jit(solution)/shard_map/filter/pallas_call | solution.py:145
  201.3 4.2 %collective-permute-start.20 = (bf16[4,2,16,2048]{3,2,1,0:T(8,128)(2,1)}, bf16[4,2,16,2048]{3,2,1,0:T(8,128)(2,1)S(1)}, u32[]{:S(2)}, u32[]{:S(2)}) collective-permute-start(bf16[4,2,16,2048]{3,2,1,0:T(8,128)(2,1)} %after.4.refs_4_), channel_id=1, source_target_pairs={{0,1},{1,0},{2,3},{3,2},{4,5},{5,4},{6,7},{7,6},{8,9},{9,8},{10,11... | collective-permute-start | bytes 1572872 | tf_op jit(solution)/shard_map/ppermute | solution.py:382
  209.8 11.6 %beams.2.refs_1_.refs_11_ = f32[8,512,256]{2,1,0:T(8,128)} custom-call(s32[2]{0:T(128)} %pad_add_fusion.place.refs_0_, bf16[4,2,16,2048]{3,2,1,0:T(8,128)(2,1)} %get-tuple-element.27.rest_0_.refs_1_, bf16[4,2,16,2048]{3,2,1,0:T(8,128)(2,1)} %get-tuple-element.28.rest_0_.refs_2_, bf16[4,2,16,2048]{3,2,1,0:T(8,128)(2,1)} %after.3.refs_3_, ...), custom_call_target="tpu_custom_call" | custom-call | tf_op jit(solution)/shard_map/beams/pallas_call | solution.py:346
  225.1 14.1 %beams.3 = f32[1024,4,256]{2,1,0:T(4,128)} custom-call(s32[2]{0:T(128)} %pad_add_fusion.place.refs_0_, bf16[4,2,16,2048]{3,2,1,0:T(8,128)(2,1)} %get-tuple-element.29.rest_0_.refs_1_, bf16[4,2,16,2048]{3,2,1,0:T(8,128)(2,1)} %get-tuple-element.30.refs_1_.refs_2_, bf16[4,2,16,2048]{3,2,1,0:T(8,128)(2,1)} %copy-done.12, ...), custom_call_target="tpu_custom_call" | custom-call | tf_op jit(solution)/shard_map/beams/pallas_call | solution.py:346
  (106 shorter events, 40.9 us)
Async XLA Ops:
  0.7 6.7 %collective-permute-start = (bf16[16,256]{1,0:T(8,128)(2,1)S(1)}, bf16[16,256]{1,0:T(8,128)(2,1)S(1)}, u32[]{:S(2)}, u32[]{:S(2)}) collective-permute-start(bf16[16,256]{1,0:T(8,128)(2,1)S(1)} %constant_dynamic-slice_fusion.1), channel_id=1, source_target_pairs={{0,2},{2,0},{4,6},{6,4},{8,10},{10,8},{12,14},{14,12},{1,3},{3,1},... | collective-permute-start | bytes 24584 | tf_op jit(solution)/shard_map/ppermute | solution.py:376
  7.5 8.5 %collective-permute-start.1 = (bf16[32,256]{1,0:T(8,128)(2,1)S(1)}, bf16[32,256]{1,0:T(8,128)(2,1)S(1)}, u32[]{:S(2)}, u32[]{:S(2)}) collective-permute-start(bf16[32,256]{1,0:T(8,128)(2,1)S(1)} %pad_maximum_fusion.1), channel_id=1, source_target_pairs={{0,4},{2,6},{4,0},{6,2},{8,12},{10,14},{12,8},{14,10},{1,5},{3,7},... | collective-permute-start | bytes 49160 | tf_op jit(solution)/shard_map/ppermute | solution.py:388
  8.8 7.2 %collective-permute-start.2 = (bf16[32,256]{1,0:T(8,128)(2,1)S(1)}, bf16[32,256]{1,0:T(8,128)(2,1)S(1)}, u32[]{:S(2)}, u32[]{:S(2)}) collective-permute-start(bf16[32,256]{1,0:T(8,128)(2,1)S(1)} %pad_maximum_fusion.1), channel_id=1, source_target_pairs={{0,8},{2,10},{4,12},{6,14},{8,0},{10,2},{12,4},{14,6},{1,9},{3,11}... | collective-permute-start | bytes 49160 | tf_op jit(solution)/shard_map/ppermute | solution.py:388
  8.8 7.2 %collective-permute-start.3 = (bf16[32,256]{1,0:T(8,128)(2,1)S(1)}, bf16[32,256]{1,0:T(8,128)(2,1)S(1)}, u32[]{:S(2)}, u32[]{:S(2)}) collective-permute-start(bf16[32,256]{1,0:T(8,128)(2,1)S(1)} %pad_maximum_fusion.1), channel_id=1, source_target_pairs={{0,12},{2,14},{4,8},{6,10},{8,4},{10,6},{12,0},{14,2},{1,13},{3,15... | collective-permute-start | bytes 49160 | tf_op jit(solution)/shard_map/ppermute | solution.py:388
  16.0 23.0 %collective-permute-start.4 = (bf16[4,2,32,2048]{3,2,1,0:T(8,128)(2,1)S(1)}, bf16[4,2,32,2048]{3,2,1,0:T(8,128)(2,1)}, u32[]{:S(2)}, u32[]{:S(2)}) collective-permute-start(bf16[4,2,32,2048]{3,2,1,0:T(8,128)(2,1)S(1)} %get-tuple-element.21), channel_id=1, source_target_pairs={{0,2},{2,0},{4,6},{6,4},{8,10},{10,8},{12,14},{14,12},{1,3},{3,1},... | collective-permute-start | bytes 3145736 | tf_op jit(solution)/shard_map/ppermute | solution.py:376
  16.3 45.2 %collective-permute-start.7 = (bf16[4,2,32,2048]{3,2,1,0:T(8,128)(2,1)}, bf16[4,2,32,2048]{3,2,1,0:T(8,128)(2,1)}, u32[]{:S(2)}, u32[]{:S(2)}) collective-permute-start(bf16[4,2,32,2048]{3,2,1,0:T(8,128)(2,1)} %get-tuple-element.22), channel_id=1, source_target_pairs={{0,2},{2,0},{4,6},{6,4},{8,10},{10,8},{12,14},{14,12},{1,3},{3,1},... | collective-permute-start | bytes 3145736 | tf_op jit(solution)/shard_map/ppermute | solution.py:376
  17.5 91.9 %collective-permute-start.5 = (bf16[2,4,2,32,2048]{4,3,2,1,0:T(8,128)(2,1)}, bf16[2,4,2,32,2048]{4,3,2,1,0:T(8,128)(2,1)S(1)}, u32[]{:S(2)}, u32[]{:S(2)}) collective-permute-start(bf16[2,4,2,32,2048]{4,3,2,1,0:T(8,128)(2,1)} %bitcast.23.own), channel_id=1, source_target_pairs={{0,4},{2,6},{4,8},{6,10},{8,12},{10,14},{1,5},{3,7},{5,9},{7,11},{... | collective-permute-start | bytes 6291464 | tf_op jit(solution)/shard_map/ppermute | solution.py:379
  39.0 47.9 %collective-permute-start.6 = (bf16[4,2,32,2048]{3,2,1,0:T(8,128)(2,1)}, bf16[4,2,32,2048]{3,2,1,0:T(8,128)(2,1)S(1)}, u32[]{:S(2)}, u32[]{:S(2)}) collective-permute-start(bf16[4,2,32,2048]{3,2,1,0:T(8,128)(2,1)} %collective-permute-done.4.other), channel_id=1, source_target_pairs={{0,4},{2,6},{4,8},{6,10},{8,12},{10,14},{1,5},{3,7},{5,9},{7,11},{... | collective-permute-start | bytes 3145736 | tf_op jit(solution)/shard_map/ppermute | solution.py:379
  61.5 47.9 %collective-permute-start.8 = (bf16[4,2,32,2048]{3,2,1,0:T(8,128)(2,1)}, bf16[4,2,32,2048]{3,2,1,0:T(8,128)(2,1)}, u32[]{:S(2)}, u32[]{:S(2)}) collective-permute-start(bf16[4,2,32,2048]{3,2,1,0:T(8,128)(2,1)} %collective-permute-done.7.other), channel_id=1, source_target_pairs={{0,4},{2,6},{4,8},{6,10},{8,12},{10,14},{1,5},{3,7},{5,9},{7,11},{... | collective-permute-start | bytes 3145736 | tf_op jit(solution)/shard_map/ppermute | solution.py:379
  113.5 22.9 %collective-permute-start.11 = (bf16[7,2,16,2048]{3,2,1,0:T(8,128)(2,1)}, bf16[7,2,16,2048]{3,2,1,0:T(8,128)(2,1)S(1)}, u32[]{:S(2)}, u32[]{:S(2)}) collective-permute-start(bf16[7,2,16,2048]{3,2,1,0:T(8,128)(2,1)} %onward.6), channel_id=1, source_target_pairs={{4,8},{6,10},{8,12},{10,14},{5,9},{7,11},{9,13},{11,15},{20,24},{2... | collective-permute-start | bytes 2752520 | tf_op jit(solution)/shard_map/ppermute | solution.py:379
  120.5 33.6 %collective-permute-start.10 = (bf16[7,2,16,2048]{3,2,1,0:T(8,128)(2,1)}, bf16[7,2,16,2048]{3,2,1,0:T(8,128)(2,1)}, u32[]{:S(2)}, u32[]{:S(2)}) collective-permute-start(bf16[7,2,16,2048]{3,2,1,0:T(8,128)(2,1)} %onward.5.rest_0_), channel_id=1, source_target_pairs={{4,8},{6,10},{8,12},{10,14},{5,9},{7,11},{9,13},{11,15},{20,24},{2... | collective-permute-start | bytes 2752520 | tf_op jit(solution)/shard_map/ppermute | solution.py:379
  125.2 48.5 %collective-permute-start.9 = (bf16[7,2,16,2048]{3,2,1,0:T(8,128)(2,1)}, bf16[7,2,16,2048]{3,2,1,0:T(8,128)(2,1)S(1)}, u32[]{:S(2)}, u32[]{:S(2)}) collective-permute-start(bf16[7,2,16,2048]{3,2,1,0:T(8,128)(2,1)} %onward.4.rest_1_), channel_id=1, source_target_pairs={{4,8},{6,10},{8,12},{10,14},{5,9},{7,11},{9,13},{11,15},{20,24},{2... | collective-permute-start | bytes 2752520 | tf_op jit(solution)/shard_map/ppermute | solution.py:379
  129.8 63.6 %collective-permute-start.12 = (bf16[7,2,16,2048]{3,2,1,0:T(8,128)(2,1)}, bf16[7,2,16,2048]{3,2,1,0:T(8,128)(2,1)S(1)}, u32[]{:S(2)}, u32[]{:S(2)}) collective-permute-start(bf16[7,2,16,2048]{3,2,1,0:T(8,128)(2,1)} %onward.7.rest_2_), channel_id=1, source_target_pairs={{4,8},{6,10},{8,12},{10,14},{5,9},{7,11},{9,13},{11,15},{20,24},{2... | collective-permute-start | bytes 2752520 | tf_op jit(solution)/shard_map/ppermute | solution.py:379
  160.3 40.1 %collective-permute-start.16 = (bf16[4,2,16,2048]{3,2,1,0:T(8,128)(2,1)}, bf16[4,2,16,2048]{3,2,1,0:T(8,128)(2,1)S(1)}, u32[]{:S(2)}, u32[]{:S(2)}) collective-permute-start(bf16[4,2,16,2048]{3,2,1,0:T(8,128)(2,1)} %get-tuple-element.34), channel_id=1, source_target_pairs={{0,2},{2,0},{4,6},{6,4},{8,10},{10,8},{12,14},{14,12},{1,3},{3,1},... | collective-permute-start | bytes 1572872 | tf_op jit(solution)/shard_map/ppermute | solution.py:376
  160.5 44.9 %collective-permute-start.15 = (bf16[4,2,16,2048]{3,2,1,0:T(8,128)(2,1)S(1)}, bf16[4,2,16,2048]{3,2,1,0:T(8,128)(2,1)S(1)}, u32[]{:S(2)}, u32[]{:S(2)}) collective-permute-start(bf16[4,2,16,2048]{3,2,1,0:T(8,128)(2,1)S(1)} %copy-done.24), channel_id=1, source_target_pairs={{0,2},{2,0},{4,6},{6,4},{8,10},{10,8},{12,14},{14,12},{1,3},{3,1},... | collective-permute-start | bytes 1572872 | tf_op jit(solution)/shard_map/ppermute | solution.py:376
  161.8 44.5 %collective-permute-start.18 = (bf16[4,2,16,2048]{3,2,1,0:T(8,128)(2,1)}, bf16[4,2,16,2048]{3,2,1,0:T(8,128)(2,1)S(1)}, u32[]{:S(2)}, u32[]{:S(2)}) collective-permute-start(bf16[4,2,16,2048]{3,2,1,0:T(8,128)(2,1)} %get-tuple-element.28.rest_0_.refs_2_), channel_id=1, source_target_pairs={{0,1},{1,0},{2,3},{3,2},{4,5},{5,4},{6,7},{7,6},{8,9},{9,8},{10,11... | collective-permute-start | bytes 1572872 | tf_op jit(solution)/shard_map/ppermute | solution.py:382
  173.8 33.4 %collective-permute-start.17 = (bf16[4,2,16,2048]{3,2,1,0:T(8,128)(2,1)S(1)}, bf16[4,2,16,2048]{3,2,1,0:T(8,128)(2,1)S(1)}, u32[]{:S(2)}, u32[]{:S(2)}) collective-permute-start(bf16[4,2,16,2048]{3,2,1,0:T(8,128)(2,1)S(1)} %copy-done.4), channel_id=1, source_target_pairs={{0,1},{1,0},{2,3},{3,2},{4,5},{5,4},{6,7},{7,6},{8,9},{9,8},{10,11... | collective-permute-start | bytes 1572872 | tf_op jit(solution)/shard_map/ppermute | solution.py:382
  193.4 14.6 %collective-permute-start.13 = (bf16[4,2,16,2048]{3,2,1,0:T(8,128)(2,1)}, bf16[4,2,16,2048]{3,2,1,0:T(8,128)(2,1)S(1)}, u32[]{:S(2)}, u32[]{:S(2)}) collective-permute-start(bf16[4,2,16,2048]{3,2,1,0:T(8,128)(2,1)} %get-tuple-element.31), channel_id=1, source_target_pairs={{0,2},{2,0},{4,6},{6,4},{8,10},{10,8},{12,14},{14,12},{1,3},{3,1},... | collective-permute-start | bytes 1572872 | tf_op jit(solution)/shard_map/ppermute | solution.py:376
  201.3 6.8 %collective-permute-start.20 = (bf16[4,2,16,2048]{3,2,1,0:T(8,128)(2,1)}, bf16[4,2,16,2048]{3,2,1,0:T(8,128)(2,1)S(1)}, u32[]{:S(2)}, u32[]{:S(2)}) collective-permute-start(bf16[4,2,16,2048]{3,2,1,0:T(8,128)(2,1)} %after.4.refs_4_), channel_id=1, source_target_pairs={{0,1},{1,0},{2,3},{3,2},{4,5},{5,4},{6,7},{7,6},{8,9},{9,8},{10,11... | collective-permute-start | bytes 1572872 | tf_op jit(solution)/shard_map/ppermute | solution.py:382
  206.3 2.3 collective-permute-start.19
  206.3 15.1 %collective-permute-start.14 = (bf16[4,2,16,2048]{3,2,1,0:T(8,128)(2,1)S(1)}, bf16[4,2,16,2048]{3,2,1,0:T(8,128)(2,1)S(1)}, u32[]{:S(2)}, u32[]{:S(2)}) collective-permute-start(bf16[4,2,16,2048]{3,2,1,0:T(8,128)(2,1)S(1)} %copy-done.23), channel_id=1, source_target_pairs={{0,2},{2,0},{4,6},{6,4},{8,10},{10,8},{12,14},{14,12},{1,3},{3,1},... | collective-permute-start | bytes 1572872 | tf_op jit(solution)/shard_map/ppermute | solution.py:376
  207.2 15.4 %collective-permute-start.22 = (bf16[4,2,16,2048]{3,2,1,0:T(8,128)(2,1)S(1)}, bf16[4,2,16,2048]{3,2,1,0:T(8,128)(2,1)S(1)}, u32[]{:S(2)}, u32[]{:S(2)}) collective-permute-start(bf16[4,2,16,2048]{3,2,1,0:T(8,128)(2,1)S(1)} %copy-done.3), channel_id=1, source_target_pairs={{0,1},{1,0},{2,3},{3,2},{4,5},{5,4},{6,7},{7,6},{8,9},{9,8},{10,11... | collective-permute-start | bytes 1572872 | tf_op jit(solution)/shard_map/ppermute | solution.py:382
  208.0 14.6 %collective-permute-start.21 = (bf16[4,2,16,2048]{3,2,1,0:T(8,128)(2,1)S(1)}, bf16[4,2,16,2048]{3,2,1,0:T(8,128)(2,1)S(1)}, u32[]{:S(2)}, u32[]{:S(2)}) collective-permute-start(bf16[4,2,16,2048]{3,2,1,0:T(8,128)(2,1)S(1)} %copy-done.5), channel_id=1, source_target_pairs={{0,1},{1,0},{2,3},{3,2},{4,5},{5,4},{6,7},{7,6},{8,9},{9,8},{10,11... | collective-permute-start | bytes 1572872 | tf_op jit(solution)/shard_map/ppermute | solution.py:382
  208.1 14.5 %collective-permute-start.23 = (bf16[4,2,16,2048]{3,2,1,0:T(8,128)(2,1)S(1)}, bf16[4,2,16,2048]{3,2,1,0:T(8,128)(2,1)S(1)}, u32[]{:S(2)}, u32[]{:S(2)}) collective-permute-start(bf16[4,2,16,2048]{3,2,1,0:T(8,128)(2,1)S(1)} %collective-permute-done.13.refs_3_), channel_id=1, source_target_pairs={{0,1},{1,0},{2,3},{3,2},{4,5},{5,4},{6,7},{7,6},{8,9},{9,8},{10,11... | collective-permute-start | bytes 1572872 | tf_op jit(solution)/shard_map/ppermute | solution.py:382
  (26 other events, 128.1 us)

commit v3 on v2

--- a/solution.py
+++ b/solution.py
@@ -80,10 +80,51 @@
         in_specs=[pl.BlockSpec(memory_space=pl.ANY)] * (1 + len(earlier)),
         out_specs=pl.BlockSpec(memory_space=pl.ANY),
         input_output_aliases={0: 0},
-        compiler_params=pltpu.CompilerParams(vmem_limit_bytes=VMEM_LIMIT),
         cost_estimate=cost(0),
         name="after",
     )(block, *earlier)
+
+
+def split_kernel(cuts, place, voltages, own, *rest):
+    outs, (own_buffer, other_buffer, sems) = rest[: len(cuts)], rest[len(cuts) :]
+    half = own.shape[0]
+    side = place[0]
+
+    def load(start, buffer, k):
+        return pltpu.make_async_copy(voltages.at[pl.ds(start * half, half)], buffer, sems.at[k])
+
+    stores = [pltpu.make_async_copy(own_buffer, own, sems.at[2])]
+    for k, (out, (pol, low, size)) in enumerate(zip(outs, cuts)):
+        stores.append(pltpu.make_async_copy(other_buffer.at[low : low + size, pol], out, sems.at[3 + k]))
+    load(side, own_buffer, 0).start()
+    load(1 - side, other_buffer, 1).start()
+    load(side, own_buffer, 0).wait()
+    stores[0].start()
+    load(1 - side, other_buffer, 1).wait()
+    for copy in stores[1:]:
+        copy.start()
+    for copy in stores:
+        copy.wait()
+
+
+def split(place, voltages, cuts):
+    stations, pols, frames, parts, samples = voltages.shape
+    half = (stations // 2, pols, frames, parts, samples)
+    shapes = [half] + [(size, frames, parts, samples) for _, _, size in cuts]
+    return pl.pallas_call(
+        functools.partial(split_kernel, cuts),
+        out_shape=[jax.ShapeDtypeStruct(shape, BF16) for shape in shapes],
+        in_specs=[pl.BlockSpec(memory_space=pltpu.SMEM), pl.BlockSpec(memory_space=pl.ANY)],
+        out_specs=[pl.BlockSpec(memory_space=pl.ANY)] * len(shapes),
+        scratch_shapes=[
+            pltpu.VMEM(half, BF16),
+            pltpu.VMEM(half, BF16),
+            pltpu.SemaphoreType.DMA((3 + len(cuts),)),
+        ],
+        compiler_params=pltpu.CompilerParams(vmem_limit_bytes=VMEM_LIMIT),
+        cost_estimate=cost(3),
+        name="split",
+    )(place, voltages)
 
 
 def filter_kernel(place, taps, own, other, own_back, other_back, far, *rest):
@@ -105,10 +146,10 @@
             lanes = pl.ds(pl.multiple_of(i % lane_tiles * LANES, LANES), LANES)
             part = i // lane_tiles % 2
             rows = pl.ds(pl.multiple_of(i // (2 * lane_tiles) * SB, SB), SB)
-            tap_rows = [jnp.broadcast_to(taps[k : k + 1, lanes], (SB, LANES)) for k in range(tap_count)]
+            tap_rows = [taps[k, :, lanes][None] for k in range(tap_count)]
             sums = [None] * count
             for j, (ref, index) in enumerate(window):
-                value = ref[index, part, rows, lanes].astype(F32)
+                value = ref[index, part, rows, lanes].astype(F32).reshape(SB // 8, 8, LANES)
                 for f in range(count):
                     k = f + history - j
                     if 0 <= k <= history:
@@ -116,7 +157,7 @@
                         sums[f] = term if sums[f] is None else sums[f] + term
             for f in range(count):
                 out = first_out if f < frames else second_out
-                out[f % frames, part, rows, lanes] = sums[f].astype(BF16)
+                out[f % frames, part, rows, lanes] = sums[f].reshape(SB, LANES).astype(BF16)
             return carry
 
         lax.fori_loop(0, 2 * tiles * lane_tiles, step, 0, unroll=2)
@@ -148,7 +189,7 @@
         grid_spec=pltpu.PrefetchScalarGridSpec(
             num_scalar_prefetch=1,
             grid=(samples // block,),
-            in_specs=[pl.BlockSpec((taps.shape[0], block), lambda i, place: (0, i))]
+            in_specs=[pl.BlockSpec((taps.shape[0], 8, block), lambda i, place: (0, 0, i))]
             + [both, one, both, one, spec(far.shape[0], 0)]
             + [pl.BlockSpec(memory_space=pl.ANY)] * len(earlier),
             out_specs=[spec(frames, 0)] * 2,
@@ -199,7 +240,8 @@
     )(place, own_back, other_back, *earlier)
 
 
-def weight_kernel(table, index, mask, out):
+def weight_kernel(table, index, mask, *rest):
+    out = rest[-1]
     groups, depth, width = out.shape
     beams = width // 2
     half = depth // 2
@@ -208,87 +250,120 @@
         hit = jnp.where((rows == index[q : q + 1, :]) & (mask[q : q + 1, :] != 0), 1.0, 0.0).astype(BF16)
         picked = lax.dot_general(table[...], hit, (((0,), (0,)), ((), ())), preferred_element_type=F32)
         picked = picked.reshape(groups, 2, SB, beams)
-        low = q * SB
+        low = q % 2 * half + q // 2 * SB
         re, im = picked[:, 0], picked[:, 1]
         out[:, low : low + SB, :beams] = re.astype(BF16)
         out[:, low : low + SB, beams:] = im.astype(BF16)
-        out[:, half + low : half + low + SB, :beams] = (-im).astype(BF16)
-        out[:, half + low : half + low + SB, beams:] = re.astype(BF16)
-
-
-def beam_weights(table, index, mask):
+        low += half // 2
+        out[:, low : low + SB, :beams] = (-im).astype(BF16)
+        out[:, low : low + SB, beams:] = re.astype(BF16)
+
+
+def beam_weights(table, index, mask, earlier):
     blocks, beams = index.shape
     groups = table.shape[1] // (2 * SB)
     shape = (groups, 2 * blocks * SB, 2 * beams)
     return pl.pallas_call(
         weight_kernel,
         out_shape=jax.ShapeDtypeStruct(shape, BF16),
+        in_specs=[pl.BlockSpec(memory_space=pltpu.VMEM)] * 3 + [pl.BlockSpec(memory_space=pl.ANY)] * len(earlier),
         compiler_params=pltpu.CompilerParams(vmem_limit_bytes=VMEM_LIMIT),
         cost_estimate=cost(4),
         name="weights",
-    )(table, index, mask)
-
-
-def beam_kernel(source_count, has_earlier, *refs):
+    )(table, index, mask, *earlier)
+
+
+def transform(sources, table, mixed, spectra):
+    frames = sources[0].shape[0]
+    station_count = sum(ref.shape[2] for ref in sources)
+    groups = spectra.shape[0]
+    rows_of = table.shape[2] // 2 // groups
+
+    low = 0
+    for ref in sources:
+        tiles = ref.shape[2] // SB
+
+        def radix(i, carry, ref=ref, low=low, tiles=tiles):
+            f, rows = i // tiles, pl.ds(pl.multiple_of(i % tiles * SB, SB), SB)
+            values = [
+                tuple(ref[f, part, rows, a * LANES : (a + 1) * LANES].astype(F32) for part in range(2))
+                for a in range(RADIX)
+            ]
+            target = pl.ds(pl.multiple_of(f * station_count + low + i % tiles * SB, SB), SB)
+            for b, (re, im) in enumerate(sixteen_points(values)):
+                mixed[b, target, :LANES] = re.astype(BF16)
+                mixed[b, target, LANES:] = im.astype(BF16)
+            return carry
+
+        lax.fori_loop(0, frames * tiles, radix, 0)
+        low += ref.shape[2]
+
+    def step(b, carry):
+        product = lax.dot_general(table[0, b], mixed[b], (((1,), (1,)), ((), ())), preferred_element_type=F32)
+        product = product.reshape(2, groups, rows_of, frames * station_count)
+        value = [
+            jnp.concatenate([product[part, :, :, f * station_count : (f + 1) * station_count] for f in range(frames)], axis=1)
+            for part in range(2)
+        ]
+        spectra[:, b] = jnp.concatenate(value, axis=2).astype(BF16)
+        return carry
+
+    lax.fori_loop(0, RADIX, step, 0, unroll=4)
+
+
+def spectra_kernel(place, *refs):
+    *sources, table, out, mixed = refs
+    transform(sources, table, mixed, out)
+
+
+def spectra_shape(sources, channels, groups):
+    frames = sources[0].shape[0]
+    return (groups, RADIX, frames * channels // groups // RADIX, 2 * sum(s.shape[2] for s in sources))
+
+
+def mixed_shape(sources):
+    return (RADIX, sources[0].shape[0] * sum(s.shape[2] for s in sources), 2 * LANES)
+
+
+def station_spectra(place, sources, table, channels, groups):
+    shape = spectra_shape(sources, channels, groups)
+    return pl.pallas_call(
+        spectra_kernel,
+        out_shape=jax.ShapeDtypeStruct(shape, BF16),
+        grid_spec=pltpu.PrefetchScalarGridSpec(
+            num_scalar_prefetch=1,
+            grid=(1,),
+            in_specs=[pl.BlockSpec(s.shape, lambda i, place: (0, 0, 0, 0)) for s in sources]
+            + [pl.BlockSpec((1,) + table.shape[1:], lambda i, place: (place[1], 0, 0, 0))],
+            out_specs=pl.BlockSpec(shape, lambda i, place: (0, 0, 0, 0)),
+            scratch_shapes=[pltpu.VMEM(mixed_shape(sources), BF16)],
+        ),
+        compiler_params=pltpu.CompilerParams(vmem_limit_bytes=VMEM_LIMIT),
+        cost_estimate=cost(5),
+        name="spectra",
+    )(place, *sources, table)
+
+
+def beam_kernel(source_count, has_earlier, place, first, *refs):
     refs = list(refs)
-    refs.pop(0)
     sources = [refs.pop(0) for _ in range(source_count)]
     table, weights = refs.pop(0), refs.pop(0)
     earlier = refs.pop(0) if has_earlier else None
-    out, mixed, spectra = refs[:3]
+    out, mixed, second = refs[:3]
     step = pl.program_id(0)
     frames = sources[0].shape[0]
-    station_count = sum(ref.shape[2] for ref in sources)
-    groups = spectra.shape[0]
     beams = weights.shape[2] // 2
-    rows_of = table.shape[2] // 2 // groups
-    pair = 2
+    rows_of = first.shape[2] // frames
     lane_tiles = beams // LANES
     per_channel = lane_tiles * frames
 
     @pl.when(step == 0)
     def _():
-        low = 0
-        for ref in sources:
-            tiles = ref.shape[2] // SB
-
-            def radix(i, carry, ref=ref, low=low, tiles=tiles):
-                f, rows = i // tiles, pl.ds(pl.multiple_of(i % tiles * SB, SB), SB)
-                values = [
-                    tuple(ref[f, part, rows, a * LANES : (a + 1) * LANES].astype(F32) for part in range(2))
-                    for a in range(RADIX)
-                ]
-                target = pl.ds(pl.multiple_of(f * station_count + low + i % tiles * SB, SB), SB)
-                for b, (re, im) in enumerate(sixteen_points(values)):
-                    mixed[b, target, :LANES] = re.astype(BF16)
-                    mixed[b, target, LANES:] = im.astype(BF16)
-                return carry
-
-            lax.fori_loop(0, frames * tiles, radix, 0)
-            low += ref.shape[2]
-
-        def transform(b, carry):
-            for start in range(0, frames, pair):
-                product = lax.dot_general(
-                    table[0, b],
-                    mixed[b, start * station_count : (start + pair) * station_count],
-                    (((1,), (1,)), ((), ())),
-                    preferred_element_type=F32,
-                )
-                product = product.reshape(2, groups, rows_of, pair * station_count)
-                rows = slice(start * rows_of, (start + pair) * rows_of)
-                for part in range(2):
-                    value = jnp.concatenate(
-                        [product[part, :, :, f * station_count : (f + 1) * station_count] for f in range(pair)], axis=1
-                    )
-                    columns = slice(part * station_count, (part + 1) * station_count)
-                    spectra[:, b, rows, columns] = value.astype(BF16)
-            return carry
-
-        lax.fori_loop(0, RADIX, transform, 0, unroll=4)
+        transform(sources, table, mixed, second)
 
     for k in range(weights.shape[0]):
-        rows = spectra[step * weights.shape[0] + k].reshape(RADIX * frames * rows_of, 2 * station_count)
+        rows = jnp.concatenate([first[k], second[step * weights.shape[0] + k]], axis=2)
+        rows = rows.reshape(RADIX * frames * rows_of, rows.shape[2])
         beam = jnp.dot(rows, weights[k], preferred_element_type=F32)
         re, im = beam[:, :beams], beam[:, beams:]
         power = re * re + im * im
@@ -316,24 +391,21 @@
         lax.fori_loop(0, out.shape[0], finish, 0, unroll=8)
 
 
-def beam_power(place, sources, table, weights, earlier, channels):
+def beam_power(place, first, sources, table, weights, earlier, channels):
     frames, _, _, samples = sources[0].shape
     groups, depth, width = weights.shape
     beams = width // 2
-    station_count = sum(s.shape[2] for s in sources)
     at_once = 2
     flat = (groups, channels // groups * frames, beams)
     flat_spec = pl.BlockSpec((at_once,) + flat[1:], lambda i, place: (i, 0, 0))
-    in_specs = [pl.BlockSpec(s.shape, lambda i, place: (0, 0, 0, 0)) for s in sources]
+    in_specs = [pl.BlockSpec((at_once,) + first.shape[1:], lambda i, place: (i, 0, 0, 0))]
+    in_specs += [pl.BlockSpec(s.shape, lambda i, place: (0, 0, 0, 0)) for s in sources]
     in_specs += [
         pl.BlockSpec((1,) + table.shape[1:], lambda i, place: (place[1], 0, 0, 0)),
         pl.BlockSpec((at_once, depth, width), lambda i, place: (i, 0, 0)),
     ]
-    operands = list(sources) + [table, weights]
-    scratch = [
-        pltpu.VMEM((RADIX, frames * station_count, 2 * LANES), BF16),
-        pltpu.VMEM((groups, RADIX, frames * channels // groups // RADIX, 2 * station_count), BF16),
-    ]
+    operands = [first] + list(sources) + [table, weights]
+    scratch = [pltpu.VMEM(mixed_shape(sources), BF16), pltpu.VMEM(spectra_shape(sources, channels, groups), BF16)]
     if earlier is None:
         out_shape = jax.ShapeDtypeStruct(flat, F32)
         out_spec = flat_spec
@@ -381,6 +453,14 @@
     def swap(block):
         return lax.ppermute(block, "stn", [(0, 1), (1, 0)])
 
+    def laid(block):
+        return jnp.moveaxis(block, 0, -2)
+
+    quarter = half // 2
+    cuts = [(pol, 0, half) for pol in range(pols)]
+    own, *other = split(place, voltages, cuts)
+    own, other = laid(own), [pair(laid(block)) for block in other]
+
     columns = weight_blocks.shape[1] // CORES
     shard = lax.dynamic_slice_in_dim(weight_blocks, core * columns, columns, 1)
     shard = jnp.concatenate([shard, pair(shard)])
@@ -388,13 +468,6 @@
         lax.ppermute(shard, "tm", [(i, i ^ far) for i in range(time_devices)]) for far in range(2, time_devices, 2)
     ]
 
-    other = [lax.dynamic_slice_in_dim(voltages, half * (1 - side), half, 0)[:, p].transpose(1, 2, 0, 3) for p in range(pols)]
-    own = lax.dynamic_slice_in_dim(voltages, half * side, half, 0).transpose(1, 2, 3, 0, 4)
-    other, own, shards = lax.optimization_barrier((other, own, shards))
-    other = [pair(block) for block in other]
-    own_back = hop(own)
-    other_back = [hop(block) for block in other]
-
     def ordered(rows):
         rows = rows.T.reshape(2, 2, 2, -1)
         rows = flipped(rows, core)
@@ -402,35 +475,32 @@
         return rows.reshape(8, -1)
 
     index = block_index ^ (lax.axis_index("tm") * weight_blocks.shape[0])
-    weights = beam_weights(jnp.concatenate(shards), ordered(index), ordered(use_mask))
+    weights = beam_weights(jnp.concatenate(shards), ordered(index), ordered(use_mask), other)
     table = jnp.asarray(dft_tables(samples))
-
-    chunks = [(pol, low, half // 2) for pol in range(pols) for low in (0, half // 2)]
-    further = [
-        onward(place, own_back, other_back[pol], pol, low, size, history - 2 * frames, other_back)
-        for pol, low, size in chunks
-    ]
+    taps = jnp.broadcast_to(filter_taps[:, None, :], (history + 1, 8, samples))
+
+    own_back = hop(own)
+    other_back = [hop(other[0])]
+    chunks = [(pol, low) for pol in range(pols) for low in (0, quarter)]
+    further = []
+    for pol, low in chunks:
+        if pol >= len(other_back):
+            other_back.append(hop(after(other[pol], further[0])))
+        further.append(onward(place, own_back, other_back[pol], pol, low, quarter, history - 2 * frames, [weights]))
     far = [hop(block, 2) for block in further]
-    keeps, sends = [], []
-    for (pol, low, _), block in zip(chunks, far):
-        earlier = keeps[-1:] if keeps else further[1:] + [weights]
+    keeps, sents, power = [], [], None
+    for k, (pol, low) in enumerate(chunks):
+        earlier = sents[-1:] + ([power] if k == len(chunks) - 1 else [])
         keep, send = filter_frames(
-            place, filter_taps, own, other[pol], own_back, other_back[pol], block, pol, low, earlier
+            place, taps, own, other[pol], own_back, other_back[pol], far[k], pol, low, earlier
         )
         keeps.append(keep)
-        sends.append(send)
-    sents = [pair(block) for block in sends]
-    sents[:2] = [after(block, keeps[-1]) for block in sents[:2]]
-
-    def power_of(pol, earlier):
-        here = [i for i, chunk in enumerate(chunks) if chunk[0] == pol]
-        sources = [keeps[i] for i in here] + [sents[i] for i in here]
-        sources += [swap(block) for block in sources]
-        return beam_power(place, sources, table, weights, earlier, samples // CORES)
-
-    power = power_of(0, None)
-    sents[-1] = after(sents[-1], power)
-    return power_of(1, power)
+        sents.append(pair(send))
+        if k % 2 == 1:
+            sources = [[keeps[i], sents[i], swap(keeps[i]), swap(sents[i])] for i in (k - 1, k)]
+            first = station_spectra(place, sources[0], table, samples // CORES, weights.shape[0])
+            power = beam_power(place, first, sources[1], table, weights, power, samples // CORES)
+    return power
 
 
 def solution(mesh):

time: 241 us -> 257 us (1.066)
  Pallas kernels: 63.8 us -> 78.4 us
  starting transfers between devices: 52.9 us -> 43.8 us
  waiting for transfers between devices: 100 us -> 107 us
  local copies, waits for them, and re-layouts: 20.8 us -> 25.1 us
    ppermute x3, waiting for transfers between devices: 0.01 us -> 27.2 us  [body(): lax.ppermute(shard, 'tm', [(i, i ^ far) for i in range(time_devices)])]
    ppermute x7, waiting for transfers between devices: 62.7 us -> 35.8 us  [hop(): lax.ppermute(block, 'tm', [(i, i + 2) for i in range(skip, time_devices -...]
    pallas_call x0 -> x3, Pallas kernels: none -> 17.5 us  [the longest x2 13.2 us: station_spectra(): pl.pallas_call(spectra_kernel, out_shape=jax.ShapeDtypeStruct(shape, BF16...]
    ppermute x8, starting transfers between devices: 22.6 us -> 12.4 us  [swap(): return lax.ppermute(block, 'stn', [(0, 1), (1, 0)])]
    ppermute x7, waiting for transfers between devices: 35.8 us -> 43.9 us  [pair(): return lax.ppermute(block, 'tm', [(i, i ^ 1) for i in range(time_devices)])]
    pallas_call x0 -> x3, local copies, waits for them, and re-layouts: none -> 6.96 us  [split(): pl.pallas_call(functools.partial(split_kernel, cuts), out_shape=[jax.Shap...]
    unnamed x51 -> x67, local copies, waits for them, and re-layouts: 10.7 us -> 15.8 us
    dynamic_slice x2 -> x0, local copies, waits for them, and re-layouts: 3.38 us -> none  [the longest x1 3.38 us: body(): lax.dynamic_slice_in_dim(voltages, half * side, half, 0)]
  transfers between devices with their start and end apart: 25 -> 25, of which waited for: 8 -> 8; matrix products, arithmetic and copies ran while one was open for 6% -> 3% of each run, Pallas kernels for 20% -> 21%
where the time goes in v3:
time: 257 us; the launch traced here: 255 us
  waiting for transfers between devices  107 us (42%)
  Pallas kernels  78.4 us (31%)
  starting transfers between devices  43.8 us (17%)
  local copies, waits for them, and re-layouts  25.1 us (10%)
    ppermute x7, waiting for transfers between devices, pair(): return lax.ppermute(block, 'tm', [(i, i ^ 1) for i in range(time_devices)])  43.9 us
    ppermute x7, waiting for transfers between devices, hop(): lax.ppermute(block, 'tm', [(i, i + 2) for i in range(skip, time_devices -...  35.8 us
    ppermute x3, waiting for transfers between devices, body(): lax.ppermute(shard, 'tm', [(i, i ^ far) for i in range(time_devices)])  27.2 us
    pallas_call x4, Pallas kernels, filter_frames(): pl.pallas_call(filter_kernel, out_shape=(shape, shape), grid_spec=pltpu.P...  24.8 us
    ppermute x7, starting transfers between devices, hop(): lax.ppermute(block, 'tm', [(i, i + 2) for i in range(skip, time_devices -...  24.7 us
    pallas_call x2, Pallas kernels, beam_power(): pl.pallas_call(functools.partial(beam_kernel, len(sources), earlier is no...  22.6 us
    unnamed x67, local copies, waits for them, and re-layouts  15.8 us
    pallas_call x2, Pallas kernels, station_spectra(): pl.pallas_call(spectra_kernel, out_shape=jax.ShapeDtypeStruct(shape, BF16...  13.2 us
  transfers between devices with their start and end apart: 25, of which 8 were waited for; matrix products, arithmetic and copies ran while one was open for 3% of the time, Pallas kernels for 21%

profile of v3, /device:TPU:17, one launch (start us, length us, event | category | flops | bytes accessed | tf_op | source)
XLA Modules:
  0.0 255.1 jit_solution(17698465177962372426)
XLA Ops:
  0.6 4.3 %split.1 = (bf16[32,2,4,2,2048]{4,3,2,1,0:T(2,128)(2,1)}, bf16[32,4,2,2048]{3,2,1,0:T(2,128)(2,1)}, bf16[32,4,2,2048]{3,2,1,0:T(2,128)(2,1)}) custom-call(s32[2]{0:T(128)} %pad_add_fusion.place, bf16[64,2,4,2,2048]{4,3,2,1,0:T(2,128)(2,1)} %voltages.1), custom_call_target="tpu_custom_call" | custom-call | bytes 9900000 | tf_op jit(solution)/shard_map/split/pallas_call | solution.py:114
  4.9 2.9 %copy.15 = bf16[32,4,2,2048]{3,0,2,1:T(8,128)(2,1)} copy(bf16[32,4,2,2048]{3,2,1,0:T(2,128)(2,1)} %get-tuple-element.18) | data formatting | bytes 2097152 | tf_op jit(solution)/shard_map/split/pallas_call | solution.py:114
  11.5 3.3 %collective-permute-start.1 = (bf16[2,4,2,32,2048]{4,3,2,1,0:T(8,128)(2,1)}, bf16[2,4,2,32,2048]{4,3,2,1,0:T(8,128)(2,1)S(1)}, u32[]{:S(2)}, u32[]{:S(2)}) collective-permute-start(bf16[2,4,2,32,2048]{4,3,2,1,0:T(8,128)(2,1)} %bitcast.19.own), channel_id=1, source_target_pairs={{0,4},{2,6},{4,8},{6,10},{8,12},{10,14},{1,5},{3,7},{5,9},{7,11},{... | collective-permute-start | bytes 6291464 | tf_op jit(solution)/shard_map/ppermute | solution.py:451
  18.0 14.2 %collective-permute-done.2.rest_0_.other = bf16[4,2,32,2048]{3,2,1,0:T(8,128)(2,1)} collective-permute-done((bf16[4,2,32,2048]{3,2,1,0:T(8,128)(2,1)}, bf16[4,2,32,2048]{3,2,1,0:T(8,128)(2,1)}, u32[]{:S(2)}, u32[]{:S(2)}) %collective-permute-start.2) | collective-permute-done | bytes 1048608 | tf_op jit(solution)/shard_map/ppermute | solution.py:448
  32.2 3.2 %collective-permute-start.3 = (bf16[4,2,32,2048]{3,2,1,0:T(8,128)(2,1)}, bf16[4,2,32,2048]{3,2,1,0:T(8,128)(2,1)}, u32[]{:S(2)}, u32[]{:S(2)}) collective-permute-start(bf16[4,2,32,2048]{3,2,1,0:T(8,128)(2,1)} %collective-permute-done.2.rest_0_.other), channel_id=1, source_target_pairs={{0,4},{2,6},{4,8},{6,10},{8,12},{10,14},{1,5},{3,7},{5,9},{7,11},{... | collective-permute-start | bytes 3145736 | tf_op jit(solution)/shard_map/ppermute | solution.py:451
  36.6 18.1 %collective-permute-done.4 = bf16[16,256]{1,0:T(8,128)(2,1)S(1)} collective-permute-done((bf16[16,256]{1,0:T(8,128)(2,1)S(1)}, bf16[16,256]{1,0:T(8,128)(2,1)S(1)}, u32[]{:S(2)}, u32[]{:S(2)}) %collective-permute-start.4) | collective-permute-done | bytes 8224 | tf_op jit(solution)/shard_map/ppermute | solution.py:448
  56.1 25.8 %collective-permute-done.5 = bf16[32,256]{1,0:T(8,128)(2,1)S(1)} collective-permute-done((bf16[32,256]{1,0:T(8,128)(2,1)S(1)}, bf16[32,256]{1,0:T(8,128)(2,1)S(1)}, u32[]{:S(2)}, u32[]{:S(2)}) %collective-permute-start.5) | collective-permute-done | bytes 16416 | tf_op jit(solution)/shard_map/ppermute | solution.py:468
  92.9 6.2 %collective-permute-start.11 = (bf16[7,2,16,2048]{3,2,1,0:T(8,128)(2,1)}, bf16[7,2,16,2048]{3,2,1,0:T(8,128)(2,1)S(1)}, u32[]{:S(2)}, u32[]{:S(2)}) collective-permute-start(bf16[7,2,16,2048]{3,2,1,0:T(8,128)(2,1)} %onward.4.refs_1_), channel_id=1, source_target_pairs={{4,8},{6,10},{8,12},{10,14},{5,9},{7,11},{9,13},{11,15},{20,24},{2... | collective-permute-start | bytes 2752520 | tf_op jit(solution)/shard_map/ppermute | solution.py:451
  106.7 9.2 %collective-permute-done.11.far = bf16[7,2,16,2048]{3,2,1,0:T(8,128)(2,1)S(1)} collective-permute-done((bf16[7,2,16,2048]{3,2,1,0:T(8,128)(2,1)}, bf16[7,2,16,2048]{3,2,1,0:T(8,128)(2,1)S(1)}, u32[]{:S(2)}, u32[]{:S(2)}) %collective-permute-start.11) | collective-permute-done | bytes 917536 | tf_op jit(solution)/shard_map/ppermute | solution.py:451
  117.2 6.2 %filter.4 = (bf16[4,2,16,2048]{3,2,1,0:T(8,128)(2,1)}, bf16[4,2,16,2048]{3,2,1,0:T(8,128)(2,1)}) custom-call(s32[2]{0:T(128)} %pad_add_fusion.place, f32[16,8,2048]{2,1,0:T(8,128)} %broadcast_in_dim.2.taps, bf16[2,4,2,32,2048]{4,3,2,1,0:T(8,128)(2,1)} %bitcast.19.own, bf16[4,2,32,2048]{3,2,1,0:T(8,128)(2,1)} %collective-permute-done.2.rest_0_.other, ...), custom_call_target="tpu_custom_call" | custom-call | bytes 13200000 | tf_op jit(solution)/shard_map/filter/pallas_call | solution.py:186
  123.5 14.8 %collective-permute-done.8.other_back = bf16[4,2,32,2048]{3,2,1,0:T(8,128)(2,1)S(1)} collective-permute-done((bf16[4,2,32,2048]{3,2,1,0:T(8,128)(2,1)}, bf16[4,2,32,2048]{3,2,1,0:T(8,128)(2,1)S(1)}, u32[]{:S(2)}, u32[]{:S(2)}) %collective-permute-start.8) | collective-permute-done | bytes 1048608 | tf_op jit(solution)/shard_map/ppermute | solution.py:451
  139.4 2.8 %onward.5 = bf16[7,2,16,2048]{3,2,1,0:T(8,128)(2,1)} custom-call(s32[2]{0:T(128)} %pad_add_fusion.place, bf16[2,4,2,32,2048]{4,3,2,1,0:T(8,128)(2,1)} %copy-done, bf16[4,2,32,2048]{3,2,1,0:T(8,128)(2,1)} %copy-done.1, bf16[8,256,512]{2,1,0:T(8,128)(2,1)} %weights.1.rest_0_.refs_5_), custom_call_target="tpu_custom_call" | custom-call | bytes 4950000 | tf_op jit(solution)/shard_map/onward/pallas_call | solution.py:224
  142.1 4.1 %collective-permute-start.9 = (bf16[7,2,16,2048]{3,2,1,0:T(8,128)(2,1)}, bf16[7,2,16,2048]{3,2,1,0:T(8,128)(2,1)S(1)}, u32[]{:S(2)}, u32[]{:S(2)}) collective-permute-start(bf16[7,2,16,2048]{3,2,1,0:T(8,128)(2,1)} %onward.5), channel_id=1, source_target_pairs={{4,8},{6,10},{8,12},{10,14},{5,9},{7,11},{9,13},{11,15},{20,24},{2... | collective-permute-start | bytes 2752520 | tf_op jit(solution)/shard_map/ppermute | solution.py:451
  146.2 11.8 %collective-permute-done.10.far = bf16[7,2,16,2048]{3,2,1,0:T(8,128)(2,1)S(1)} collective-permute-done((bf16[7,2,16,2048]{3,2,1,0:T(8,128)(2,1)}, bf16[7,2,16,2048]{3,2,1,0:T(8,128)(2,1)S(1)}, u32[]{:S(2)}, u32[]{:S(2)}) %collective-permute-start.10) | collective-permute-done | bytes 917536 | tf_op jit(solution)/shard_map/ppermute | solution.py:451
  159.8 6.2 %filter.5 = (bf16[4,2,16,2048]{3,2,1,0:T(8,128)(2,1)}, bf16[4,2,16,2048]{3,2,1,0:T(8,128)(2,1)}) custom-call(s32[2]{0:T(128)} %pad_add_fusion.place, f32[16,8,2048]{2,1,0:T(8,128)} %broadcast_in_dim.2.taps, bf16[2,4,2,32,2048]{4,3,2,1,0:T(8,128)(2,1)} %bitcast.19.own, bf16[4,2,32,2048]{3,2,1,0:T(8,128)(2,1)} %collective-permute-done.2.rest_0_.other, ...), custom_call_target="tpu_custom_call" | custom-call | bytes 13200000 | tf_op jit(solution)/shard_map/filter/pallas_call | solution.py:186
  166.2 7.9 %collective-permute-start.18 = (bf16[4,2,16,2048]{3,2,1,0:T(8,128)(2,1)S(1)}, bf16[4,2,16,2048]{3,2,1,0:T(8,128)(2,1)S(1)}, u32[]{:S(2)}, u32[]{:S(2)}) collective-permute-start(bf16[4,2,16,2048]{3,2,1,0:T(8,128)(2,1)S(1)} %copy-done.20), channel_id=1, source_target_pairs={{0,1},{1,0},{2,3},{3,2},{4,5},{5,4},{6,7},{7,6},{8,9},{9,8},{10,11... | collective-permute-start | bytes 1572872 | tf_op jit(solution)/shard_map/ppermute | solution.py:454
  176.8 4.0 %collective-permute-start.17 = (bf16[7,2,16,2048]{3,2,1,0:T(8,128)(2,1)}, bf16[7,2,16,2048]{3,2,1,0:T(8,128)(2,1)S(1)}, u32[]{:S(2)}, u32[]{:S(2)}) collective-permute-start(bf16[7,2,16,2048]{3,2,1,0:T(8,128)(2,1)} %onward.7), channel_id=1, source_target_pairs={{4,8},{6,10},{8,12},{10,14},{5,9},{7,11},{9,13},{11,15},{20,24},{2... | collective-permute-start | bytes 2752520 | tf_op jit(solution)/shard_map/ppermute | solution.py:451
  184.0 6.2 %filter.6 = (bf16[4,2,16,2048]{3,2,1,0:T(8,128)(2,1)}, bf16[4,2,16,2048]{3,2,1,0:T(8,128)(2,1)}) custom-call(s32[2]{0:T(128)} %pad_add_fusion.place, f32[16,8,2048]{2,1,0:T(8,128)} %broadcast_in_dim.2.taps, bf16[2,4,2,32,2048]{4,3,2,1,0:T(8,128)(2,1)} %bitcast.19.own, bf16[4,2,32,2048]{3,2,1,0:T(8,128)(2,1)} %copy-done.2, ...), custom_call_target="tpu_custom_call" | custom-call | bytes 13200000 | tf_op jit(solution)/shard_map/filter/pallas_call | solution.py:186
  191.8 6.6 %spectra.3.first = bf16[8,16,32,128]{3,2,1,0:T(8,128)(2,1)} custom-call(s32[2]{0:T(128)} %pad_add_fusion.place, bf16[4,2,16,2048]{3,2,1,0:T(8,128)(2,1)} %get-tuple-element.23.refs_0_, bf16[4,2,16,2048]{3,2,1,0:T(8,128)(2,1)} %copy-done.6, bf16[4,2,16,2048]{3,2,1,0:T(8,128)(2,1)} %copy-done.22, bf16[4,2,16,2048]{3,2,1,0:T(8,128)(2,1)} %copy-done.23, ...), custom_call_target="tpu_custom_call" | custom-call | bytes 16500000 | tf_op jit(solution)/shard_map/spectra/pallas_call | solution.py:330
  200.1 9.9 %beams.2.rest_1_.refs_6_ = f32[8,512,256]{2,1,0:T(8,128)} custom-call(s32[2]{0:T(128)} %pad_add_fusion.place, bf16[8,16,32,128]{3,2,1,0:T(8,128)(2,1)} %spectra.3.first, bf16[4,2,16,2048]{3,2,1,0:T(8,128)(2,1)} %get-tuple-element.24.refs_0_, bf16[4,2,16,2048]{3,2,1,0:T(8,128)(2,1)} %copy-done.4, bf16[4,2,16,2048]{3,2,1,0:T(8,128)(2,1)} %copy-done.16, ...), custom_call_target="tpu_custom_call" | custom-call | tf_op jit(solution)/shard_map/beams/pallas_call | solution.py:418
  211.8 6.2 %filter.7 = (bf16[4,2,16,2048]{3,2,1,0:T(8,128)(2,1)}, bf16[4,2,16,2048]{3,2,1,0:T(8,128)(2,1)}) custom-call(s32[2]{0:T(128)} %pad_add_fusion.place, f32[16,8,2048]{2,1,0:T(8,128)} %broadcast_in_dim.2.taps, bf16[2,4,2,32,2048]{4,3,2,1,0:T(8,128)(2,1)} %bitcast.19.own, bf16[4,2,32,2048]{3,2,1,0:T(8,128)(2,1)} %copy-done.2, ...), custom_call_target="tpu_custom_call" | custom-call | bytes 13200000 | tf_op jit(solution)/shard_map/filter/pallas_call | solution.py:186
  220.0 11.6 %collective-permute-done.22.refs_1_ = bf16[4,2,16,2048]{3,2,1,0:T(8,128)(2,1)S(1)} collective-permute-done((bf16[4,2,16,2048]{3,2,1,0:T(8,128)(2,1)}, bf16[4,2,16,2048]{3,2,1,0:T(8,128)(2,1)S(1)}, u32[]{:S(2)}, u32[]{:S(2)}) %collective-permute-start.22) | collective-permute-done | bytes 524320 | tf_op jit(solution)/shard_map/ppermute | solution.py:448
  234.2 6.6 %spectra.2.first = bf16[8,16,32,128]{3,2,1,0:T(8,128)(2,1)} custom-call(s32[2]{0:T(128)} %pad_add_fusion.place, bf16[4,2,16,2048]{3,2,1,0:T(8,128)(2,1)} %get-tuple-element.21.refs_0_, bf16[4,2,16,2048]{3,2,1,0:T(8,128)(2,1)} %copy-done.8, bf16[4,2,16,2048]{3,2,1,0:T(8,128)(2,1)} %copy-done.24, bf16[4,2,16,2048]{3,2,1,0:T(8,128)(2,1)} %copy-done.25, ...), custom_call_target="tpu_custom_call" | custom-call | bytes 16500000 | tf_op jit(solution)/shard_map/spectra/pallas_call | solution.py:330
  242.5 12.6 %beams.3 = f32[1024,4,256]{2,1,0:T(4,128)} custom-call(s32[2]{0:T(128)} %pad_add_fusion.place, bf16[8,16,32,128]{3,2,1,0:T(8,128)(2,1)} %spectra.2.first, bf16[4,2,16,2048]{3,2,1,0:T(8,128)(2,1)} %get-tuple-element.25.refs_0_, bf16[4,2,16,2048]{3,2,1,0:T(8,128)(2,1)} %copy-done.15, bf16[4,2,16,2048]{3,2,1,0:T(8,128)(2,1)} %copy-done.17, ...), custom_call_target="tpu_custom_call" | custom-call | tf_op jit(solution)/shard_map/beams/pallas_call | solution.py:418
  (123 shorter events, 50.2 us)
Async XLA Ops:
  7.8 24.3 %collective-permute-start.2 = (bf16[4,2,32,2048]{3,2,1,0:T(8,128)(2,1)}, bf16[4,2,32,2048]{3,2,1,0:T(8,128)(2,1)}, u32[]{:S(2)}, u32[]{:S(2)}) collective-permute-start(bf16[4,2,32,2048]{3,2,1,0:T(8,128)(2,1)} %bitcast.20), channel_id=1, source_target_pairs={{0,2},{2,0},{4,6},{6,4},{8,10},{10,8},{12,14},{14,12},{1,3},{3,1},... | collective-permute-start | bytes 3145736 | tf_op jit(solution)/shard_map/ppermute | solution.py:448
  11.5 77.2 %collective-permute-start.1 = (bf16[2,4,2,32,2048]{4,3,2,1,0:T(8,128)(2,1)}, bf16[2,4,2,32,2048]{4,3,2,1,0:T(8,128)(2,1)S(1)}, u32[]{:S(2)}, u32[]{:S(2)}) collective-permute-start(bf16[2,4,2,32,2048]{4,3,2,1,0:T(8,128)(2,1)} %bitcast.19.own), channel_id=1, source_target_pairs={{0,4},{2,6},{4,8},{6,10},{8,12},{10,14},{1,5},{3,7},{5,9},{7,11},{... | collective-permute-start | bytes 6291464 | tf_op jit(solution)/shard_map/ppermute | solution.py:451
  16.4 68.0 %collective-permute-start = (bf16[4,2,32,2048]{3,2,1,0:T(8,128)(2,1)}, bf16[4,2,32,2048]{3,2,1,0:T(8,128)(2,1)S(1)}, u32[]{:S(2)}, u32[]{:S(2)}) collective-permute-start(bf16[4,2,32,2048]{3,2,1,0:T(8,128)(2,1)} %bitcast.21), channel_id=1, source_target_pairs={{0,2},{2,0},{4,6},{6,4},{8,10},{10,8},{12,14},{14,12},{1,3},{3,1},... | collective-permute-start | bytes 3145736 | tf_op jit(solution)/shard_map/ppermute | solution.py:448
  16.7 38.0 %collective-permute-start.4 = (bf16[16,256]{1,0:T(8,128)(2,1)S(1)}, bf16[16,256]{1,0:T(8,128)(2,1)S(1)}, u32[]{:S(2)}, u32[]{:S(2)}) collective-permute-start(bf16[16,256]{1,0:T(8,128)(2,1)S(1)} %get-tuple-element.28), channel_id=1, source_target_pairs={{0,2},{2,0},{4,6},{6,4},{8,10},{10,8},{12,14},{14,12},{1,3},{3,1},... | collective-permute-start | bytes 24584 | tf_op jit(solution)/shard_map/ppermute | solution.py:448
  32.2 56.6 %collective-permute-start.3 = (bf16[4,2,32,2048]{3,2,1,0:T(8,128)(2,1)}, bf16[4,2,32,2048]{3,2,1,0:T(8,128)(2,1)}, u32[]{:S(2)}, u32[]{:S(2)}) collective-permute-start(bf16[4,2,32,2048]{3,2,1,0:T(8,128)(2,1)} %collective-permute-done.2.rest_0_.other), channel_id=1, source_target_pairs={{0,4},{2,6},{4,8},{6,10},{8,12},{10,14},{1,5},{3,7},{5,9},{7,11},{... | collective-permute-start | bytes 3145736 | tf_op jit(solution)/shard_map/ppermute | solution.py:451
  54.7 27.1 %collective-permute-start.5 = (bf16[32,256]{1,0:T(8,128)(2,1)S(1)}, bf16[32,256]{1,0:T(8,128)(2,1)S(1)}, u32[]{:S(2)}, u32[]{:S(2)}) collective-permute-start(bf16[32,256]{1,0:T(8,128)(2,1)S(1)} %pad_maximum_fusion), channel_id=1, source_target_pairs={{0,4},{2,6},{4,0},{6,2},{8,12},{10,14},{12,8},{14,10},{1,5},{3,7},... | collective-permute-start | bytes 49160 | tf_op jit(solution)/shard_map/ppermute | solution.py:468
  56.0 27.0 %collective-permute-start.6 = (bf16[32,256]{1,0:T(8,128)(2,1)S(1)}, bf16[32,256]{1,0:T(8,128)(2,1)S(1)}, u32[]{:S(2)}, u32[]{:S(2)}) collective-permute-start(bf16[32,256]{1,0:T(8,128)(2,1)S(1)} %pad_maximum_fusion), channel_id=1, source_target_pairs={{0,8},{2,10},{4,12},{6,14},{8,0},{10,2},{12,4},{14,6},{1,9},{3,11}... | collective-permute-start | bytes 49160 | tf_op jit(solution)/shard_map/ppermute | solution.py:468
  92.9 23.0 %collective-permute-start.11 = (bf16[7,2,16,2048]{3,2,1,0:T(8,128)(2,1)}, bf16[7,2,16,2048]{3,2,1,0:T(8,128)(2,1)S(1)}, u32[]{:S(2)}, u32[]{:S(2)}) collective-permute-start(bf16[7,2,16,2048]{3,2,1,0:T(8,128)(2,1)} %onward.4.refs_1_), channel_id=1, source_target_pairs={{4,8},{6,10},{8,12},{10,14},{5,9},{7,11},{9,13},{11,15},{20,24},{2... | collective-permute-start | bytes 2752520 | tf_op jit(solution)/shard_map/ppermute | solution.py:451
  100.1 38.3 %collective-permute-start.8 = (bf16[4,2,32,2048]{3,2,1,0:T(8,128)(2,1)}, bf16[4,2,32,2048]{3,2,1,0:T(8,128)(2,1)S(1)}, u32[]{:S(2)}, u32[]{:S(2)}) collective-permute-start(bf16[4,2,32,2048]{3,2,1,0:T(8,128)(2,1)} %after.1), channel_id=1, source_target_pairs={{0,4},{2,6},{4,8},{6,10},{8,12},{10,14},{1,5},{3,7},{5,9},{7,11},{... | collective-permute-start | bytes 3145736 | tf_op jit(solution)/shard_map/ppermute | solution.py:451
  104.8 53.2 %collective-permute-start.10 = (bf16[7,2,16,2048]{3,2,1,0:T(8,128)(2,1)}, bf16[7,2,16,2048]{3,2,1,0:T(8,128)(2,1)S(1)}, u32[]{:S(2)}, u32[]{:S(2)}) collective-permute-start(bf16[7,2,16,2048]{3,2,1,0:T(8,128)(2,1)} %onward.6), channel_id=1, source_target_pairs={{4,8},{6,10},{8,12},{10,14},{5,9},{7,11},{9,13},{11,15},{20,24},{2... | collective-permute-start | bytes 2752520 | tf_op jit(solution)/shard_map/ppermute | solution.py:451
  123.3 34.7 %collective-permute-start.12 = (bf16[4,2,16,2048]{3,2,1,0:T(8,128)(2,1)}, bf16[4,2,16,2048]{3,2,1,0:T(8,128)(2,1)S(1)}, u32[]{:S(2)}, u32[]{:S(2)}) collective-permute-start(bf16[4,2,16,2048]{3,2,1,0:T(8,128)(2,1)} %get-tuple-element.19), channel_id=1, source_target_pairs={{0,2},{2,0},{4,6},{6,4},{8,10},{10,8},{12,14},{14,12},{1,3},{3,1},... | collective-permute-start | bytes 1572872 | tf_op jit(solution)/shard_map/ppermute | solution.py:448
  142.1 40.9 %collective-permute-start.9 = (bf16[7,2,16,2048]{3,2,1,0:T(8,128)(2,1)}, bf16[7,2,16,2048]{3,2,1,0:T(8,128)(2,1)S(1)}, u32[]{:S(2)}, u32[]{:S(2)}) collective-permute-start(bf16[7,2,16,2048]{3,2,1,0:T(8,128)(2,1)} %onward.5), channel_id=1, source_target_pairs={{4,8},{6,10},{8,12},{10,14},{5,9},{7,11},{9,13},{11,15},{20,24},{2... | collective-permute-start | bytes 2752520 | tf_op jit(solution)/shard_map/ppermute | solution.py:451
  166.0 15.3 %collective-permute-start.13 = (bf16[4,2,16,2048]{3,2,1,0:T(8,128)(2,1)}, bf16[4,2,16,2048]{3,2,1,0:T(8,128)(2,1)S(1)}, u32[]{:S(2)}, u32[]{:S(2)}) collective-permute-start(bf16[4,2,16,2048]{3,2,1,0:T(8,128)(2,1)} %get-tuple-element.20), channel_id=1, source_target_pairs={{0,2},{2,0},{4,6},{6,4},{8,10},{10,8},{12,14},{14,12},{1,3},{3,1},... | collective-permute-start | bytes 1572872 | tf_op jit(solution)/shard_map/ppermute | solution.py:448
  166.2 24.0 %collective-permute-start.18 = (bf16[4,2,16,2048]{3,2,1,0:T(8,128)(2,1)S(1)}, bf16[4,2,16,2048]{3,2,1,0:T(8,128)(2,1)S(1)}, u32[]{:S(2)}, u32[]{:S(2)}) collective-permute-start(bf16[4,2,16,2048]{3,2,1,0:T(8,128)(2,1)S(1)} %copy-done.20), channel_id=1, source_target_pairs={{0,1},{1,0},{2,3},{3,2},{4,5},{5,4},{6,7},{7,6},{8,9},{9,8},{10,11... | collective-permute-start | bytes 1572872 | tf_op jit(solution)/shard_map/ppermute | solution.py:454
  176.8 33.2 %collective-permute-start.17 = (bf16[7,2,16,2048]{3,2,1,0:T(8,128)(2,1)}, bf16[7,2,16,2048]{3,2,1,0:T(8,128)(2,1)S(1)}, u32[]{:S(2)}, u32[]{:S(2)}) collective-permute-start(bf16[7,2,16,2048]{3,2,1,0:T(8,128)(2,1)} %onward.7), channel_id=1, source_target_pairs={{4,8},{6,10},{8,12},{10,14},{5,9},{7,11},{9,13},{11,15},{20,24},{2... | collective-permute-start | bytes 2752520 | tf_op jit(solution)/shard_map/ppermute | solution.py:451
  180.8 9.6 %collective-permute-start.19 = (bf16[4,2,16,2048]{3,2,1,0:T(8,128)(2,1)S(1)}, bf16[4,2,16,2048]{3,2,1,0:T(8,128)(2,1)S(1)}, u32[]{:S(2)}, u32[]{:S(2)}) collective-permute-start(bf16[4,2,16,2048]{3,2,1,0:T(8,128)(2,1)S(1)} %copy-done.7), channel_id=1, source_target_pairs={{0,1},{1,0},{2,3},{3,2},{4,5},{5,4},{6,7},{7,6},{8,9},{9,8},{10,11... | collective-permute-start | bytes 1572872 | tf_op jit(solution)/shard_map/ppermute | solution.py:454
  181.3 17.1 %collective-permute-start.20 = (bf16[4,2,16,2048]{3,2,1,0:T(8,128)(2,1)S(1)}, bf16[4,2,16,2048]{3,2,1,0:T(8,128)(2,1)S(1)}, u32[]{:S(2)}, u32[]{:S(2)}) collective-permute-start(bf16[4,2,16,2048]{3,2,1,0:T(8,128)(2,1)S(1)} %copy-done.14), channel_id=1, source_target_pairs={{0,1},{1,0},{2,3},{3,2},{4,5},{5,4},{6,7},{7,6},{8,9},{9,8},{10,11... | collective-permute-start | bytes 1572872 | tf_op jit(solution)/shard_map/ppermute | solution.py:454
  183.0 15.5 %collective-permute-start.21 = (bf16[4,2,16,2048]{3,2,1,0:T(8,128)(2,1)S(1)}, bf16[4,2,16,2048]{3,2,1,0:T(8,128)(2,1)S(1)}, u32[]{:S(2)}, u32[]{:S(2)}) collective-permute-start(bf16[4,2,16,2048]{3,2,1,0:T(8,128)(2,1)S(1)} %collective-permute-done.13.rest_0_.refs_1_), channel_id=1, source_target_pairs={{0,1},{1,0},{2,3},{3,2},{4,5},{5,4},{6,7},{7,6},{8,9},{9,8},{10,11... | collective-permute-start | bytes 1572872 | tf_op jit(solution)/shard_map/ppermute | solution.py:454
  190.2 19.8 %collective-permute-start.14 = (bf16[4,2,16,2048]{3,2,1,0:T(8,128)(2,1)}, bf16[4,2,16,2048]{3,2,1,0:T(8,128)(2,1)S(1)}, u32[]{:S(2)}, u32[]{:S(2)}) collective-permute-start(bf16[4,2,16,2048]{3,2,1,0:T(8,128)(2,1)} %get-tuple-element.22), channel_id=1, source_target_pairs={{0,2},{2,0},{4,6},{6,4},{8,10},{10,8},{12,14},{14,12},{1,3},{3,1},... | collective-permute-start | bytes 1572872 | tf_op jit(solution)/shard_map/ppermute | solution.py:448
  218.0 13.6 %collective-permute-start.22 = (bf16[4,2,16,2048]{3,2,1,0:T(8,128)(2,1)}, bf16[4,2,16,2048]{3,2,1,0:T(8,128)(2,1)S(1)}, u32[]{:S(2)}, u32[]{:S(2)}) collective-permute-start(bf16[4,2,16,2048]{3,2,1,0:T(8,128)(2,1)} %get-tuple-element.26), channel_id=1, source_target_pairs={{0,2},{2,0},{4,6},{6,4},{8,10},{10,8},{12,14},{14,12},{1,3},{3,1},... | collective-permute-start | bytes 1572872 | tf_op jit(solution)/shard_map/ppermute | solution.py:448
  218.7 13.8 %collective-permute-start.15 = (bf16[4,2,16,2048]{3,2,1,0:T(8,128)(2,1)S(1)}, bf16[4,2,16,2048]{3,2,1,0:T(8,128)(2,1)S(1)}, u32[]{:S(2)}, u32[]{:S(2)}) collective-permute-start(bf16[4,2,16,2048]{3,2,1,0:T(8,128)(2,1)S(1)} %copy-done.21), channel_id=1, source_target_pairs={{0,1},{1,0},{2,3},{3,2},{4,5},{5,4},{6,7},{7,6},{8,9},{9,8},{10,11... | collective-permute-start | bytes 1572872 | tf_op jit(solution)/shard_map/ppermute | solution.py:454
  219.5 13.1 %collective-permute-start.16 = (bf16[4,2,16,2048]{3,2,1,0:T(8,128)(2,1)}, bf16[4,2,16,2048]{3,2,1,0:T(8,128)(2,1)S(1)}, u32[]{:S(2)}, u32[]{:S(2)}) collective-permute-start(bf16[4,2,16,2048]{3,2,1,0:T(8,128)(2,1)} %copy-done.8), channel_id=1, source_target_pairs={{0,1},{1,0},{2,3},{3,2},{4,5},{5,4},{6,7},{7,6},{8,9},{9,8},{10,11... | collective-permute-start | bytes 1572872 | tf_op jit(solution)/shard_map/ppermute | solution.py:454
  219.5 21.3 %collective-permute-start.23 = (bf16[4,2,16,2048]{3,2,1,0:T(8,128)(2,1)}, bf16[4,2,16,2048]{3,2,1,0:T(8,128)(2,1)S(1)}, u32[]{:S(2)}, u32[]{:S(2)}) collective-permute-start(bf16[4,2,16,2048]{3,2,1,0:T(8,128)(2,1)} %get-tuple-element.25.refs_0_), channel_id=1, source_target_pairs={{0,1},{1,0},{2,3},{3,2},{4,5},{5,4},{6,7},{7,6},{8,9},{9,8},{10,11... | collective-permute-start | bytes 1572872 | tf_op jit(solution)/shard_map/ppermute | solution.py:454
  231.6 9.2 %collective-permute-start.24 = (bf16[4,2,16,2048]{3,2,1,0:T(8,128)(2,1)S(1)}, bf16[4,2,16,2048]{3,2,1,0:T(8,128)(2,1)S(1)}, u32[]{:S(2)}, u32[]{:S(2)}) collective-permute-start(bf16[4,2,16,2048]{3,2,1,0:T(8,128)(2,1)S(1)} %collective-permute-done.22.refs_1_), channel_id=1, source_target_pairs={{0,1},{1,0},{2,3},{3,2},{4,5},{5,4},{6,7},{7,6},{8,9},{9,8},{10,11... | collective-permute-start | bytes 1572872 | tf_op jit(solution)/shard_map/ppermute | solution.py:454
  (32 other events, 146.6 us)

commit v4 on v2

--- a/solution.py
+++ b/solution.py
@@ -80,83 +80,188 @@
         in_specs=[pl.BlockSpec(memory_space=pl.ANY)] * (1 + len(earlier)),
         out_specs=pl.BlockSpec(memory_space=pl.ANY),
         input_output_aliases={0: 0},
-        compiler_params=pltpu.CompilerParams(vmem_limit_bytes=VMEM_LIMIT),
         cost_estimate=cost(0),
         name="after",
     )(block, *earlier)
 
 
-def filter_kernel(place, taps, own, other, own_back, other_back, far, *rest):
-    keep, send = rest[-2:]
+def cut_kernel(mine, place, voltages, *rest):
+    outs, (buffer, loads, stores) = rest[-3 - len(mine) : -3], rest[-3:]
+    stations = buffer.shape[0]
+    pieces = loads.shape[0]
+    size = stations // pieces
+    start = jnp.where(place[0] == mine[0][0], 0, stations)
+
+    def load(k):
+        return pltpu.make_async_copy(
+            voltages.at[pl.ds(start + k * size, size)], buffer.at[pl.ds(k * size, size)], loads.at[k]
+        )
+
+    def store(k, i):
+        source = buffer.at[pl.ds(k * size, size)]
+        if mine[i][1] is not None:
+            source = source.at[:, mine[i][1]]
+        return pltpu.make_async_copy(source, outs[i].at[pl.ds(k * size, size)], stores.at[k, i])
+
+    every = [(k, i) for k in range(pieces) for i in range(len(mine))]
+    for k in range(pieces):
+        load(k).start()
+    for k in range(pieces):
+        load(k).wait()
+        for i in range(len(mine)):
+            store(k, i).start()
+    for k, i in every:
+        store(k, i).wait()
+
+
+def cut(place, voltages, mine, earlier=()):
+    stations, pols, frames, parts, samples = voltages.shape
+    half = stations // 2
+    pieces = 4
+    shapes = [(half,) + ((pols,) if pol is None else ()) + (frames, parts, samples) for _, pol in mine]
+    anywhere = pl.BlockSpec(memory_space=pl.ANY)
+    return pl.pallas_call(
+        functools.partial(cut_kernel, mine),
+        out_shape=[jax.ShapeDtypeStruct(shape, BF16) for shape in shapes],
+        in_specs=[pl.BlockSpec(memory_space=pltpu.SMEM), anywhere] + [anywhere] * len(earlier),
+        out_specs=[anywhere] * len(shapes),
+        scratch_shapes=[
+            pltpu.VMEM((half, pols, frames, parts, samples), BF16),
+            pltpu.SemaphoreType.DMA((pieces,)),
+            pltpu.SemaphoreType.DMA((pieces, len(mine))),
+        ],
+        compiler_params=pltpu.CompilerParams(vmem_limit_bytes=VMEM_LIMIT),
+        cost_estimate=cost(2),
+        name="cut",
+    )(place, voltages, *earlier)
+
+
+def weighted(taps, window, count, lanes, part, rows, sums):
     tap_count = taps.shape[0]
-    history = tap_count - 1
+    tap_rows = [taps[k, :, lanes][None] for k in range(tap_count)]
+    for j, ref, index in window:
+        value = ref[index, part, rows, lanes].astype(F32).reshape(SB // 8, 8, LANES)
+        for f in range(count):
+            k = f - j
+            if 0 <= k < tap_count:
+                term = tap_rows[k] * value
+                sums[f] = term if sums[f] is None else sums[f] + term
+    return sums
+
+
+def over_tiles(stations, samples, step):
+    tiles, lane_tiles = stations // SB, samples // LANES
+
+    def body(i, carry):
+        lanes = pl.ds(pl.multiple_of(i % lane_tiles * LANES, LANES), LANES)
+        rows = pl.ds(pl.multiple_of(i // (2 * lane_tiles) * SB, SB), SB)
+        step(lanes, i // lane_tiles % 2, rows)
+        return carry
+
+    lax.fori_loop(0, 2 * tiles * lane_tiles, body, 0, unroll=2)
+
+
+def near_kernel(place, taps, own, other, own_back, other_back, *rest):
+    partial = rest[-1]
     frames = own.shape[0]
     count = 2 * frames
-    stations, samples = own.shape[2:]
-    tiles = stations // SB
-    lane_tiles = samples // LANES
-
-    def run(first, second, first_back, second_back, first_out, second_out):
-        window = [(far, i) for i in range(far.shape[0])]
-        for ref in (first_back, second_back, first, second):
-            window += [(ref, i) for i in range(frames)]
-
-        def step(i, carry):
-            lanes = pl.ds(pl.multiple_of(i % lane_tiles * LANES, LANES), LANES)
-            part = i // lane_tiles % 2
-            rows = pl.ds(pl.multiple_of(i // (2 * lane_tiles) * SB, SB), SB)
-            tap_rows = [jnp.broadcast_to(taps[k : k + 1, lanes], (SB, LANES)) for k in range(tap_count)]
-            sums = [None] * count
-            for j, (ref, index) in enumerate(window):
-                value = ref[index, part, rows, lanes].astype(F32)
-                for f in range(count):
-                    k = f + history - j
-                    if 0 <= k <= history:
-                        term = tap_rows[k] * value
-                        sums[f] = term if sums[f] is None else sums[f] + term
+
+    def run(first, second, first_back, second_back):
+        window = []
+        for start, ref in ((-count, first_back), (frames - count, second_back), (0, first), (frames, second)):
+            window += [(start + i, ref, i) for i in range(frames)]
+
+        def step(lanes, part, rows):
+            sums = weighted(taps, window, count, lanes, part, rows, [None] * count)
+            for f in range(count):
+                partial[f, part, rows, lanes] = sums[f].reshape(SB, LANES)
+
+        over_tiles(*own.shape[2:], step)
+
+    @pl.when(place[0] == 0)
+    def _():
+        run(own, other, own_back, other_back)
+
+    @pl.when(place[0] == 1)
+    def _():
+        run(other, own, other_back, own_back)
+
+
+def far_kernel(place, taps, partial, far, *rest):
+    keep, send = rest[-2:]
+    frames = keep.shape[0]
+    count = 2 * frames
+    history = taps.shape[0] - 1
+
+    def run(first_out, second_out):
+        window = [(i - history, far, i) for i in range(far.shape[0])]
+
+        def step(lanes, part, rows):
+            sums = [partial[f, part, rows, lanes].reshape(SB // 8, 8, LANES) for f in range(count)]
+            sums = weighted(taps, window, count, lanes, part, rows, sums)
             for f in range(count):
                 out = first_out if f < frames else second_out
-                out[f % frames, part, rows, lanes] = sums[f].astype(BF16)
-            return carry
-
-        lax.fori_loop(0, 2 * tiles * lane_tiles, step, 0, unroll=2)
+                out[f % frames, part, rows, lanes] = sums[f].reshape(SB, LANES).astype(BF16)
+
+        over_tiles(*keep.shape[2:], step)
 
     @pl.when(place[0] == 0)
     def _():
-        run(own, other, own_back, other_back, keep, send)
+        run(keep, send)
 
     @pl.when(place[0] == 1)
     def _():
-        run(other, own, other_back, own_back, send, keep)
-
-
-def filter_frames(place, taps, own, other, own_back, other_back, far, pol, low, earlier=()):
-    frames, _, _, samples = other.shape
+        run(send, keep)
+
+
+def near_filter(place, taps, own, other, own_back, other_back, pol, earlier):
+    frames, parts, stations, samples = other.shape
+    block = 512
+    both = pl.BlockSpec((None, frames, parts, stations, block), lambda i, place: (pol, 0, 0, 0, i))
+    one = pl.BlockSpec((frames, parts, stations, block), lambda i, place: (0, 0, 0, i))
+    return pl.pallas_call(
+        near_kernel,
+        out_shape=jax.ShapeDtypeStruct((2 * frames, parts, stations, samples), F32),
+        grid_spec=pltpu.PrefetchScalarGridSpec(
+            num_scalar_prefetch=1,
+            grid=(samples // block,),
+            in_specs=[pl.BlockSpec((taps.shape[0], 8, block), lambda i, place: (0, 0, i)), both, one, both, one]
+            + [pl.BlockSpec(memory_space=pl.ANY)] * len(earlier),
+            out_specs=pl.BlockSpec((2 * frames, parts, stations, block), lambda i, place: (0, 0, 0, i)),
+        ),
+        compiler_params=pltpu.CompilerParams(vmem_limit_bytes=VMEM_LIMIT),
+        cost_estimate=cost(10),
+        name="near",
+    )(place, taps, own, other, own_back, other_back, *earlier)
+
+
+def far_filter(place, taps, partial, far, low, earlier):
+    count, parts, _, samples = partial.shape
     stations = far.shape[2]
     block = 512
-    where = low // stations
-
-    def spec(depth, station_block):
-        return pl.BlockSpec((depth, 2, stations, block), lambda i, place: (0, 0, station_block, i))
-
-    both = pl.BlockSpec((None, frames, 2, stations, block), lambda i, place: (pol, 0, 0, where, i))
-    one = spec(frames, where)
-    shape = jax.ShapeDtypeStruct((frames, 2, stations, samples), BF16)
-    return pl.pallas_call(
-        filter_kernel,
+
+    def spec(depth, where):
+        return pl.BlockSpec((depth, parts, stations, block), lambda i, place: (0, 0, where, i))
+
+    shape = jax.ShapeDtypeStruct((count // 2, parts, stations, samples), BF16)
+    return pl.pallas_call(
+        far_kernel,
         out_shape=(shape, shape),
         grid_spec=pltpu.PrefetchScalarGridSpec(
             num_scalar_prefetch=1,
             grid=(samples // block,),
-            in_specs=[pl.BlockSpec((taps.shape[0], block), lambda i, place: (0, i))]
-            + [both, one, both, one, spec(far.shape[0], 0)]
+            in_specs=[
+                pl.BlockSpec((taps.shape[0], 8, block), lambda i, place: (0, 0, i)),
+                spec(count, low // stations),
+                spec(far.shape[0], 0),
+            ]
             + [pl.BlockSpec(memory_space=pl.ANY)] * len(earlier),
-            out_specs=[spec(frames, 0)] * 2,
+            out_specs=[spec(count // 2, 0)] * 2,
         ),
         compiler_params=pltpu.CompilerParams(vmem_limit_bytes=VMEM_LIMIT),
-        cost_estimate=cost(8 * stations / 32),
-        name="filter",
-    )(place, taps, own, other, own_back, other_back, far, *earlier)
+        cost_estimate=cost(3),
+        name="far",
+    )(place, taps, partial, far, *earlier)
 
 
 def onward_kernel(place, own_back, other_back, *rest):
@@ -199,7 +304,8 @@
     )(place, own_back, other_back, *earlier)
 
 
-def weight_kernel(table, index, mask, out):
+def weight_kernel(table, index, mask, *rest):
+    out = rest[-1]
     groups, depth, width = out.shape
     beams = width // 2
     half = depth // 2
@@ -212,21 +318,23 @@
         re, im = picked[:, 0], picked[:, 1]
         out[:, low : low + SB, :beams] = re.astype(BF16)
         out[:, low : low + SB, beams:] = im.astype(BF16)
-        out[:, half + low : half + low + SB, :beams] = (-im).astype(BF16)
-        out[:, half + low : half + low + SB, beams:] = re.astype(BF16)
-
-
-def beam_weights(table, index, mask):
+        low += half
+        out[:, low : low + SB, :beams] = (-im).astype(BF16)
+        out[:, low : low + SB, beams:] = re.astype(BF16)
+
+
+def beam_weights(table, index, mask, earlier):
     blocks, beams = index.shape
     groups = table.shape[1] // (2 * SB)
     shape = (groups, 2 * blocks * SB, 2 * beams)
     return pl.pallas_call(
         weight_kernel,
         out_shape=jax.ShapeDtypeStruct(shape, BF16),
+        in_specs=[pl.BlockSpec(memory_space=pltpu.VMEM)] * 3 + [pl.BlockSpec(memory_space=pl.ANY)] * len(earlier),
         compiler_params=pltpu.CompilerParams(vmem_limit_bytes=VMEM_LIMIT),
         cost_estimate=cost(4),
         name="weights",
-    )(table, index, mask)
+    )(table, index, mask, *earlier)
 
 
 def beam_kernel(source_count, has_earlier, *refs):
@@ -381,19 +489,28 @@
     def swap(block):
         return lax.ppermute(block, "stn", [(0, 1), (1, 0)])
 
+    def laid(block):
+        return jnp.moveaxis(block, 0, -2)
+
     columns = weight_blocks.shape[1] // CORES
     shard = lax.dynamic_slice_in_dim(weight_blocks, core * columns, columns, 1)
-    shard = jnp.concatenate([shard, pair(shard)])
-    shards = [shard] + [
-        lax.ppermute(shard, "tm", [(i, i ^ far) for i in range(time_devices)]) for far in range(2, time_devices, 2)
-    ]
-
-    other = [lax.dynamic_slice_in_dim(voltages, half * (1 - side), half, 0)[:, p].transpose(1, 2, 0, 3) for p in range(pols)]
-    own = lax.dynamic_slice_in_dim(voltages, half * side, half, 0).transpose(1, 2, 3, 0, 4)
-    other, own, shards = lax.optimization_barrier((other, own, shards))
+
+    def doubled(block, distance):
+        arrived = lax.ppermute(block, "tm", [(i, i ^ distance) for i in range(time_devices)])
+        return jnp.concatenate([block, arrived])
+
+    for distance in (1, 2):
+        shard = doubled(shard, distance)
+    (own,) = cut(place, voltages, [(0, None)], [shard])
+    distance = 4
+    while distance < time_devices:
+        shard = doubled(shard, distance)
+        distance *= 2
+    other = cut(place, voltages, [(1, pol) for pol in range(pols)])
+    own_back = laid(after(hop(own)))
+    own = laid(own)
     other = [pair(block) for block in other]
-    own_back = hop(own)
-    other_back = [hop(block) for block in other]
+    other = [laid(after(other[0]))] + [laid(after(block, shard)) for block in other[1:]]
 
     def ordered(rows):
         rows = rows.T.reshape(2, 2, 2, -1)
@@ -402,35 +519,32 @@
         return rows.reshape(8, -1)
 
     index = block_index ^ (lax.axis_index("tm") * weight_blocks.shape[0])
-    weights = beam_weights(jnp.concatenate(shards), ordered(index), ordered(use_mask))
+    weights = beam_weights(shard, ordered(index), ordered(use_mask), other)
     table = jnp.asarray(dft_tables(samples))
-
-    chunks = [(pol, low, half // 2) for pol in range(pols) for low in (0, half // 2)]
-    further = [
-        onward(place, own_back, other_back[pol], pol, low, size, history - 2 * frames, other_back)
-        for pol, low, size in chunks
-    ]
+    taps = jnp.broadcast_to(filter_taps[:, None, :], (history + 1, 8, samples))
+
+    quarter = half // 2
+    chunks = [(pol, low) for pol in range(pols) for low in (0, quarter)]
+    other_back = [hop(other[0])]
+    further, partial = [], []
+    for pol, low in chunks:
+        if pol >= len(other_back):
+            other_back.append(hop(after(other[pol], further[0])))
+        further.append(onward(place, own_back, other_back[pol], pol, low, quarter, history - 2 * frames))
+        if low:
+            partial.append(near_filter(place, taps, own, other[pol], own_back, other_back[pol], pol, further[-2:] + [weights]))
     far = [hop(block, 2) for block in further]
-    keeps, sends = [], []
-    for (pol, low, _), block in zip(chunks, far):
-        earlier = keeps[-1:] if keeps else further[1:] + [weights]
-        keep, send = filter_frames(
-            place, filter_taps, own, other[pol], own_back, other_back[pol], block, pol, low, earlier
-        )
+    keeps, sents, power = [], [], None
+    for k, (pol, low) in enumerate(chunks):
+        earlier = sents[-1:] + ([power] if k == len(chunks) - 1 else [])
+        keep, send = far_filter(place, taps, partial[pol], far[k], low, earlier)
         keeps.append(keep)
-        sends.append(send)
-    sents = [pair(block) for block in sends]
-    sents[:2] = [after(block, keeps[-1]) for block in sents[:2]]
-
-    def power_of(pol, earlier):
-        here = [i for i, chunk in enumerate(chunks) if chunk[0] == pol]
-        sources = [keeps[i] for i in here] + [sents[i] for i in here]
-        sources += [swap(block) for block in sources]
-        return beam_power(place, sources, table, weights, earlier, samples // CORES)
-
-    power = power_of(0, None)
-    sents[-1] = after(sents[-1], power)
-    return power_of(1, power)
+        sents.append(pair(send))
+        if low:
+            sources = keeps[-2:] + sents[-2:]
+            sources += [swap(block) for block in sources]
+            power = beam_power(place, sources, table, weights, power, samples // CORES)
+    return power
 
 
 def solution(mesh):

time: 241 us -> 244 us (1.012)
  Pallas kernels: 63.8 us -> 81.2 us
  starting transfers between devices: 52.9 us -> 41.6 us
  waiting for transfers between devices: 100 us -> 93.2 us
  local copies, waits for them, and re-layouts: 20.8 us -> 24.4 us
    ppermute x3, waiting for transfers between devices: 0.01 us -> 45.5 us  [doubled(): lax.ppermute(block, 'tm', [(i, i ^ distance) for i in range(time_devices)])]
    ppermute x7, waiting for transfers between devices: 62.7 us -> 18.8 us  [hop(): lax.ppermute(block, 'tm', [(i, i + 2) for i in range(skip, time_devices -...]
    pallas_call x4 -> x8, Pallas kernels: 24.5 us -> 41.8 us  [the longest x4 20 us: far_filter(): pl.pallas_call(far_kernel, out_shape=(shape, shape), grid_spec=pltpu.Pref...]
    pallas_call x0 -> x4, local copies, waits for them, and re-layouts: none -> 10.2 us  [the longest x3 7.7 us: after(): pl.pallas_call(lambda *refs: None, out_shape=jax.ShapeDtypeStruct(block.s...]
    ppermute x8, starting transfers between devices: 22.6 us -> 13.2 us  [swap(): return lax.ppermute(block, 'stn', [(0, 1), (1, 0)])]
    ppermute x7 -> x6, waiting for transfers between devices: 35.8 us -> 27.4 us  [pair(): return lax.ppermute(block, 'tm', [(i, i ^ 1) for i in range(time_devices)])]
    dynamic_slice x1 -> x0, local copies, waits for them, and re-layouts: 3.38 us -> none  [body(): lax.dynamic_slice_in_dim(voltages, half * side, half, 0)]
    slice x1 -> x0, local copies, waits for them, and re-layouts: 3.34 us -> none  [body(): lax.dynamic_slice_in_dim(voltages, half * (1 - side), half, 0)[:, p]]
  transfers between devices with their start and end apart: 25 -> 24, of which waited for: 8 -> 7; matrix products, arithmetic and copies ran while one was open for 6% -> 6% of each run, Pallas kernels for 20% -> 26%
where the time goes in v4:
time: 244 us; the launch traced here: 243 us
  waiting for transfers between devices  93.2 us (38%)
  Pallas kernels  81.2 us (33%)
  starting transfers between devices  41.6 us (17%)
  local copies, waits for them, and re-layouts  24.4 us (10%)
    ppermute x3, waiting for transfers between devices, doubled(): lax.ppermute(block, 'tm', [(i, i ^ distance) for i in range(time_devices)])  45.5 us
    ppermute x6, waiting for transfers between devices, pair(): return lax.ppermute(block, 'tm', [(i, i ^ 1) for i in range(time_devices)])  27.4 us
    pallas_call x2, Pallas kernels, beam_power(): pl.pallas_call(functools.partial(beam_kernel, len(sources), earlier is no...  25.7 us
    ppermute x7, starting transfers between devices, hop(): lax.ppermute(block, 'tm', [(i, i + 2) for i in range(skip, time_devices -...  21.2 us
    pallas_call x4, Pallas kernels, far_filter(): pl.pallas_call(far_kernel, out_shape=(shape, shape), grid_spec=pltpu.Pref...  20 us
    ppermute x7, waiting for transfers between devices, hop(): lax.ppermute(block, 'tm', [(i, i + 2) for i in range(skip, time_devices -...  18.8 us
    pallas_call x2, Pallas kernels, near_filter(): pl.pallas_call(near_kernel, out_shape=jax.ShapeDtypeStruct((2 * frames, p...  15.7 us
    ppermute x8, starting transfers between devices, swap(): return lax.ppermute(block, 'stn', [(0, 1), (1, 0)])  13.2 us
  transfers between devices with their start and end apart: 24, of which 7 were waited for; matrix products, arithmetic and copies ran while one was open for 6% of the time, Pallas kernels for 26%

profile of v4, /device:TPU:17, one launch (start us, length us, event | category | flops | bytes accessed | tf_op | source)
XLA Modules:
  0.0 242.5 jit_solution(878128148156400639)
XLA Ops:
  5.2 3.1 %cut.3 = (bf16[32,4,2,2048]{3,2,1,0:T(2,128)(2,1)}, bf16[32,4,2,2048]{3,2,1,0:T(2,128)(2,1)}) custom-call(s32[2]{0:T(128)} %pad_add_fusion.place.refs_0_, bf16[64,2,4,2,2048]{4,3,2,1,0:T(2,128)(2,1)} %voltages.3), custom_call_target="tpu_custom_call" | custom-call | bytes 6600000 | tf_op jit(solution)/shard_map/cut/pallas_call | solution.py:123
  10.2 3.1 %cut.2 = bf16[32,2,4,2,2048]{4,3,2,1,0:T(2,128)(2,1)} custom-call(s32[2]{0:T(128)} %pad_add_fusion.place.refs_0_, bf16[64,2,4,2,2048]{4,3,2,1,0:T(2,128)(2,1)} %voltages.3, bf16[64,256]{1,0:T(8,128)(2,1)} %pad_maximum_fusion.1.rest_0_), custom_call_target="tpu_custom_call" | custom-call | bytes 6600000 | tf_op jit(solution)/shard_map/cut/pallas_call | solution.py:123
  15.3 15.8 %collective-permute-done.5.refs_0_ = bf16[32,4,2,2048]{3,2,1,0:T(2,128)(2,1)S(1)} collective-permute-done((bf16[32,4,2,2048]{3,2,1,0:T(2,128)(2,1)}, bf16[32,4,2,2048]{3,2,1,0:T(2,128)(2,1)S(1)}, u32[]{:S(2)}, u32[]{:S(2)}) %collective-permute-start.5) | collective-permute-done | bytes 1048608 | tf_op jit(solution)/shard_map/ppermute | solution.py:484
  37.5 44.2 %collective-permute-done.3 = bf16[64,256]{1,0:T(8,128)(2,1)S(1)} collective-permute-done((bf16[64,256]{1,0:T(8,128)(2,1)S(1)}, bf16[64,256]{1,0:T(8,128)(2,1)S(1)}, u32[]{:S(2)}, u32[]{:S(2)}) %collective-permute-start.3) | collective-permute-done | bytes 32800 | tf_op jit(solution)/shard_map/ppermute | solution.py:499
  82.4 4.1 %copy.19 = bf16[32,2,4,2,2048]{4,0,3,2,1:T(8,128)(2,1)} copy(bf16[32,2,4,2,2048]{4,3,2,1,0:T(2,128)(2,1)} %after.5) | data formatting | bytes 4194304 | tf_op jit(solution)/shard_map/after/pallas_call | solution.py:77
  87.4 2.7 %onward.4.refs_1_.rest_0_ = bf16[7,2,16,2048]{3,2,1,0:T(8,128)(2,1)} custom-call(s32[2]{0:T(128)} %pad_add_fusion.place.refs_0_, bf16[2,4,2,32,2048]{4,3,2,1,0:T(8,128)(2,1)} %bitcast.25, bf16[4,2,32,2048]{3,2,1,0:T(8,128)(2,1)} %copy-done.4), custom_call_target="tpu_custom_call" | custom-call | bytes 4950000 | tf_op jit(solution)/shard_map/onward/pallas_call | solution.py:288
  90.1 4.7 %collective-permute-start.10 = (bf16[7,2,16,2048]{3,2,1,0:T(8,128)(2,1)}, bf16[7,2,16,2048]{3,2,1,0:T(8,128)(2,1)}, u32[]{:S(2)}, u32[]{:S(2)}) collective-permute-start(bf16[7,2,16,2048]{3,2,1,0:T(8,128)(2,1)} %onward.4.refs_1_.rest_0_), channel_id=1, source_target_pairs={{4,8},{6,10},{8,12},{10,14},{5,9},{7,11},{9,13},{11,15},{20,24},{2... | collective-permute-start | bytes 2752520 | tf_op jit(solution)/shard_map/ppermute | solution.py:487
  101.0 2.8 %onward.7.rest_1_ = bf16[7,2,16,2048]{3,2,1,0:T(8,128)(2,1)} custom-call(s32[2]{0:T(128)} %pad_add_fusion.place.refs_0_, bf16[2,4,2,32,2048]{4,3,2,1,0:T(8,128)(2,1)} %bitcast.26, bf16[4,2,32,2048]{3,2,1,0:T(8,128)(2,1)} %copy-done.4), custom_call_target="tpu_custom_call" | custom-call | bytes 4950000 | tf_op jit(solution)/shard_map/onward/pallas_call | solution.py:288
  109.5 2.7 %weights.1.rest_2_.refs_10_ = bf16[8,256,512]{2,1,0:T(8,128)(2,1)} custom-call(bf16[128,256]{1,0:T(8,128)(2,1)} %pad_maximum_fusion.refs_1_.table, s32[8,256]{1,0:T(8,128)} %reshape.14.index, s32[8,256]{1,0:T(8,128)} %reshape.16.mask, bf16[4,2,32,2048]{3,2,1,0:T(8,128)(2,1)} %bitcast.37, bf16[4,2,32,2048]{3,2,1,0:T(8,128)(2,1)} %bitcast.34), custom_call_target="tpu_custom_call" | custom-call | bytes 13200000 | tf_op jit(solution)/shard_map/weights/pallas_call | solution.py:330
  113.3 7.8 %near.3.partial = f32[8,2,32,2048]{3,2,1,0:T(8,128)} custom-call(s32[2]{0:T(128)} %pad_add_fusion.place.refs_0_, f32[16,8,2048]{2,1,0:T(8,128)} %broadcast_in_dim.2.taps, bf16[2,4,2,32,2048]{4,3,2,1,0:T(8,128)(2,1)} %bitcast.31, bf16[4,2,32,2048]{3,2,1,0:T(8,128)(2,1)} %bitcast.38, bf16[2,4,2,32,2048]{4,3,2,1,0:T(8,128)(2,1)} %bitcast.27, ...), custom_call_target="tpu_custom_call" | custom-call | bytes 33000000 | tf_op jit(solution)/shard_map/near/pallas_call | solution.py:222
  121.1 5.0 %far.4 = (bf16[4,2,16,2048]{3,2,1,0:T(8,128)(2,1)}, bf16[4,2,16,2048]{3,2,1,0:T(8,128)(2,1)}) custom-call(s32[2]{0:T(128)} %pad_add_fusion.place.refs_0_, f32[16,8,2048]{2,1,0:T(8,128)} %broadcast_in_dim.2.taps, f32[8,2,32,2048]{3,2,1,0:T(8,128)} %near.3.partial, bf16[7,2,16,2048]{3,2,1,0:T(8,128)(2,1)} %collective-permute-done.10.far), custom_call_target="tpu_custom_call" | custom-call | bytes 9900000 | tf_op jit(solution)/shard_map/far/pallas_call | solution.py:247
  126.3 6.9 %collective-permute-done.7.other_back = bf16[4,2,32,2048]{3,2,1,0:T(8,128)(2,1)S(1)} collective-permute-done((bf16[4,2,32,2048]{3,2,1,0:T(8,128)(2,1)}, bf16[4,2,32,2048]{3,2,1,0:T(8,128)(2,1)S(1)}, u32[]{:S(2)}, u32[]{:S(2)}) %collective-permute-start.7) | collective-permute-done | bytes 1048608 | tf_op jit(solution)/shard_map/ppermute | solution.py:487
  134.2 2.7 %onward.5.rest_0_ = bf16[7,2,16,2048]{3,2,1,0:T(8,128)(2,1)} custom-call(s32[2]{0:T(128)} %pad_add_fusion.place.refs_0_, bf16[2,4,2,32,2048]{4,3,2,1,0:T(8,128)(2,1)} %bitcast.28, bf16[4,2,32,2048]{3,2,1,0:T(8,128)(2,1)} %copy-done.3), custom_call_target="tpu_custom_call" | custom-call | bytes 4950000 | tf_op jit(solution)/shard_map/onward/pallas_call | solution.py:288
  136.9 4.1 %collective-permute-start.8 = (bf16[7,2,16,2048]{3,2,1,0:T(8,128)(2,1)}, bf16[7,2,16,2048]{3,2,1,0:T(8,128)(2,1)S(1)}, u32[]{:S(2)}, u32[]{:S(2)}) collective-permute-start(bf16[7,2,16,2048]{3,2,1,0:T(8,128)(2,1)} %onward.5.rest_0_), channel_id=1, source_target_pairs={{4,8},{6,10},{8,12},{10,14},{5,9},{7,11},{9,13},{11,15},{20,24},{2... | collective-permute-start | bytes 2752520 | tf_op jit(solution)/shard_map/ppermute | solution.py:487
  141.1 11.9 %collective-permute-done.9.far = bf16[7,2,16,2048]{3,2,1,0:T(8,128)(2,1)} collective-permute-done((bf16[7,2,16,2048]{3,2,1,0:T(8,128)(2,1)}, bf16[7,2,16,2048]{3,2,1,0:T(8,128)(2,1)}, u32[]{:S(2)}, u32[]{:S(2)}) %collective-permute-start.9) | collective-permute-done | bytes 917536 | tf_op jit(solution)/shard_map/ppermute | solution.py:487
  153.7 5.0 %far.5 = (bf16[4,2,16,2048]{3,2,1,0:T(8,128)(2,1)}, bf16[4,2,16,2048]{3,2,1,0:T(8,128)(2,1)}) custom-call(s32[2]{0:T(128)} %pad_add_fusion.place.refs_0_, f32[16,8,2048]{2,1,0:T(8,128)} %broadcast_in_dim.2.taps, f32[8,2,32,2048]{3,2,1,0:T(8,128)} %near.3.partial, bf16[7,2,16,2048]{3,2,1,0:T(8,128)(2,1)} %collective-permute-done.9.far, ...), custom_call_target="tpu_custom_call" | custom-call | bytes 9900000 | tf_op jit(solution)/shard_map/far/pallas_call | solution.py:247
  159.0 9.6 %collective-permute-start.15 = (bf16[4,2,16,2048]{3,2,1,0:T(8,128)(2,1)S(1)}, bf16[4,2,16,2048]{3,2,1,0:T(8,128)(2,1)S(1)}, u32[]{:S(2)}, u32[]{:S(2)}) collective-permute-start(bf16[4,2,16,2048]{3,2,1,0:T(8,128)(2,1)S(1)} %copy-done.14), channel_id=1, source_target_pairs={{0,1},{1,0},{2,3},{3,2},{4,5},{5,4},{6,7},{7,6},{8,9},{9,8},{10,11... | collective-permute-start | bytes 1572872 | tf_op jit(solution)/shard_map/ppermute | solution.py:490
  171.3 4.4 %collective-permute-start.13 = (bf16[7,2,16,2048]{3,2,1,0:T(8,128)(2,1)}, bf16[7,2,16,2048]{3,2,1,0:T(8,128)(2,1)S(1)}, u32[]{:S(2)}, u32[]{:S(2)}) collective-permute-start(bf16[7,2,16,2048]{3,2,1,0:T(8,128)(2,1)} %onward.6.rest_1_), channel_id=1, source_target_pairs={{4,8},{6,10},{8,12},{10,14},{5,9},{7,11},{9,13},{11,15},{20,24},{2... | collective-permute-start | bytes 2752520 | tf_op jit(solution)/shard_map/ppermute | solution.py:487
  175.7 7.8 %near.2.partial = f32[8,2,32,2048]{3,2,1,0:T(8,128)} custom-call(s32[2]{0:T(128)} %pad_add_fusion.place.refs_0_, f32[16,8,2048]{2,1,0:T(8,128)} %broadcast_in_dim.2.taps, bf16[2,4,2,32,2048]{4,3,2,1,0:T(8,128)(2,1)} %bitcast.32, bf16[4,2,32,2048]{3,2,1,0:T(8,128)(2,1)} %bitcast.35, bf16[2,4,2,32,2048]{4,3,2,1,0:T(8,128)(2,1)} %bitcast.30, ...), custom_call_target="tpu_custom_call" | custom-call | bytes 33000000 | tf_op jit(solution)/shard_map/near/pallas_call | solution.py:222
  185.1 5.0 %far.6 = (bf16[4,2,16,2048]{3,2,1,0:T(8,128)(2,1)}, bf16[4,2,16,2048]{3,2,1,0:T(8,128)(2,1)}) custom-call(s32[2]{0:T(128)} %pad_add_fusion.place.refs_0_, f32[16,8,2048]{2,1,0:T(8,128)} %broadcast_in_dim.2.taps, f32[8,2,32,2048]{3,2,1,0:T(8,128)} %near.2.partial, bf16[7,2,16,2048]{3,2,1,0:T(8,128)(2,1)} %copy-done.13, bf16[4,2,16,2048]{3,2,1,0:T(8,128)(2,1)} %copy-done.11), custom_call_target="tpu_custom_call" | custom-call | bytes 9900000 | tf_op jit(solution)/shard_map/far/pallas_call | solution.py:247
  193.2 11.6 %beams.2.rest_1_.refs_11_ = f32[8,512,256]{2,1,0:T(8,128)} custom-call(s32[2]{0:T(128)} %pad_add_fusion.place.refs_0_, bf16[4,2,16,2048]{3,2,1,0:T(8,128)(2,1)} %get-tuple-element.21.refs_1_, bf16[4,2,16,2048]{3,2,1,0:T(8,128)(2,1)} %get-tuple-element.22.refs_2_, bf16[4,2,16,2048]{3,2,1,0:T(8,128)(2,1)} %copy-done.9, bf16[4,2,16,2048]{3,2,1,0:T(8,128)(2,1)} %copy-done.11, ...), custom_call_target="tpu_custom_call" | custom-call | tf_op jit(solution)/shard_map/beams/pallas_call | solution.py:454
  206.5 5.0 %far.7 = (bf16[4,2,16,2048]{3,2,1,0:T(8,128)(2,1)}, bf16[4,2,16,2048]{3,2,1,0:T(8,128)(2,1)}) custom-call(s32[2]{0:T(128)} %pad_add_fusion.place.refs_0_, f32[16,8,2048]{2,1,0:T(8,128)} %broadcast_in_dim.2.taps, f32[8,2,32,2048]{3,2,1,0:T(8,128)} %near.2.partial, bf16[7,2,16,2048]{3,2,1,0:T(8,128)(2,1)} %copy-done.12, bf16[4,2,16,2048]{3,2,1,0:T(8,128)(2,1)} %copy-done.8, ...), custom_call_target="tpu_custom_call" | custom-call | bytes 9900000 | tf_op jit(solution)/shard_map/far/pallas_call | solution.py:247
  213.1 11.6 %collective-permute-done.19.refs_4_ = bf16[4,2,16,2048]{3,2,1,0:T(8,128)(2,1)S(1)} collective-permute-done((bf16[4,2,16,2048]{3,2,1,0:T(8,128)(2,1)}, bf16[4,2,16,2048]{3,2,1,0:T(8,128)(2,1)S(1)}, u32[]{:S(2)}, u32[]{:S(2)}) %collective-permute-start.19) | collective-permute-done | bytes 524320 | tf_op jit(solution)/shard_map/ppermute | solution.py:484
  228.4 14.1 %beams.3 = f32[1024,4,256]{2,1,0:T(4,128)} custom-call(s32[2]{0:T(128)} %pad_add_fusion.place.refs_0_, bf16[4,2,16,2048]{3,2,1,0:T(8,128)(2,1)} %get-tuple-element.19.refs_1_, bf16[4,2,16,2048]{3,2,1,0:T(8,128)(2,1)} %get-tuple-element.23.refs_2_, bf16[4,2,16,2048]{3,2,1,0:T(8,128)(2,1)} %copy-done.8, bf16[4,2,16,2048]{3,2,1,0:T(8,128)(2,1)} %copy-done.19, ...), custom_call_target="tpu_custom_call" | custom-call | tf_op jit(solution)/shard_map/beams/pallas_call | solution.py:454
  (122 shorter events, 46.5 us)
Async XLA Ops:
  0.7 2.5 %collective-permute-start = (bf16[16,256]{1,0:T(8,128)(2,1)S(1)}, bf16[16,256]{1,0:T(8,128)(2,1)S(1)}, u32[]{:S(2)}, u32[]{:S(2)}) collective-permute-start(bf16[16,256]{1,0:T(8,128)(2,1)S(1)} %constant_dynamic-slice_fusion), channel_id=1, source_target_pairs={{0,2},{2,0},{4,6},{6,4},{8,10},{10,8},{12,14},{14,12},{1,3},{3,1},... | collective-permute-start | bytes 24584 | tf_op jit(solution)/shard_map/ppermute | solution.py:499
  3.2 6.3 %collective-permute-start.1 = (bf16[32,256]{1,0:T(8,128)(2,1)S(1)}, bf16[32,256]{1,0:T(8,128)(2,1)S(1)}, u32[]{:S(2)}, u32[]{:S(2)}) collective-permute-start(bf16[32,256]{1,0:T(8,128)(2,1)S(1)} %pad_maximum_fusion.2), channel_id=1, source_target_pairs={{0,4},{2,6},{4,0},{6,2},{8,12},{10,14},{12,8},{14,10},{1,5},{3,7},... | collective-permute-start | bytes 49160 | tf_op jit(solution)/shard_map/ppermute | solution.py:499
  8.2 22.9 %collective-permute-start.5 = (bf16[32,4,2,2048]{3,2,1,0:T(2,128)(2,1)}, bf16[32,4,2,2048]{3,2,1,0:T(2,128)(2,1)S(1)}, u32[]{:S(2)}, u32[]{:S(2)}) collective-permute-start(bf16[32,4,2,2048]{3,2,1,0:T(2,128)(2,1)} %get-tuple-element.16), channel_id=1, source_target_pairs={{0,2},{2,0},{4,6},{6,4},{8,10},{10,8},{12,14},{14,12},{1,3},{3,1},... | collective-permute-start | bytes 3145736 | tf_op jit(solution)/shard_map/ppermute | solution.py:484
  13.3 69.1 %collective-permute-start.4 = (bf16[32,2,4,2,2048]{4,3,2,1,0:T(2,128)(2,1)}, bf16[32,2,4,2,2048]{4,3,2,1,0:T(2,128)(2,1)}, u32[]{:S(2)}, u32[]{:S(2)}) collective-permute-start(bf16[32,2,4,2,2048]{4,3,2,1,0:T(2,128)(2,1)} %cut.2), channel_id=1, source_target_pairs={{0,4},{2,6},{4,8},{6,10},{8,12},{10,14},{1,5},{3,7},{5,9},{7,11},{... | collective-permute-start | bytes 6291464 | tf_op jit(solution)/shard_map/ppermute | solution.py:487
  34.0 52.5 %collective-permute-start.6 = (bf16[4,2,32,2048]{3,2,1,0:T(8,128)(2,1)S(1)}, bf16[4,2,32,2048]{3,2,1,0:T(8,128)(2,1)S(1)}, u32[]{:S(2)}, u32[]{:S(2)}) collective-permute-start(bf16[4,2,32,2048]{3,2,1,0:T(8,128)(2,1)S(1)} %bitcast.36), channel_id=1, source_target_pairs={{0,4},{2,6},{4,8},{6,10},{8,12},{10,14},{1,5},{3,7},{5,9},{7,11},{... | collective-permute-start | bytes 3145736 | tf_op jit(solution)/shard_map/ppermute | solution.py:487
  36.1 58.7 %collective-permute-start.2 = (bf16[32,4,2,2048]{3,2,1,0:T(2,128)(2,1)}, bf16[32,4,2,2048]{3,2,1,0:T(2,128)(2,1)S(1)}, u32[]{:S(2)}, u32[]{:S(2)}) collective-permute-start(bf16[32,4,2,2048]{3,2,1,0:T(2,128)(2,1)} %get-tuple-element.15), channel_id=1, source_target_pairs={{0,2},{2,0},{4,6},{6,4},{8,10},{10,8},{12,14},{14,12},{1,3},{3,1},... | collective-permute-start | bytes 3145736 | tf_op jit(solution)/shard_map/ppermute | solution.py:484
  37.4 44.3 %collective-permute-start.3 = (bf16[64,256]{1,0:T(8,128)(2,1)S(1)}, bf16[64,256]{1,0:T(8,128)(2,1)S(1)}, u32[]{:S(2)}, u32[]{:S(2)}) collective-permute-start(bf16[64,256]{1,0:T(8,128)(2,1)S(1)} %copy-done.26), channel_id=1, source_target_pairs={{0,8},{2,10},{4,12},{6,14},{8,0},{10,2},{12,4},{14,6},{1,9},{3,11}... | collective-permute-start | bytes 98312 | tf_op jit(solution)/shard_map/ppermute | solution.py:499
  90.1 31.0 %collective-permute-start.10 = (bf16[7,2,16,2048]{3,2,1,0:T(8,128)(2,1)}, bf16[7,2,16,2048]{3,2,1,0:T(8,128)(2,1)}, u32[]{:S(2)}, u32[]{:S(2)}) collective-permute-start(bf16[7,2,16,2048]{3,2,1,0:T(8,128)(2,1)} %onward.4.refs_1_.rest_0_), channel_id=1, source_target_pairs={{4,8},{6,10},{8,12},{10,14},{5,9},{7,11},{9,13},{11,15},{20,24},{2... | collective-permute-start | bytes 2752520 | tf_op jit(solution)/shard_map/ppermute | solution.py:487
  99.0 34.3 %collective-permute-start.7 = (bf16[4,2,32,2048]{3,2,1,0:T(8,128)(2,1)}, bf16[4,2,32,2048]{3,2,1,0:T(8,128)(2,1)S(1)}, u32[]{:S(2)}, u32[]{:S(2)}) collective-permute-start(bf16[4,2,32,2048]{3,2,1,0:T(8,128)(2,1)} %after.7), channel_id=1, source_target_pairs={{0,4},{2,6},{4,8},{6,10},{8,12},{10,14},{1,5},{3,7},{5,9},{7,11},{... | collective-permute-start | bytes 3145736 | tf_op jit(solution)/shard_map/ppermute | solution.py:487
  103.9 49.1 %collective-permute-start.9 = (bf16[7,2,16,2048]{3,2,1,0:T(8,128)(2,1)}, bf16[7,2,16,2048]{3,2,1,0:T(8,128)(2,1)}, u32[]{:S(2)}, u32[]{:S(2)}) collective-permute-start(bf16[7,2,16,2048]{3,2,1,0:T(8,128)(2,1)} %onward.7.rest_1_), channel_id=1, source_target_pairs={{4,8},{6,10},{8,12},{10,14},{5,9},{7,11},{9,13},{11,15},{20,24},{2... | collective-permute-start | bytes 2752520 | tf_op jit(solution)/shard_map/ppermute | solution.py:487
  126.2 26.8 %collective-permute-start.11 = (bf16[4,2,16,2048]{3,2,1,0:T(8,128)(2,1)}, bf16[4,2,16,2048]{3,2,1,0:T(8,128)(2,1)S(1)}, u32[]{:S(2)}, u32[]{:S(2)}) collective-permute-start(bf16[4,2,16,2048]{3,2,1,0:T(8,128)(2,1)} %get-tuple-element.17), channel_id=1, source_target_pairs={{0,2},{2,0},{4,6},{6,4},{8,10},{10,8},{12,14},{14,12},{1,3},{3,1},... | collective-permute-start | bytes 1572872 | tf_op jit(solution)/shard_map/ppermute | solution.py:484
  136.9 47.2 %collective-permute-start.8 = (bf16[7,2,16,2048]{3,2,1,0:T(8,128)(2,1)}, bf16[7,2,16,2048]{3,2,1,0:T(8,128)(2,1)S(1)}, u32[]{:S(2)}, u32[]{:S(2)}) collective-permute-start(bf16[7,2,16,2048]{3,2,1,0:T(8,128)(2,1)} %onward.5.rest_0_), channel_id=1, source_target_pairs={{4,8},{6,10},{8,12},{10,14},{5,9},{7,11},{9,13},{11,15},{20,24},{2... | collective-permute-start | bytes 2752520 | tf_op jit(solution)/shard_map/ppermute | solution.py:487
  158.7 25.1 %collective-permute-start.12 = (bf16[4,2,16,2048]{3,2,1,0:T(8,128)(2,1)}, bf16[4,2,16,2048]{3,2,1,0:T(8,128)(2,1)S(1)}, u32[]{:S(2)}, u32[]{:S(2)}) collective-permute-start(bf16[4,2,16,2048]{3,2,1,0:T(8,128)(2,1)} %get-tuple-element.18), channel_id=1, source_target_pairs={{0,2},{2,0},{4,6},{6,4},{8,10},{10,8},{12,14},{14,12},{1,3},{3,1},... | collective-permute-start | bytes 1572872 | tf_op jit(solution)/shard_map/ppermute | solution.py:484
  159.0 31.1 %collective-permute-start.15 = (bf16[4,2,16,2048]{3,2,1,0:T(8,128)(2,1)S(1)}, bf16[4,2,16,2048]{3,2,1,0:T(8,128)(2,1)S(1)}, u32[]{:S(2)}, u32[]{:S(2)}) collective-permute-start(bf16[4,2,16,2048]{3,2,1,0:T(8,128)(2,1)S(1)} %copy-done.14), channel_id=1, source_target_pairs={{0,1},{1,0},{2,3},{3,2},{4,5},{5,4},{6,7},{7,6},{8,9},{9,8},{10,11... | collective-permute-start | bytes 1572872 | tf_op jit(solution)/shard_map/ppermute | solution.py:490
  171.3 33.5 %collective-permute-start.13 = (bf16[7,2,16,2048]{3,2,1,0:T(8,128)(2,1)}, bf16[7,2,16,2048]{3,2,1,0:T(8,128)(2,1)S(1)}, u32[]{:S(2)}, u32[]{:S(2)}) collective-permute-start(bf16[7,2,16,2048]{3,2,1,0:T(8,128)(2,1)} %onward.6.rest_1_), channel_id=1, source_target_pairs={{4,8},{6,10},{8,12},{10,14},{5,9},{7,11},{9,13},{11,15},{20,24},{2... | collective-permute-start | bytes 2752520 | tf_op jit(solution)/shard_map/ppermute | solution.py:487
  183.5 7.9 %collective-permute-start.16 = (bf16[4,2,16,2048]{3,2,1,0:T(8,128)(2,1)S(1)}, bf16[4,2,16,2048]{3,2,1,0:T(8,128)(2,1)S(1)}, u32[]{:S(2)}, u32[]{:S(2)}) collective-permute-start(bf16[4,2,16,2048]{3,2,1,0:T(8,128)(2,1)S(1)} %copy-done.16), channel_id=1, source_target_pairs={{0,1},{1,0},{2,3},{3,2},{4,5},{5,4},{6,7},{7,6},{8,9},{9,8},{10,11... | collective-permute-start | bytes 1572872 | tf_op jit(solution)/shard_map/ppermute | solution.py:490
  183.8 7.6 %collective-permute-start.17 = (bf16[4,2,16,2048]{3,2,1,0:T(8,128)(2,1)S(1)}, bf16[4,2,16,2048]{3,2,1,0:T(8,128)(2,1)S(1)}, u32[]{:S(2)}, u32[]{:S(2)}) collective-permute-start(bf16[4,2,16,2048]{3,2,1,0:T(8,128)(2,1)S(1)} %copy-done.10), channel_id=1, source_target_pairs={{0,1},{1,0},{2,3},{3,2},{4,5},{5,4},{6,7},{7,6},{8,9},{9,8},{10,11... | collective-permute-start | bytes 1572872 | tf_op jit(solution)/shard_map/ppermute | solution.py:490
  184.1 7.3 %collective-permute-start.18 = (bf16[4,2,16,2048]{3,2,1,0:T(8,128)(2,1)S(1)}, bf16[4,2,16,2048]{3,2,1,0:T(8,128)(2,1)S(1)}, u32[]{:S(2)}, u32[]{:S(2)}) collective-permute-start(bf16[4,2,16,2048]{3,2,1,0:T(8,128)(2,1)S(1)} %collective-permute-done.12.rest_0_.refs_4_), channel_id=1, source_target_pairs={{0,1},{1,0},{2,3},{3,2},{4,5},{5,4},{6,7},{7,6},{8,9},{9,8},{10,11... | collective-permute-start | bytes 1572872 | tf_op jit(solution)/shard_map/ppermute | solution.py:490
  190.1 14.6 %collective-permute-start.14 = (bf16[4,2,16,2048]{3,2,1,0:T(8,128)(2,1)}, bf16[4,2,16,2048]{3,2,1,0:T(8,128)(2,1)S(1)}, u32[]{:S(2)}, u32[]{:S(2)}) collective-permute-start(bf16[4,2,16,2048]{3,2,1,0:T(8,128)(2,1)} %get-tuple-element.20), channel_id=1, source_target_pairs={{0,2},{2,0},{4,6},{6,4},{8,10},{10,8},{12,14},{14,12},{1,3},{3,1},... | collective-permute-start | bytes 1572872 | tf_op jit(solution)/shard_map/ppermute | solution.py:484
  211.5 13.1 %collective-permute-start.19 = (bf16[4,2,16,2048]{3,2,1,0:T(8,128)(2,1)}, bf16[4,2,16,2048]{3,2,1,0:T(8,128)(2,1)S(1)}, u32[]{:S(2)}, u32[]{:S(2)}) collective-permute-start(bf16[4,2,16,2048]{3,2,1,0:T(8,128)(2,1)} %get-tuple-element.24), channel_id=1, source_target_pairs={{0,2},{2,0},{4,6},{6,4},{8,10},{10,8},{12,14},{14,12},{1,3},{3,1},... | collective-permute-start | bytes 1572872 | tf_op jit(solution)/shard_map/ppermute | solution.py:484
  211.7 14.3 %collective-permute-start.20 = (bf16[4,2,16,2048]{3,2,1,0:T(8,128)(2,1)S(1)}, bf16[4,2,16,2048]{3,2,1,0:T(8,128)(2,1)S(1)}, u32[]{:S(2)}, u32[]{:S(2)}) collective-permute-start(bf16[4,2,16,2048]{3,2,1,0:T(8,128)(2,1)S(1)} %copy-done.15), channel_id=1, source_target_pairs={{0,1},{1,0},{2,3},{3,2},{4,5},{5,4},{6,7},{7,6},{8,9},{9,8},{10,11... | collective-permute-start | bytes 1572872 | tf_op jit(solution)/shard_map/ppermute | solution.py:490
  212.6 13.5 %collective-permute-start.21 = (bf16[4,2,16,2048]{3,2,1,0:T(8,128)(2,1)}, bf16[4,2,16,2048]{3,2,1,0:T(8,128)(2,1)S(1)}, u32[]{:S(2)}, u32[]{:S(2)}) collective-permute-start(bf16[4,2,16,2048]{3,2,1,0:T(8,128)(2,1)} %get-tuple-element.23.refs_2_), channel_id=1, source_target_pairs={{0,1},{1,0},{2,3},{3,2},{4,5},{5,4},{6,7},{7,6},{8,9},{9,8},{10,11... | collective-permute-start | bytes 1572872 | tf_op jit(solution)/shard_map/ppermute | solution.py:490
  212.6 13.5 %collective-permute-start.22 = (bf16[4,2,16,2048]{3,2,1,0:T(8,128)(2,1)}, bf16[4,2,16,2048]{3,2,1,0:T(8,128)(2,1)S(1)}, u32[]{:S(2)}, u32[]{:S(2)}) collective-permute-start(bf16[4,2,16,2048]{3,2,1,0:T(8,128)(2,1)} %copy-done.8), channel_id=1, source_target_pairs={{0,1},{1,0},{2,3},{3,2},{4,5},{5,4},{6,7},{7,6},{8,9},{9,8},{10,11... | collective-permute-start | bytes 1572872 | tf_op jit(solution)/shard_map/ppermute | solution.py:490
  224.6 3.0 %collective-permute-start.23 = (bf16[4,2,16,2048]{3,2,1,0:T(8,128)(2,1)S(1)}, bf16[4,2,16,2048]{3,2,1,0:T(8,128)(2,1)S(1)}, u32[]{:S(2)}, u32[]{:S(2)}) collective-permute-start(bf16[4,2,16,2048]{3,2,1,0:T(8,128)(2,1)S(1)} %collective-permute-done.19.refs_4_), channel_id=1, source_target_pairs={{0,1},{1,0},{2,3},{3,2},{4,5},{5,4},{6,7},{7,6},{8,9},{9,8},{10,11... | collective-permute-start | bytes 1572872 | tf_op jit(solution)/shard_map/ppermute | solution.py:490
  (30 other events, 164.5 us)

commit v5 on v4

--- a/solution.py
+++ b/solution.py
@@ -238,7 +238,7 @@
 def far_filter(place, taps, partial, far, low, earlier):
     count, parts, _, samples = partial.shape
     stations = far.shape[2]
-    block = 512
+    block = samples // 2
 
     def spec(depth, where):
         return pl.BlockSpec((depth, parts, stations, block), lambda i, place: (0, 0, where, i))
@@ -343,7 +343,8 @@
     sources = [refs.pop(0) for _ in range(source_count)]
     table, weights = refs.pop(0), refs.pop(0)
     earlier = refs.pop(0) if has_earlier else None
-    out, mixed, spectra = refs[:3]
+    out, mixed, spectra, sems, *refs = refs
+    held, refs = refs[:source_count], refs[source_count:]
     step = pl.program_id(0)
     frames = sources[0].shape[0]
     station_count = sum(ref.shape[2] for ref in sources)
@@ -357,7 +358,11 @@
     @pl.when(step == 0)
     def _():
         low = 0
-        for ref in sources:
+        copies = [pltpu.make_async_copy(ref, to, sems.at[k]) for k, (ref, to) in enumerate(zip(sources, held))]
+        for copy in copies:
+            copy.start()
+        for copy, ref in zip(copies, held):
+            copy.wait()
             tiles = ref.shape[2] // SB
 
             def radix(i, carry, ref=ref, low=low, tiles=tiles):
@@ -409,14 +414,14 @@
                 at = (b * frames + f) * rows_of
                 for t in range(lane_tiles):
                     start = (k * rows_of * RADIX + b) * per_channel + t * frames + f
-                    refs[3][pl.ds(start, rows_of, stride=RADIX * per_channel), :] = power[
+                    refs[0][pl.ds(start, rows_of, stride=RADIX * per_channel), :] = power[
                         at : at + rows_of, t * LANES : (t + 1) * LANES
                     ]
 
     if has_earlier:
 
         def finish(c, carry):
-            value = refs[3][pl.ds(pl.multiple_of(c * per_channel, per_channel), per_channel), :]
+            value = refs[0][pl.ds(pl.multiple_of(c * per_channel, per_channel), per_channel), :]
             for t in range(lane_tiles):
                 out[c, :, t * LANES : (t + 1) * LANES] = value[t * frames : (t + 1) * frames]
             return carry
@@ -432,7 +437,7 @@
     at_once = 2
     flat = (groups, channels // groups * frames, beams)
     flat_spec = pl.BlockSpec((at_once,) + flat[1:], lambda i, place: (i, 0, 0))
-    in_specs = [pl.BlockSpec(s.shape, lambda i, place: (0, 0, 0, 0)) for s in sources]
+    in_specs = [pl.BlockSpec(memory_space=pltpu.HBM) for s in sources]
     in_specs += [
         pl.BlockSpec((1,) + table.shape[1:], lambda i, place: (place[1], 0, 0, 0)),
         pl.BlockSpec((at_once, depth, width), lambda i, place: (i, 0, 0)),
@@ -441,7 +446,9 @@
     scratch = [
         pltpu.VMEM((RADIX, frames * station_count, 2 * LANES), BF16),
         pltpu.VMEM((groups, RADIX, frames * channels // groups // RADIX, 2 * station_count), BF16),
+        pltpu.SemaphoreType.DMA((len(sources),)),
     ]
+    scratch += [pltpu.VMEM(s.shape, BF16) for s in sources]
     if earlier is None:
         out_shape = jax.ShapeDtypeStruct(flat, F32)
         out_spec = flat_spec
@@ -494,23 +501,17 @@
 
     columns = weight_blocks.shape[1] // CORES
     shard = lax.dynamic_slice_in_dim(weight_blocks, core * columns, columns, 1)
-
-    def doubled(block, distance):
-        arrived = lax.ppermute(block, "tm", [(i, i ^ distance) for i in range(time_devices)])
-        return jnp.concatenate([block, arrived])
-
-    for distance in (1, 2):
-        shard = doubled(shard, distance)
-    (own,) = cut(place, voltages, [(0, None)], [shard])
-    distance = 4
-    while distance < time_devices:
-        shard = doubled(shard, distance)
-        distance *= 2
-    other = cut(place, voltages, [(1, pol) for pol in range(pols)])
+    shards = [shard] + [
+        lax.ppermute(shard, "tm", [(i, i ^ far) for i in range(time_devices)]) for far in range(2, time_devices, 2)
+    ]
+    (own,) = cut(place, voltages, [(0, None)])
+    own = after(own, *shards[1:])
+    other = cut(place, voltages, [(1, pol) for pol in range(pols)], [own])
     own_back = laid(after(hop(own)))
     own = laid(own)
-    other = [pair(block) for block in other]
-    other = [laid(after(other[0]))] + [laid(after(block, shard)) for block in other[1:]]
+    other = [laid(after(pair(block))) for block in other]
+    shards = jnp.concatenate(shards)
+    shards = jnp.concatenate([shards, pair(shards)])
 
     def ordered(rows):
         rows = rows.T.reshape(2, 2, 2, -1)
@@ -518,8 +519,10 @@
         rows = flipped(rows.swapaxes(0, 1), side).swapaxes(0, 1)
         return rows.reshape(8, -1)
 
-    index = block_index ^ (lax.axis_index("tm") * weight_blocks.shape[0])
-    weights = beam_weights(shard, ordered(index), ordered(use_mask), other)
+    each = weight_blocks.shape[0]
+    apart = block_index // each ^ lax.axis_index("tm")
+    index = (apart % 2 * (time_devices // 2) + apart // 2) * each + block_index % each
+    weights = beam_weights(shards, ordered(index), ordered(use_mask), other)
     table = jnp.asarray(dft_tables(samples))
     taps = jnp.broadcast_to(filter_taps[:, None, :], (history + 1, 8, samples))
 
@@ -536,7 +539,7 @@
     far = [hop(block, 2) for block in further]
     keeps, sents, power = [], [], None
     for k, (pol, low) in enumerate(chunks):
-        earlier = sents[-1:] + ([power] if k == len(chunks) - 1 else [])
+        earlier = sents[-1:] + ([power] if k == len(chunks) - 1 else []) + (partial[1:] if k == 1 else [])
         keep, send = far_filter(place, taps, partial[pol], far[k], low, earlier)
         keeps.append(keep)
         sents.append(pair(send))

time: 244 us -> 232 us (0.951)
  waiting for transfers between devices: 93.2 us -> 78.2 us
  starting transfers between devices: 41.6 us -> 48.6 us
  Pallas kernels: 81.2 us -> 77.1 us
    ppermute x3, waiting for transfers between devices: 45.5 us -> 0.01 us  [body(): lax.ppermute(shard, 'tm', [(i, i ^ far) for i in range(time_devices)])]
    ppermute x6 -> x7, waiting for transfers between devices: 27.4 us -> 44.4 us  [pair(): return lax.ppermute(block, 'tm', [(i, i ^ 1) for i in range(time_devices)])]
    ppermute x7, waiting for transfers between devices: 18.8 us -> 32.2 us  [hop(): lax.ppermute(block, 'tm', [(i, i + 2) for i in range(skip, time_devices -...]
    ppermute x8, starting transfers between devices: 13.2 us -> 20.5 us  [swap(): return lax.ppermute(block, 'stn', [(0, 1), (1, 0)])]
    pallas_call x4, Pallas kernels: 20 us -> 16.4 us  [far_filter(): pl.pallas_call(far_kernel, out_shape=(shape, shape), grid_spec=pltpu.Pref...]
    pallas_call x3 -> x4, local copies, waits for them, and re-layouts: 7.7 us -> 11.2 us  [after(): pl.pallas_call(lambda *refs: None, out_shape=jax.ShapeDtypeStruct(block.s...]
    pallas_call x1 -> x0, local copies, waits for them, and re-layouts: 2.51 us -> none  [cut(): pl.pallas_call(functools.partial(cut_kernel, mine), out_shape=[jax.ShapeD...]
    unnamed x61 -> x69, local copies, waits for them, and re-layouts: 11.9 us -> 11.9 us
  transfers between devices with their start and end apart: 24 -> 25, of which waited for: 7 -> 7; matrix products, arithmetic and copies ran while one was open for 6% -> 7% of each run, Pallas kernels for 26% -> 23%
where the time goes in v5:
time: 232 us; the launch traced here: 231 us
  waiting for transfers between devices  78.2 us (34%)
  Pallas kernels  77.1 us (33%)
  starting transfers between devices  48.6 us (21%)
  local copies, waits for them, and re-layouts  25.4 us (11%)
    ppermute x7, waiting for transfers between devices, pair(): return lax.ppermute(block, 'tm', [(i, i ^ 1) for i in range(time_devices)])  44.4 us
    ppermute x7, waiting for transfers between devices, hop(): lax.ppermute(block, 'tm', [(i, i + 2) for i in range(skip, time_devices -...  32.2 us
    pallas_call x2, Pallas kernels, beam_power(): pl.pallas_call(functools.partial(beam_kernel, len(sources), earlier is no...  25.1 us
    ppermute x8, starting transfers between devices, swap(): return lax.ppermute(block, 'stn', [(0, 1), (1, 0)])  20.5 us
    ppermute x7, starting transfers between devices, hop(): lax.ppermute(block, 'tm', [(i, i + 2) for i in range(skip, time_devices -...  19.8 us
    pallas_call x4, Pallas kernels, far_filter(): pl.pallas_call(far_kernel, out_shape=(shape, shape), grid_spec=pltpu.Pref...  16.4 us
    pallas_call x2, Pallas kernels, near_filter(): pl.pallas_call(near_kernel, out_shape=jax.ShapeDtypeStruct((2 * frames, p...  15.7 us
    unnamed x69, local copies, waits for them, and re-layouts  11.9 us
  transfers between devices with their start and end apart: 25, of which 7 were waited for; matrix products, arithmetic and copies ran while one was open for 7% of the time, Pallas kernels for 23%

profile of v5, /device:TPU:17, one launch (start us, length us, event | category | flops | bytes accessed | tf_op | source)
XLA Modules:
  0.0 230.5 jit_solution(12661711555343248398)
XLA Ops:
  0.9 3.2 %collective-permute-start.1 = (bf16[16,256]{1,0:T(8,128)(2,1)S(1)}, bf16[16,256]{1,0:T(8,128)(2,1)S(1)}, u32[]{:S(2)}, u32[]{:S(2)}) collective-permute-start(bf16[16,256]{1,0:T(8,128)(2,1)S(1)} %get-tuple-element.26), channel_id=1, source_target_pairs={{0,8},{2,10},{4,12},{6,14},{8,0},{10,2},{12,4},{14,6},{1,9},{3,11}... | collective-permute-start | bytes 24584 | tf_op jit(solution)/shard_map/ppermute | solution.py:505
  4.7 3.1 %cut.2.refs_0_ = bf16[32,2,4,2,2048]{4,3,2,1,0:T(2,128)(2,1)} custom-call(s32[2]{0:T(128)} %pad_add_fusion.place.refs_0_, bf16[64,2,4,2,2048]{4,3,2,1,0:T(2,128)(2,1)} %voltages.3), custom_call_target="tpu_custom_call" | custom-call | bytes 6600000 | tf_op jit(solution)/shard_map/cut/pallas_call | solution.py:123
  9.1 3.3 %cut.3 = (bf16[32,4,2,2048]{3,2,1,0:T(2,128)(2,1)}, bf16[32,4,2,2048]{3,2,1,0:T(2,128)(2,1)}) custom-call(s32[2]{0:T(128)} %pad_add_fusion.place.refs_0_, bf16[64,2,4,2,2048]{4,3,2,1,0:T(2,128)(2,1)} %voltages.3, bf16[32,2,4,2,2048]{4,3,2,1,0:T(2,128)(2,1)} %after.5.rest_0_), custom_call_target="tpu_custom_call" | custom-call | bytes 6600000 | tf_op jit(solution)/shard_map/cut/pallas_call | solution.py:123
  13.7 3.4 %collective-permute-start.4 = (bf16[32,2,4,2,2048]{4,3,2,1,0:T(2,128)(2,1)S(1)}, bf16[32,2,4,2,2048]{4,3,2,1,0:T(2,128)(2,1)}, u32[]{:S(2)}, u32[]{:S(2)}) collective-permute-start(bf16[32,2,4,2,2048]{4,3,2,1,0:T(2,128)(2,1)S(1)} %copy-done), channel_id=1, source_target_pairs={{0,4},{2,6},{4,8},{6,10},{8,12},{10,14},{1,5},{3,7},{5,9},{7,11},{... | collective-permute-start | bytes 6291464 | tf_op jit(solution)/shard_map/ppermute | solution.py:494
  17.4 18.8 %collective-permute-done.5.refs_0_ = bf16[32,4,2,2048]{3,2,1,0:T(2,128)(2,1)} collective-permute-done((bf16[32,4,2,2048]{3,2,1,0:T(2,128)(2,1)}, bf16[32,4,2,2048]{3,2,1,0:T(2,128)(2,1)}, u32[]{:S(2)}, u32[]{:S(2)}) %collective-permute-start.5) | collective-permute-done | bytes 1048608 | tf_op jit(solution)/shard_map/ppermute | solution.py:491
  38.9 3.1 %collective-permute-start.6 = (bf16[4,2,32,2048]{3,2,1,0:T(8,128)(2,1)}, bf16[4,2,32,2048]{3,2,1,0:T(8,128)(2,1)}, u32[]{:S(2)}, u32[]{:S(2)}) collective-permute-start(bf16[4,2,32,2048]{3,2,1,0:T(8,128)(2,1)} %bitcast.23.rest_0_.other), channel_id=1, source_target_pairs={{0,4},{2,6},{4,8},{6,10},{8,12},{10,14},{1,5},{3,7},{5,9},{7,11},{... | collective-permute-start | bytes 3145736 | tf_op jit(solution)/shard_map/ppermute | solution.py:494
  42.1 16.5 %collective-permute-done.3.refs_0_ = bf16[32,4,2,2048]{3,2,1,0:T(2,128)(2,1)S(1)} collective-permute-done((bf16[32,4,2,2048]{3,2,1,0:T(2,128)(2,1)}, bf16[32,4,2,2048]{3,2,1,0:T(2,128)(2,1)S(1)}, u32[]{:S(2)}, u32[]{:S(2)}) %collective-permute-start.3) | collective-permute-done | bytes 1048608 | tf_op jit(solution)/shard_map/ppermute | solution.py:491
  62.8 4.1 %copy.20 = bf16[32,2,4,2,2048]{4,0,3,2,1:T(8,128)(2,1)} copy(bf16[32,2,4,2,2048]{4,3,2,1,0:T(2,128)(2,1)} %after.7) | data formatting | bytes 4194304 | tf_op jit(solution)/shard_map/after/pallas_call | solution.py:77
  66.9 16.8 %collective-permute-done.6.other_back = bf16[4,2,32,2048]{3,2,1,0:T(8,128)(2,1)} collective-permute-done((bf16[4,2,32,2048]{3,2,1,0:T(8,128)(2,1)}, bf16[4,2,32,2048]{3,2,1,0:T(8,128)(2,1)}, u32[]{:S(2)}, u32[]{:S(2)}) %collective-permute-start.6) | collective-permute-done | bytes 1048608 | tf_op jit(solution)/shard_map/ppermute | solution.py:494
  86.5 3.2 %collective-permute-start.11 = (bf16[7,2,16,2048]{3,2,1,0:T(8,128)(2,1)}, bf16[7,2,16,2048]{3,2,1,0:T(8,128)(2,1)}, u32[]{:S(2)}, u32[]{:S(2)}) collective-permute-start(bf16[7,2,16,2048]{3,2,1,0:T(8,128)(2,1)} %onward.4.refs_1_.rest_0_), channel_id=1, source_target_pairs={{4,8},{6,10},{8,12},{10,14},{5,9},{7,11},{9,13},{11,15},{20,24},{2... | collective-permute-start | bytes 2752520 | tf_op jit(solution)/shard_map/ppermute | solution.py:494
  104.7 7.8 %near.3.partial = f32[8,2,32,2048]{3,2,1,0:T(8,128)} custom-call(s32[2]{0:T(128)} %pad_add_fusion.place.refs_0_, f32[16,8,2048]{2,1,0:T(8,128)} %broadcast_in_dim.2.taps, bf16[2,4,2,32,2048]{4,3,2,1,0:T(8,128)(2,1)} %bitcast.31, bf16[4,2,32,2048]{3,2,1,0:T(8,128)(2,1)} %bitcast.23.rest_0_.other, bf16[2,4,2,32,2048]{4,3,2,1,0:T(8,128)(2,1)} %bitcast.27, ...), custom_call_target="tpu_custom_call" | custom-call | bytes 33000000 | tf_op jit(solution)/shard_map/near/pallas_call | solution.py:222
  112.5 4.1 %far.4 = (bf16[4,2,16,2048]{3,2,1,0:T(8,128)(2,1)}, bf16[4,2,16,2048]{3,2,1,0:T(8,128)(2,1)}) custom-call(s32[2]{0:T(128)} %pad_add_fusion.place.refs_0_, f32[16,8,2048]{2,1,0:T(8,128)} %broadcast_in_dim.2.taps, f32[8,2,32,2048]{3,2,1,0:T(8,128)} %near.3.partial, bf16[7,2,16,2048]{3,2,1,0:T(8,128)(2,1)} %collective-permute-done.11.far), custom_call_target="tpu_custom_call" | custom-call | bytes 9900000 | tf_op jit(solution)/shard_map/far/pallas_call | solution.py:247
  117.9 12.7 %collective-permute-done.7.other_back = bf16[4,2,32,2048]{3,2,1,0:T(8,128)(2,1)S(1)} collective-permute-done((bf16[4,2,32,2048]{3,2,1,0:T(8,128)(2,1)}, bf16[4,2,32,2048]{3,2,1,0:T(8,128)(2,1)S(1)}, u32[]{:S(2)}, u32[]{:S(2)}) %collective-permute-start.7) | collective-permute-done | bytes 1048608 | tf_op jit(solution)/shard_map/ppermute | solution.py:494
  139.7 7.8 %near.2.rest_1_.partial = f32[8,2,32,2048]{3,2,1,0:T(8,128)} custom-call(s32[2]{0:T(128)} %pad_add_fusion.place.refs_0_, f32[16,8,2048]{2,1,0:T(8,128)} %broadcast_in_dim.2.taps, bf16[2,4,2,32,2048]{4,3,2,1,0:T(8,128)(2,1)} %bitcast.32, bf16[4,2,32,2048]{3,2,1,0:T(8,128)(2,1)} %bitcast.35, bf16[2,4,2,32,2048]{4,3,2,1,0:T(8,128)(2,1)} %bitcast.30, ...), custom_call_target="tpu_custom_call" | custom-call | bytes 33000000 | tf_op jit(solution)/shard_map/near/pallas_call | solution.py:222
  152.0 4.1 %far.5 = (bf16[4,2,16,2048]{3,2,1,0:T(8,128)(2,1)}, bf16[4,2,16,2048]{3,2,1,0:T(8,128)(2,1)}) custom-call(s32[2]{0:T(128)} %pad_add_fusion.place.refs_0_, f32[16,8,2048]{2,1,0:T(8,128)} %broadcast_in_dim.2.taps, f32[8,2,32,2048]{3,2,1,0:T(8,128)} %near.3.partial, bf16[7,2,16,2048]{3,2,1,0:T(8,128)(2,1)} %copy-done.8, bf16[4,2,16,2048]{3,2,1,0:T(8,128)(2,1)} %copy-done.5, ...), custom_call_target="tpu_custom_call" | custom-call | bytes 9900000 | tf_op jit(solution)/shard_map/far/pallas_call | solution.py:247
  156.3 6.6 %collective-permute-start.16 = (bf16[4,2,16,2048]{3,2,1,0:T(8,128)(2,1)S(1)}, bf16[4,2,16,2048]{3,2,1,0:T(8,128)(2,1)S(1)}, u32[]{:S(2)}, u32[]{:S(2)}) collective-permute-start(bf16[4,2,16,2048]{3,2,1,0:T(8,128)(2,1)S(1)} %copy-done.11), channel_id=1, source_target_pairs={{0,1},{1,0},{2,3},{3,2},{4,5},{5,4},{6,7},{7,6},{8,9},{9,8},{10,11... | collective-permute-start | bytes 1572872 | tf_op jit(solution)/shard_map/ppermute | solution.py:497
  162.9 3.5 %collective-permute-start.14 = (bf16[7,2,16,2048]{3,2,1,0:T(8,128)(2,1)S(1)}, bf16[7,2,16,2048]{3,2,1,0:T(8,128)(2,1)S(1)}, u32[]{:S(2)}, u32[]{:S(2)}) collective-permute-start(bf16[7,2,16,2048]{3,2,1,0:T(8,128)(2,1)S(1)} %copy-done.4), channel_id=1, source_target_pairs={{4,8},{6,10},{8,12},{10,14},{5,9},{7,11},{9,13},{11,15},{20,24},{2... | collective-permute-start | bytes 2752520 | tf_op jit(solution)/shard_map/ppermute | solution.py:494
  166.8 5.0 %collective-permute-start.18 = (bf16[4,2,16,2048]{3,2,1,0:T(8,128)(2,1)}, bf16[4,2,16,2048]{3,2,1,0:T(8,128)(2,1)S(1)}, u32[]{:S(2)}, u32[]{:S(2)}) collective-permute-start(bf16[4,2,16,2048]{3,2,1,0:T(8,128)(2,1)} %copy-done.5), channel_id=1, source_target_pairs={{0,1},{1,0},{2,3},{3,2},{4,5},{5,4},{6,7},{7,6},{8,9},{9,8},{10,11... | collective-permute-start | bytes 1572872 | tf_op jit(solution)/shard_map/ppermute | solution.py:497
  171.8 4.4 %collective-permute-start.19 = (bf16[4,2,16,2048]{3,2,1,0:T(8,128)(2,1)S(1)}, bf16[4,2,16,2048]{3,2,1,0:T(8,128)(2,1)S(1)}, u32[]{:S(2)}, u32[]{:S(2)}) collective-permute-start(bf16[4,2,16,2048]{3,2,1,0:T(8,128)(2,1)S(1)} %collective-permute-done.13.rest_0_.refs_4_), channel_id=1, source_target_pairs={{0,1},{1,0},{2,3},{3,2},{4,5},{5,4},{6,7},{7,6},{8,9},{9,8},{10,11... | collective-permute-start | bytes 1572872 | tf_op jit(solution)/shard_map/ppermute | solution.py:497
  176.2 4.1 %far.6 = (bf16[4,2,16,2048]{3,2,1,0:T(8,128)(2,1)}, bf16[4,2,16,2048]{3,2,1,0:T(8,128)(2,1)}) custom-call(s32[2]{0:T(128)} %pad_add_fusion.place.refs_0_, f32[16,8,2048]{2,1,0:T(8,128)} %broadcast_in_dim.2.taps, f32[8,2,32,2048]{3,2,1,0:T(8,128)} %near.2.rest_1_.partial, bf16[7,2,16,2048]{3,2,1,0:T(8,128)(2,1)} %copy-done.10, bf16[4,2,16,2048]{3,2,1,0:T(8,128)(2,1)} %copy-done.7), custom_call_target="tpu_custom_call" | custom-call | bytes 9900000 | tf_op jit(solution)/shard_map/far/pallas_call | solution.py:247
  182.4 11.3 %beams.2.rest_1_.refs_11_ = f32[8,512,256]{2,1,0:T(8,128)} custom-call(s32[2]{0:T(128)} %pad_add_fusion.place.refs_0_, bf16[4,2,16,2048]{3,2,1,0:T(8,128)(2,1)} %get-tuple-element.21.refs_1_, bf16[4,2,16,2048]{3,2,1,0:T(8,128)(2,1)} %get-tuple-element.22.refs_2_, bf16[4,2,16,2048]{3,2,1,0:T(8,128)(2,1)} %copy-done.5, bf16[4,2,16,2048]{3,2,1,0:T(8,128)(2,1)} %copy-done.7, ...), custom_call_target="tpu_custom_call" | custom-call | tf_op jit(solution)/shard_map/beams/pallas_call | solution.py:461
  195.5 4.1 %far.7 = (bf16[4,2,16,2048]{3,2,1,0:T(8,128)(2,1)}, bf16[4,2,16,2048]{3,2,1,0:T(8,128)(2,1)}) custom-call(s32[2]{0:T(128)} %pad_add_fusion.place.refs_0_, f32[16,8,2048]{2,1,0:T(8,128)} %broadcast_in_dim.2.taps, f32[8,2,32,2048]{3,2,1,0:T(8,128)} %near.2.rest_1_.partial, bf16[7,2,16,2048]{3,2,1,0:T(8,128)(2,1)} %copy-done.9, ...), custom_call_target="tpu_custom_call" | custom-call | bytes 9900000 | tf_op jit(solution)/shard_map/far/pallas_call | solution.py:247
  202.9 9.1 %collective-permute-done.20.refs_4_ = bf16[4,2,16,2048]{3,2,1,0:T(8,128)(2,1)S(1)} collective-permute-done((bf16[4,2,16,2048]{3,2,1,0:T(8,128)(2,1)}, bf16[4,2,16,2048]{3,2,1,0:T(8,128)(2,1)S(1)}, u32[]{:S(2)}, u32[]{:S(2)}) %collective-permute-start.20) | collective-permute-done | bytes 524320 | tf_op jit(solution)/shard_map/ppermute | solution.py:491
  216.5 13.9 %beams.3 = f32[1024,4,256]{2,1,0:T(4,128)} custom-call(s32[2]{0:T(128)} %pad_add_fusion.place.refs_0_, bf16[4,2,16,2048]{3,2,1,0:T(8,128)(2,1)} %get-tuple-element.19.refs_1_, bf16[4,2,16,2048]{3,2,1,0:T(8,128)(2,1)} %get-tuple-element.23.refs_2_, bf16[4,2,16,2048]{3,2,1,0:T(8,128)(2,1)} %copy-done.6, bf16[4,2,16,2048]{3,2,1,0:T(8,128)(2,1)} %copy-done.15, ...), custom_call_target="tpu_custom_call" | custom-call | tf_op jit(solution)/shard_map/beams/pallas_call | solution.py:461
  (131 shorter events, 55.9 us)
Async XLA Ops:
  0.7 7.1 %collective-permute-start.2 = (bf16[16,256]{1,0:T(8,128)(2,1)S(1)}, bf16[16,256]{1,0:T(8,128)(2,1)S(1)}, u32[]{:S(2)}, u32[]{:S(2)}) collective-permute-start(bf16[16,256]{1,0:T(8,128)(2,1)S(1)} %get-tuple-element.26), channel_id=1, source_target_pairs={{0,12},{2,14},{4,8},{6,10},{8,4},{10,6},{12,0},{14,2},{1,13},{3,15... | collective-permute-start | bytes 24584 | tf_op jit(solution)/shard_map/ppermute | solution.py:505
  0.9 7.0 %collective-permute-start.1 = (bf16[16,256]{1,0:T(8,128)(2,1)S(1)}, bf16[16,256]{1,0:T(8,128)(2,1)S(1)}, u32[]{:S(2)}, u32[]{:S(2)}) collective-permute-start(bf16[16,256]{1,0:T(8,128)(2,1)S(1)} %get-tuple-element.26), channel_id=1, source_target_pairs={{0,8},{2,10},{4,12},{6,14},{8,0},{10,2},{12,4},{14,6},{1,9},{3,11}... | collective-permute-start | bytes 24584 | tf_op jit(solution)/shard_map/ppermute | solution.py:505
  4.1 3.8 %collective-permute-start = (bf16[16,256]{1,0:T(8,128)(2,1)S(1)}, bf16[16,256]{1,0:T(8,128)(2,1)S(1)}, u32[]{:S(2)}, u32[]{:S(2)}) collective-permute-start(bf16[16,256]{1,0:T(8,128)(2,1)S(1)} %get-tuple-element.26), channel_id=1, source_target_pairs={{0,4},{2,6},{4,0},{6,2},{8,12},{10,14},{12,8},{14,10},{1,5},{3,7},... | collective-permute-start | bytes 24584 | tf_op jit(solution)/shard_map/ppermute | solution.py:505
  12.4 23.8 %collective-permute-start.5 = (bf16[32,4,2,2048]{3,2,1,0:T(2,128)(2,1)}, bf16[32,4,2,2048]{3,2,1,0:T(2,128)(2,1)}, u32[]{:S(2)}, u32[]{:S(2)}) collective-permute-start(bf16[32,4,2,2048]{3,2,1,0:T(2,128)(2,1)} %get-tuple-element.16), channel_id=1, source_target_pairs={{0,2},{2,0},{4,6},{6,4},{8,10},{10,8},{12,14},{14,12},{1,3},{3,1},... | collective-permute-start | bytes 3145736 | tf_op jit(solution)/shard_map/ppermute | solution.py:491
  13.7 48.8 %collective-permute-start.4 = (bf16[32,2,4,2,2048]{4,3,2,1,0:T(2,128)(2,1)S(1)}, bf16[32,2,4,2,2048]{4,3,2,1,0:T(2,128)(2,1)}, u32[]{:S(2)}, u32[]{:S(2)}) collective-permute-start(bf16[32,2,4,2,2048]{4,3,2,1,0:T(2,128)(2,1)S(1)} %copy-done), channel_id=1, source_target_pairs={{0,4},{2,6},{4,8},{6,10},{8,12},{10,14},{1,5},{3,7},{5,9},{7,11},{... | collective-permute-start | bytes 6291464 | tf_op jit(solution)/shard_map/ppermute | solution.py:494
  17.1 41.6 %collective-permute-start.3 = (bf16[32,4,2,2048]{3,2,1,0:T(2,128)(2,1)}, bf16[32,4,2,2048]{3,2,1,0:T(2,128)(2,1)S(1)}, u32[]{:S(2)}, u32[]{:S(2)}) collective-permute-start(bf16[32,4,2,2048]{3,2,1,0:T(2,128)(2,1)} %get-tuple-element.15), channel_id=1, source_target_pairs={{0,2},{2,0},{4,6},{6,4},{8,10},{10,8},{12,14},{14,12},{1,3},{3,1},... | collective-permute-start | bytes 3145736 | tf_op jit(solution)/shard_map/ppermute | solution.py:491
  38.9 44.8 %collective-permute-start.6 = (bf16[4,2,32,2048]{3,2,1,0:T(8,128)(2,1)}, bf16[4,2,32,2048]{3,2,1,0:T(8,128)(2,1)}, u32[]{:S(2)}, u32[]{:S(2)}) collective-permute-start(bf16[4,2,32,2048]{3,2,1,0:T(8,128)(2,1)} %bitcast.23.rest_0_.other), channel_id=1, source_target_pairs={{0,4},{2,6},{4,8},{6,10},{8,12},{10,14},{1,5},{3,7},{5,9},{7,11},{... | collective-permute-start | bytes 3145736 | tf_op jit(solution)/shard_map/ppermute | solution.py:494
  86.5 26.1 %collective-permute-start.11 = (bf16[7,2,16,2048]{3,2,1,0:T(8,128)(2,1)}, bf16[7,2,16,2048]{3,2,1,0:T(8,128)(2,1)}, u32[]{:S(2)}, u32[]{:S(2)}) collective-permute-start(bf16[7,2,16,2048]{3,2,1,0:T(8,128)(2,1)} %onward.4.refs_1_.rest_0_), channel_id=1, source_target_pairs={{4,8},{6,10},{8,12},{10,14},{5,9},{7,11},{9,13},{11,15},{20,24},{2... | collective-permute-start | bytes 2752520 | tf_op jit(solution)/shard_map/ppermute | solution.py:494
  89.7 40.9 %collective-permute-start.7 = (bf16[4,2,32,2048]{3,2,1,0:T(8,128)(2,1)}, bf16[4,2,32,2048]{3,2,1,0:T(8,128)(2,1)S(1)}, u32[]{:S(2)}, u32[]{:S(2)}) collective-permute-start(bf16[4,2,32,2048]{3,2,1,0:T(8,128)(2,1)} %after.9), channel_id=1, source_target_pairs={{0,4},{2,6},{4,8},{6,10},{8,12},{10,14},{1,5},{3,7},{5,9},{7,11},{... | collective-permute-start | bytes 3145736 | tf_op jit(solution)/shard_map/ppermute | solution.py:494
  92.9 7.4 %collective-permute-start.8 = (bf16[64,256]{1,0:T(8,128)(2,1)S(1)}, bf16[64,256]{1,0:T(8,128)(2,1)S(1)}, u32[]{:S(2)}, u32[]{:S(2)}) collective-permute-start(bf16[64,256]{1,0:T(8,128)(2,1)S(1)} %pad_maximum_fusion), channel_id=1, source_target_pairs={{0,2},{2,0},{4,6},{6,4},{8,10},{10,8},{12,14},{14,12},{1,3},{3,1},... | collective-permute-start | bytes 98312 | tf_op jit(solution)/shard_map/ppermute | solution.py:491
  95.9 54.4 %collective-permute-start.10 = (bf16[7,2,16,2048]{3,2,1,0:T(8,128)(2,1)}, bf16[7,2,16,2048]{3,2,1,0:T(8,128)(2,1)S(1)}, u32[]{:S(2)}, u32[]{:S(2)}) collective-permute-start(bf16[7,2,16,2048]{3,2,1,0:T(8,128)(2,1)} %onward.7.rest_1_), channel_id=1, source_target_pairs={{4,8},{6,10},{8,12},{10,14},{5,9},{7,11},{9,13},{11,15},{20,24},{2... | collective-permute-start | bytes 2752520 | tf_op jit(solution)/shard_map/ppermute | solution.py:494
  116.6 33.6 %collective-permute-start.12 = (bf16[4,2,16,2048]{3,2,1,0:T(8,128)(2,1)}, bf16[4,2,16,2048]{3,2,1,0:T(8,128)(2,1)S(1)}, u32[]{:S(2)}, u32[]{:S(2)}) collective-permute-start(bf16[4,2,16,2048]{3,2,1,0:T(8,128)(2,1)} %get-tuple-element.17), channel_id=1, source_target_pairs={{0,2},{2,0},{4,6},{6,4},{8,10},{10,8},{12,14},{14,12},{1,3},{3,1},... | collective-permute-start | bytes 1572872 | tf_op jit(solution)/shard_map/ppermute | solution.py:491
  134.2 37.6 %collective-permute-start.9 = (bf16[7,2,16,2048]{3,2,1,0:T(8,128)(2,1)}, bf16[7,2,16,2048]{3,2,1,0:T(8,128)(2,1)S(1)}, u32[]{:S(2)}, u32[]{:S(2)}) collective-permute-start(bf16[7,2,16,2048]{3,2,1,0:T(8,128)(2,1)} %onward.5.rest_0_), channel_id=1, source_target_pairs={{4,8},{6,10},{8,12},{10,14},{5,9},{7,11},{9,13},{11,15},{20,24},{2... | collective-permute-start | bytes 2752520 | tf_op jit(solution)/shard_map/ppermute | solution.py:494
  156.1 10.7 %collective-permute-start.13 = (bf16[4,2,16,2048]{3,2,1,0:T(8,128)(2,1)}, bf16[4,2,16,2048]{3,2,1,0:T(8,128)(2,1)S(1)}, u32[]{:S(2)}, u32[]{:S(2)}) collective-permute-start(bf16[4,2,16,2048]{3,2,1,0:T(8,128)(2,1)} %get-tuple-element.18), channel_id=1, source_target_pairs={{0,2},{2,0},{4,6},{6,4},{8,10},{10,8},{12,14},{14,12},{1,3},{3,1},... | collective-permute-start | bytes 1572872 | tf_op jit(solution)/shard_map/ppermute | solution.py:491
  156.3 24.0 %collective-permute-start.16 = (bf16[4,2,16,2048]{3,2,1,0:T(8,128)(2,1)S(1)}, bf16[4,2,16,2048]{3,2,1,0:T(8,128)(2,1)S(1)}, u32[]{:S(2)}, u32[]{:S(2)}) collective-permute-start(bf16[4,2,16,2048]{3,2,1,0:T(8,128)(2,1)S(1)} %copy-done.11), channel_id=1, source_target_pairs={{0,1},{1,0},{2,3},{3,2},{4,5},{5,4},{6,7},{7,6},{8,9},{9,8},{10,11... | collective-permute-start | bytes 1572872 | tf_op jit(solution)/shard_map/ppermute | solution.py:497
  162.9 30.8 %collective-permute-start.14 = (bf16[7,2,16,2048]{3,2,1,0:T(8,128)(2,1)S(1)}, bf16[7,2,16,2048]{3,2,1,0:T(8,128)(2,1)S(1)}, u32[]{:S(2)}, u32[]{:S(2)}) collective-permute-start(bf16[7,2,16,2048]{3,2,1,0:T(8,128)(2,1)S(1)} %copy-done.4), channel_id=1, source_target_pairs={{4,8},{6,10},{8,12},{10,14},{5,9},{7,11},{9,13},{11,15},{20,24},{2... | collective-permute-start | bytes 2752520 | tf_op jit(solution)/shard_map/ppermute | solution.py:494
  166.5 14.2 %collective-permute-start.17 = (bf16[4,2,16,2048]{3,2,1,0:T(8,128)(2,1)}, bf16[4,2,16,2048]{3,2,1,0:T(8,128)(2,1)S(1)}, u32[]{:S(2)}, u32[]{:S(2)}) collective-permute-start(bf16[4,2,16,2048]{3,2,1,0:T(8,128)(2,1)} %get-tuple-element.22.refs_2_), channel_id=1, source_target_pairs={{0,1},{1,0},{2,3},{3,2},{4,5},{5,4},{6,7},{7,6},{8,9},{9,8},{10,11... | collective-permute-start | bytes 1572872 | tf_op jit(solution)/shard_map/ppermute | solution.py:497
  166.8 13.8 %collective-permute-start.18 = (bf16[4,2,16,2048]{3,2,1,0:T(8,128)(2,1)}, bf16[4,2,16,2048]{3,2,1,0:T(8,128)(2,1)S(1)}, u32[]{:S(2)}, u32[]{:S(2)}) collective-permute-start(bf16[4,2,16,2048]{3,2,1,0:T(8,128)(2,1)} %copy-done.5), channel_id=1, source_target_pairs={{0,1},{1,0},{2,3},{3,2},{4,5},{5,4},{6,7},{7,6},{8,9},{9,8},{10,11... | collective-permute-start | bytes 1572872 | tf_op jit(solution)/shard_map/ppermute | solution.py:497
  171.8 8.8 %collective-permute-start.19 = (bf16[4,2,16,2048]{3,2,1,0:T(8,128)(2,1)S(1)}, bf16[4,2,16,2048]{3,2,1,0:T(8,128)(2,1)S(1)}, u32[]{:S(2)}, u32[]{:S(2)}) collective-permute-start(bf16[4,2,16,2048]{3,2,1,0:T(8,128)(2,1)S(1)} %collective-permute-done.13.rest_0_.refs_4_), channel_id=1, source_target_pairs={{0,1},{1,0},{2,3},{3,2},{4,5},{5,4},{6,7},{7,6},{8,9},{9,8},{10,11... | collective-permute-start | bytes 1572872 | tf_op jit(solution)/shard_map/ppermute | solution.py:497
  180.3 13.4 %collective-permute-start.15 = (bf16[4,2,16,2048]{3,2,1,0:T(8,128)(2,1)}, bf16[4,2,16,2048]{3,2,1,0:T(8,128)(2,1)S(1)}, u32[]{:S(2)}, u32[]{:S(2)}) collective-permute-start(bf16[4,2,16,2048]{3,2,1,0:T(8,128)(2,1)} %get-tuple-element.20), channel_id=1, source_target_pairs={{0,2},{2,0},{4,6},{6,4},{8,10},{10,8},{12,14},{14,12},{1,3},{3,1},... | collective-permute-start | bytes 1572872 | tf_op jit(solution)/shard_map/ppermute | solution.py:491
  199.6 12.4 %collective-permute-start.20 = (bf16[4,2,16,2048]{3,2,1,0:T(8,128)(2,1)}, bf16[4,2,16,2048]{3,2,1,0:T(8,128)(2,1)S(1)}, u32[]{:S(2)}, u32[]{:S(2)}) collective-permute-start(bf16[4,2,16,2048]{3,2,1,0:T(8,128)(2,1)} %get-tuple-element.24), channel_id=1, source_target_pairs={{0,2},{2,0},{4,6},{6,4},{8,10},{10,8},{12,14},{14,12},{1,3},{3,1},... | collective-permute-start | bytes 1572872 | tf_op jit(solution)/shard_map/ppermute | solution.py:491
  200.8 13.3 %collective-permute-start.21 = (bf16[4,2,16,2048]{3,2,1,0:T(8,128)(2,1)S(1)}, bf16[4,2,16,2048]{3,2,1,0:T(8,128)(2,1)S(1)}, u32[]{:S(2)}, u32[]{:S(2)}) collective-permute-start(bf16[4,2,16,2048]{3,2,1,0:T(8,128)(2,1)S(1)} %copy-done.12), channel_id=1, source_target_pairs={{0,1},{1,0},{2,3},{3,2},{4,5},{5,4},{6,7},{7,6},{8,9},{9,8},{10,11... | collective-permute-start | bytes 1572872 | tf_op jit(solution)/shard_map/ppermute | solution.py:497
  202.4 11.8 %collective-permute-start.22 = (bf16[4,2,16,2048]{3,2,1,0:T(8,128)(2,1)}, bf16[4,2,16,2048]{3,2,1,0:T(8,128)(2,1)S(1)}, u32[]{:S(2)}, u32[]{:S(2)}) collective-permute-start(bf16[4,2,16,2048]{3,2,1,0:T(8,128)(2,1)} %get-tuple-element.23.refs_2_), channel_id=1, source_target_pairs={{0,1},{1,0},{2,3},{3,2},{4,5},{5,4},{6,7},{7,6},{8,9},{9,8},{10,11... | collective-permute-start | bytes 1572872 | tf_op jit(solution)/shard_map/ppermute | solution.py:497
  202.4 11.8 %collective-permute-start.23 = (bf16[4,2,16,2048]{3,2,1,0:T(8,128)(2,1)}, bf16[4,2,16,2048]{3,2,1,0:T(8,128)(2,1)S(1)}, u32[]{:S(2)}, u32[]{:S(2)}) collective-permute-start(bf16[4,2,16,2048]{3,2,1,0:T(8,128)(2,1)} %copy-done.6), channel_id=1, source_target_pairs={{0,1},{1,0},{2,3},{3,2},{4,5},{5,4},{6,7},{7,6},{8,9},{9,8},{10,11... | collective-permute-start | bytes 1572872 | tf_op jit(solution)/shard_map/ppermute | solution.py:497
  (33 other events, 147.1 us)

commit v6 on v5

--- a/solution.py
+++ b/solution.py
@@ -85,53 +85,66 @@
     )(block, *earlier)
 
 
-def cut_kernel(mine, place, voltages, *rest):
-    outs, (buffer, loads, stores) = rest[-3 - len(mine) : -3], rest[-3:]
-    stations = buffer.shape[0]
-    pieces = loads.shape[0]
-    size = stations // pieces
-    start = jnp.where(place[0] == mine[0][0], 0, stations)
-
-    def load(k):
+def cut_kernel(cuts, place, voltages, *rest):
+    (own, *outs), (buffer, loads, stores) = rest[-4 - len(cuts) : -3], rest[-3:]
+    half = own.shape[0]
+    pieces = loads.shape[1]
+    size = half // pieces
+    side = place[0]
+
+    def load(h, k):
+        start = jnp.where(side == h, 0, half) + k * size
         return pltpu.make_async_copy(
-            voltages.at[pl.ds(start + k * size, size)], buffer.at[pl.ds(k * size, size)], loads.at[k]
+            voltages.at[pl.ds(start, size)], buffer.at[h, pl.ds(k * size, size)], loads.at[h, k]
         )
 
-    def store(k, i):
-        source = buffer.at[pl.ds(k * size, size)]
-        if mine[i][1] is not None:
-            source = source.at[:, mine[i][1]]
-        return pltpu.make_async_copy(source, outs[i].at[pl.ds(k * size, size)], stores.at[k, i])
-
-    every = [(k, i) for k in range(pieces) for i in range(len(mine))]
-    for k in range(pieces):
-        load(k).start()
-    for k in range(pieces):
-        load(k).wait()
-        for i in range(len(mine)):
-            store(k, i).start()
-    for k, i in every:
-        store(k, i).wait()
-
-
-def cut(place, voltages, mine, earlier=()):
+    def store(h, k):
+        copies = []
+        if h == 0:
+            copies.append(pltpu.make_async_copy(buffer.at[0, pl.ds(k * size, size)], own.at[pl.ds(k * size, size)], stores.at[0, k]))
+        else:
+            for pol in range(voltages.shape[1]):
+                for out, (which, low, count) in zip(outs, cuts):
+                    if which == pol and low <= k * size < low + count:
+                        copies.append(
+                            pltpu.make_async_copy(
+                                buffer.at[1, pl.ds(k * size, size), pol],
+                                out.at[pl.ds(k * size - low, size)],
+                                stores.at[1 + pol, k],
+                            )
+                        )
+        return copies
+
+    order = [(h, k) for h in range(2) for k in range(pieces)]
+    for h, k in order:
+        load(h, k).start()
+    for h, k in order:
+        load(h, k).wait()
+        for copy in store(h, k):
+            copy.start()
+    for h, k in order:
+        for copy in store(h, k):
+            copy.wait()
+
+
+def cut(place, voltages, cuts, earlier):
     stations, pols, frames, parts, samples = voltages.shape
     half = stations // 2
     pieces = 4
-    shapes = [(half,) + ((pols,) if pol is None else ()) + (frames, parts, samples) for _, pol in mine]
-    anywhere = pl.BlockSpec(memory_space=pl.ANY)
-    return pl.pallas_call(
-        functools.partial(cut_kernel, mine),
+    shapes = [(half, pols, frames, parts, samples)] + [(size, frames, parts, samples) for _, _, size in cuts]
+    anywhere = pl.BlockSpec(memory_space=pltpu.HBM)
+    return pl.pallas_call(
+        functools.partial(cut_kernel, cuts),
         out_shape=[jax.ShapeDtypeStruct(shape, BF16) for shape in shapes],
-        in_specs=[pl.BlockSpec(memory_space=pltpu.SMEM), anywhere] + [anywhere] * len(earlier),
+        in_specs=[pl.BlockSpec(memory_space=pltpu.SMEM), anywhere] + [pl.BlockSpec(memory_space=pl.ANY)] * len(earlier),
         out_specs=[anywhere] * len(shapes),
         scratch_shapes=[
-            pltpu.VMEM((half, pols, frames, parts, samples), BF16),
-            pltpu.SemaphoreType.DMA((pieces,)),
-            pltpu.SemaphoreType.DMA((pieces, len(mine))),
+            pltpu.VMEM((2,) + shapes[0], BF16),
+            pltpu.SemaphoreType.DMA((2, pieces)),
+            pltpu.SemaphoreType.DMA((1 + pols, pieces)),
         ],
         compiler_params=pltpu.CompilerParams(vmem_limit_bytes=VMEM_LIMIT),
-        cost_estimate=cost(2),
+        cost_estimate=cost(4),
         name="cut",
     )(place, voltages, *earlier)
 
@@ -187,14 +200,16 @@
         run(other, own, other_back, own_back)
 
 
-def far_kernel(place, taps, partial, far, *rest):
+def far_kernel(place, taps, partial, straight, mixed, *rest):
     keep, send = rest[-2:]
     frames = keep.shape[0]
     count = 2 * frames
-    history = taps.shape[0] - 1
-
-    def run(first_out, second_out):
-        window = [(i - history, far, i) for i in range(far.shape[0])]
+    first = 1 - 2 * count
+
+    def run(early, late, early_low, late_low, first_out, second_out):
+        window = [(first + i, early, early_low + i) for i in range(frames - 1)]
+        window += [(first + frames - 1, mixed, 0)]
+        window += [(first + frames + i, late, late_low + i) for i in range(frames - 1)]
 
         def step(lanes, part, rows):
             sums = [partial[f, part, rows, lanes].reshape(SB // 8, 8, LANES) for f in range(count)]
@@ -207,11 +222,11 @@
 
     @pl.when(place[0] == 0)
     def _():
-        run(keep, send)
+        run(straight, mixed, 0, 1, keep, send)
 
     @pl.when(place[0] == 1)
     def _():
-        run(send, keep)
+        run(mixed, straight, 1, 0, send, keep)
 
 
 def near_filter(place, taps, own, other, own_back, other_back, pol, earlier):
@@ -230,20 +245,20 @@
             out_specs=pl.BlockSpec((2 * frames, parts, stations, block), lambda i, place: (0, 0, 0, i)),
         ),
         compiler_params=pltpu.CompilerParams(vmem_limit_bytes=VMEM_LIMIT),
-        cost_estimate=cost(10),
+        cost_estimate=cost(8 * stations / 32),
         name="near",
     )(place, taps, own, other, own_back, other_back, *earlier)
 
 
-def far_filter(place, taps, partial, far, low, earlier):
+def far_filter(place, taps, partial, straight, mixed, low, earlier):
     count, parts, _, samples = partial.shape
-    stations = far.shape[2]
+    frames, _, stations, _ = mixed.shape
     block = samples // 2
 
     def spec(depth, where):
         return pl.BlockSpec((depth, parts, stations, block), lambda i, place: (0, 0, where, i))
 
-    shape = jax.ShapeDtypeStruct((count // 2, parts, stations, samples), BF16)
+    shape = jax.ShapeDtypeStruct((frames, parts, stations, samples), BF16)
     return pl.pallas_call(
         far_kernel,
         out_shape=(shape, shape),
@@ -253,50 +268,48 @@
             in_specs=[
                 pl.BlockSpec((taps.shape[0], 8, block), lambda i, place: (0, 0, i)),
                 spec(count, low // stations),
-                spec(far.shape[0], 0),
+                spec(frames - 1, low // stations),
+                spec(frames, 0),
             ]
             + [pl.BlockSpec(memory_space=pl.ANY)] * len(earlier),
-            out_specs=[spec(count // 2, 0)] * 2,
+            out_specs=[spec(frames, 0)] * 2,
         ),
         compiler_params=pltpu.CompilerParams(vmem_limit_bytes=VMEM_LIMIT),
         cost_estimate=cost(3),
         name="far",
-    )(place, taps, partial, far, *earlier)
+    )(place, taps, partial, straight, mixed, *earlier)
 
 
 def onward_kernel(place, own_back, other_back, *rest):
-    far = rest[-1]
-    frames = own_back.shape[0]
-    kept = far.shape[0] - frames
-
-    def run(first, second):
-        far[:kept] = first[frames - kept :]
-        far[kept:] = second[...]
+    out = rest[-1]
 
     @pl.when(place[0] == 0)
     def _():
-        run(own_back, other_back)
+        out[:1] = other_back[:1]
 
     @pl.when(place[0] == 1)
     def _():
-        run(other_back, own_back)
-
-
-def onward(place, own_back, other_back, pol, low, stations, history, earlier=()):
+        out[:1] = own_back[...]
+
+    out[1:] = other_back[1:]
+
+
+def onward(place, own_back, other_back, pol, low, stations, earlier=()):
     frames, parts, _, samples = other_back.shape
     where = low // stations
+    shape = (frames, parts, stations, samples)
     return pl.pallas_call(
         onward_kernel,
-        out_shape=jax.ShapeDtypeStruct((history, parts, stations, samples), BF16),
+        out_shape=jax.ShapeDtypeStruct(shape, BF16),
         grid_spec=pltpu.PrefetchScalarGridSpec(
             num_scalar_prefetch=1,
             grid=(parts,),
             in_specs=[
-                pl.BlockSpec((None, frames, 1, stations, samples), lambda i, place: (pol, 0, i, where, 0)),
+                pl.BlockSpec((None, 1, 1, stations, samples), lambda i, place: (pol, 0, i, where, 0)),
                 pl.BlockSpec((frames, 1, stations, samples), lambda i, place: (0, i, where, 0)),
             ]
             + [pl.BlockSpec(memory_space=pl.ANY)] * len(earlier),
-            out_specs=pl.BlockSpec((history, 1, stations, samples), lambda i, place: (0, i, 0, 0)),
+            out_specs=pl.BlockSpec((frames, 1, stations, samples), lambda i, place: (0, i, 0, 0)),
         ),
         compiler_params=pltpu.CompilerParams(vmem_limit_bytes=VMEM_LIMIT),
         cost_estimate=cost(3 * stations / 32),
@@ -314,7 +327,7 @@
         hit = jnp.where((rows == index[q : q + 1, :]) & (mask[q : q + 1, :] != 0), 1.0, 0.0).astype(BF16)
         picked = lax.dot_general(table[...], hit, (((0,), (0,)), ((), ())), preferred_element_type=F32)
         picked = picked.reshape(groups, 2, SB, beams)
-        low = q * SB
+        low = q % 2 * (half // 2) + q // 2 * SB
         re, im = picked[:, 0], picked[:, 1]
         out[:, low : low + SB, :beams] = re.astype(BF16)
         out[:, low : low + SB, beams:] = im.astype(BF16)
@@ -337,9 +350,53 @@
     )(table, index, mask, *earlier)
 
 
-def beam_kernel(source_count, has_earlier, *refs):
+def radix(source, mixed, low):
+    tiles = source.shape[2] // SB
+
+    def step(i, carry):
+        f, tile = i // tiles, i % tiles
+        rows = pl.ds(pl.multiple_of(tile * SB, SB), SB)
+        values = [
+            tuple(source[f, part, rows, a * LANES : (a + 1) * LANES].astype(F32) for part in range(2))
+            for a in range(RADIX)
+        ]
+        target = pl.ds(pl.multiple_of(low + tile * SB, SB), SB)
+        for b, (re, im) in enumerate(sixteen_points(values)):
+            mixed[b, f, target, :LANES] = re.astype(BF16)
+            mixed[b, f, target, LANES:] = im.astype(BF16)
+        return carry
+
+    lax.fori_loop(0, source.shape[0] * tiles, step, 0)
+
+
+def radix_kernel(place, *refs):
+    *sources, mixed = refs
+    low = 0
+    for ref in sources:
+        radix(ref, mixed, low)
+        low += ref.shape[2]
+
+
+def radix_stage(place, sources):
+    frames, parts, _, samples = sources[0].shape
+    stations = sum(s.shape[2] for s in sources)
+    return pl.pallas_call(
+        radix_kernel,
+        out_shape=jax.ShapeDtypeStruct((RADIX, frames, stations, 2 * LANES), BF16),
+        grid_spec=pltpu.PrefetchScalarGridSpec(
+            num_scalar_prefetch=1,
+            grid=(frames,),
+            in_specs=[pl.BlockSpec((1, parts, s.shape[2], samples), lambda i, place: (i, 0, 0, 0)) for s in sources],
+            out_specs=pl.BlockSpec((RADIX, 1, stations, 2 * LANES), lambda i, place: (0, i, 0, 0)),
+        ),
+        compiler_params=pltpu.CompilerParams(vmem_limit_bytes=VMEM_LIMIT),
+        cost_estimate=cost(3),
+        name="radix",
+    )(place, *sources)
+
+
+def beam_kernel(source_count, has_earlier, place, first, *refs):
     refs = list(refs)
-    refs.pop(0)
     sources = [refs.pop(0) for _ in range(source_count)]
     table, weights = refs.pop(0), refs.pop(0)
     earlier = refs.pop(0) if has_earlier else None
@@ -347,7 +404,7 @@
     held, refs = refs[:source_count], refs[source_count:]
     step = pl.program_id(0)
     frames = sources[0].shape[0]
-    station_count = sum(ref.shape[2] for ref in sources)
+    station_count = mixed.shape[2]
     groups = spectra.shape[0]
     beams = weights.shape[2] // 2
     rows_of = table.shape[2] // 2 // groups
@@ -357,34 +414,22 @@
 
     @pl.when(step == 0)
     def _():
-        low = 0
         copies = [pltpu.make_async_copy(ref, to, sems.at[k]) for k, (ref, to) in enumerate(zip(sources, held))]
+        copies.append(pltpu.make_async_copy(first, mixed.at[:, :, : first.shape[2]], sems.at[source_count]))
         for copy in copies:
             copy.start()
+        low = first.shape[2]
         for copy, ref in zip(copies, held):
             copy.wait()
-            tiles = ref.shape[2] // SB
-
-            def radix(i, carry, ref=ref, low=low, tiles=tiles):
-                f, rows = i // tiles, pl.ds(pl.multiple_of(i % tiles * SB, SB), SB)
-                values = [
-                    tuple(ref[f, part, rows, a * LANES : (a + 1) * LANES].astype(F32) for part in range(2))
-                    for a in range(RADIX)
-                ]
-                target = pl.ds(pl.multiple_of(f * station_count + low + i % tiles * SB, SB), SB)
-                for b, (re, im) in enumerate(sixteen_points(values)):
-                    mixed[b, target, :LANES] = re.astype(BF16)
-                    mixed[b, target, LANES:] = im.astype(BF16)
-                return carry
-
-            lax.fori_loop(0, frames * tiles, radix, 0)
+            radix(ref, mixed, low)
             low += ref.shape[2]
+        copies[-1].wait()
 
         def transform(b, carry):
             for start in range(0, frames, pair):
                 product = lax.dot_general(
                     table[0, b],
-                    mixed[b, start * station_count : (start + pair) * station_count],
+                    mixed[b, start : start + pair].reshape(pair * station_count, 2 * LANES),
                     (((1,), (1,)), ((), ())),
                     preferred_element_type=F32,
                 )
@@ -429,24 +474,24 @@
         lax.fori_loop(0, out.shape[0], finish, 0, unroll=8)
 
 
-def beam_power(place, sources, table, weights, earlier, channels):
+def beam_power(place, first, sources, table, weights, earlier, channels):
     frames, _, _, samples = sources[0].shape
     groups, depth, width = weights.shape
     beams = width // 2
-    station_count = sum(s.shape[2] for s in sources)
+    station_count = first.shape[2] + sum(s.shape[2] for s in sources)
     at_once = 2
     flat = (groups, channels // groups * frames, beams)
     flat_spec = pl.BlockSpec((at_once,) + flat[1:], lambda i, place: (i, 0, 0))
-    in_specs = [pl.BlockSpec(memory_space=pltpu.HBM) for s in sources]
+    in_specs = [pl.BlockSpec(memory_space=pltpu.HBM) for s in (first, *sources)]
     in_specs += [
         pl.BlockSpec((1,) + table.shape[1:], lambda i, place: (place[1], 0, 0, 0)),
         pl.BlockSpec((at_once, depth, width), lambda i, place: (i, 0, 0)),
     ]
-    operands = list(sources) + [table, weights]
+    operands = [first] + list(sources) + [table, weights]
     scratch = [
-        pltpu.VMEM((RADIX, frames * station_count, 2 * LANES), BF16),
+        pltpu.VMEM((RADIX, frames, station_count, 2 * LANES), BF16),
         pltpu.VMEM((groups, RADIX, frames * channels // groups // RADIX, 2 * station_count), BF16),
-        pltpu.SemaphoreType.DMA((len(sources),)),
+        pltpu.SemaphoreType.DMA((len(sources) + 1,)),
     ]
     scratch += [pltpu.VMEM(s.shape, BF16) for s in sources]
     if earlier is None:
@@ -504,9 +549,7 @@
     shards = [shard] + [
         lax.ppermute(shard, "tm", [(i, i ^ far) for i in range(time_devices)]) for far in range(2, time_devices, 2)
     ]
-    (own,) = cut(place, voltages, [(0, None)])
-    own = after(own, *shards[1:])
-    other = cut(place, voltages, [(1, pol) for pol in range(pols)], [own])
+    own, *other = cut(place, voltages, [(pol, 0, half) for pol in range(pols)], shards[1:])
     own_back = laid(after(hop(own)))
     own = laid(own)
     other = [laid(after(pair(block))) for block in other]
@@ -529,25 +572,28 @@
     quarter = half // 2
     chunks = [(pol, low) for pol in range(pols) for low in (0, quarter)]
     other_back = [hop(other[0])]
-    further, partial = [], []
-    for pol, low in chunks:
-        if pol >= len(other_back):
-            other_back.append(hop(after(other[pol], further[0])))
-        further.append(onward(place, own_back, other_back[pol], pol, low, quarter, history - 2 * frames))
-        if low:
-            partial.append(near_filter(place, taps, own, other[pol], own_back, other_back[pol], pol, further[-2:] + [weights]))
+    straight = [hop(own_back[0, 1:], 2)]
+    further = [onward(place, own_back, other_back[0], 0, low, quarter) for low in (0, quarter)]
+    other_back.append(hop(after(other[1], further[0])))
+    straight.append(hop(after(own_back[1, 1:], further[0]), 2))
+    further += [onward(place, own_back, other_back[1], 1, low, quarter) for low in (0, quarter)]
+    partial = []
+    for pol in range(pols):
+        earlier = further[: 2 * pol + 2] + [weights]
+        partial.append(near_filter(place, taps, own, other[pol], own_back, other_back[pol], pol, earlier))
     far = [hop(block, 2) for block in further]
-    keeps, sents, power = [], [], None
+    keeps, sents, sources, power = [], [], [], None
     for k, (pol, low) in enumerate(chunks):
-        earlier = sents[-1:] + ([power] if k == len(chunks) - 1 else []) + (partial[1:] if k == 1 else [])
-        keep, send = far_filter(place, taps, partial[pol], far[k], low, earlier)
+        earlier = sents[-1:] + partial[k : k + 1] + ([power] if k == len(chunks) - 1 else [])
+        keep, send = far_filter(place, taps, partial[pol], straight[pol], far[k], low, earlier)
         keeps.append(keep)
         sents.append(pair(send))
-        if low:
-            sources = keeps[-2:] + sents[-2:]
-            sources += [swap(block) for block in sources]
-            power = beam_power(place, sources, table, weights, power, samples // CORES)
-    return power
+        sources.append([keep, sents[-1], swap(keep), swap(sents[-1])])
+        if k == 2:
+            radixed = radix_stage(place, sources[0])
+            power = beam_power(place, radixed, sources[1], table, weights, None, samples // CORES)
+    radixed = radix_stage(place, sources[2])
+    return beam_power(place, radixed, sources[3], table, weights, power, samples // CORES)
 
 
 def solution(mesh):

time: 232 us -> 243 us (1.047)
  Pallas kernels: 77.1 us -> 82.5 us
  local copies, waits for them, and re-layouts: 25.4 us -> 29 us
  waiting for transfers between devices: 78.2 us -> 81.1 us
    ppermute x7 -> x9, waiting for transfers between devices: 32.2 us -> 47 us  [hop(): lax.ppermute(block, 'tm', [(i, i + 2) for i in range(skip, time_devices -...]
    ppermute x7, waiting for transfers between devices: 44.4 us -> 32.6 us  [pair(): return lax.ppermute(block, 'tm', [(i, i ^ 1) for i in range(time_devices)])]
    pallas_call x6 -> x7, Pallas kernels: 17.2 us -> 24.6 us  [the longest x2 10.2 us: radix_stage(): pl.pallas_call(radix_kernel, out_shape=jax.ShapeDtypeStruct((RADIX, frame...]
    pallas_call x4 -> x3, local copies, waits for them, and re-layouts: 11.2 us -> 6.35 us  [after(): pl.pallas_call(lambda *refs: None, out_shape=jax.ShapeDtypeStruct(block.s...]
    unnamed x69 -> x77, local copies, waits for them, and re-layouts: 11.9 us -> 16.5 us
    ppermute x8, starting transfers between devices: 20.5 us -> 16 us  [swap(): return lax.ppermute(block, 'stn', [(0, 1), (1, 0)])]
    pallas_call x0 -> x1, local copies, waits for them, and re-layouts: none -> 2.47 us  [cut(): pl.pallas_call(functools.partial(cut_kernel, cuts), out_shape=[jax.ShapeD...]
    ppermute x7 -> x9, starting transfers between devices: 19.8 us -> 22 us  [hop(): lax.ppermute(block, 'tm', [(i, i + 2) for i in range(skip, time_devices -...]
  transfers between devices with their start and end apart: 25 -> 27, of which waited for: 7 -> 7; matrix products, arithmetic and copies ran while one was open for 7% -> 6% of each run, Pallas kernels for 23% -> 25%
where the time goes in v6:
time: 243 us; the launch traced here: 242 us
  Pallas kernels  82.5 us (34%)
  waiting for transfers between devices  81.1 us (33%)
  starting transfers between devices  47.7 us (20%)
  local copies, waits for them, and re-layouts  29 us (12%)
    ppermute x9, waiting for transfers between devices, hop(): lax.ppermute(block, 'tm', [(i, i + 2) for i in range(skip, time_devices -...  47 us
    ppermute x7, waiting for transfers between devices, pair(): return lax.ppermute(block, 'tm', [(i, i ^ 1) for i in range(time_devices)])  32.6 us
    pallas_call x2, Pallas kernels, beam_power(): pl.pallas_call(functools.partial(beam_kernel, len(sources), earlier is no...  23.1 us
    ppermute x9, starting transfers between devices, hop(): lax.ppermute(block, 'tm', [(i, i + 2) for i in range(skip, time_devices -...  22 us
    unnamed x77, local copies, waits for them, and re-layouts  16.5 us
    pallas_call x4, Pallas kernels, far_filter(): pl.pallas_call(far_kernel, out_shape=(shape, shape), grid_spec=pltpu.Pref...  16.4 us
    ppermute x8, starting transfers between devices, swap(): return lax.ppermute(block, 'stn', [(0, 1), (1, 0)])  16 us
    pallas_call x2, Pallas kernels, near_filter(): pl.pallas_call(near_kernel, out_shape=jax.ShapeDtypeStruct((2 * frames, p...  15.7 us
  transfers between devices with their start and end apart: 27, of which 7 were waited for; matrix products, arithmetic and copies ran while one was open for 6% of the time, Pallas kernels for 25%

profile of v6, /device:TPU:17, one launch (start us, length us, event | category | flops | bytes accessed | tf_op | source)
XLA Modules:
  0.0 241.6 jit_solution(1513798922949718428)
XLA Ops:
  6.6 4.3 %cut.1 = (bf16[32,2,4,2,2048]{4,3,2,1,0:T(2,128)(2,1)}, bf16[32,4,2,2048]{3,2,1,0:T(2,128)(2,1)}, bf16[32,4,2,2048]{3,2,1,0:T(2,128)(2,1)}) custom-call(s32[2]{0:T(128)} %pad_add_fusion.place, bf16[64,2,4,2,2048]{4,3,2,1,0:T(2,128)(2,1)} %voltages.1, bf16[16,256]{1,0:T(8,128)(2,1)} %copy-done.28, bf16[16,256]{1,0:T(8,128)(2,1)} %copy-done.30, ...), custom_call_target="tpu_custom_call" | custom-call | bytes 13200000 | tf_op jit(solution)/shard_map/cut/pallas_call | solution.py:136
  10.9 2.7 %collective-permute-start.4 = (bf16[32,2,4,2,2048]{4,3,2,1,0:T(2,128)(2,1)}, bf16[32,2,4,2,2048]{4,3,2,1,0:T(2,128)(2,1)S(1)}, u32[]{:S(2)}, u32[]{:S(2)}) collective-permute-start(bf16[32,2,4,2,2048]{4,3,2,1,0:T(2,128)(2,1)} %get-tuple-element.16), channel_id=1, source_target_pairs={{0,4},{2,6},{4,8},{6,10},{8,12},{10,14},{1,5},{3,7},{5,9},{7,11},{... | collective-permute-start | bytes 6291464 | tf_op jit(solution)/shard_map/ppermute | solution.py:539
  15.3 21.0 %collective-permute-done.5.refs_0_ = bf16[32,4,2,2048]{3,2,1,0:T(2,128)(2,1)S(1)} collective-permute-done((bf16[32,4,2,2048]{3,2,1,0:T(2,128)(2,1)}, bf16[32,4,2,2048]{3,2,1,0:T(2,128)(2,1)S(1)}, u32[]{:S(2)}, u32[]{:S(2)}) %collective-permute-start.5) | collective-permute-done | bytes 1048608 | tf_op jit(solution)/shard_map/ppermute | solution.py:536
  41.7 16.4 %collective-permute-done.4.refs_0_ = bf16[32,2,4,2,2048]{4,3,2,1,0:T(2,128)(2,1)S(1)} collective-permute-done((bf16[32,2,4,2,2048]{4,3,2,1,0:T(2,128)(2,1)}, bf16[32,2,4,2,2048]{4,3,2,1,0:T(2,128)(2,1)S(1)}, u32[]{:S(2)}, u32[]{:S(2)}) %collective-permute-start.4) | collective-permute-done | bytes 2097184 | tf_op jit(solution)/shard_map/ppermute | solution.py:539
  59.4 2.7 %copy.20 = bf16[32,2,4,2,2048]{4,0,3,2,1:T(8,128)(2,1)S(1)} copy(bf16[32,2,4,2,2048]{4,3,2,1,0:T(2,128)(2,1)} %after.6) | data formatting | bytes 4194304 | tf_op jit(solution)/shard_map/after/pallas_call | solution.py:77
  63.6 2.8 %collective-permute-start.11 = (bf16[3,2,32,2048]{3,2,1,0:T(8,128)(2,1)}, bf16[3,2,32,2048]{3,2,1,0:T(8,128)(2,1)}, u32[]{:S(2)}, u32[]{:S(2)}) collective-permute-start(bf16[3,2,32,2048]{3,2,1,0:T(8,128)(2,1)} %get-tuple-element.29), channel_id=1, source_target_pairs={{4,8},{6,10},{8,12},{10,14},{5,9},{7,11},{9,13},{11,15},{20,24},{2... | collective-permute-start | bytes 2359304 | tf_op jit(solution)/shard_map/ppermute | solution.py:539
  69.9 10.7 %collective-permute-done.6.other_back = bf16[4,2,32,2048]{3,2,1,0:T(8,128)(2,1)} collective-permute-done((bf16[4,2,32,2048]{3,2,1,0:T(8,128)(2,1)S(1)}, bf16[4,2,32,2048]{3,2,1,0:T(8,128)(2,1)}, u32[]{:S(2)}, u32[]{:S(2)}) %collective-permute-start.6) | collective-permute-done | bytes 1048608 | tf_op jit(solution)/shard_map/ppermute | solution.py:539
  83.1 3.0 %collective-permute-start.13 = (bf16[4,2,16,2048]{3,2,1,0:T(8,128)(2,1)}, bf16[4,2,16,2048]{3,2,1,0:T(8,128)(2,1)}, u32[]{:S(2)}, u32[]{:S(2)}) collective-permute-start(bf16[4,2,16,2048]{3,2,1,0:T(8,128)(2,1)} %onward.4.refs_1_.rest_0_), channel_id=1, source_target_pairs={{4,8},{6,10},{8,12},{10,14},{5,9},{7,11},{9,13},{11,15},{20,24},{2... | collective-permute-start | bytes 1572872 | tf_op jit(solution)/shard_map/ppermute | solution.py:539
  100.7 7.9 %near.3.partial.rest_0_ = f32[8,2,32,2048]{3,2,1,0:T(8,128)} custom-call(s32[2]{0:T(128)} %pad_add_fusion.place, f32[16,8,2048]{2,1,0:T(8,128)} %broadcast_in_dim.2.taps, bf16[2,4,2,32,2048]{4,3,2,1,0:T(8,128)(2,1)} %bitcast.36, bf16[4,2,32,2048]{3,2,1,0:T(8,128)(2,1)} %bitcast.43, bf16[2,4,2,32,2048]{4,3,2,1,0:T(8,128)(2,1)} %bitcast.32, ...), custom_call_target="tpu_custom_call" | custom-call | bytes 26400000 | tf_op jit(solution)/shard_map/near/pallas_call | solution.py:237
  108.7 4.1 %far.4 = (bf16[4,2,16,2048]{3,2,1,0:T(8,128)(2,1)}, bf16[4,2,16,2048]{3,2,1,0:T(8,128)(2,1)}) custom-call(s32[2]{0:T(128)} %pad_add_fusion.place, f32[16,8,2048]{2,1,0:T(8,128)} %broadcast_in_dim.2.taps, f32[8,2,32,2048]{3,2,1,0:T(8,128)} %near.3.partial.rest_0_, bf16[3,2,32,2048]{3,2,1,0:T(8,128)(2,1)} %collective-permute-done.11.straight, ...), custom_call_target="tpu_custom_call" | custom-call | bytes 9900000 | tf_op jit(solution)/shard_map/far/pallas_call | solution.py:262
  116.7 14.3 %collective-permute-done.7.other_back = bf16[4,2,32,2048]{3,2,1,0:T(8,128)(2,1)S(1)} collective-permute-done((bf16[4,2,32,2048]{3,2,1,0:T(8,128)(2,1)}, bf16[4,2,32,2048]{3,2,1,0:T(8,128)(2,1)S(1)}, u32[]{:S(2)}, u32[]{:S(2)}) %collective-permute-start.7) | collective-permute-done | bytes 1048608 | tf_op jit(solution)/shard_map/ppermute | solution.py:539
  134.5 2.8 %collective-permute-start.10 = (bf16[4,2,16,2048]{3,2,1,0:T(8,128)(2,1)}, bf16[4,2,16,2048]{3,2,1,0:T(8,128)(2,1)S(1)}, u32[]{:S(2)}, u32[]{:S(2)}) collective-permute-start(bf16[4,2,16,2048]{3,2,1,0:T(8,128)(2,1)} %onward.6.rest_2_), channel_id=1, source_target_pairs={{4,8},{6,10},{8,12},{10,14},{5,9},{7,11},{9,13},{11,15},{20,24},{2... | collective-permute-start | bytes 1572872 | tf_op jit(solution)/shard_map/ppermute | solution.py:539
  139.9 7.8 %near.2.rest_1_.partial = f32[8,2,32,2048]{3,2,1,0:T(8,128)} custom-call(s32[2]{0:T(128)} %pad_add_fusion.place, f32[16,8,2048]{2,1,0:T(8,128)} %broadcast_in_dim.2.taps, bf16[2,4,2,32,2048]{4,3,2,1,0:T(8,128)(2,1)} %bitcast.37, bf16[4,2,32,2048]{3,2,1,0:T(8,128)(2,1)} %bitcast.40, bf16[2,4,2,32,2048]{4,3,2,1,0:T(8,128)(2,1)} %bitcast.35, ...), custom_call_target="tpu_custom_call" | custom-call | bytes 26400000 | tf_op jit(solution)/shard_map/near/pallas_call | solution.py:237
  149.4 4.1 %far.5 = (bf16[4,2,16,2048]{3,2,1,0:T(8,128)(2,1)}, bf16[4,2,16,2048]{3,2,1,0:T(8,128)(2,1)}) custom-call(s32[2]{0:T(128)} %pad_add_fusion.place, f32[16,8,2048]{2,1,0:T(8,128)} %broadcast_in_dim.2.taps, f32[8,2,32,2048]{3,2,1,0:T(8,128)} %near.3.partial.rest_0_, bf16[3,2,32,2048]{3,2,1,0:T(8,128)(2,1)} %collective-permute-done.11.straight, ...), custom_call_target="tpu_custom_call" | custom-call | bytes 9900000 | tf_op jit(solution)/shard_map/far/pallas_call | solution.py:262
  154.6 6.2 %collective-permute-start.20 = (bf16[4,2,16,2048]{3,2,1,0:T(8,128)(2,1)S(1)}, bf16[4,2,16,2048]{3,2,1,0:T(8,128)(2,1)S(1)}, u32[]{:S(2)}, u32[]{:S(2)}) collective-permute-start(bf16[4,2,16,2048]{3,2,1,0:T(8,128)(2,1)S(1)} %copy-done.13), channel_id=1, source_target_pairs={{0,1},{1,0},{2,3},{3,2},{4,5},{5,4},{6,7},{7,6},{8,9},{9,8},{10,11... | collective-permute-start | bytes 1572872 | tf_op jit(solution)/shard_map/ppermute | solution.py:542
  164.8 5.6 %collective-permute-done.10.mixed = bf16[4,2,16,2048]{3,2,1,0:T(8,128)(2,1)S(1)} collective-permute-done((bf16[4,2,16,2048]{3,2,1,0:T(8,128)(2,1)}, bf16[4,2,16,2048]{3,2,1,0:T(8,128)(2,1)S(1)}, u32[]{:S(2)}, u32[]{:S(2)}) %collective-permute-start.10) | collective-permute-done | bytes 524320 | tf_op jit(solution)/shard_map/ppermute | solution.py:539
  170.3 5.7 %collective-permute-start.22 = (bf16[4,2,16,2048]{3,2,1,0:T(8,128)(2,1)}, bf16[4,2,16,2048]{3,2,1,0:T(8,128)(2,1)S(1)}, u32[]{:S(2)}, u32[]{:S(2)}) collective-permute-start(bf16[4,2,16,2048]{3,2,1,0:T(8,128)(2,1)} %get-tuple-element.24.refs_0_), channel_id=1, source_target_pairs={{0,1},{1,0},{2,3},{3,2},{4,5},{5,4},{6,7},{7,6},{8,9},{9,8},{10,11... | collective-permute-start | bytes 1572872 | tf_op jit(solution)/shard_map/ppermute | solution.py:542
  176.8 4.1 %far.6 = (bf16[4,2,16,2048]{3,2,1,0:T(8,128)(2,1)}, bf16[4,2,16,2048]{3,2,1,0:T(8,128)(2,1)}) custom-call(s32[2]{0:T(128)} %pad_add_fusion.place, f32[16,8,2048]{2,1,0:T(8,128)} %broadcast_in_dim.2.taps, f32[8,2,32,2048]{3,2,1,0:T(8,128)} %near.2.rest_1_.partial, bf16[3,2,32,2048]{3,2,1,0:T(8,128)(2,1)} %copy-done.6, bf16[4,2,16,2048]{3,2,1,0:T(8,128)(2,1)} %copy-done.12, ...), custom_call_target="tpu_custom_call" | custom-call | bytes 9900000 | tf_op jit(solution)/shard_map/far/pallas_call | solution.py:262
  183.0 5.1 %radix.3.first = bf16[16,4,64,256]{3,2,1,0:T(8,128)(2,1)} custom-call(s32[2]{0:T(128)} %pad_add_fusion.place, bf16[4,2,16,2048]{3,2,1,0:T(8,128)(2,1)} %get-tuple-element.23.refs_0_, bf16[4,2,16,2048]{3,2,1,0:T(8,128)(2,1)} %copy-done.8, bf16[4,2,16,2048]{3,2,1,0:T(8,128)(2,1)} %copy-done.17, bf16[4,2,16,2048]{3,2,1,0:T(8,128)(2,1)} %copy-done.20), custom_call_target="tpu_custom_call" | custom-call | bytes 9900000 | tf_op jit(solution)/shard_map/radix/pallas_call | solution.py:383
  189.7 10.3 %beams.2.rest_1_.refs_6_ = f32[8,512,256]{2,1,0:T(8,128)} custom-call(s32[2]{0:T(128)} %pad_add_fusion.place, bf16[16,4,64,256]{3,2,1,0:T(8,128)(2,1)} %radix.3.first, bf16[4,2,16,2048]{3,2,1,0:T(8,128)(2,1)} %get-tuple-element.24.refs_0_, bf16[4,2,16,2048]{3,2,1,0:T(8,128)(2,1)} %copy-done.7, bf16[4,2,16,2048]{3,2,1,0:T(8,128)(2,1)} %copy-done.19, ...), custom_call_target="tpu_custom_call" | custom-call | tf_op jit(solution)/shard_map/beams/pallas_call | solution.py:506
  201.6 4.1 %far.7 = (bf16[4,2,16,2048]{3,2,1,0:T(8,128)(2,1)}, bf16[4,2,16,2048]{3,2,1,0:T(8,128)(2,1)}) custom-call(s32[2]{0:T(128)} %pad_add_fusion.place, f32[16,8,2048]{2,1,0:T(8,128)} %broadcast_in_dim.2.taps, f32[8,2,32,2048]{3,2,1,0:T(8,128)} %near.2.rest_1_.partial, bf16[3,2,32,2048]{3,2,1,0:T(8,128)(2,1)} %copy-done.6, bf16[4,2,16,2048]{3,2,1,0:T(8,128)(2,1)} %copy-done.15, ...), custom_call_target="tpu_custom_call" | custom-call | bytes 9900000 | tf_op jit(solution)/shard_map/far/pallas_call | solution.py:262
  207.4 11.6 %collective-permute-done.24.refs_1_ = bf16[4,2,16,2048]{3,2,1,0:T(8,128)(2,1)S(1)} collective-permute-done((bf16[4,2,16,2048]{3,2,1,0:T(8,128)(2,1)}, bf16[4,2,16,2048]{3,2,1,0:T(8,128)(2,1)S(1)}, u32[]{:S(2)}, u32[]{:S(2)}) %collective-permute-start.24) | collective-permute-done | bytes 524320 | tf_op jit(solution)/shard_map/ppermute | solution.py:536
  221.8 5.1 %radix.2.first = bf16[16,4,64,256]{3,2,1,0:T(8,128)(2,1)} custom-call(s32[2]{0:T(128)} %pad_add_fusion.place, bf16[4,2,16,2048]{3,2,1,0:T(8,128)(2,1)} %get-tuple-element.21.refs_0_, bf16[4,2,16,2048]{3,2,1,0:T(8,128)(2,1)} %copy-done.9, bf16[4,2,16,2048]{3,2,1,0:T(8,128)(2,1)} %copy-done.23, bf16[4,2,16,2048]{3,2,1,0:T(8,128)(2,1)} %copy-done.25), custom_call_target="tpu_custom_call" | custom-call | bytes 9900000 | tf_op jit(solution)/shard_map/radix/pallas_call | solution.py:383
  228.6 12.9 %beams.3 = f32[1024,4,256]{2,1,0:T(4,128)} custom-call(s32[2]{0:T(128)} %pad_add_fusion.place, bf16[16,4,64,256]{3,2,1,0:T(8,128)(2,1)} %radix.2.first, bf16[4,2,16,2048]{3,2,1,0:T(8,128)(2,1)} %get-tuple-element.25.refs_0_, bf16[4,2,16,2048]{3,2,1,0:T(8,128)(2,1)} %copy-done.18, bf16[4,2,16,2048]{3,2,1,0:T(8,128)(2,1)} %copy-done.21, ...), custom_call_target="tpu_custom_call" | custom-call | tf_op jit(solution)/shard_map/beams/pallas_call | solution.py:506
  (145 shorter events, 65.7 us)
Async XLA Ops:
  10.9 47.2 %collective-permute-start.4 = (bf16[32,2,4,2,2048]{4,3,2,1,0:T(2,128)(2,1)}, bf16[32,2,4,2,2048]{4,3,2,1,0:T(2,128)(2,1)S(1)}, u32[]{:S(2)}, u32[]{:S(2)}) collective-permute-start(bf16[32,2,4,2,2048]{4,3,2,1,0:T(2,128)(2,1)} %get-tuple-element.16), channel_id=1, source_target_pairs={{0,4},{2,6},{4,8},{6,10},{8,12},{10,14},{1,5},{3,7},{5,9},{7,11},{... | collective-permute-start | bytes 6291464 | tf_op jit(solution)/shard_map/ppermute | solution.py:539
  13.6 22.7 %collective-permute-start.5 = (bf16[32,4,2,2048]{3,2,1,0:T(2,128)(2,1)}, bf16[32,4,2,2048]{3,2,1,0:T(2,128)(2,1)S(1)}, u32[]{:S(2)}, u32[]{:S(2)}) collective-permute-start(bf16[32,4,2,2048]{3,2,1,0:T(2,128)(2,1)} %get-tuple-element.18), channel_id=1, source_target_pairs={{0,2},{2,0},{4,6},{6,4},{8,10},{10,8},{12,14},{14,12},{1,3},{3,1},... | collective-permute-start | bytes 3145736 | tf_op jit(solution)/shard_map/ppermute | solution.py:536
  15.0 52.1 %collective-permute-start.3 = (bf16[32,4,2,2048]{3,2,1,0:T(2,128)(2,1)}, bf16[32,4,2,2048]{3,2,1,0:T(2,128)(2,1)}, u32[]{:S(2)}, u32[]{:S(2)}) collective-permute-start(bf16[32,4,2,2048]{3,2,1,0:T(2,128)(2,1)} %get-tuple-element.17), channel_id=1, source_target_pairs={{0,2},{2,0},{4,6},{6,4},{8,10},{10,8},{12,14},{14,12},{1,3},{3,1},... | collective-permute-start | bytes 3145736 | tf_op jit(solution)/shard_map/ppermute | solution.py:536
  39.1 41.4 %collective-permute-start.6 = (bf16[4,2,32,2048]{3,2,1,0:T(8,128)(2,1)S(1)}, bf16[4,2,32,2048]{3,2,1,0:T(8,128)(2,1)}, u32[]{:S(2)}, u32[]{:S(2)}) collective-permute-start(bf16[4,2,32,2048]{3,2,1,0:T(8,128)(2,1)S(1)} %bitcast.41), channel_id=1, source_target_pairs={{0,4},{2,6},{4,8},{6,10},{8,12},{10,14},{1,5},{3,7},{5,9},{7,11},{... | collective-permute-start | bytes 3145736 | tf_op jit(solution)/shard_map/ppermute | solution.py:539
  63.6 45.1 %collective-permute-start.11 = (bf16[3,2,32,2048]{3,2,1,0:T(8,128)(2,1)}, bf16[3,2,32,2048]{3,2,1,0:T(8,128)(2,1)}, u32[]{:S(2)}, u32[]{:S(2)}) collective-permute-start(bf16[3,2,32,2048]{3,2,1,0:T(8,128)(2,1)} %get-tuple-element.29), channel_id=1, source_target_pairs={{4,8},{6,10},{8,12},{10,14},{5,9},{7,11},{9,13},{11,15},{20,24},{2... | collective-permute-start | bytes 2359304 | tf_op jit(solution)/shard_map/ppermute | solution.py:539
  83.1 25.5 %collective-permute-start.13 = (bf16[4,2,16,2048]{3,2,1,0:T(8,128)(2,1)}, bf16[4,2,16,2048]{3,2,1,0:T(8,128)(2,1)}, u32[]{:S(2)}, u32[]{:S(2)}) collective-permute-start(bf16[4,2,16,2048]{3,2,1,0:T(8,128)(2,1)} %onward.4.refs_1_.rest_0_), channel_id=1, source_target_pairs={{4,8},{6,10},{8,12},{10,14},{5,9},{7,11},{9,13},{11,15},{20,24},{2... | collective-permute-start | bytes 1572872 | tf_op jit(solution)/shard_map/ppermute | solution.py:539
  86.1 44.9 %collective-permute-start.7 = (bf16[4,2,32,2048]{3,2,1,0:T(8,128)(2,1)}, bf16[4,2,32,2048]{3,2,1,0:T(8,128)(2,1)S(1)}, u32[]{:S(2)}, u32[]{:S(2)}) collective-permute-start(bf16[4,2,32,2048]{3,2,1,0:T(8,128)(2,1)} %after.8), channel_id=1, source_target_pairs={{0,4},{2,6},{4,8},{6,10},{8,12},{10,14},{1,5},{3,7},{5,9},{7,11},{... | collective-permute-start | bytes 3145736 | tf_op jit(solution)/shard_map/ppermute | solution.py:539
  88.1 3.7 %collective-permute-start.8 = (bf16[64,256]{1,0:T(8,128)(2,1)S(1)}, bf16[64,256]{1,0:T(8,128)(2,1)S(1)}, u32[]{:S(2)}, u32[]{:S(2)}) collective-permute-start(bf16[64,256]{1,0:T(8,128)(2,1)S(1)} %pad_maximum_fusion), channel_id=1, source_target_pairs={{0,2},{2,0},{4,6},{6,4},{8,10},{10,8},{12,14},{14,12},{1,3},{3,1},... | collective-permute-start | bytes 98312 | tf_op jit(solution)/shard_map/ppermute | solution.py:536
  97.7 50.1 %collective-permute-start.12 = (bf16[4,2,16,2048]{3,2,1,0:T(8,128)(2,1)}, bf16[4,2,16,2048]{3,2,1,0:T(8,128)(2,1)S(1)}, u32[]{:S(2)}, u32[]{:S(2)}) collective-permute-start(bf16[4,2,16,2048]{3,2,1,0:T(8,128)(2,1)} %onward.5.rest_1_), channel_id=1, source_target_pairs={{4,8},{6,10},{8,12},{10,14},{5,9},{7,11},{9,13},{11,15},{20,24},{2... | collective-permute-start | bytes 1572872 | tf_op jit(solution)/shard_map/ppermute | solution.py:539
  112.7 35.0 %collective-permute-start.14 = (bf16[4,2,16,2048]{3,2,1,0:T(8,128)(2,1)}, bf16[4,2,16,2048]{3,2,1,0:T(8,128)(2,1)S(1)}, u32[]{:S(2)}, u32[]{:S(2)}) collective-permute-start(bf16[4,2,16,2048]{3,2,1,0:T(8,128)(2,1)} %get-tuple-element.19), channel_id=1, source_target_pairs={{0,2},{2,0},{4,6},{6,4},{8,10},{10,8},{12,14},{14,12},{1,3},{3,1},... | collective-permute-start | bytes 1572872 | tf_op jit(solution)/shard_map/ppermute | solution.py:536
  114.0 49.0 %collective-permute-start.9 = (bf16[3,2,32,2048]{3,2,1,0:T(8,128)(2,1)}, bf16[3,2,32,2048]{3,2,1,0:T(8,128)(2,1)S(1)}, u32[]{:S(2)}, u32[]{:S(2)}) collective-permute-start(bf16[3,2,32,2048]{3,2,1,0:T(8,128)(2,1)} %after.9), channel_id=1, source_target_pairs={{4,8},{6,10},{8,12},{10,14},{5,9},{7,11},{9,13},{11,15},{20,24},{2... | collective-permute-start | bytes 2359304 | tf_op jit(solution)/shard_map/ppermute | solution.py:539
  134.5 35.8 %collective-permute-start.10 = (bf16[4,2,16,2048]{3,2,1,0:T(8,128)(2,1)}, bf16[4,2,16,2048]{3,2,1,0:T(8,128)(2,1)S(1)}, u32[]{:S(2)}, u32[]{:S(2)}) collective-permute-start(bf16[4,2,16,2048]{3,2,1,0:T(8,128)(2,1)} %onward.6.rest_2_), channel_id=1, source_target_pairs={{4,8},{6,10},{8,12},{10,14},{5,9},{7,11},{9,13},{11,15},{20,24},{2... | collective-permute-start | bytes 1572872 | tf_op jit(solution)/shard_map/ppermute | solution.py:539
  153.5 22.5 %collective-permute-start.15 = (bf16[4,2,16,2048]{3,2,1,0:T(8,128)(2,1)}, bf16[4,2,16,2048]{3,2,1,0:T(8,128)(2,1)S(1)}, u32[]{:S(2)}, u32[]{:S(2)}) collective-permute-start(bf16[4,2,16,2048]{3,2,1,0:T(8,128)(2,1)} %get-tuple-element.20), channel_id=1, source_target_pairs={{0,2},{2,0},{4,6},{6,4},{8,10},{10,8},{12,14},{14,12},{1,3},{3,1},... | collective-permute-start | bytes 1572872 | tf_op jit(solution)/shard_map/ppermute | solution.py:536
  154.6 26.3 %collective-permute-start.20 = (bf16[4,2,16,2048]{3,2,1,0:T(8,128)(2,1)S(1)}, bf16[4,2,16,2048]{3,2,1,0:T(8,128)(2,1)S(1)}, u32[]{:S(2)}, u32[]{:S(2)}) collective-permute-start(bf16[4,2,16,2048]{3,2,1,0:T(8,128)(2,1)S(1)} %copy-done.13), channel_id=1, source_target_pairs={{0,1},{1,0},{2,3},{3,2},{4,5},{5,4},{6,7},{7,6},{8,9},{9,8},{10,11... | collective-permute-start | bytes 1572872 | tf_op jit(solution)/shard_map/ppermute | solution.py:542
  160.8 39.2 %collective-permute-start.19 = (bf16[4,2,16,2048]{3,2,1,0:T(8,128)(2,1)S(1)}, bf16[4,2,16,2048]{3,2,1,0:T(8,128)(2,1)S(1)}, u32[]{:S(2)}, u32[]{:S(2)}) collective-permute-start(bf16[4,2,16,2048]{3,2,1,0:T(8,128)(2,1)S(1)} %copy-done.11), channel_id=1, source_target_pairs={{4,8},{6,10},{8,12},{10,14},{5,9},{7,11},{9,13},{11,15},{20,24},{2... | collective-permute-start | bytes 1572872 | tf_op jit(solution)/shard_map/ppermute | solution.py:539
  162.9 19.2 %collective-permute-start.21 = (bf16[4,2,16,2048]{3,2,1,0:T(8,128)(2,1)}, bf16[4,2,16,2048]{3,2,1,0:T(8,128)(2,1)S(1)}, u32[]{:S(2)}, u32[]{:S(2)}) collective-permute-start(bf16[4,2,16,2048]{3,2,1,0:T(8,128)(2,1)} %copy-done.8), channel_id=1, source_target_pairs={{0,1},{1,0},{2,3},{3,2},{4,5},{5,4},{6,7},{7,6},{8,9},{9,8},{10,11... | collective-permute-start | bytes 1572872 | tf_op jit(solution)/shard_map/ppermute | solution.py:542
  170.3 17.7 %collective-permute-start.22 = (bf16[4,2,16,2048]{3,2,1,0:T(8,128)(2,1)}, bf16[4,2,16,2048]{3,2,1,0:T(8,128)(2,1)S(1)}, u32[]{:S(2)}, u32[]{:S(2)}) collective-permute-start(bf16[4,2,16,2048]{3,2,1,0:T(8,128)(2,1)} %get-tuple-element.24.refs_0_), channel_id=1, source_target_pairs={{0,1},{1,0},{2,3},{3,2},{4,5},{5,4},{6,7},{7,6},{8,9},{9,8},{10,11... | collective-permute-start | bytes 1572872 | tf_op jit(solution)/shard_map/ppermute | solution.py:542
  176.0 12.1 %collective-permute-start.23 = (bf16[4,2,16,2048]{3,2,1,0:T(8,128)(2,1)S(1)}, bf16[4,2,16,2048]{3,2,1,0:T(8,128)(2,1)S(1)}, u32[]{:S(2)}, u32[]{:S(2)}) collective-permute-start(bf16[4,2,16,2048]{3,2,1,0:T(8,128)(2,1)S(1)} %collective-permute-done.15.rest_0_.refs_1_), channel_id=1, source_target_pairs={{0,1},{1,0},{2,3},{3,2},{4,5},{5,4},{6,7},{7,6},{8,9},{9,8},{10,11... | collective-permute-start | bytes 1572872 | tf_op jit(solution)/shard_map/ppermute | solution.py:542
  180.9 19.1 %collective-permute-start.16 = (bf16[4,2,16,2048]{3,2,1,0:T(8,128)(2,1)}, bf16[4,2,16,2048]{3,2,1,0:T(8,128)(2,1)S(1)}, u32[]{:S(2)}, u32[]{:S(2)}) collective-permute-start(bf16[4,2,16,2048]{3,2,1,0:T(8,128)(2,1)} %get-tuple-element.22), channel_id=1, source_target_pairs={{0,2},{2,0},{4,6},{6,4},{8,10},{10,8},{12,14},{14,12},{1,3},{3,1},... | collective-permute-start | bytes 1572872 | tf_op jit(solution)/shard_map/ppermute | solution.py:536
  205.7 13.3 %collective-permute-start.24 = (bf16[4,2,16,2048]{3,2,1,0:T(8,128)(2,1)}, bf16[4,2,16,2048]{3,2,1,0:T(8,128)(2,1)S(1)}, u32[]{:S(2)}, u32[]{:S(2)}) collective-permute-start(bf16[4,2,16,2048]{3,2,1,0:T(8,128)(2,1)} %get-tuple-element.26), channel_id=1, source_target_pairs={{0,2},{2,0},{4,6},{6,4},{8,10},{10,8},{12,14},{14,12},{1,3},{3,1},... | collective-permute-start | bytes 1572872 | tf_op jit(solution)/shard_map/ppermute | solution.py:536
  206.4 13.8 %collective-permute-start.17 = (bf16[4,2,16,2048]{3,2,1,0:T(8,128)(2,1)S(1)}, bf16[4,2,16,2048]{3,2,1,0:T(8,128)(2,1)S(1)}, u32[]{:S(2)}, u32[]{:S(2)}) collective-permute-start(bf16[4,2,16,2048]{3,2,1,0:T(8,128)(2,1)S(1)} %copy-done.14), channel_id=1, source_target_pairs={{0,1},{1,0},{2,3},{3,2},{4,5},{5,4},{6,7},{7,6},{8,9},{9,8},{10,11... | collective-permute-start | bytes 1572872 | tf_op jit(solution)/shard_map/ppermute | solution.py:542
  206.8 13.4 %collective-permute-start.18 = (bf16[4,2,16,2048]{3,2,1,0:T(8,128)(2,1)}, bf16[4,2,16,2048]{3,2,1,0:T(8,128)(2,1)S(1)}, u32[]{:S(2)}, u32[]{:S(2)}) collective-permute-start(bf16[4,2,16,2048]{3,2,1,0:T(8,128)(2,1)} %copy-done.9), channel_id=1, source_target_pairs={{0,1},{1,0},{2,3},{3,2},{4,5},{5,4},{6,7},{7,6},{8,9},{9,8},{10,11... | collective-permute-start | bytes 1572872 | tf_op jit(solution)/shard_map/ppermute | solution.py:542
  206.9 20.0 %collective-permute-start.25 = (bf16[4,2,16,2048]{3,2,1,0:T(8,128)(2,1)}, bf16[4,2,16,2048]{3,2,1,0:T(8,128)(2,1)S(1)}, u32[]{:S(2)}, u32[]{:S(2)}) collective-permute-start(bf16[4,2,16,2048]{3,2,1,0:T(8,128)(2,1)} %get-tuple-element.25.refs_0_), channel_id=1, source_target_pairs={{0,1},{1,0},{2,3},{3,2},{4,5},{5,4},{6,7},{7,6},{8,9},{9,8},{10,11... | collective-permute-start | bytes 1572872 | tf_op jit(solution)/shard_map/ppermute | solution.py:542
  219.0 8.0 %collective-permute-start.26 = (bf16[4,2,16,2048]{3,2,1,0:T(8,128)(2,1)S(1)}, bf16[4,2,16,2048]{3,2,1,0:T(8,128)(2,1)S(1)}, u32[]{:S(2)}, u32[]{:S(2)}) collective-permute-start(bf16[4,2,16,2048]{3,2,1,0:T(8,128)(2,1)S(1)} %collective-permute-done.24.refs_1_), channel_id=1, source_target_pairs={{0,1},{1,0},{2,3},{3,2},{4,5},{5,4},{6,7},{7,6},{8,9},{9,8},{10,11... | collective-permute-start | bytes 1572872 | tf_op jit(solution)/shard_map/ppermute | solution.py:542
  (39 other events, 167.8 us)

commit v7 on v6

--- a/solution.py
+++ b/solution.py
@@ -200,17 +200,13 @@
         run(other, own, other_back, own_back)
 
 
-def far_kernel(place, taps, partial, straight, mixed, *rest):
+def far_kernel(place, taps, partial, far, *rest):
     keep, send = rest[-2:]
     frames = keep.shape[0]
     count = 2 * frames
-    first = 1 - 2 * count
-
-    def run(early, late, early_low, late_low, first_out, second_out):
-        window = [(first + i, early, early_low + i) for i in range(frames - 1)]
-        window += [(first + frames - 1, mixed, 0)]
-        window += [(first + frames + i, late, late_low + i) for i in range(frames - 1)]
-
+    window = [(i + 1 - 2 * count, far, i) for i in range(far.shape[0])]
+
+    def run(first_out, second_out):
         def step(lanes, part, rows):
             sums = [partial[f, part, rows, lanes].reshape(SB // 8, 8, LANES) for f in range(count)]
             sums = weighted(taps, window, count, lanes, part, rows, sums)
@@ -222,11 +218,11 @@
 
     @pl.when(place[0] == 0)
     def _():
-        run(straight, mixed, 0, 1, keep, send)
+        run(keep, send)
 
     @pl.when(place[0] == 1)
     def _():
-        run(mixed, straight, 1, 0, send, keep)
+        run(send, keep)
 
 
 def near_filter(place, taps, own, other, own_back, other_back, pol, earlier):
@@ -250,71 +246,69 @@
     )(place, taps, own, other, own_back, other_back, *earlier)
 
 
-def far_filter(place, taps, partial, straight, mixed, low, earlier):
-    count, parts, _, samples = partial.shape
-    frames, _, stations, _ = mixed.shape
-    block = samples // 2
-
-    def spec(depth, where):
-        return pl.BlockSpec((depth, parts, stations, block), lambda i, place: (0, 0, where, i))
-
-    shape = jax.ShapeDtypeStruct((frames, parts, stations, samples), BF16)
+def far_filter(place, taps, partial, far, low, size, earlier):
+    count, parts, stations, _ = partial.shape
+    frames = count // 2
+    block = math.gcd(512, low, size)
+
+    def spec(depth, start):
+        return pl.BlockSpec((depth, parts, stations, block), lambda i, place: (0, 0, 0, start // block + i))
+
+    shape = jax.ShapeDtypeStruct((frames, parts, stations, size), BF16)
     return pl.pallas_call(
         far_kernel,
         out_shape=(shape, shape),
         grid_spec=pltpu.PrefetchScalarGridSpec(
             num_scalar_prefetch=1,
-            grid=(samples // block,),
-            in_specs=[
-                pl.BlockSpec((taps.shape[0], 8, block), lambda i, place: (0, 0, i)),
-                spec(count, low // stations),
-                spec(frames - 1, low // stations),
-                spec(frames, 0),
-            ]
+            grid=(size // block,),
+            in_specs=[pl.BlockSpec((taps.shape[0], 8, block), lambda i, place: (0, 0, low // block + i))]
+            + [spec(count, low), spec(far.shape[0], 0)]
             + [pl.BlockSpec(memory_space=pl.ANY)] * len(earlier),
             out_specs=[spec(frames, 0)] * 2,
         ),
         compiler_params=pltpu.CompilerParams(vmem_limit_bytes=VMEM_LIMIT),
-        cost_estimate=cost(3),
+        cost_estimate=cost(1),
         name="far",
-    )(place, taps, partial, straight, mixed, *earlier)
-
-
-def onward_kernel(place, own_back, other_back, *rest):
-    out = rest[-1]
+    )(place, taps, partial, far, *earlier)
+
+
+def onward_kernel(place, own_back, other_back, far):
+    frames = own_back.shape[0]
+
+    def run(first, second):
+        far[: frames - 1] = first[1:]
+        far[frames - 1 :] = second[...]
 
     @pl.when(place[0] == 0)
     def _():
-        out[:1] = other_back[:1]
+        run(own_back, other_back)
 
     @pl.when(place[0] == 1)
     def _():
-        out[:1] = own_back[...]
-
-    out[1:] = other_back[1:]
-
-
-def onward(place, own_back, other_back, pol, low, stations, earlier=()):
-    frames, parts, _, samples = other_back.shape
-    where = low // stations
-    shape = (frames, parts, stations, samples)
+        run(other_back, own_back)
+
+
+def onward(place, own_back, other_back, pol, low, size):
+    frames, parts, stations, _ = other_back.shape
+    depth = 2 * frames - 1
+    block = math.gcd(low, size)
+    where = low // block
     return pl.pallas_call(
         onward_kernel,
-        out_shape=jax.ShapeDtypeStruct(shape, BF16),
+        out_shape=jax.ShapeDtypeStruct((depth, parts, stations, size), BF16),
         grid_spec=pltpu.PrefetchScalarGridSpec(
             num_scalar_prefetch=1,
-            grid=(parts,),
+            grid=(parts, size // block),
             in_specs=[
-                pl.BlockSpec((None, 1, 1, stations, samples), lambda i, place: (pol, 0, i, where, 0)),
-                pl.BlockSpec((frames, 1, stations, samples), lambda i, place: (0, i, where, 0)),
-            ]
-            + [pl.BlockSpec(memory_space=pl.ANY)] * len(earlier),
-            out_specs=pl.BlockSpec((frames, 1, stations, samples), lambda i, place: (0, i, 0, 0)),
+                pl.BlockSpec((None, frames, 1, stations, block), lambda i, j, place: (pol, 0, i, 0, where + j)),
+                pl.BlockSpec((frames, 1, stations, block), lambda i, j, place: (0, i, 0, where + j)),
+            ],
+            out_specs=pl.BlockSpec((depth, 1, stations, block), lambda i, j, place: (0, i, 0, j)),
         ),
         compiler_params=pltpu.CompilerParams(vmem_limit_bytes=VMEM_LIMIT),
-        cost_estimate=cost(3 * stations / 32),
+        cost_estimate=cost(3),
         name="onward",
-    )(place, own_back, other_back, *earlier)
+    )(place, own_back, other_back)
 
 
 def weight_kernel(table, index, mask, *rest):
@@ -327,7 +321,7 @@
         hit = jnp.where((rows == index[q : q + 1, :]) & (mask[q : q + 1, :] != 0), 1.0, 0.0).astype(BF16)
         picked = lax.dot_general(table[...], hit, (((0,), (0,)), ((), ())), preferred_element_type=F32)
         picked = picked.reshape(groups, 2, SB, beams)
-        low = q % 2 * (half // 2) + q // 2 * SB
+        low = q * SB
         re, im = picked[:, 0], picked[:, 1]
         out[:, low : low + SB, :beams] = re.astype(BF16)
         out[:, low : low + SB, beams:] = im.astype(BF16)
@@ -350,61 +344,20 @@
     )(table, index, mask, *earlier)
 
 
-def radix(source, mixed, low):
-    tiles = source.shape[2] // SB
-
-    def step(i, carry):
-        f, tile = i // tiles, i % tiles
-        rows = pl.ds(pl.multiple_of(tile * SB, SB), SB)
-        values = [
-            tuple(source[f, part, rows, a * LANES : (a + 1) * LANES].astype(F32) for part in range(2))
-            for a in range(RADIX)
-        ]
-        target = pl.ds(pl.multiple_of(low + tile * SB, SB), SB)
-        for b, (re, im) in enumerate(sixteen_points(values)):
-            mixed[b, f, target, :LANES] = re.astype(BF16)
-            mixed[b, f, target, LANES:] = im.astype(BF16)
-        return carry
-
-    lax.fori_loop(0, source.shape[0] * tiles, step, 0)
-
-
-def radix_kernel(place, *refs):
-    *sources, mixed = refs
-    low = 0
-    for ref in sources:
-        radix(ref, mixed, low)
-        low += ref.shape[2]
-
-
-def radix_stage(place, sources):
-    frames, parts, _, samples = sources[0].shape
-    stations = sum(s.shape[2] for s in sources)
-    return pl.pallas_call(
-        radix_kernel,
-        out_shape=jax.ShapeDtypeStruct((RADIX, frames, stations, 2 * LANES), BF16),
-        grid_spec=pltpu.PrefetchScalarGridSpec(
-            num_scalar_prefetch=1,
-            grid=(frames,),
-            in_specs=[pl.BlockSpec((1, parts, s.shape[2], samples), lambda i, place: (i, 0, 0, 0)) for s in sources],
-            out_specs=pl.BlockSpec((RADIX, 1, stations, 2 * LANES), lambda i, place: (0, i, 0, 0)),
-        ),
-        compiler_params=pltpu.CompilerParams(vmem_limit_bytes=VMEM_LIMIT),
-        cost_estimate=cost(3),
-        name="radix",
-    )(place, *sources)
-
-
-def beam_kernel(source_count, has_earlier, place, first, *refs):
+def beam_kernel(source_count, ranges, later_count, has_earlier, *refs):
     refs = list(refs)
+    refs.pop(0)
     sources = [refs.pop(0) for _ in range(source_count)]
     table, weights = refs.pop(0), refs.pop(0)
     earlier = refs.pop(0) if has_earlier else None
+    refs = refs[later_count:]
     out, mixed, spectra, sems, *refs = refs
     held, refs = refs[:source_count], refs[source_count:]
     step = pl.program_id(0)
     frames = sources[0].shape[0]
-    station_count = mixed.shape[2]
+    stations = sources[0].shape[2]
+    tiles = stations // SB
+    station_count = stations * (source_count // ranges)
     groups = spectra.shape[0]
     beams = weights.shape[2] // 2
     rows_of = table.shape[2] // 2 // groups
@@ -415,21 +368,31 @@
     @pl.when(step == 0)
     def _():
         copies = [pltpu.make_async_copy(ref, to, sems.at[k]) for k, (ref, to) in enumerate(zip(sources, held))]
-        copies.append(pltpu.make_async_copy(first, mixed.at[:, :, : first.shape[2]], sems.at[source_count]))
         for copy in copies:
             copy.start()
-        low = first.shape[2]
-        for copy, ref in zip(copies, held):
-            copy.wait()
-            radix(ref, mixed, low)
-            low += ref.shape[2]
-        copies[-1].wait()
+        for k in range(0, source_count, ranges):
+            for copy in copies[k : k + ranges]:
+                copy.wait()
+            pieces = []
+            for ref in held[k : k + ranges]:
+                pieces += [(ref, slice(n, n + LANES)) for n in range(0, ref.shape[3], LANES)]
+
+            def radix(i, carry, pieces=pieces, low=k // ranges * stations):
+                f, rows = i // tiles, pl.ds(pl.multiple_of(i % tiles * SB, SB), SB)
+                values = [tuple(ref[f, part, rows, lanes].astype(F32) for part in range(2)) for ref, lanes in pieces]
+                target = pl.ds(pl.multiple_of(f * station_count + low + i % tiles * SB, SB), SB)
+                for b, (re, im) in enumerate(sixteen_points(values)):
+                    mixed[b, target, :LANES] = re.astype(BF16)
+                    mixed[b, target, LANES:] = im.astype(BF16)
+                return carry
+
+            lax.fori_loop(0, frames * tiles, radix, 0)
 
         def transform(b, carry):
             for start in range(0, frames, pair):
                 product = lax.dot_general(
                     table[0, b],
-                    mixed[b, start : start + pair].reshape(pair * station_count, 2 * LANES),
+                    mixed[b, start * station_count : (start + pair) * station_count],
                     (((1,), (1,)), ((), ())),
                     preferred_element_type=F32,
                 )
@@ -474,24 +437,25 @@
         lax.fori_loop(0, out.shape[0], finish, 0, unroll=8)
 
 
-def beam_power(place, first, sources, table, weights, earlier, channels):
-    frames, _, _, samples = sources[0].shape
+def beam_power(place, sources, ranges, table, weights, earlier, channels, later=()):
+    frames = sources[0].shape[0]
     groups, depth, width = weights.shape
     beams = width // 2
-    station_count = first.shape[2] + sum(s.shape[2] for s in sources)
+    station_count = sum(s.shape[2] for s in sources) // ranges
     at_once = 2
     flat = (groups, channels // groups * frames, beams)
     flat_spec = pl.BlockSpec((at_once,) + flat[1:], lambda i, place: (i, 0, 0))
-    in_specs = [pl.BlockSpec(memory_space=pltpu.HBM) for s in (first, *sources)]
+    in_specs = [pl.BlockSpec(memory_space=pltpu.HBM) for s in sources]
     in_specs += [
         pl.BlockSpec((1,) + table.shape[1:], lambda i, place: (place[1], 0, 0, 0)),
         pl.BlockSpec((at_once, depth, width), lambda i, place: (i, 0, 0)),
     ]
-    operands = [first] + list(sources) + [table, weights]
+    operands = list(sources) + [table, weights]
+    free = [pl.BlockSpec(memory_space=pl.ANY)] * len(later)
     scratch = [
-        pltpu.VMEM((RADIX, frames, station_count, 2 * LANES), BF16),
+        pltpu.VMEM((RADIX, frames * station_count, 2 * LANES), BF16),
         pltpu.VMEM((groups, RADIX, frames * channels // groups // RADIX, 2 * station_count), BF16),
-        pltpu.SemaphoreType.DMA((len(sources) + 1,)),
+        pltpu.SemaphoreType.DMA((len(sources),)),
     ]
     scratch += [pltpu.VMEM(s.shape, BF16) for s in sources]
     if earlier is None:
@@ -504,19 +468,19 @@
         in_specs.append(flat_spec)
         scratch.append(pltpu.VMEM((math.prod(out_spec.block_shape) // LANES, LANES), F32))
     return pl.pallas_call(
-        functools.partial(beam_kernel, len(sources), earlier is not None),
+        functools.partial(beam_kernel, len(sources), ranges, len(later), earlier is not None),
         out_shape=out_shape,
         grid_spec=pltpu.PrefetchScalarGridSpec(
             num_scalar_prefetch=1,
             grid=(groups // at_once,),
-            in_specs=in_specs,
+            in_specs=in_specs + free,
             out_specs=out_spec,
             scratch_shapes=scratch,
         ),
         compiler_params=pltpu.CompilerParams(vmem_limit_bytes=VMEM_LIMIT),
         cost_estimate=cost(0),
         name="beams",
-    )(place, *operands)
+    )(place, *operands, *later)
 
 
 def flipped(rows, bit):
@@ -549,7 +513,8 @@
     shards = [shard] + [
         lax.ppermute(shard, "tm", [(i, i ^ far) for i in range(time_devices)]) for far in range(2, time_devices, 2)
     ]
-    own, *other = cut(place, voltages, [(pol, 0, half) for pol in range(pols)], shards[1:])
+    own, *other = cut(place, voltages, [(pol, 0, half) for pol in range(pols)], [])
+    own = after(own, *shards[1:])
     own_back = laid(after(hop(own)))
     own = laid(own)
     other = [laid(after(pair(block))) for block in other]
@@ -569,31 +534,28 @@
     table = jnp.asarray(dft_tables(samples))
     taps = jnp.broadcast_to(filter_taps[:, None, :], (history + 1, 8, samples))
 
-    quarter = half // 2
-    chunks = [(pol, low) for pol in range(pols) for low in (0, quarter)]
-    other_back = [hop(other[0])]
-    straight = [hop(own_back[0, 1:], 2)]
-    further = [onward(place, own_back, other_back[0], 0, low, quarter) for low in (0, quarter)]
-    other_back.append(hop(after(other[1], further[0])))
-    straight.append(hop(after(own_back[1, 1:], further[0]), 2))
-    further += [onward(place, own_back, other_back[1], 1, low, quarter) for low in (0, quarter)]
-    partial = []
-    for pol in range(pols):
-        earlier = further[: 2 * pol + 2] + [weights]
-        partial.append(near_filter(place, taps, own, other[pol], own_back, other_back[pol], pol, earlier))
+    chunks = [(pol, low, samples // 2) for pol in range(pols) for low in (0, samples // 2)]
+    other_back = [hop(block) for block in other]
+    further = [onward(place, own_back, other_back[pol], pol, low, size) for pol, low, size in chunks]
     far = [hop(block, 2) for block in further]
-    keeps, sents, sources, power = [], [], [], None
-    for k, (pol, low) in enumerate(chunks):
-        earlier = sents[-1:] + partial[k : k + 1] + ([power] if k == len(chunks) - 1 else [])
-        keep, send = far_filter(place, taps, partial[pol], straight[pol], far[k], low, earlier)
+    keeps, sents, partial = [], [], []
+
+    def power_of(pol, earlier, later=()):
+        here = [k for k, chunk in enumerate(chunks) if chunk[0] == pol]
+        mine, pairs = [keeps[k] for k in here], [sents[k] for k in here]
+        sources = mine + pairs + [swap(block) for block in mine + pairs]
+        return beam_power(place, sources, len(here), table, weights, earlier, samples // CORES, later)
+
+    for k, (pol, low, size) in enumerate(chunks):
+        if pol >= len(partial):
+            gates = further + keeps[1:2] if pol else further[:2] + [weights]
+            partial.append(near_filter(place, taps, own, other[pol], own_back, other_back[pol], pol, gates))
+        keep, send = far_filter(place, taps, partial[pol], far[k], low, size, sents[-1:])
         keeps.append(keep)
         sents.append(pair(send))
-        sources.append([keep, sents[-1], swap(keep), swap(sents[-1])])
-        if k == 2:
-            radixed = radix_stage(place, sources[0])
-            power = beam_power(place, radixed, sources[1], table, weights, None, samples // CORES)
-    radixed = radix_stage(place, sources[2])
-    return beam_power(place, radixed, sources[3], table, weights, power, samples // CORES)
+    power = power_of(0, None, keeps[-1:])
+    sents[-1] = after(sents[-1], power)
+    return power_of(1, power)
 
 
 def solution(mesh):

time: 243 us -> 224 us (0.922)
  Pallas kernels: 82.5 us -> 75.2 us
  waiting for transfers between devices: 81.1 us -> 75.9 us
  starting transfers between devices: 47.7 us -> 44 us
  local copies, waits for them, and re-layouts: 29 us -> 25.6 us
    pallas_call x8 -> x6, Pallas kernels: 43.5 us -> 36.8 us  [the longest x2 25.9 us: beam_power(): pl.pallas_call(functools.partial(beam_kernel, len(sources), ranges, len(l...]
    ppermute x9 -> x7, waiting for transfers between devices: 47 us -> 41.6 us  [hop(): lax.ppermute(block, 'tm', [(i, i + 2) for i in range(skip, time_devices -...]
    ppermute x8, starting transfers between devices: 16 us -> 11.3 us  [swap(): return lax.ppermute(block, 'stn', [(0, 1), (1, 0)])]
    ppermute x9 -> x7, starting transfers between devices: 22 us -> 26.3 us  [hop(): lax.ppermute(block, 'tm', [(i, i + 2) for i in range(skip, time_devices -...]
    pallas_call x3 -> x4, local copies, waits for them, and re-layouts: 6.35 us -> 10.2 us  [after(): pl.pallas_call(lambda *refs: None, out_shape=jax.ShapeDtypeStruct(block.s...]
    unnamed x77 -> x76, local copies, waits for them, and re-layouts: 16.5 us -> 13.1 us
    ppermute x7, starting transfers between devices: 7.09 us -> 3.75 us  [pair(): return lax.ppermute(block, 'tm', [(i, i ^ 1) for i in range(time_devices)])]
    pallas_call x1 -> x0, local copies, waits for them, and re-layouts: 2.47 us -> none  [cut(): pl.pallas_call(functools.partial(cut_kernel, cuts), out_shape=[jax.ShapeD...]
  transfers between devices with their start and end apart: 27 -> 25, of which waited for: 7 -> 7; matrix products, arithmetic and copies ran while one was open for 6% -> 6% of each run, Pallas kernels for 25% -> 27%
where the time goes in v7:
time: 224 us; the launch traced here: 222 us
  waiting for transfers between devices  75.9 us (34%)
  Pallas kernels  75.2 us (34%)
  starting transfers between devices  44 us (20%)
  local copies, waits for them, and re-layouts  25.6 us (11%)
    ppermute x7, waiting for transfers between devices, hop(): lax.ppermute(block, 'tm', [(i, i + 2) for i in range(skip, time_devices -...  41.6 us
    ppermute x7, waiting for transfers between devices, pair(): return lax.ppermute(block, 'tm', [(i, i ^ 1) for i in range(time_devices)])  32.6 us
    ppermute x7, starting transfers between devices, hop(): lax.ppermute(block, 'tm', [(i, i + 2) for i in range(skip, time_devices -...  26.3 us
    pallas_call x2, Pallas kernels, beam_power(): pl.pallas_call(functools.partial(beam_kernel, len(sources), ranges, len(l...  25.9 us
    pallas_call x4, Pallas kernels, far_filter(): pl.pallas_call(far_kernel, out_shape=(shape, shape), grid_spec=pltpu.Pref...  15.7 us
    pallas_call x2, Pallas kernels, near_filter(): pl.pallas_call(near_kernel, out_shape=jax.ShapeDtypeStruct((2 * frames, p...  15.7 us
    unnamed x76, local copies, waits for them, and re-layouts  13.1 us
    ppermute x8, starting transfers between devices, swap(): return lax.ppermute(block, 'stn', [(0, 1), (1, 0)])  11.3 us
  transfers between devices with their start and end apart: 25, of which 7 were waited for; matrix products, arithmetic and copies ran while one was open for 6% of the time, Pallas kernels for 27%

profile of v7, /device:TPU:17, one launch (start us, length us, event | category | flops | bytes accessed | tf_op | source)
XLA Modules:
  0.0 221.8 jit_solution(3468227206653570159)
XLA Ops:
  3.9 4.3 %cut.1 = (bf16[32,2,4,2,2048]{4,3,2,1,0:T(2,128)(2,1)}, bf16[32,4,2,2048]{3,2,1,0:T(2,128)(2,1)}, bf16[32,4,2,2048]{3,2,1,0:T(2,128)(2,1)}) custom-call(s32[2]{0:T(128)} %pad_add_fusion.place.refs_0_, bf16[64,2,4,2,2048]{4,3,2,1,0:T(2,128)(2,1)} %voltages.1), custom_call_target="tpu_custom_call" | custom-call | bytes 13200000 | tf_op jit(solution)/shard_map/cut/pallas_call | solution.py:136
  10.2 4.1 %collective-permute-start.4 = (bf16[32,2,4,2,2048]{4,3,2,1,0:T(2,128)(2,1)}, bf16[32,2,4,2,2048]{4,3,2,1,0:T(2,128)(2,1)}, u32[]{:S(2)}, u32[]{:S(2)}) collective-permute-start(bf16[32,2,4,2,2048]{4,3,2,1,0:T(2,128)(2,1)} %after.5), channel_id=1, source_target_pairs={{0,4},{2,6},{4,8},{6,10},{8,12},{10,14},{1,5},{3,7},{5,9},{7,11},{... | collective-permute-start | bytes 6291464 | tf_op jit(solution)/shard_map/ppermute | solution.py:503
  14.6 17.2 %collective-permute-done.6.refs_0_ = bf16[32,4,2,2048]{3,2,1,0:T(2,128)(2,1)S(1)} collective-permute-done((bf16[32,4,2,2048]{3,2,1,0:T(2,128)(2,1)}, bf16[32,4,2,2048]{3,2,1,0:T(2,128)(2,1)S(1)}, u32[]{:S(2)}, u32[]{:S(2)}) %collective-permute-start.6) | collective-permute-done | bytes 1048608 | tf_op jit(solution)/shard_map/ppermute | solution.py:500
  34.6 4.1 %collective-permute-start.7 = (bf16[4,2,32,2048]{3,2,1,0:T(8,128)(2,1)S(1)}, bf16[4,2,32,2048]{3,2,1,0:T(8,128)(2,1)}, u32[]{:S(2)}, u32[]{:S(2)}) collective-permute-start(bf16[4,2,32,2048]{3,2,1,0:T(8,128)(2,1)S(1)} %bitcast.36), channel_id=1, source_target_pairs={{0,4},{2,6},{4,8},{6,10},{8,12},{10,14},{1,5},{3,7},{5,9},{7,11},{... | collective-permute-start | bytes 3145736 | tf_op jit(solution)/shard_map/ppermute | solution.py:503
  38.8 15.4 %collective-permute-done.3.refs_0_ = bf16[32,4,2,2048]{3,2,1,0:T(2,128)(2,1)S(1)} collective-permute-done((bf16[32,4,2,2048]{3,2,1,0:T(2,128)(2,1)}, bf16[32,4,2,2048]{3,2,1,0:T(2,128)(2,1)S(1)}, u32[]{:S(2)}, u32[]{:S(2)}) %collective-permute-start.3) | collective-permute-done | bytes 1048608 | tf_op jit(solution)/shard_map/ppermute | solution.py:500
  57.1 4.1 %collective-permute-start.5 = (bf16[4,2,32,2048]{3,2,1,0:T(8,128)(2,1)S(1)}, bf16[4,2,32,2048]{3,2,1,0:T(8,128)(2,1)S(1)}, u32[]{:S(2)}, u32[]{:S(2)}) collective-permute-start(bf16[4,2,32,2048]{3,2,1,0:T(8,128)(2,1)S(1)} %bitcast.33), channel_id=1, source_target_pairs={{0,4},{2,6},{4,8},{6,10},{8,12},{10,14},{1,5},{3,7},{5,9},{7,11},{... | collective-permute-start | bytes 3145736 | tf_op jit(solution)/shard_map/ppermute | solution.py:503
  61.2 4.1 %copy.20 = bf16[32,2,4,2,2048]{4,0,3,2,1:T(8,128)(2,1)} copy(bf16[32,2,4,2,2048]{4,3,2,1,0:T(2,128)(2,1)} %after.7) | data formatting | bytes 4194304 | tf_op jit(solution)/shard_map/after/pallas_call | solution.py:77
  65.3 14.9 %collective-permute-done.7.other_back = bf16[4,2,32,2048]{3,2,1,0:T(8,128)(2,1)} collective-permute-done((bf16[4,2,32,2048]{3,2,1,0:T(8,128)(2,1)S(1)}, bf16[4,2,32,2048]{3,2,1,0:T(8,128)(2,1)}, u32[]{:S(2)}, u32[]{:S(2)}) %collective-permute-start.7) | collective-permute-done | bytes 1048608 | tf_op jit(solution)/shard_map/ppermute | solution.py:503
  82.9 4.1 %collective-permute-start.10 = (bf16[7,2,32,1024]{3,2,1,0:T(8,128)(2,1)}, bf16[7,2,32,1024]{3,2,1,0:T(8,128)(2,1)S(1)}, u32[]{:S(2)}, u32[]{:S(2)}) collective-permute-start(bf16[7,2,32,1024]{3,2,1,0:T(8,128)(2,1)} %onward.4.rest_0_), channel_id=1, source_target_pairs={{4,8},{6,10},{8,12},{10,14},{5,9},{7,11},{9,13},{11,15},{20,24},{2... | collective-permute-start | bytes 2752520 | tf_op jit(solution)/shard_map/ppermute | solution.py:503
  88.5 2.9 %onward.5.rest_1_ = bf16[7,2,32,1024]{3,2,1,0:T(8,128)(2,1)} custom-call(s32[2]{0:T(128)} %pad_add_fusion.place.refs_0_, bf16[2,4,2,32,2048]{4,3,2,1,0:T(8,128)(2,1)} %bitcast.26, bf16[4,2,32,2048]{3,2,1,0:T(8,128)(2,1)} %collective-permute-done.7.other_back), custom_call_target="tpu_custom_call" | custom-call | bytes 9900000 | tf_op jit(solution)/shard_map/onward/pallas_call | solution.py:296
  100.3 7.8 %near.2.partial = f32[8,2,32,2048]{3,2,1,0:T(8,128)} custom-call(s32[2]{0:T(128)} %pad_add_fusion.place.refs_0_, f32[16,8,2048]{2,1,0:T(8,128)} %broadcast_in_dim.2.taps, bf16[2,4,2,32,2048]{4,3,2,1,0:T(8,128)(2,1)} %bitcast.31, bf16[4,2,32,2048]{3,2,1,0:T(8,128)(2,1)} %bitcast.38, bf16[2,4,2,32,2048]{4,3,2,1,0:T(8,128)(2,1)} %bitcast.27, ...), custom_call_target="tpu_custom_call" | custom-call | bytes 26400000 | tf_op jit(solution)/shard_map/near/pallas_call | solution.py:233
  108.1 14.2 %collective-permute-done.10.far = bf16[7,2,32,1024]{3,2,1,0:T(8,128)(2,1)S(1)} collective-permute-done((bf16[7,2,32,1024]{3,2,1,0:T(8,128)(2,1)}, bf16[7,2,32,1024]{3,2,1,0:T(8,128)(2,1)S(1)}, u32[]{:S(2)}, u32[]{:S(2)}) %collective-permute-start.10) | collective-permute-done | bytes 917536 | tf_op jit(solution)/shard_map/ppermute | solution.py:503
  123.2 3.9 %far.4 = (bf16[4,2,32,1024]{3,2,1,0:T(8,128)(2,1)}, bf16[4,2,32,1024]{3,2,1,0:T(8,128)(2,1)}) custom-call(s32[2]{0:T(128)} %pad_add_fusion.place.refs_0_, f32[16,8,2048]{2,1,0:T(8,128)} %broadcast_in_dim.2.taps, f32[8,2,32,2048]{3,2,1,0:T(8,128)} %near.2.partial, bf16[7,2,32,1024]{3,2,1,0:T(8,128)(2,1)} %copy-done.12), custom_call_target="tpu_custom_call" | custom-call | bytes 3300000 | tf_op jit(solution)/shard_map/far/pallas_call | solution.py:258
  131.0 4.0 %collective-permute-start.12 = (bf16[7,2,32,1024]{3,2,1,0:T(8,128)(2,1)}, bf16[7,2,32,1024]{3,2,1,0:T(8,128)(2,1)S(1)}, u32[]{:S(2)}, u32[]{:S(2)}) collective-permute-start(bf16[7,2,32,1024]{3,2,1,0:T(8,128)(2,1)} %onward.6.rest_2_), channel_id=1, source_target_pairs={{4,8},{6,10},{8,12},{10,14},{5,9},{7,11},{9,13},{11,15},{20,24},{2... | collective-permute-start | bytes 2752520 | tf_op jit(solution)/shard_map/ppermute | solution.py:503
  135.0 6.9 %collective-permute-done.9.far = bf16[7,2,32,1024]{3,2,1,0:T(8,128)(2,1)S(1)} collective-permute-done((bf16[7,2,32,1024]{3,2,1,0:T(8,128)(2,1)}, bf16[7,2,32,1024]{3,2,1,0:T(8,128)(2,1)S(1)}, u32[]{:S(2)}, u32[]{:S(2)}) %collective-permute-start.9) | collective-permute-done | bytes 917536 | tf_op jit(solution)/shard_map/ppermute | solution.py:503
  143.7 3.9 %far.5 = (bf16[4,2,32,1024]{3,2,1,0:T(8,128)(2,1)}, bf16[4,2,32,1024]{3,2,1,0:T(8,128)(2,1)}) custom-call(s32[2]{0:T(128)} %pad_add_fusion.place.refs_0_, f32[16,8,2048]{2,1,0:T(8,128)} %broadcast_in_dim.2.taps, f32[8,2,32,2048]{3,2,1,0:T(8,128)} %near.2.partial, bf16[7,2,32,1024]{3,2,1,0:T(8,128)(2,1)} %copy-done.13, bf16[4,2,32,1024]{3,2,1,0:T(8,128)(2,1)} %copy-done.8), custom_call_target="tpu_custom_call" | custom-call | bytes 3300000 | tf_op jit(solution)/shard_map/far/pallas_call | solution.py:258
  150.5 4.0 %collective-permute-start.14 = (bf16[7,2,32,1024]{3,2,1,0:T(8,128)(2,1)}, bf16[7,2,32,1024]{3,2,1,0:T(8,128)(2,1)S(1)}, u32[]{:S(2)}, u32[]{:S(2)}) collective-permute-start(bf16[7,2,32,1024]{3,2,1,0:T(8,128)(2,1)} %onward.7.rest_3_), channel_id=1, source_target_pairs={{4,8},{6,10},{8,12},{10,14},{5,9},{7,11},{9,13},{11,15},{20,24},{2... | collective-permute-start | bytes 2752520 | tf_op jit(solution)/shard_map/ppermute | solution.py:503
  154.5 7.8 %near.3.partial = f32[8,2,32,2048]{3,2,1,0:T(8,128)} custom-call(s32[2]{0:T(128)} %pad_add_fusion.place.refs_0_, f32[16,8,2048]{2,1,0:T(8,128)} %broadcast_in_dim.2.taps, bf16[2,4,2,32,2048]{4,3,2,1,0:T(8,128)(2,1)} %bitcast.32, bf16[4,2,32,2048]{3,2,1,0:T(8,128)(2,1)} %bitcast.35, bf16[2,4,2,32,2048]{4,3,2,1,0:T(8,128)(2,1)} %bitcast.30, ...), custom_call_target="tpu_custom_call" | custom-call | bytes 26400000 | tf_op jit(solution)/shard_map/near/pallas_call | solution.py:233
  164.1 3.9 %far.6 = (bf16[4,2,32,1024]{3,2,1,0:T(8,128)(2,1)}, bf16[4,2,32,1024]{3,2,1,0:T(8,128)(2,1)}) custom-call(s32[2]{0:T(128)} %pad_add_fusion.place.refs_0_, f32[16,8,2048]{2,1,0:T(8,128)} %broadcast_in_dim.2.taps, f32[8,2,32,2048]{3,2,1,0:T(8,128)} %near.3.partial, bf16[7,2,32,1024]{3,2,1,0:T(8,128)(2,1)} %copy-done.15, bf16[4,2,32,1024]{3,2,1,0:T(8,128)(2,1)} %copy-done.11), custom_call_target="tpu_custom_call" | custom-call | bytes 3300000 | tf_op jit(solution)/shard_map/far/pallas_call | solution.py:258
  169.3 5.9 %collective-permute-start.17 = (bf16[4,2,32,1024]{3,2,1,0:T(8,128)(2,1)S(1)}, bf16[4,2,32,1024]{3,2,1,0:T(8,128)(2,1)S(1)}, u32[]{:S(2)}, u32[]{:S(2)}) collective-permute-start(bf16[4,2,32,1024]{3,2,1,0:T(8,128)(2,1)S(1)} %copy-done.16), channel_id=1, source_target_pairs={{0,1},{1,0},{2,3},{3,2},{4,5},{5,4},{6,7},{7,6},{8,9},{9,8},{10,11... | collective-permute-start | bytes 1572872 | tf_op jit(solution)/shard_map/ppermute | solution.py:506
  175.7 5.6 %collective-permute-done.14.far = bf16[7,2,32,1024]{3,2,1,0:T(8,128)(2,1)S(1)} collective-permute-done((bf16[7,2,32,1024]{3,2,1,0:T(8,128)(2,1)}, bf16[7,2,32,1024]{3,2,1,0:T(8,128)(2,1)S(1)}, u32[]{:S(2)}, u32[]{:S(2)}) %collective-permute-start.14) | collective-permute-done | bytes 917536 | tf_op jit(solution)/shard_map/ppermute | solution.py:503
  184.8 3.9 %far.7 = (bf16[4,2,32,1024]{3,2,1,0:T(8,128)(2,1)}, bf16[4,2,32,1024]{3,2,1,0:T(8,128)(2,1)}) custom-call(s32[2]{0:T(128)} %pad_add_fusion.place.refs_0_, f32[16,8,2048]{2,1,0:T(8,128)} %broadcast_in_dim.2.taps, f32[8,2,32,2048]{3,2,1,0:T(8,128)} %near.3.partial, bf16[7,2,32,1024]{3,2,1,0:T(8,128)(2,1)} %copy-done.14, bf16[4,2,32,1024]{3,2,1,0:T(8,128)(2,1)} %copy-done.10), custom_call_target="tpu_custom_call" | custom-call | bytes 3300000 | tf_op jit(solution)/shard_map/far/pallas_call | solution.py:258
  192.1 11.6 %beams.2.refs_1_.refs_11_ = f32[8,512,256]{2,1,0:T(8,128)} custom-call(s32[2]{0:T(128)} %pad_add_fusion.place.refs_0_, bf16[4,2,32,1024]{3,2,1,0:T(8,128)(2,1)} %get-tuple-element.26.refs_1_, bf16[4,2,32,1024]{3,2,1,0:T(8,128)(2,1)} %get-tuple-element.20.rest_4_.refs_2_, bf16[4,2,32,1024]{3,2,1,0:T(8,128)(2,1)} %copy-done.8, ...), custom_call_target="tpu_custom_call" | custom-call | tf_op jit(solution)/shard_map/beams/pallas_call | solution.py:470
  207.5 14.3 %beams.3 = f32[1024,4,256]{2,1,0:T(4,128)} custom-call(s32[2]{0:T(128)} %pad_add_fusion.place.refs_0_, bf16[4,2,32,1024]{3,2,1,0:T(8,128)(2,1)} %get-tuple-element.22.refs_1_, bf16[4,2,32,1024]{3,2,1,0:T(8,128)(2,1)} %get-tuple-element.24.refs_11_.refs_2_, bf16[4,2,32,1024]{3,2,1,0:T(8,128)(2,1)} %copy-done.10, bf16[4,2,32,1024]{3,2,1,0:T(8,128)(2,1)} %after.9.refs_4_, ...), custom_call_target="tpu_custom_call" | custom-call | tf_op jit(solution)/shard_map/beams/pallas_call | solution.py:470
  (137 shorter events, 48.4 us)
Async XLA Ops:
  0.7 8.8 %collective-permute-start = (bf16[16,256]{1,0:T(8,128)(2,1)S(1)}, bf16[16,256]{1,0:T(8,128)(2,1)S(1)}, u32[]{:S(2)}, u32[]{:S(2)}) collective-permute-start(bf16[16,256]{1,0:T(8,128)(2,1)S(1)} %get-tuple-element.28), channel_id=1, source_target_pairs={{0,4},{2,6},{4,0},{6,2},{8,12},{10,14},{12,8},{14,10},{1,5},{3,7},... | collective-permute-start | bytes 24584 | tf_op jit(solution)/shard_map/ppermute | solution.py:514
  2.0 7.5 %collective-permute-start.1 = (bf16[16,256]{1,0:T(8,128)(2,1)S(1)}, bf16[16,256]{1,0:T(8,128)(2,1)S(1)}, u32[]{:S(2)}, u32[]{:S(2)}) collective-permute-start(bf16[16,256]{1,0:T(8,128)(2,1)S(1)} %get-tuple-element.28), channel_id=1, source_target_pairs={{0,8},{2,10},{4,12},{6,14},{8,0},{10,2},{12,4},{14,6},{1,9},{3,11}... | collective-permute-start | bytes 24584 | tf_op jit(solution)/shard_map/ppermute | solution.py:514
  2.1 7.5 %collective-permute-start.2 = (bf16[16,256]{1,0:T(8,128)(2,1)S(1)}, bf16[16,256]{1,0:T(8,128)(2,1)S(1)}, u32[]{:S(2)}, u32[]{:S(2)}) collective-permute-start(bf16[16,256]{1,0:T(8,128)(2,1)S(1)} %get-tuple-element.28), channel_id=1, source_target_pairs={{0,12},{2,14},{4,8},{6,10},{8,4},{10,6},{12,0},{14,2},{1,13},{3,15... | collective-permute-start | bytes 24584 | tf_op jit(solution)/shard_map/ppermute | solution.py:514
  8.2 23.5 %collective-permute-start.6 = (bf16[32,4,2,2048]{3,2,1,0:T(2,128)(2,1)}, bf16[32,4,2,2048]{3,2,1,0:T(2,128)(2,1)S(1)}, u32[]{:S(2)}, u32[]{:S(2)}) collective-permute-start(bf16[32,4,2,2048]{3,2,1,0:T(2,128)(2,1)} %get-tuple-element.18), channel_id=1, source_target_pairs={{0,2},{2,0},{4,6},{6,4},{8,10},{10,8},{12,14},{14,12},{1,3},{3,1},... | collective-permute-start | bytes 3145736 | tf_op jit(solution)/shard_map/ppermute | solution.py:500
  10.2 51.0 %collective-permute-start.4 = (bf16[32,2,4,2,2048]{4,3,2,1,0:T(2,128)(2,1)}, bf16[32,2,4,2,2048]{4,3,2,1,0:T(2,128)(2,1)}, u32[]{:S(2)}, u32[]{:S(2)}) collective-permute-start(bf16[32,2,4,2,2048]{4,3,2,1,0:T(2,128)(2,1)} %after.5), channel_id=1, source_target_pairs={{0,4},{2,6},{4,8},{6,10},{8,12},{10,14},{1,5},{3,7},{5,9},{7,11},{... | collective-permute-start | bytes 6291464 | tf_op jit(solution)/shard_map/ppermute | solution.py:503
  14.3 39.9 %collective-permute-start.3 = (bf16[32,4,2,2048]{3,2,1,0:T(2,128)(2,1)}, bf16[32,4,2,2048]{3,2,1,0:T(2,128)(2,1)S(1)}, u32[]{:S(2)}, u32[]{:S(2)}) collective-permute-start(bf16[32,4,2,2048]{3,2,1,0:T(2,128)(2,1)} %get-tuple-element.17), channel_id=1, source_target_pairs={{0,2},{2,0},{4,6},{6,4},{8,10},{10,8},{12,14},{14,12},{1,3},{3,1},... | collective-permute-start | bytes 3145736 | tf_op jit(solution)/shard_map/ppermute | solution.py:500
  34.6 45.6 %collective-permute-start.7 = (bf16[4,2,32,2048]{3,2,1,0:T(8,128)(2,1)S(1)}, bf16[4,2,32,2048]{3,2,1,0:T(8,128)(2,1)}, u32[]{:S(2)}, u32[]{:S(2)}) collective-permute-start(bf16[4,2,32,2048]{3,2,1,0:T(8,128)(2,1)S(1)} %bitcast.36), channel_id=1, source_target_pairs={{0,4},{2,6},{4,8},{6,10},{8,12},{10,14},{1,5},{3,7},{5,9},{7,11},{... | collective-permute-start | bytes 3145736 | tf_op jit(solution)/shard_map/ppermute | solution.py:503
  57.1 70.3 %collective-permute-start.5 = (bf16[4,2,32,2048]{3,2,1,0:T(8,128)(2,1)S(1)}, bf16[4,2,32,2048]{3,2,1,0:T(8,128)(2,1)S(1)}, u32[]{:S(2)}, u32[]{:S(2)}) collective-permute-start(bf16[4,2,32,2048]{3,2,1,0:T(8,128)(2,1)S(1)} %bitcast.33), channel_id=1, source_target_pairs={{0,4},{2,6},{4,8},{6,10},{8,12},{10,14},{1,5},{3,7},{5,9},{7,11},{... | collective-permute-start | bytes 3145736 | tf_op jit(solution)/shard_map/ppermute | solution.py:503
  82.9 39.4 %collective-permute-start.10 = (bf16[7,2,32,1024]{3,2,1,0:T(8,128)(2,1)}, bf16[7,2,32,1024]{3,2,1,0:T(8,128)(2,1)S(1)}, u32[]{:S(2)}, u32[]{:S(2)}) collective-permute-start(bf16[7,2,32,1024]{3,2,1,0:T(8,128)(2,1)} %onward.4.rest_0_), channel_id=1, source_target_pairs={{4,8},{6,10},{8,12},{10,14},{5,9},{7,11},{9,13},{11,15},{20,24},{2... | collective-permute-start | bytes 2752520 | tf_op jit(solution)/shard_map/ppermute | solution.py:503
  88.2 7.6 %collective-permute-start.8 = (bf16[64,256]{1,0:T(8,128)(2,1)S(1)}, bf16[64,256]{1,0:T(8,128)(2,1)S(1)}, u32[]{:S(2)}, u32[]{:S(2)}) collective-permute-start(bf16[64,256]{1,0:T(8,128)(2,1)S(1)} %pad_maximum_fusion), channel_id=1, source_target_pairs={{0,2},{2,0},{4,6},{6,4},{8,10},{10,8},{12,14},{14,12},{1,3},{3,1},... | collective-permute-start | bytes 98312 | tf_op jit(solution)/shard_map/ppermute | solution.py:500
  91.4 50.6 %collective-permute-start.9 = (bf16[7,2,32,1024]{3,2,1,0:T(8,128)(2,1)}, bf16[7,2,32,1024]{3,2,1,0:T(8,128)(2,1)S(1)}, u32[]{:S(2)}, u32[]{:S(2)}) collective-permute-start(bf16[7,2,32,1024]{3,2,1,0:T(8,128)(2,1)} %onward.5.rest_1_), channel_id=1, source_target_pairs={{4,8},{6,10},{8,12},{10,14},{5,9},{7,11},{9,13},{11,15},{20,24},{2... | collective-permute-start | bytes 2752520 | tf_op jit(solution)/shard_map/ppermute | solution.py:503
  127.1 14.8 %collective-permute-start.11 = (bf16[4,2,32,1024]{3,2,1,0:T(8,128)(2,1)}, bf16[4,2,32,1024]{3,2,1,0:T(8,128)(2,1)S(1)}, u32[]{:S(2)}, u32[]{:S(2)}) collective-permute-start(bf16[4,2,32,1024]{3,2,1,0:T(8,128)(2,1)} %get-tuple-element.19), channel_id=1, source_target_pairs={{0,2},{2,0},{4,6},{6,4},{8,10},{10,8},{12,14},{14,12},{1,3},{3,1},... | collective-permute-start | bytes 1572872 | tf_op jit(solution)/shard_map/ppermute | solution.py:500
  131.0 31.3 %collective-permute-start.12 = (bf16[7,2,32,1024]{3,2,1,0:T(8,128)(2,1)}, bf16[7,2,32,1024]{3,2,1,0:T(8,128)(2,1)S(1)}, u32[]{:S(2)}, u32[]{:S(2)}) collective-permute-start(bf16[7,2,32,1024]{3,2,1,0:T(8,128)(2,1)} %onward.6.rest_2_), channel_id=1, source_target_pairs={{4,8},{6,10},{8,12},{10,14},{5,9},{7,11},{9,13},{11,15},{20,24},{2... | collective-permute-start | bytes 2752520 | tf_op jit(solution)/shard_map/ppermute | solution.py:503
  147.6 14.8 %collective-permute-start.13 = (bf16[4,2,32,1024]{3,2,1,0:T(8,128)(2,1)}, bf16[4,2,32,1024]{3,2,1,0:T(8,128)(2,1)S(1)}, u32[]{:S(2)}, u32[]{:S(2)}) collective-permute-start(bf16[4,2,32,1024]{3,2,1,0:T(8,128)(2,1)} %get-tuple-element.21), channel_id=1, source_target_pairs={{0,2},{2,0},{4,6},{6,4},{8,10},{10,8},{12,14},{14,12},{1,3},{3,1},... | collective-permute-start | bytes 1572872 | tf_op jit(solution)/shard_map/ppermute | solution.py:500
  150.5 30.8 %collective-permute-start.14 = (bf16[7,2,32,1024]{3,2,1,0:T(8,128)(2,1)}, bf16[7,2,32,1024]{3,2,1,0:T(8,128)(2,1)S(1)}, u32[]{:S(2)}, u32[]{:S(2)}) collective-permute-start(bf16[7,2,32,1024]{3,2,1,0:T(8,128)(2,1)} %onward.7.rest_3_), channel_id=1, source_target_pairs={{4,8},{6,10},{8,12},{10,14},{5,9},{7,11},{9,13},{11,15},{20,24},{2... | collective-permute-start | bytes 2752520 | tf_op jit(solution)/shard_map/ppermute | solution.py:503
  168.0 15.9 %collective-permute-start.15 = (bf16[4,2,32,1024]{3,2,1,0:T(8,128)(2,1)}, bf16[4,2,32,1024]{3,2,1,0:T(8,128)(2,1)S(1)}, u32[]{:S(2)}, u32[]{:S(2)}) collective-permute-start(bf16[4,2,32,1024]{3,2,1,0:T(8,128)(2,1)} %get-tuple-element.23), channel_id=1, source_target_pairs={{0,2},{2,0},{4,6},{6,4},{8,10},{10,8},{12,14},{14,12},{1,3},{3,1},... | collective-permute-start | bytes 1572872 | tf_op jit(solution)/shard_map/ppermute | solution.py:500
  169.3 19.7 %collective-permute-start.17 = (bf16[4,2,32,1024]{3,2,1,0:T(8,128)(2,1)S(1)}, bf16[4,2,32,1024]{3,2,1,0:T(8,128)(2,1)S(1)}, u32[]{:S(2)}, u32[]{:S(2)}) collective-permute-start(bf16[4,2,32,1024]{3,2,1,0:T(8,128)(2,1)S(1)} %copy-done.16), channel_id=1, source_target_pairs={{0,1},{1,0},{2,3},{3,2},{4,5},{5,4},{6,7},{7,6},{8,9},{9,8},{10,11... | collective-permute-start | bytes 1572872 | tf_op jit(solution)/shard_map/ppermute | solution.py:506
  175.2 15.2 %collective-permute-start.18 = (bf16[4,2,32,1024]{3,2,1,0:T(8,128)(2,1)S(1)}, bf16[4,2,32,1024]{3,2,1,0:T(8,128)(2,1)S(1)}, u32[]{:S(2)}, u32[]{:S(2)}) collective-permute-start(bf16[4,2,32,1024]{3,2,1,0:T(8,128)(2,1)S(1)} %copy-done.6), channel_id=1, source_target_pairs={{0,1},{1,0},{2,3},{3,2},{4,5},{5,4},{6,7},{7,6},{8,9},{9,8},{10,11... | collective-permute-start | bytes 1572872 | tf_op jit(solution)/shard_map/ppermute | solution.py:506
  175.2 15.2 %collective-permute-start.19 = (bf16[4,2,32,1024]{3,2,1,0:T(8,128)(2,1)S(1)}, bf16[4,2,32,1024]{3,2,1,0:T(8,128)(2,1)S(1)}, u32[]{:S(2)}, u32[]{:S(2)}) collective-permute-start(bf16[4,2,32,1024]{3,2,1,0:T(8,128)(2,1)S(1)} %copy-done.9), channel_id=1, source_target_pairs={{0,1},{1,0},{2,3},{3,2},{4,5},{5,4},{6,7},{7,6},{8,9},{9,8},{10,11... | collective-permute-start | bytes 1572872 | tf_op jit(solution)/shard_map/ppermute | solution.py:506
  181.3 9.6 %collective-permute-start.20 = (bf16[4,2,32,1024]{3,2,1,0:T(8,128)(2,1)}, bf16[4,2,32,1024]{3,2,1,0:T(8,128)(2,1)S(1)}, u32[]{:S(2)}, u32[]{:S(2)}) collective-permute-start(bf16[4,2,32,1024]{3,2,1,0:T(8,128)(2,1)} %copy-done.11), channel_id=1, source_target_pairs={{0,1},{1,0},{2,3},{3,2},{4,5},{5,4},{6,7},{7,6},{8,9},{9,8},{10,11... | collective-permute-start | bytes 1572872 | tf_op jit(solution)/shard_map/ppermute | solution.py:506
  188.8 15.0 %collective-permute-start.16 = (bf16[4,2,32,1024]{3,2,1,0:T(8,128)(2,1)}, bf16[4,2,32,1024]{3,2,1,0:T(8,128)(2,1)S(1)}, u32[]{:S(2)}, u32[]{:S(2)}) collective-permute-start(bf16[4,2,32,1024]{3,2,1,0:T(8,128)(2,1)} %get-tuple-element.25), channel_id=1, source_target_pairs={{0,2},{2,0},{4,6},{6,4},{8,10},{10,8},{12,14},{14,12},{1,3},{3,1},... | collective-permute-start | bytes 1572872 | tf_op jit(solution)/shard_map/ppermute | solution.py:500
  189.0 15.9 %collective-permute-start.21 = (bf16[4,2,32,1024]{3,2,1,0:T(8,128)(2,1)S(1)}, bf16[4,2,32,1024]{3,2,1,0:T(8,128)(2,1)S(1)}, u32[]{:S(2)}, u32[]{:S(2)}) collective-permute-start(bf16[4,2,32,1024]{3,2,1,0:T(8,128)(2,1)S(1)} %copy-done.17), channel_id=1, source_target_pairs={{0,1},{1,0},{2,3},{3,2},{4,5},{5,4},{6,7},{7,6},{8,9},{9,8},{10,11... | collective-permute-start | bytes 1572872 | tf_op jit(solution)/shard_map/ppermute | solution.py:506
  190.3 14.6 %collective-permute-start.22 = (bf16[4,2,32,1024]{3,2,1,0:T(8,128)(2,1)}, bf16[4,2,32,1024]{3,2,1,0:T(8,128)(2,1)S(1)}, u32[]{:S(2)}, u32[]{:S(2)}) collective-permute-start(bf16[4,2,32,1024]{3,2,1,0:T(8,128)(2,1)} %get-tuple-element.24.refs_11_.refs_2_), channel_id=1, source_target_pairs={{0,1},{1,0},{2,3},{3,2},{4,5},{5,4},{6,7},{7,6},{8,9},{9,8},{10,11... | collective-permute-start | bytes 1572872 | tf_op jit(solution)/shard_map/ppermute | solution.py:506
  190.4 14.5 %collective-permute-start.23 = (bf16[4,2,32,1024]{3,2,1,0:T(8,128)(2,1)}, bf16[4,2,32,1024]{3,2,1,0:T(8,128)(2,1)S(1)}, u32[]{:S(2)}, u32[]{:S(2)}) collective-permute-start(bf16[4,2,32,1024]{3,2,1,0:T(8,128)(2,1)} %copy-done.10), channel_id=1, source_target_pairs={{0,1},{1,0},{2,3},{3,2},{4,5},{5,4},{6,7},{7,6},{8,9},{9,8},{10,11... | collective-permute-start | bytes 1572872 | tf_op jit(solution)/shard_map/ppermute | solution.py:506
  (37 other events, 231.1 us)

commit v8 on v7

--- a/solution.py
+++ b/solution.py
@@ -15,7 +15,7 @@
 RADIX = 16
 LANES = 128
 CORES = 2
-VMEM_LIMIT = 56 * 1024 * 1024
+VMEM_LIMIT = 63 * 1024 * 1024
 F32 = jnp.float32
 BF16 = jnp.bfloat16
 
@@ -249,10 +249,11 @@
 def far_filter(place, taps, partial, far, low, size, earlier):
     count, parts, stations, _ = partial.shape
     frames = count // 2
-    block = math.gcd(512, low, size)
+    block = size // 2
 
     def spec(depth, start):
-        return pl.BlockSpec((depth, parts, stations, block), lambda i, place: (0, 0, 0, start // block + i))
+        shape = (pl.Element(depth), pl.Element(parts), pl.Element(stations), pl.Element(block))
+        return pl.BlockSpec(shape, lambda i, place: (0, 0, 0, pl.multiple_of(start + i * block, LANES)))
 
     shape = jax.ShapeDtypeStruct((frames, parts, stations, size), BF16)
     return pl.pallas_call(
@@ -261,7 +262,12 @@
         grid_spec=pltpu.PrefetchScalarGridSpec(
             num_scalar_prefetch=1,
             grid=(size // block,),
-            in_specs=[pl.BlockSpec((taps.shape[0], 8, block), lambda i, place: (0, 0, low // block + i))]
+            in_specs=[
+                pl.BlockSpec(
+                    (pl.Element(taps.shape[0]), pl.Element(8), pl.Element(block)),
+                    lambda i, place: (0, 0, pl.multiple_of(low + i * block, LANES)),
+                )
+            ]
             + [spec(count, low), spec(far.shape[0], 0)]
             + [pl.BlockSpec(memory_space=pl.ANY)] * len(earlier),
             out_specs=[spec(frames, 0)] * 2,
@@ -273,7 +279,8 @@
 
 
 def onward_kernel(place, own_back, other_back, far):
-    frames = own_back.shape[0]
+    frames = other_back.shape[0]
+    own_back = own_back.at[0]
 
     def run(first, second):
         far[: frames - 1] = first[1:]
@@ -291,19 +298,19 @@
 def onward(place, own_back, other_back, pol, low, size):
     frames, parts, stations, _ = other_back.shape
     depth = 2 * frames - 1
-    block = math.gcd(low, size)
-    where = low // block
+
+    def spec(depth, *before):
+        shape = tuple(pl.Element(n) for n in (1,) * len(before) + (depth, 1, stations, size))
+        return pl.BlockSpec(shape, lambda i, place: before + (0, i, 0, low))
+
     return pl.pallas_call(
         onward_kernel,
         out_shape=jax.ShapeDtypeStruct((depth, parts, stations, size), BF16),
         grid_spec=pltpu.PrefetchScalarGridSpec(
             num_scalar_prefetch=1,
-            grid=(parts, size // block),
-            in_specs=[
-                pl.BlockSpec((None, frames, 1, stations, block), lambda i, j, place: (pol, 0, i, 0, where + j)),
-                pl.BlockSpec((frames, 1, stations, block), lambda i, j, place: (0, i, 0, where + j)),
-            ],
-            out_specs=pl.BlockSpec((depth, 1, stations, block), lambda i, j, place: (0, i, 0, j)),
+            grid=(parts,),
+            in_specs=[spec(frames, pol), spec(frames)],
+            out_specs=pl.BlockSpec((depth, 1, stations, size), lambda i, place: (0, i, 0, 0)),
         ),
         compiler_params=pltpu.CompilerParams(vmem_limit_bytes=VMEM_LIMIT),
         cost_estimate=cost(3),
@@ -352,7 +359,7 @@
     earlier = refs.pop(0) if has_earlier else None
     refs = refs[later_count:]
     out, mixed, spectra, sems, *refs = refs
-    held, refs = refs[:source_count], refs[source_count:]
+    held = refs
     step = pl.program_id(0)
     frames = sources[0].shape[0]
     stations = sources[0].shape[2]
@@ -363,7 +370,6 @@
     rows_of = table.shape[2] // 2 // groups
     pair = 2
     lane_tiles = beams // LANES
-    per_channel = lane_tiles * frames
 
     @pl.when(step == 0)
     def _():
@@ -420,21 +426,9 @@
         for b in range(RADIX):
             for f in range(frames):
                 at = (b * frames + f) * rows_of
+                channels = pl.ds(k * rows_of * RADIX + b, rows_of, stride=RADIX)
                 for t in range(lane_tiles):
-                    start = (k * rows_of * RADIX + b) * per_channel + t * frames + f
-                    refs[0][pl.ds(start, rows_of, stride=RADIX * per_channel), :] = power[
-                        at : at + rows_of, t * LANES : (t + 1) * LANES
-                    ]
-
-    if has_earlier:
-
-        def finish(c, carry):
-            value = refs[0][pl.ds(pl.multiple_of(c * per_channel, per_channel), per_channel), :]
-            for t in range(lane_tiles):
-                out[c, :, t * LANES : (t + 1) * LANES] = value[t * frames : (t + 1) * frames]
-            return carry
-
-        lax.fori_loop(0, out.shape[0], finish, 0, unroll=8)
+                    out[channels, t, f, :] = power[at : at + rows_of, t * LANES : (t + 1) * LANES]
 
 
 def beam_power(place, sources, ranges, table, weights, earlier, channels, later=()):
@@ -462,11 +456,10 @@
         out_shape = jax.ShapeDtypeStruct(flat, F32)
         out_spec = flat_spec
     else:
-        out_shape = jax.ShapeDtypeStruct((channels, frames, beams), F32)
-        out_spec = pl.BlockSpec((channels // groups * at_once, frames, beams), lambda i, place: (i, 0, 0))
+        out_shape = jax.ShapeDtypeStruct((channels, beams // LANES, frames, LANES), F32)
+        out_spec = pl.BlockSpec((channels // groups * at_once,) + out_shape.shape[1:], lambda i, place: (i, 0, 0, 0))
         operands.append(earlier)
         in_specs.append(flat_spec)
-        scratch.append(pltpu.VMEM((math.prod(out_spec.block_shape) // LANES, LANES), F32))
     return pl.pallas_call(
         functools.partial(beam_kernel, len(sources), ranges, len(later), earlier is not None),
         out_shape=out_shape,
@@ -534,28 +527,31 @@
     table = jnp.asarray(dft_tables(samples))
     taps = jnp.broadcast_to(filter_taps[:, None, :], (history + 1, 8, samples))
 
-    chunks = [(pol, low, samples // 2) for pol in range(pols) for low in (0, samples // 2)]
+    parts_of = [(samples // 2, samples // 2), (5 * samples // 8, 3 * samples // 8)]
+    chunks = [(pol, sum(sizes[:i]), size) for pol, sizes in enumerate(parts_of) for i, size in enumerate(sizes)]
     other_back = [hop(block) for block in other]
     further = [onward(place, own_back, other_back[pol], pol, low, size) for pol, low, size in chunks]
     far = [hop(block, 2) for block in further]
-    keeps, sents, partial = [], [], []
+    partial = []
+    for pol in range(pols):
+        gates = further[: 2 * pol + 2] + [weights]
+        partial.append(near_filter(place, taps, own, other[pol], own_back, other_back[pol], pol, gates))
+    keeps, sents, power = [], [], None
 
     def power_of(pol, earlier, later=()):
-        here = [k for k, chunk in enumerate(chunks) if chunk[0] == pol]
-        mine, pairs = [keeps[k] for k in here], [sents[k] for k in here]
+        mine, pairs = keeps[2 * pol : 2 * pol + 2], sents[2 * pol : 2 * pol + 2]
         sources = mine + pairs + [swap(block) for block in mine + pairs]
-        return beam_power(place, sources, len(here), table, weights, earlier, samples // CORES, later)
+        return beam_power(place, sources, 2, table, weights, earlier, samples // CORES, later)
 
     for k, (pol, low, size) in enumerate(chunks):
-        if pol >= len(partial):
-            gates = further + keeps[1:2] if pol else further[:2] + [weights]
-            partial.append(near_filter(place, taps, own, other[pol], own_back, other_back[pol], pol, gates))
-        keep, send = far_filter(place, taps, partial[pol], far[k], low, size, sents[-1:])
+        gates = {0: [], 1: [*sents[:1], partial[1]], 2: sents[1:2], 3: [power]}[k]
+        keep, send = far_filter(place, taps, partial[pol], far[k], low, size, gates)
         keeps.append(keep)
         sents.append(pair(send))
-    power = power_of(0, None, keeps[-1:])
-    sents[-1] = after(sents[-1], power)
-    return power_of(1, power)
+        if k == 2:
+            power = power_of(0, None, [keep])
+    power = power_of(1, power)
+    return jnp.moveaxis(power, 1, 2).reshape(power.shape[0], power.shape[2], -1)
 
 
 def solution(mesh):

time: 224 us -> 221 us (0.987)
  waiting for transfers between devices: 75.9 us -> 66.5 us
  other arithmetic: 0.65 us -> 4.19 us
  starting transfers between devices: 44 us -> 46.4 us
    ppermute x7, waiting for transfers between devices: 41.6 us -> 26.6 us  [hop(): lax.ppermute(block, 'tm', [(i, i + 2) for i in range(skip, time_devices -...]
    ppermute x7, waiting for transfers between devices: 32.6 us -> 39.9 us  [pair(): return lax.ppermute(block, 'tm', [(i, i ^ 1) for i in range(time_devices)])]
    unnamed x76 -> x38, local copies, waits for them, and re-layouts: 13.1 us -> 9.57 us
    ppermute x8, starting transfers between devices: 11.3 us -> 14 us  [swap(): return lax.ppermute(block, 'stn', [(0, 1), (1, 0)])]
    pallas_call x4, local copies, waits for them, and re-layouts: 10.2 us -> 12.8 us  [after(): pl.pallas_call(lambda *refs: None, out_shape=jax.ShapeDtypeStruct(block.s...]
  transfers between devices with their start and end apart: 25 -> 25, of which waited for: 7 -> 6; matrix products, arithmetic and copies ran while one was open for 6% -> 11% of each run, Pallas kernels for 27% -> 28%
where the time goes in v8:
time: 221 us; the launch traced here: 219 us
  Pallas kernels  74.8 us (34%)
  waiting for transfers between devices  66.5 us (30%)
  starting transfers between devices  46.4 us (21%)
  local copies, waits for them, and re-layouts  26.4 us (12%)
  other arithmetic  4.19 us (2%)
    ppermute x7, waiting for transfers between devices, pair(): return lax.ppermute(block, 'tm', [(i, i ^ 1) for i in range(time_devices)])  39.9 us
    ppermute x7, waiting for transfers between devices, hop(): lax.ppermute(block, 'tm', [(i, i + 2) for i in range(skip, time_devices -...  26.6 us
    ppermute x7, starting transfers between devices, hop(): lax.ppermute(block, 'tm', [(i, i + 2) for i in range(skip, time_devices -...  26.1 us
    pallas_call x2, Pallas kernels, beam_power(): pl.pallas_call(functools.partial(beam_kernel, len(sources), ranges, len(l...  25.3 us
    pallas_call x4, Pallas kernels, far_filter(): pl.pallas_call(far_kernel, out_shape=(shape, shape), grid_spec=pltpu.Pref...  15.9 us
    pallas_call x2, Pallas kernels, near_filter(): pl.pallas_call(near_kernel, out_shape=jax.ShapeDtypeStruct((2 * frames, p...  15.7 us
    ppermute x8, starting transfers between devices, swap(): return lax.ppermute(block, 'stn', [(0, 1), (1, 0)])  14 us
    pallas_call x4, local copies, waits for them, and re-layouts, after(): pl.pallas_call(lambda *refs: None, out_shape=jax.ShapeDtypeStruct(block.s...  12.8 us
  transfers between devices with their start and end apart: 25, of which 6 were waited for; matrix products, arithmetic and copies ran while one was open for 11% of the time, Pallas kernels for 28%

profile of v8, /device:TPU:17, one launch (start us, length us, event | category | flops | bytes accessed | tf_op | source)
XLA Modules:
  0.0 218.5 jit_solution(3152587041037556554)
XLA Ops:
  4.0 4.3 %cut.1 = (bf16[32,2,4,2,2048]{4,3,2,1,0:T(2,128)(2,1)}, bf16[32,4,2,2048]{3,2,1,0:T(2,128)(2,1)}, bf16[32,4,2,2048]{3,2,1,0:T(2,128)(2,1)}) custom-call(s32[2]{0:T(128)} %pad_add_fusion.place.refs_0_, bf16[64,2,4,2,2048]{4,3,2,1,0:T(2,128)(2,1)} %voltages.1), custom_call_target="tpu_custom_call" | custom-call | bytes 13200000 | tf_op jit(solution)/shard_map/cut/pallas_call | solution.py:136
  10.2 4.1 %collective-permute-start.4 = (bf16[32,2,4,2,2048]{4,3,2,1,0:T(2,128)(2,1)}, bf16[32,2,4,2,2048]{4,3,2,1,0:T(2,128)(2,1)}, u32[]{:S(2)}, u32[]{:S(2)}) collective-permute-start(bf16[32,2,4,2,2048]{4,3,2,1,0:T(2,128)(2,1)} %after.4), channel_id=1, source_target_pairs={{0,4},{2,6},{4,8},{6,10},{8,12},{10,14},{1,5},{3,7},{5,9},{7,11},{... | collective-permute-start | bytes 6291464 | tf_op jit(solution)/shard_map/ppermute | solution.py:496
  14.6 17.2 %collective-permute-done.6.refs_0_ = bf16[32,4,2,2048]{3,2,1,0:T(2,128)(2,1)S(1)} collective-permute-done((bf16[32,4,2,2048]{3,2,1,0:T(2,128)(2,1)}, bf16[32,4,2,2048]{3,2,1,0:T(2,128)(2,1)S(1)}, u32[]{:S(2)}, u32[]{:S(2)}) %collective-permute-start.6) | collective-permute-done | bytes 1048608 | tf_op jit(solution)/shard_map/ppermute | solution.py:493
  34.6 4.1 %collective-permute-start.7 = (bf16[4,2,32,2048]{3,2,1,0:T(8,128)(2,1)S(1)}, bf16[4,2,32,2048]{3,2,1,0:T(8,128)(2,1)S(1)}, u32[]{:S(2)}, u32[]{:S(2)}) collective-permute-start(bf16[4,2,32,2048]{3,2,1,0:T(8,128)(2,1)S(1)} %bitcast.36), channel_id=1, source_target_pairs={{0,4},{2,6},{4,8},{6,10},{8,12},{10,14},{1,5},{3,7},{5,9},{7,11},{... | collective-permute-start | bytes 3145736 | tf_op jit(solution)/shard_map/ppermute | solution.py:496
  38.8 15.5 %collective-permute-done.3.refs_0_ = bf16[32,4,2,2048]{3,2,1,0:T(2,128)(2,1)S(1)} collective-permute-done((bf16[32,4,2,2048]{3,2,1,0:T(2,128)(2,1)}, bf16[32,4,2,2048]{3,2,1,0:T(2,128)(2,1)S(1)}, u32[]{:S(2)}, u32[]{:S(2)}) %collective-permute-start.3) | collective-permute-done | bytes 1048608 | tf_op jit(solution)/shard_map/ppermute | solution.py:493
  58.0 4.1 %collective-permute-start.5 = (bf16[4,2,32,2048]{3,2,1,0:T(8,128)(2,1)}, bf16[4,2,32,2048]{3,2,1,0:T(8,128)(2,1)}, u32[]{:S(2)}, u32[]{:S(2)}) collective-permute-start(bf16[4,2,32,2048]{3,2,1,0:T(8,128)(2,1)} %bitcast.27.rest_1_.other), channel_id=1, source_target_pairs={{0,4},{2,6},{4,8},{6,10},{8,12},{10,14},{1,5},{3,7},{5,9},{7,11},{... | collective-permute-start | bytes 3145736 | tf_op jit(solution)/shard_map/ppermute | solution.py:496
  62.8 4.1 %copy.19 = bf16[32,2,4,2,2048]{4,0,3,2,1:T(8,128)(2,1)} copy(bf16[32,2,4,2,2048]{4,3,2,1,0:T(2,128)(2,1)} %after.6) | data formatting | bytes 4194304 | tf_op jit(solution)/shard_map/after/pallas_call | solution.py:77
  66.9 13.2 %collective-permute-done.7.other_back = bf16[4,2,32,2048]{3,2,1,0:T(8,128)(2,1)S(1)} collective-permute-done((bf16[4,2,32,2048]{3,2,1,0:T(8,128)(2,1)S(1)}, bf16[4,2,32,2048]{3,2,1,0:T(8,128)(2,1)S(1)}, u32[]{:S(2)}, u32[]{:S(2)}) %collective-permute-start.7) | collective-permute-done | bytes 1048608 | tf_op jit(solution)/shard_map/ppermute | solution.py:496
  83.8 4.1 %collective-permute-start.11 = (bf16[7,2,32,1024]{3,2,1,0:T(8,128)(2,1)}, bf16[7,2,32,1024]{3,2,1,0:T(8,128)(2,1)S(1)}, u32[]{:S(2)}, u32[]{:S(2)}) collective-permute-start(bf16[7,2,32,1024]{3,2,1,0:T(8,128)(2,1)} %onward.4.rest_0_), channel_id=1, source_target_pairs={{4,8},{6,10},{8,12},{10,14},{5,9},{7,11},{9,13},{11,15},{20,24},{2... | collective-permute-start | bytes 2752520 | tf_op jit(solution)/shard_map/ppermute | solution.py:496
  99.0 4.1 %copy.20 = bf16[32,2,4,2,2048]{4,0,3,2,1:T(8,128)(2,1)} copy(bf16[32,2,4,2,2048]{4,3,2,1,0:T(2,128)(2,1)} %after.4) | data formatting | bytes 4194304 | tf_op jit(solution)/shard_map/after/pallas_call | solution.py:77
  105.9 3.7 %collective-permute-start.9 = (bf16[7,2,32,1280]{3,2,1,0:T(8,128)(2,1)}, bf16[7,2,32,1280]{3,2,1,0:T(8,128)(2,1)}, u32[]{:S(2)}, u32[]{:S(2)}) collective-permute-start(bf16[7,2,32,1280]{3,2,1,0:T(8,128)(2,1)} %onward.6.rest_2_), channel_id=1, source_target_pairs={{4,8},{6,10},{8,12},{10,14},{5,9},{7,11},{9,13},{11,15},{20,24},{2... | collective-permute-start | bytes 3440648 | tf_op jit(solution)/shard_map/ppermute | solution.py:496
  115.7 7.9 %near.3.partial = f32[8,2,32,2048]{3,2,1,0:T(8,128)} custom-call(s32[2]{0:T(128)} %pad_add_fusion.place.refs_0_, f32[16,8,2048]{2,1,0:T(8,128)} %broadcast_in_dim.2.taps, bf16[2,4,2,32,2048]{4,3,2,1,0:T(8,128)(2,1)} %bitcast.34, bf16[4,2,32,2048]{3,2,1,0:T(8,128)(2,1)} %bitcast.38, bf16[2,4,2,32,2048]{4,3,2,1,0:T(8,128)(2,1)} %bitcast.31, ...), custom_call_target="tpu_custom_call" | custom-call | bytes 26400000 | tf_op jit(solution)/shard_map/near/pallas_call | solution.py:233
  124.5 4.0 %far.4 = (bf16[4,2,32,1024]{3,2,1,0:T(8,128)(2,1)}, bf16[4,2,32,1024]{3,2,1,0:T(8,128)(2,1)}) custom-call(s32[2]{0:T(128)} %pad_add_fusion.place.refs_0_, f32[16,8,2048]{2,1,0:T(8,128)} %broadcast_in_dim.2.taps, f32[8,2,32,2048]{3,2,1,0:T(8,128)} %near.3.partial, bf16[7,2,32,1024]{3,2,1,0:T(8,128)(2,1)} %copy-done.6), custom_call_target="tpu_custom_call" | custom-call | bytes 3300000 | tf_op jit(solution)/shard_map/far/pallas_call | solution.py:259
  131.4 7.8 %near.2.rest_1_.partial = f32[8,2,32,2048]{3,2,1,0:T(8,128)} custom-call(s32[2]{0:T(128)} %pad_add_fusion.place.refs_0_, f32[16,8,2048]{2,1,0:T(8,128)} %broadcast_in_dim.2.taps, bf16[2,4,2,32,2048]{4,3,2,1,0:T(8,128)(2,1)} %bitcast.35, bf16[4,2,32,2048]{3,2,1,0:T(8,128)(2,1)} %bitcast.27.rest_1_.other, bf16[2,4,2,32,2048]{4,3,2,1,0:T(8,128)(2,1)} %bitcast.33, ...), custom_call_target="tpu_custom_call" | custom-call | bytes 26400000 | tf_op jit(solution)/shard_map/near/pallas_call | solution.py:233
  142.0 3.9 %far.5 = (bf16[4,2,32,1024]{3,2,1,0:T(8,128)(2,1)}, bf16[4,2,32,1024]{3,2,1,0:T(8,128)(2,1)}) custom-call(s32[2]{0:T(128)} %pad_add_fusion.place.refs_0_, f32[16,8,2048]{2,1,0:T(8,128)} %broadcast_in_dim.2.taps, f32[8,2,32,2048]{3,2,1,0:T(8,128)} %near.3.partial, bf16[7,2,32,1024]{3,2,1,0:T(8,128)(2,1)} %collective-permute-done.10.far, ...), custom_call_target="tpu_custom_call" | custom-call | bytes 3300000 | tf_op jit(solution)/shard_map/far/pallas_call | solution.py:259
  146.1 5.3 %collective-permute-start.15 = (bf16[4,2,32,1024]{3,2,1,0:T(8,128)(2,1)}, bf16[4,2,32,1024]{3,2,1,0:T(8,128)(2,1)}, u32[]{:S(2)}, u32[]{:S(2)}) collective-permute-start(bf16[4,2,32,1024]{3,2,1,0:T(8,128)(2,1)} %get-tuple-element.22.refs_1_), channel_id=1, source_target_pairs={{0,1},{1,0},{2,3},{3,2},{4,5},{5,4},{6,7},{7,6},{8,9},{9,8},{10,11... | collective-permute-start | bytes 1572872 | tf_op jit(solution)/shard_map/ppermute | solution.py:499
  151.5 4.1 %collective-permute-start.14 = (bf16[7,2,32,768]{3,2,1,0:T(8,128)(2,1)S(1)}, bf16[7,2,32,768]{3,2,1,0:T(8,128)(2,1)}, u32[]{:S(2)}, u32[]{:S(2)}) collective-permute-start(bf16[7,2,32,768]{3,2,1,0:T(8,128)(2,1)S(1)} %copy-done.4), channel_id=1, source_target_pairs={{4,8},{6,10},{8,12},{10,14},{5,9},{7,11},{9,13},{11,15},{20,24},{2... | collective-permute-start | bytes 2064392 | tf_op jit(solution)/shard_map/ppermute | solution.py:496
  155.9 10.6 %collective-permute-done.9.far = bf16[7,2,32,1280]{3,2,1,0:T(8,128)(2,1)} collective-permute-done((bf16[7,2,32,1280]{3,2,1,0:T(8,128)(2,1)}, bf16[7,2,32,1280]{3,2,1,0:T(8,128)(2,1)}, u32[]{:S(2)}, u32[]{:S(2)}) %collective-permute-start.9) | collective-permute-done | bytes 1146912 | tf_op jit(solution)/shard_map/ppermute | solution.py:496
  166.6 5.0 %collective-permute-start.17 = (bf16[4,2,32,1024]{3,2,1,0:T(8,128)(2,1)}, bf16[4,2,32,1024]{3,2,1,0:T(8,128)(2,1)}, u32[]{:S(2)}, u32[]{:S(2)}) collective-permute-start(bf16[4,2,32,1024]{3,2,1,0:T(8,128)(2,1)} %collective-permute-done.12.rest_0_.refs_3_), channel_id=1, source_target_pairs={{0,1},{1,0},{2,3},{3,2},{4,5},{5,4},{6,7},{7,6},{8,9},{9,8},{10,11... | collective-permute-start | bytes 1572872 | tf_op jit(solution)/shard_map/ppermute | solution.py:499
  171.6 4.4 %far.6 = (bf16[4,2,32,1280]{3,2,1,0:T(8,128)(2,1)}, bf16[4,2,32,1280]{3,2,1,0:T(8,128)(2,1)}) custom-call(s32[2]{0:T(128)} %pad_add_fusion.place.refs_0_, f32[16,8,2048]{2,1,0:T(8,128)} %broadcast_in_dim.2.taps, f32[8,2,32,2048]{3,2,1,0:T(8,128)} %near.2.rest_1_.partial, bf16[7,2,32,1280]{3,2,1,0:T(8,128)(2,1)} %collective-permute-done.9.far, ...), custom_call_target="tpu_custom_call" | custom-call | bytes 3300000 | tf_op jit(solution)/shard_map/far/pallas_call | solution.py:259
  176.2 11.6 %beams.2.rest_0_.refs_11_ = f32[8,512,256]{2,1,0:T(8,128)} custom-call(s32[2]{0:T(128)} %pad_add_fusion.place.refs_0_, bf16[4,2,32,1024]{3,2,1,0:T(8,128)(2,1)} %get-tuple-element.22.refs_1_, bf16[4,2,32,1024]{3,2,1,0:T(8,128)(2,1)} %get-tuple-element.23.refs_2_, bf16[4,2,32,1024]{3,2,1,0:T(8,128)(2,1)} %collective-permute-done.12.rest_0_.refs_3_, ...), custom_call_target="tpu_custom_call" | custom-call | tf_op jit(solution)/shard_map/beams/pallas_call | solution.py:463
  187.8 3.6 %far.7 = (bf16[4,2,32,768]{3,2,1,0:T(8,128)(2,1)}, bf16[4,2,32,768]{3,2,1,0:T(8,128)(2,1)}) custom-call(s32[2]{0:T(128)} %pad_add_fusion.place.refs_0_, f32[16,8,2048]{2,1,0:T(8,128)} %broadcast_in_dim.2.taps, f32[8,2,32,2048]{3,2,1,0:T(8,128)} %near.2.rest_1_.partial, bf16[7,2,32,768]{3,2,1,0:T(8,128)(2,1)} %collective-permute-done.14.far, ...), custom_call_target="tpu_custom_call" | custom-call | bytes 3300000 | tf_op jit(solution)/shard_map/far/pallas_call | solution.py:259
  194.3 7.2 %collective-permute-done.20.refs_4_ = bf16[4,2,32,768]{3,2,1,0:T(8,128)(2,1)S(1)} collective-permute-done((bf16[4,2,32,768]{3,2,1,0:T(8,128)(2,1)}, bf16[4,2,32,768]{3,2,1,0:T(8,128)(2,1)S(1)}, u32[]{:S(2)}, u32[]{:S(2)}) %collective-permute-start.20) | collective-permute-done | bytes 393248 | tf_op jit(solution)/shard_map/ppermute | solution.py:493
  204.9 13.6 %beams.3 = f32[1024,2,4,128]{3,2,1,0:T(4,128)} custom-call(s32[2]{0:T(128)} %pad_add_fusion.place.refs_0_, bf16[4,2,32,1280]{3,2,1,0:T(8,128)(2,1)} %get-tuple-element.21.refs_11_.refs_1_, bf16[4,2,32,768]{3,2,1,0:T(8,128)(2,1)} %get-tuple-element.24.refs_2_, bf16[4,2,32,1280]{3,2,1,0:T(8,128)(2,1)} %collective-permute-done.19.refs_3_, ...), custom_call_target="tpu_custom_call" | custom-call | tf_op jit(solution)/shard_map/beams/pallas_call | solution.py:463
  (98 shorter events, 50.7 us)
Async XLA Ops:
  0.7 8.9 %collective-permute-start = (bf16[16,256]{1,0:T(8,128)(2,1)S(1)}, bf16[16,256]{1,0:T(8,128)(2,1)S(1)}, u32[]{:S(2)}, u32[]{:S(2)}) collective-permute-start(bf16[16,256]{1,0:T(8,128)(2,1)S(1)} %get-tuple-element.28), channel_id=1, source_target_pairs={{0,4},{2,6},{4,0},{6,2},{8,12},{10,14},{12,8},{14,10},{1,5},{3,7},... | collective-permute-start | bytes 24584 | tf_op jit(solution)/shard_map/ppermute | solution.py:507
  2.0 7.6 %collective-permute-start.1 = (bf16[16,256]{1,0:T(8,128)(2,1)S(1)}, bf16[16,256]{1,0:T(8,128)(2,1)S(1)}, u32[]{:S(2)}, u32[]{:S(2)}) collective-permute-start(bf16[16,256]{1,0:T(8,128)(2,1)S(1)} %get-tuple-element.28), channel_id=1, source_target_pairs={{0,8},{2,10},{4,12},{6,14},{8,0},{10,2},{12,4},{14,6},{1,9},{3,11}... | collective-permute-start | bytes 24584 | tf_op jit(solution)/shard_map/ppermute | solution.py:507
  2.1 7.5 %collective-permute-start.2 = (bf16[16,256]{1,0:T(8,128)(2,1)S(1)}, bf16[16,256]{1,0:T(8,128)(2,1)S(1)}, u32[]{:S(2)}, u32[]{:S(2)}) collective-permute-start(bf16[16,256]{1,0:T(8,128)(2,1)S(1)} %get-tuple-element.28), channel_id=1, source_target_pairs={{0,12},{2,14},{4,8},{6,10},{8,4},{10,6},{12,0},{14,2},{1,13},{3,15... | collective-permute-start | bytes 24584 | tf_op jit(solution)/shard_map/ppermute | solution.py:507
  8.2 23.5 %collective-permute-start.6 = (bf16[32,4,2,2048]{3,2,1,0:T(2,128)(2,1)}, bf16[32,4,2,2048]{3,2,1,0:T(2,128)(2,1)S(1)}, u32[]{:S(2)}, u32[]{:S(2)}) collective-permute-start(bf16[32,4,2,2048]{3,2,1,0:T(2,128)(2,1)} %get-tuple-element.18), channel_id=1, source_target_pairs={{0,2},{2,0},{4,6},{6,4},{8,10},{10,8},{12,14},{14,12},{1,3},{3,1},... | collective-permute-start | bytes 3145736 | tf_op jit(solution)/shard_map/ppermute | solution.py:493
  10.2 52.6 %collective-permute-start.4 = (bf16[32,2,4,2,2048]{4,3,2,1,0:T(2,128)(2,1)}, bf16[32,2,4,2,2048]{4,3,2,1,0:T(2,128)(2,1)}, u32[]{:S(2)}, u32[]{:S(2)}) collective-permute-start(bf16[32,2,4,2,2048]{4,3,2,1,0:T(2,128)(2,1)} %after.4), channel_id=1, source_target_pairs={{0,4},{2,6},{4,8},{6,10},{8,12},{10,14},{1,5},{3,7},{5,9},{7,11},{... | collective-permute-start | bytes 6291464 | tf_op jit(solution)/shard_map/ppermute | solution.py:496
  14.3 39.9 %collective-permute-start.3 = (bf16[32,4,2,2048]{3,2,1,0:T(2,128)(2,1)}, bf16[32,4,2,2048]{3,2,1,0:T(2,128)(2,1)S(1)}, u32[]{:S(2)}, u32[]{:S(2)}) collective-permute-start(bf16[32,4,2,2048]{3,2,1,0:T(2,128)(2,1)} %get-tuple-element.17), channel_id=1, source_target_pairs={{0,2},{2,0},{4,6},{6,4},{8,10},{10,8},{12,14},{14,12},{1,3},{3,1},... | collective-permute-start | bytes 3145736 | tf_op jit(solution)/shard_map/ppermute | solution.py:493
  34.6 45.5 %collective-permute-start.7 = (bf16[4,2,32,2048]{3,2,1,0:T(8,128)(2,1)S(1)}, bf16[4,2,32,2048]{3,2,1,0:T(8,128)(2,1)S(1)}, u32[]{:S(2)}, u32[]{:S(2)}) collective-permute-start(bf16[4,2,32,2048]{3,2,1,0:T(8,128)(2,1)S(1)} %bitcast.36), channel_id=1, source_target_pairs={{0,4},{2,6},{4,8},{6,10},{8,12},{10,14},{1,5},{3,7},{5,9},{7,11},{... | collective-permute-start | bytes 3145736 | tf_op jit(solution)/shard_map/ppermute | solution.py:496
  58.0 45.0 %collective-permute-start.5 = (bf16[4,2,32,2048]{3,2,1,0:T(8,128)(2,1)}, bf16[4,2,32,2048]{3,2,1,0:T(8,128)(2,1)}, u32[]{:S(2)}, u32[]{:S(2)}) collective-permute-start(bf16[4,2,32,2048]{3,2,1,0:T(8,128)(2,1)} %bitcast.27.rest_1_.other), channel_id=1, source_target_pairs={{0,4},{2,6},{4,8},{6,10},{8,12},{10,14},{1,5},{3,7},{5,9},{7,11},{... | collective-permute-start | bytes 3145736 | tf_op jit(solution)/shard_map/ppermute | solution.py:496
  83.8 39.8 %collective-permute-start.11 = (bf16[7,2,32,1024]{3,2,1,0:T(8,128)(2,1)}, bf16[7,2,32,1024]{3,2,1,0:T(8,128)(2,1)S(1)}, u32[]{:S(2)}, u32[]{:S(2)}) collective-permute-start(bf16[7,2,32,1024]{3,2,1,0:T(8,128)(2,1)} %onward.4.rest_0_), channel_id=1, source_target_pairs={{4,8},{6,10},{8,12},{10,14},{5,9},{7,11},{9,13},{11,15},{20,24},{2... | collective-permute-start | bytes 2752520 | tf_op jit(solution)/shard_map/ppermute | solution.py:496
  92.1 17.6 %collective-permute-start.8 = (bf16[64,256]{1,0:T(8,128)(2,1)}, bf16[64,256]{1,0:T(8,128)(2,1)}, u32[]{:S(2)}, u32[]{:S(2)}) collective-permute-start(bf16[64,256]{1,0:T(8,128)(2,1)} %pad_maximum_fusion), channel_id=1, source_target_pairs={{0,2},{2,0},{4,6},{6,4},{8,10},{10,8},{12,14},{14,12},{1,3},{3,1},... | collective-permute-start | bytes 98312 | tf_op jit(solution)/shard_map/ppermute | solution.py:493
  95.0 47.0 %collective-permute-start.10 = (bf16[7,2,32,1024]{3,2,1,0:T(8,128)(2,1)}, bf16[7,2,32,1024]{3,2,1,0:T(8,128)(2,1)}, u32[]{:S(2)}, u32[]{:S(2)}) collective-permute-start(bf16[7,2,32,1024]{3,2,1,0:T(8,128)(2,1)} %onward.5.rest_1_), channel_id=1, source_target_pairs={{4,8},{6,10},{8,12},{10,14},{5,9},{7,11},{9,13},{11,15},{20,24},{2... | collective-permute-start | bytes 2752520 | tf_op jit(solution)/shard_map/ppermute | solution.py:496
  105.9 60.6 %collective-permute-start.9 = (bf16[7,2,32,1280]{3,2,1,0:T(8,128)(2,1)}, bf16[7,2,32,1280]{3,2,1,0:T(8,128)(2,1)}, u32[]{:S(2)}, u32[]{:S(2)}) collective-permute-start(bf16[7,2,32,1280]{3,2,1,0:T(8,128)(2,1)} %onward.6.rest_2_), channel_id=1, source_target_pairs={{4,8},{6,10},{8,12},{10,14},{5,9},{7,11},{9,13},{11,15},{20,24},{2... | collective-permute-start | bytes 3440648 | tf_op jit(solution)/shard_map/ppermute | solution.py:496
  128.5 13.5 %collective-permute-start.12 = (bf16[4,2,32,1024]{3,2,1,0:T(8,128)(2,1)}, bf16[4,2,32,1024]{3,2,1,0:T(8,128)(2,1)}, u32[]{:S(2)}, u32[]{:S(2)}) collective-permute-start(bf16[4,2,32,1024]{3,2,1,0:T(8,128)(2,1)} %get-tuple-element.19), channel_id=1, source_target_pairs={{0,2},{2,0},{4,6},{6,4},{8,10},{10,8},{12,14},{14,12},{1,3},{3,1},... | collective-permute-start | bytes 1572872 | tf_op jit(solution)/shard_map/ppermute | solution.py:493
  145.9 25.7 %collective-permute-start.13 = (bf16[4,2,32,1024]{3,2,1,0:T(8,128)(2,1)}, bf16[4,2,32,1024]{3,2,1,0:T(8,128)(2,1)}, u32[]{:S(2)}, u32[]{:S(2)}) collective-permute-start(bf16[4,2,32,1024]{3,2,1,0:T(8,128)(2,1)} %get-tuple-element.20), channel_id=1, source_target_pairs={{0,2},{2,0},{4,6},{6,4},{8,10},{10,8},{12,14},{14,12},{1,3},{3,1},... | collective-permute-start | bytes 1572872 | tf_op jit(solution)/shard_map/ppermute | solution.py:493
  146.1 29.8 %collective-permute-start.15 = (bf16[4,2,32,1024]{3,2,1,0:T(8,128)(2,1)}, bf16[4,2,32,1024]{3,2,1,0:T(8,128)(2,1)}, u32[]{:S(2)}, u32[]{:S(2)}) collective-permute-start(bf16[4,2,32,1024]{3,2,1,0:T(8,128)(2,1)} %get-tuple-element.22.refs_1_), channel_id=1, source_target_pairs={{0,1},{1,0},{2,3},{3,2},{4,5},{5,4},{6,7},{7,6},{8,9},{9,8},{10,11... | collective-permute-start | bytes 1572872 | tf_op jit(solution)/shard_map/ppermute | solution.py:499
  151.5 36.4 %collective-permute-start.14 = (bf16[7,2,32,768]{3,2,1,0:T(8,128)(2,1)S(1)}, bf16[7,2,32,768]{3,2,1,0:T(8,128)(2,1)}, u32[]{:S(2)}, u32[]{:S(2)}) collective-permute-start(bf16[7,2,32,768]{3,2,1,0:T(8,128)(2,1)S(1)} %copy-done.4), channel_id=1, source_target_pairs={{4,8},{6,10},{8,12},{10,14},{5,9},{7,11},{9,13},{11,15},{20,24},{2... | collective-permute-start | bytes 2064392 | tf_op jit(solution)/shard_map/ppermute | solution.py:496
  155.6 20.6 %collective-permute-start.16 = (bf16[4,2,32,1024]{3,2,1,0:T(8,128)(2,1)}, bf16[4,2,32,1024]{3,2,1,0:T(8,128)(2,1)}, u32[]{:S(2)}, u32[]{:S(2)}) collective-permute-start(bf16[4,2,32,1024]{3,2,1,0:T(8,128)(2,1)} %get-tuple-element.23.refs_2_), channel_id=1, source_target_pairs={{0,1},{1,0},{2,3},{3,2},{4,5},{5,4},{6,7},{7,6},{8,9},{9,8},{10,11... | collective-permute-start | bytes 1572872 | tf_op jit(solution)/shard_map/ppermute | solution.py:499
  166.6 9.6 %collective-permute-start.17 = (bf16[4,2,32,1024]{3,2,1,0:T(8,128)(2,1)}, bf16[4,2,32,1024]{3,2,1,0:T(8,128)(2,1)}, u32[]{:S(2)}, u32[]{:S(2)}) collective-permute-start(bf16[4,2,32,1024]{3,2,1,0:T(8,128)(2,1)} %collective-permute-done.12.rest_0_.refs_3_), channel_id=1, source_target_pairs={{0,1},{1,0},{2,3},{3,2},{4,5},{5,4},{6,7},{7,6},{8,9},{9,8},{10,11... | collective-permute-start | bytes 1572872 | tf_op jit(solution)/shard_map/ppermute | solution.py:499
  171.6 4.6 %collective-permute-start.18 = (bf16[4,2,32,1024]{3,2,1,0:T(8,128)(2,1)}, bf16[4,2,32,1024]{3,2,1,0:T(8,128)(2,1)}, u32[]{:S(2)}, u32[]{:S(2)}) collective-permute-start(bf16[4,2,32,1024]{3,2,1,0:T(8,128)(2,1)} %collective-permute-done.13.rest_0_.refs_4_), channel_id=1, source_target_pairs={{0,1},{1,0},{2,3},{3,2},{4,5},{5,4},{6,7},{7,6},{8,9},{9,8},{10,11... | collective-permute-start | bytes 1572872 | tf_op jit(solution)/shard_map/ppermute | solution.py:499
  176.0 17.8 %collective-permute-start.19 = (bf16[4,2,32,1280]{3,2,1,0:T(8,128)(2,1)}, bf16[4,2,32,1280]{3,2,1,0:T(8,128)(2,1)}, u32[]{:S(2)}, u32[]{:S(2)}) collective-permute-start(bf16[4,2,32,1280]{3,2,1,0:T(8,128)(2,1)} %get-tuple-element.25), channel_id=1, source_target_pairs={{0,2},{2,0},{4,6},{6,4},{8,10},{10,8},{12,14},{14,12},{1,3},{3,1},... | collective-permute-start | bytes 1966088 | tf_op jit(solution)/shard_map/ppermute | solution.py:493
  191.5 10.1 %collective-permute-start.20 = (bf16[4,2,32,768]{3,2,1,0:T(8,128)(2,1)}, bf16[4,2,32,768]{3,2,1,0:T(8,128)(2,1)S(1)}, u32[]{:S(2)}, u32[]{:S(2)}) collective-permute-start(bf16[4,2,32,768]{3,2,1,0:T(8,128)(2,1)} %get-tuple-element.26), channel_id=1, source_target_pairs={{0,2},{2,0},{4,6},{6,4},{8,10},{10,8},{12,14},{14,12},{1,3},{3,1},... | collective-permute-start | bytes 1179656 | tf_op jit(solution)/shard_map/ppermute | solution.py:493
  192.7 10.5 %collective-permute-start.21 = (bf16[4,2,32,1280]{3,2,1,0:T(8,128)(2,1)S(1)}, bf16[4,2,32,1280]{3,2,1,0:T(8,128)(2,1)S(1)}, u32[]{:S(2)}, u32[]{:S(2)}) collective-permute-start(bf16[4,2,32,1280]{3,2,1,0:T(8,128)(2,1)S(1)} %copy-done.5), channel_id=1, source_target_pairs={{0,1},{1,0},{2,3},{3,2},{4,5},{5,4},{6,7},{7,6},{8,9},{9,8},{10,11... | collective-permute-start | bytes 1966088 | tf_op jit(solution)/shard_map/ppermute | solution.py:499
  193.8 10.3 %collective-permute-start.23 = (bf16[4,2,32,1280]{3,2,1,0:T(8,128)(2,1)}, bf16[4,2,32,1280]{3,2,1,0:T(8,128)(2,1)}, u32[]{:S(2)}, u32[]{:S(2)}) collective-permute-start(bf16[4,2,32,1280]{3,2,1,0:T(8,128)(2,1)} %collective-permute-done.19.refs_3_), channel_id=1, source_target_pairs={{0,1},{1,0},{2,3},{3,2},{4,5},{5,4},{6,7},{7,6},{8,9},{9,8},{10,11... | collective-permute-start | bytes 1966088 | tf_op jit(solution)/shard_map/ppermute | solution.py:499
  193.9 10.3 %collective-permute-start.22 = (bf16[4,2,32,768]{3,2,1,0:T(8,128)(2,1)}, bf16[4,2,32,768]{3,2,1,0:T(8,128)(2,1)S(1)}, u32[]{:S(2)}, u32[]{:S(2)}) collective-permute-start(bf16[4,2,32,768]{3,2,1,0:T(8,128)(2,1)} %get-tuple-element.24.refs_2_), channel_id=1, source_target_pairs={{0,1},{1,0},{2,3},{3,2},{4,5},{5,4},{6,7},{7,6},{8,9},{9,8},{10,11... | collective-permute-start | bytes 1179656 | tf_op jit(solution)/shard_map/ppermute | solution.py:499
  (18 other events, 110.8 us)

commit v9 on v8

--- a/solution.py
+++ b/solution.py
@@ -351,18 +351,16 @@
     )(table, index, mask, *earlier)
 
 
-def beam_kernel(source_count, ranges, later_count, has_earlier, *refs):
+def beam_kernel(source_count, ranges, later_count, has_earlier, place, *refs):
     refs = list(refs)
-    refs.pop(0)
-    sources = [refs.pop(0) for _ in range(source_count)]
-    table, weights = refs.pop(0), refs.pop(0)
-    earlier = refs.pop(0) if has_earlier else None
+    inputs = [refs.pop(0) for _ in range(source_count + 2 + has_earlier)]
     refs = refs[later_count:]
-    out, mixed, spectra, sems, *refs = refs
-    held = refs
+    out, mixed, spectra, sems, *held = refs
+    inputs[source_count] = inputs[source_count].at[pl.ds(place[1], 1)]
+    copies = [pltpu.make_async_copy(ref, to, sems.at[k]) for k, (ref, to) in enumerate(zip(inputs, held))]
+    table, weights = held[source_count : source_count + 2]
     step = pl.program_id(0)
-    frames = sources[0].shape[0]
-    stations = sources[0].shape[2]
+    frames, _, stations, _ = held[0].shape
     tiles = stations // SB
     station_count = stations * (source_count // ranges)
     groups = spectra.shape[0]
@@ -370,10 +368,10 @@
     rows_of = table.shape[2] // 2 // groups
     pair = 2
     lane_tiles = beams // LANES
+    at_once = groups // pl.num_programs(0)
 
     @pl.when(step == 0)
     def _():
-        copies = [pltpu.make_async_copy(ref, to, sems.at[k]) for k, (ref, to) in enumerate(zip(sources, held))]
         for copy in copies:
             copy.start()
         for k in range(0, source_count, ranges):
@@ -393,6 +391,7 @@
                 return carry
 
             lax.fori_loop(0, frames * tiles, radix, 0)
+        copies[source_count].wait()
 
         def transform(b, carry):
             for start in range(0, frames, pair):
@@ -413,16 +412,19 @@
             return carry
 
         lax.fori_loop(0, RADIX, transform, 0, unroll=4)
-
-    for k in range(weights.shape[0]):
-        rows = spectra[step * weights.shape[0] + k].reshape(RADIX * frames * rows_of, 2 * station_count)
-        beam = jnp.dot(rows, weights[k], preferred_element_type=F32)
+        for copy in copies[source_count + 1 :]:
+            copy.wait()
+
+    for k in range(at_once):
+        group = step * at_once + k
+        rows = spectra[group].reshape(RADIX * frames * rows_of, 2 * station_count)
+        beam = jnp.dot(rows, weights[group], preferred_element_type=F32)
         re, im = beam[:, :beams], beam[:, beams:]
         power = re * re + im * im
         if not has_earlier:
             out[k] = power
             continue
-        power = power + earlier[k]
+        power = power + held[-1][group]
         for b in range(RADIX):
             for f in range(frames):
                 at = (b * frames + f) * rows_of
@@ -439,34 +441,28 @@
     at_once = 2
     flat = (groups, channels // groups * frames, beams)
     flat_spec = pl.BlockSpec((at_once,) + flat[1:], lambda i, place: (i, 0, 0))
-    in_specs = [pl.BlockSpec(memory_space=pltpu.HBM) for s in sources]
-    in_specs += [
-        pl.BlockSpec((1,) + table.shape[1:], lambda i, place: (place[1], 0, 0, 0)),
-        pl.BlockSpec((at_once, depth, width), lambda i, place: (i, 0, 0)),
-    ]
-    operands = list(sources) + [table, weights]
-    free = [pl.BlockSpec(memory_space=pl.ANY)] * len(later)
+    operands = list(sources) + [table, weights] + ([] if earlier is None else [earlier])
+    in_specs = [pl.BlockSpec(memory_space=pltpu.HBM)] * len(operands) + [pl.BlockSpec(memory_space=pl.ANY)] * len(later)
     scratch = [
         pltpu.VMEM((RADIX, frames * station_count, 2 * LANES), BF16),
         pltpu.VMEM((groups, RADIX, frames * channels // groups // RADIX, 2 * station_count), BF16),
-        pltpu.SemaphoreType.DMA((len(sources),)),
+        pltpu.SemaphoreType.DMA((len(operands),)),
     ]
-    scratch += [pltpu.VMEM(s.shape, BF16) for s in sources]
+    for k, block in enumerate(operands):
+        scratch.append(pltpu.VMEM(((1,) if k == len(sources) else block.shape[:1]) + block.shape[1:], block.dtype))
     if earlier is None:
         out_shape = jax.ShapeDtypeStruct(flat, F32)
         out_spec = flat_spec
     else:
         out_shape = jax.ShapeDtypeStruct((channels, beams // LANES, frames, LANES), F32)
         out_spec = pl.BlockSpec((channels // groups * at_once,) + out_shape.shape[1:], lambda i, place: (i, 0, 0, 0))
-        operands.append(earlier)
-        in_specs.append(flat_spec)
     return pl.pallas_call(
         functools.partial(beam_kernel, len(sources), ranges, len(later), earlier is not None),
         out_shape=out_shape,
         grid_spec=pltpu.PrefetchScalarGridSpec(
             num_scalar_prefetch=1,
             grid=(groups // at_once,),
-            in_specs=in_specs + free,
+            in_specs=in_specs,
             out_specs=out_spec,
             scratch_shapes=scratch,
         ),
@@ -501,18 +497,16 @@
     def laid(block):
         return jnp.moveaxis(block, 0, -2)
 
+    own, *other = cut(place, voltages, [(pol, 0, half) for pol in range(pols)], [])
     columns = weight_blocks.shape[1] // CORES
     shard = lax.dynamic_slice_in_dim(weight_blocks, core * columns, columns, 1)
     shards = [shard] + [
-        lax.ppermute(shard, "tm", [(i, i ^ far) for i in range(time_devices)]) for far in range(2, time_devices, 2)
+        lax.ppermute(shard, "tm", [(i, i ^ apart) for i in range(time_devices)]) for apart in range(2, time_devices, 2)
     ]
-    own, *other = cut(place, voltages, [(pol, 0, half) for pol in range(pols)], [])
-    own = after(own, *shards[1:])
-    own_back = laid(after(hop(own)))
+    own_back = laid(after(hop(own), *shards[1:]))
+    shards = jnp.concatenate(shards)
     own = laid(own)
     other = [laid(after(pair(block))) for block in other]
-    shards = jnp.concatenate(shards)
-    shards = jnp.concatenate([shards, pair(shards)])
 
     def ordered(rows):
         rows = rows.T.reshape(2, 2, 2, -1)
@@ -523,15 +517,14 @@
     each = weight_blocks.shape[0]
     apart = block_index // each ^ lax.axis_index("tm")
     index = (apart % 2 * (time_devices // 2) + apart // 2) * each + block_index % each
-    weights = beam_weights(shards, ordered(index), ordered(use_mask), other)
     table = jnp.asarray(dft_tables(samples))
     taps = jnp.broadcast_to(filter_taps[:, None, :], (history + 1, 8, samples))
 
-    parts_of = [(samples // 2, samples // 2), (5 * samples // 8, 3 * samples // 8)]
-    chunks = [(pol, sum(sizes[:i]), size) for pol, sizes in enumerate(parts_of) for i, size in enumerate(sizes)]
+    chunks = [(pol, low, samples // 2) for pol in range(pols) for low in (0, samples // 2)]
     other_back = [hop(block) for block in other]
     further = [onward(place, own_back, other_back[pol], pol, low, size) for pol, low, size in chunks]
     far = [hop(block, 2) for block in further]
+    weights = beam_weights(jnp.concatenate([shards, pair(shards)]), ordered(index), ordered(use_mask), [])
     partial = []
     for pol in range(pols):
         gates = further[: 2 * pol + 2] + [weights]
@@ -544,12 +537,12 @@
         return beam_power(place, sources, 2, table, weights, earlier, samples // CORES, later)
 
     for k, (pol, low, size) in enumerate(chunks):
-        gates = {0: [], 1: [*sents[:1], partial[1]], 2: sents[1:2], 3: [power]}[k]
+        gates = {0: [], 1: [*sents[:1], partial[1]], 2: sents[1:2], 3: sents[2:3]}[k]
         keep, send = far_filter(place, taps, partial[pol], far[k], low, size, gates)
         keeps.append(keep)
         sents.append(pair(send))
-        if k == 2:
-            power = power_of(0, None, [keep])
+    power = power_of(0, None, keeps[-1:])
+    sents[-1] = after(sents[-1], power)
     power = power_of(1, power)
     return jnp.moveaxis(power, 1, 2).reshape(power.shape[0], power.shape[2], -1)
 

time: 221 us -> 218 us (0.986)
  waiting for transfers between devices: 66.5 us -> 80.5 us
  starting transfers between devices: 46.4 us -> 35.9 us
  Pallas kernels: 74.8 us -> 69.8 us
    ppermute x3, waiting for transfers between devices: 0.01 us -> 16.7 us  [body(): lax.ppermute(shard, 'tm', [(i, i ^ apart) for i in range(time_devices)])]
    ppermute x7, starting transfers between devices: 26.1 us -> 20.6 us  [hop(): lax.ppermute(block, 'tm', [(i, i + 2) for i in range(skip, time_devices -...]
    pallas_call x2, Pallas kernels: 25.3 us -> 20.5 us  [beam_power(): pl.pallas_call(functools.partial(beam_kernel, len(sources), ranges, len(l...]
    pallas_call x4 -> x3, local copies, waits for them, and re-layouts: 12.8 us -> 8.69 us  [after(): pl.pallas_call(lambda *refs: None, out_shape=jax.ShapeDtypeStruct(block.s...]
    pallas_call x0 -> x1, local copies, waits for them, and re-layouts: none -> 4.09 us  [cut(): pl.pallas_call(functools.partial(cut_kernel, cuts), out_shape=[jax.ShapeD...]
    ppermute x8, starting transfers between devices: 14 us -> 10.1 us  [swap(): return lax.ppermute(block, 'stn', [(0, 1), (1, 0)])]
    ppermute x7, waiting for transfers between devices: 39.9 us -> 37.6 us  [pair(): return lax.ppermute(block, 'tm', [(i, i ^ 1) for i in range(time_devices)])]
    unnamed x38 -> x34, local copies, waits for them, and re-layouts: 9.57 us -> 8.15 us
  transfers between devices with their start and end apart: 25 -> 25, of which waited for: 6 -> 8; matrix products, arithmetic and copies ran while one was open for 11% -> 10% of each run, Pallas kernels for 28% -> 25%
where the time goes in v9:
time: 218 us; the launch traced here: 215 us
  waiting for transfers between devices  80.5 us (37%)
  Pallas kernels  69.8 us (32%)
  starting transfers between devices  35.9 us (16%)
  local copies, waits for them, and re-layouts  24.9 us (11%)
  other arithmetic  4.1 us (2%)
    ppermute x7, waiting for transfers between devices, pair(): return lax.ppermute(block, 'tm', [(i, i ^ 1) for i in range(time_devices)])  37.6 us
    ppermute x7, waiting for transfers between devices, hop(): lax.ppermute(block, 'tm', [(i, i + 2) for i in range(skip, time_devices -...  24.5 us
    ppermute x7, starting transfers between devices, hop(): lax.ppermute(block, 'tm', [(i, i + 2) for i in range(skip, time_devices -...  20.6 us
    pallas_call x2, Pallas kernels, beam_power(): pl.pallas_call(functools.partial(beam_kernel, len(sources), ranges, len(l...  20.5 us
    ppermute x3, waiting for transfers between devices, body(): lax.ppermute(shard, 'tm', [(i, i ^ apart) for i in range(time_devices)])  16.7 us
    pallas_call x4, Pallas kernels, far_filter(): pl.pallas_call(far_kernel, out_shape=(shape, shape), grid_spec=pltpu.Pref...  15.8 us
    pallas_call x2, Pallas kernels, near_filter(): pl.pallas_call(near_kernel, out_shape=jax.ShapeDtypeStruct((2 * frames, p...  15.7 us
    pallas_call x4, Pallas kernels, onward(): pl.pallas_call(onward_kernel, out_shape=jax.ShapeDtypeStruct((depth, part...  10.8 us
  transfers between devices with their start and end apart: 25, of which 8 were waited for; matrix products, arithmetic and copies ran while one was open for 10% of the time, Pallas kernels for 25%

profile of v9, /device:TPU:17, one launch (start us, length us, event | category | flops | bytes accessed | tf_op | source)
XLA Modules:
  0.0 215.5 jit_solution(3466669758712539995)
XLA Ops:
  0.6 4.3 %cut.1 = (bf16[32,2,4,2,2048]{4,3,2,1,0:T(2,128)(2,1)}, bf16[32,4,2,2048]{3,2,1,0:T(2,128)(2,1)}, bf16[32,4,2,2048]{3,2,1,0:T(2,128)(2,1)}) custom-call(s32[2]{0:T(128)} %pad_add_fusion.place, bf16[64,2,4,2,2048]{4,3,2,1,0:T(2,128)(2,1)} %voltages.1), custom_call_target="tpu_custom_call" | custom-call | bytes 13200000 | tf_op jit(solution)/shard_map/cut/pallas_call | solution.py:136
  6.1 3.2 %collective-permute-start.1 = (bf16[32,2,4,2,2048]{4,3,2,1,0:T(2,128)(2,1)}, bf16[32,2,4,2,2048]{4,3,2,1,0:T(2,128)(2,1)S(1)}, u32[]{:S(2)}, u32[]{:S(2)}) collective-permute-start(bf16[32,2,4,2,2048]{4,3,2,1,0:T(2,128)(2,1)} %get-tuple-element.16), channel_id=1, source_target_pairs={{0,4},{2,6},{4,8},{6,10},{8,12},{10,14},{1,5},{3,7},{5,9},{7,11},{... | collective-permute-start | bytes 6291464 | tf_op jit(solution)/shard_map/ppermute | solution.py:492
  9.7 19.5 %collective-permute-done.6.refs_0_ = bf16[32,4,2,2048]{3,2,1,0:T(2,128)(2,1)S(1)} collective-permute-done((bf16[32,4,2,2048]{3,2,1,0:T(2,128)(2,1)}, bf16[32,4,2,2048]{3,2,1,0:T(2,128)(2,1)S(1)}, u32[]{:S(2)}, u32[]{:S(2)}) %collective-permute-start.6) | collective-permute-done | bytes 1048608 | tf_op jit(solution)/shard_map/ppermute | solution.py:489
  31.9 3.2 %collective-permute-start.7 = (bf16[4,2,32,2048]{3,2,1,0:T(8,128)(2,1)S(1)}, bf16[4,2,32,2048]{3,2,1,0:T(8,128)(2,1)}, u32[]{:S(2)}, u32[]{:S(2)}) collective-permute-start(bf16[4,2,32,2048]{3,2,1,0:T(8,128)(2,1)S(1)} %bitcast.36), channel_id=1, source_target_pairs={{0,4},{2,6},{4,8},{6,10},{8,12},{10,14},{1,5},{3,7},{5,9},{7,11},{... | collective-permute-start | bytes 3145736 | tf_op jit(solution)/shard_map/ppermute | solution.py:492
  36.7 15.1 %collective-permute-done.refs_0_ = bf16[32,4,2,2048]{3,2,1,0:T(2,128)(2,1)} collective-permute-done((bf16[32,4,2,2048]{3,2,1,0:T(2,128)(2,1)}, bf16[32,4,2,2048]{3,2,1,0:T(2,128)(2,1)}, u32[]{:S(2)}, u32[]{:S(2)}) %collective-permute-start) | collective-permute-done | bytes 1048608 | tf_op jit(solution)/shard_map/ppermute | solution.py:489
  52.5 4.1 %copy.20 = bf16[32,2,4,2,2048]{4,0,3,2,1:T(8,128)(2,1)} copy(bf16[32,2,4,2,2048]{4,3,2,1,0:T(2,128)(2,1)} %get-tuple-element.16) | data formatting | bytes 4194304 | tf_op jit(solution)/shard_map/cut/pallas_call | solution.py:136
  56.6 2.8 %copy.22 = bf16[32,4,2,2048]{3,0,2,1:T(8,128)(2,1)} copy(bf16[32,4,2,2048]{3,2,1,0:T(2,128)(2,1)} %after.4) | data formatting | bytes 2097152 | tf_op jit(solution)/shard_map/after/pallas_call | solution.py:77
  59.4 16.7 %collective-permute-done.2.refs_1_ = bf16[16,256]{1,0:T(8,128)(2,1)S(1)} collective-permute-done((bf16[16,256]{1,0:T(8,128)(2,1)S(1)}, bf16[16,256]{1,0:T(8,128)(2,1)S(1)}, u32[]{:S(2)}, u32[]{:S(2)}) %collective-permute-start.2) | collective-permute-done | bytes 8224 | tf_op jit(solution)/shard_map/ppermute | solution.py:504
  76.1 4.5 %collective-permute-start.5 = (bf16[4,2,32,2048]{3,2,1,0:T(8,128)(2,1)}, bf16[4,2,32,2048]{3,2,1,0:T(8,128)(2,1)}, u32[]{:S(2)}, u32[]{:S(2)}) collective-permute-start(bf16[4,2,32,2048]{3,2,1,0:T(8,128)(2,1)} %bitcast.27.other), channel_id=1, source_target_pairs={{0,4},{2,6},{4,8},{6,10},{8,12},{10,14},{1,5},{3,7},{5,9},{7,11},{... | collective-permute-start | bytes 3145736 | tf_op jit(solution)/shard_map/ppermute | solution.py:492
  82.5 4.0 %copy.19 = bf16[32,2,4,2,2048]{4,0,3,2,1:T(8,128)(2,1)} copy(bf16[32,2,4,2,2048]{4,3,2,1,0:T(2,128)(2,1)} %after.5) | data formatting | bytes 4194304 | tf_op jit(solution)/shard_map/after/pallas_call | solution.py:77
  108.3 7.9 %near.3.partial = f32[8,2,32,2048]{3,2,1,0:T(8,128)} custom-call(s32[2]{0:T(128)} %pad_add_fusion.place, f32[16,8,2048]{2,1,0:T(8,128)} %broadcast_in_dim.2.taps, bf16[2,4,2,32,2048]{4,3,2,1,0:T(8,128)(2,1)} %bitcast.34, bf16[4,2,32,2048]{3,2,1,0:T(8,128)(2,1)} %bitcast.37, bf16[2,4,2,32,2048]{4,3,2,1,0:T(8,128)(2,1)} %bitcast.30, ...), custom_call_target="tpu_custom_call" | custom-call | bytes 26400000 | tf_op jit(solution)/shard_map/near/pallas_call | solution.py:233
  116.2 5.0 %collective-permute-done.11.far = bf16[7,2,32,1024]{3,2,1,0:T(8,128)(2,1)S(1)} collective-permute-done((bf16[7,2,32,1024]{3,2,1,0:T(8,128)(2,1)}, bf16[7,2,32,1024]{3,2,1,0:T(8,128)(2,1)S(1)}, u32[]{:S(2)}, u32[]{:S(2)}) %collective-permute-start.11) | collective-permute-done | bytes 917536 | tf_op jit(solution)/shard_map/ppermute | solution.py:492
  122.1 3.9 %far.4 = (bf16[4,2,32,1024]{3,2,1,0:T(8,128)(2,1)}, bf16[4,2,32,1024]{3,2,1,0:T(8,128)(2,1)}) custom-call(s32[2]{0:T(128)} %pad_add_fusion.place, f32[16,8,2048]{2,1,0:T(8,128)} %broadcast_in_dim.2.taps, f32[8,2,32,2048]{3,2,1,0:T(8,128)} %near.3.partial, bf16[7,2,32,1024]{3,2,1,0:T(8,128)(2,1)} %copy-done.5), custom_call_target="tpu_custom_call" | custom-call | bytes 3300000 | tf_op jit(solution)/shard_map/far/pallas_call | solution.py:259
  128.9 4.0 %collective-permute-start.9 = (bf16[7,2,32,1024]{3,2,1,0:T(8,128)(2,1)}, bf16[7,2,32,1024]{3,2,1,0:T(8,128)(2,1)}, u32[]{:S(2)}, u32[]{:S(2)}) collective-permute-start(bf16[7,2,32,1024]{3,2,1,0:T(8,128)(2,1)} %onward.6.rest_2_), channel_id=1, source_target_pairs={{4,8},{6,10},{8,12},{10,14},{5,9},{7,11},{9,13},{11,15},{20,24},{2... | collective-permute-start | bytes 2752520 | tf_op jit(solution)/shard_map/ppermute | solution.py:492
  135.6 7.8 %near.2.rest_1_.partial = f32[8,2,32,2048]{3,2,1,0:T(8,128)} custom-call(s32[2]{0:T(128)} %pad_add_fusion.place, f32[16,8,2048]{2,1,0:T(8,128)} %broadcast_in_dim.2.taps, bf16[2,4,2,32,2048]{4,3,2,1,0:T(8,128)(2,1)} %bitcast.35, bf16[4,2,32,2048]{3,2,1,0:T(8,128)(2,1)} %bitcast.27.other, bf16[2,4,2,32,2048]{4,3,2,1,0:T(8,128)(2,1)} %bitcast.33, ...), custom_call_target="tpu_custom_call" | custom-call | bytes 26400000 | tf_op jit(solution)/shard_map/near/pallas_call | solution.py:233
  143.5 4.1 %far.5 = (bf16[4,2,32,1024]{3,2,1,0:T(8,128)(2,1)}, bf16[4,2,32,1024]{3,2,1,0:T(8,128)(2,1)}) custom-call(s32[2]{0:T(128)} %pad_add_fusion.place, f32[16,8,2048]{2,1,0:T(8,128)} %broadcast_in_dim.2.taps, f32[8,2,32,2048]{3,2,1,0:T(8,128)} %near.3.partial, bf16[7,2,32,1024]{3,2,1,0:T(8,128)(2,1)} %collective-permute-done.10.far, ...), custom_call_target="tpu_custom_call" | custom-call | bytes 3300000 | tf_op jit(solution)/shard_map/far/pallas_call | solution.py:259
  150.7 9.8 %collective-permute-done.9.far = bf16[7,2,32,1024]{3,2,1,0:T(8,128)(2,1)} collective-permute-done((bf16[7,2,32,1024]{3,2,1,0:T(8,128)(2,1)}, bf16[7,2,32,1024]{3,2,1,0:T(8,128)(2,1)}, u32[]{:S(2)}, u32[]{:S(2)}) %collective-permute-start.9) | collective-permute-done | bytes 917536 | tf_op jit(solution)/shard_map/ppermute | solution.py:492
  160.5 3.9 %far.6 = (bf16[4,2,32,1024]{3,2,1,0:T(8,128)(2,1)}, bf16[4,2,32,1024]{3,2,1,0:T(8,128)(2,1)}) custom-call(s32[2]{0:T(128)} %pad_add_fusion.place, f32[16,8,2048]{2,1,0:T(8,128)} %broadcast_in_dim.2.taps, f32[8,2,32,2048]{3,2,1,0:T(8,128)} %near.2.rest_1_.partial, bf16[7,2,32,1024]{3,2,1,0:T(8,128)(2,1)} %collective-permute-done.9.far, ...), custom_call_target="tpu_custom_call" | custom-call | bytes 3300000 | tf_op jit(solution)/shard_map/far/pallas_call | solution.py:259
  164.6 5.3 %collective-permute-start.17 = (bf16[4,2,32,1024]{3,2,1,0:T(8,128)(2,1)}, bf16[4,2,32,1024]{3,2,1,0:T(8,128)(2,1)}, u32[]{:S(2)}, u32[]{:S(2)}) collective-permute-start(bf16[4,2,32,1024]{3,2,1,0:T(8,128)(2,1)} %get-tuple-element.25.refs_0_), channel_id=1, source_target_pairs={{0,1},{1,0},{2,3},{3,2},{4,5},{5,4},{6,7},{7,6},{8,9},{9,8},{10,11... | collective-permute-start | bytes 1572872 | tf_op jit(solution)/shard_map/ppermute | solution.py:495
  170.4 9.6 %collective-permute-done.14.far = bf16[7,2,32,1024]{3,2,1,0:T(8,128)(2,1)} collective-permute-done((bf16[7,2,32,1024]{3,2,1,0:T(8,128)(2,1)S(1)}, bf16[7,2,32,1024]{3,2,1,0:T(8,128)(2,1)}, u32[]{:S(2)}, u32[]{:S(2)}) %collective-permute-start.14) | collective-permute-done | bytes 917536 | tf_op jit(solution)/shard_map/ppermute | solution.py:492
  182.8 3.9 %far.7 = (bf16[4,2,32,1024]{3,2,1,0:T(8,128)(2,1)}, bf16[4,2,32,1024]{3,2,1,0:T(8,128)(2,1)}) custom-call(s32[2]{0:T(128)} %pad_add_fusion.place, f32[16,8,2048]{2,1,0:T(8,128)} %broadcast_in_dim.2.taps, f32[8,2,32,2048]{3,2,1,0:T(8,128)} %near.2.rest_1_.partial, bf16[7,2,32,1024]{3,2,1,0:T(8,128)(2,1)} %collective-permute-done.14.far, ...), custom_call_target="tpu_custom_call" | custom-call | bytes 3300000 | tf_op jit(solution)/shard_map/far/pallas_call | solution.py:259
  187.7 9.6 %beams.2.refs_1_.refs_10_ = f32[8,512,256]{2,1,0:T(8,128)} custom-call(s32[2]{0:T(128)} %pad_add_fusion.place, bf16[4,2,32,1024]{3,2,1,0:T(8,128)(2,1)} %get-tuple-element.25.refs_0_, bf16[4,2,32,1024]{3,2,1,0:T(8,128)(2,1)} %get-tuple-element.26.refs_1_, bf16[4,2,32,1024]{3,2,1,0:T(8,128)(2,1)} %collective-permute-done.12.rest_0_.refs_2_, ...), custom_call_target="tpu_custom_call" | custom-call | tf_op jit(solution)/shard_map/beams/pallas_call | solution.py:459
  197.4 3.1 %collective-permute-done.16.refs_0_ = bf16[4,2,32,1024]{3,2,1,0:T(8,128)(2,1)S(1)} collective-permute-done((bf16[4,2,32,1024]{3,2,1,0:T(8,128)(2,1)}, bf16[4,2,32,1024]{3,2,1,0:T(8,128)(2,1)S(1)}, u32[]{:S(2)}, u32[]{:S(2)}) %collective-permute-start.16) | collective-permute-done | bytes 524320 | tf_op jit(solution)/shard_map/ppermute | solution.py:489
  204.6 10.9 %beams.3 = f32[1024,2,4,128]{3,2,1,0:T(4,128)} custom-call(s32[2]{0:T(128)} %pad_add_fusion.place, bf16[4,2,32,1024]{3,2,1,0:T(8,128)(2,1)} %get-tuple-element.21.refs_0_, bf16[4,2,32,1024]{3,2,1,0:T(8,128)(2,1)} %get-tuple-element.23.refs_10_.refs_1_, bf16[4,2,32,1024]{3,2,1,0:T(8,128)(2,1)} %collective-permute-done.15.rest_0_.refs_2_, ...), custom_call_target="tpu_custom_call" | custom-call | tf_op jit(solution)/shard_map/beams/pallas_call | solution.py:459
  (94 shorter events, 49.1 us)
Async XLA Ops:
  4.8 24.3 %collective-permute-start.6 = (bf16[32,4,2,2048]{3,2,1,0:T(2,128)(2,1)}, bf16[32,4,2,2048]{3,2,1,0:T(2,128)(2,1)S(1)}, u32[]{:S(2)}, u32[]{:S(2)}) collective-permute-start(bf16[32,4,2,2048]{3,2,1,0:T(2,128)(2,1)} %get-tuple-element.18), channel_id=1, source_target_pairs={{0,2},{2,0},{4,6},{6,4},{8,10},{10,8},{12,14},{14,12},{1,3},{3,1},... | collective-permute-start | bytes 3145736 | tf_op jit(solution)/shard_map/ppermute | solution.py:489
  6.1 74.4 %collective-permute-start.1 = (bf16[32,2,4,2,2048]{4,3,2,1,0:T(2,128)(2,1)}, bf16[32,2,4,2,2048]{4,3,2,1,0:T(2,128)(2,1)S(1)}, u32[]{:S(2)}, u32[]{:S(2)}) collective-permute-start(bf16[32,2,4,2,2048]{4,3,2,1,0:T(2,128)(2,1)} %get-tuple-element.16), channel_id=1, source_target_pairs={{0,4},{2,6},{4,8},{6,10},{8,12},{10,14},{1,5},{3,7},{5,9},{7,11},{... | collective-permute-start | bytes 6291464 | tf_op jit(solution)/shard_map/ppermute | solution.py:492
  9.4 42.3 %collective-permute-start = (bf16[32,4,2,2048]{3,2,1,0:T(2,128)(2,1)}, bf16[32,4,2,2048]{3,2,1,0:T(2,128)(2,1)}, u32[]{:S(2)}, u32[]{:S(2)}) collective-permute-start(bf16[32,4,2,2048]{3,2,1,0:T(2,128)(2,1)} %get-tuple-element.17), channel_id=1, source_target_pairs={{0,2},{2,0},{4,6},{6,4},{8,10},{10,8},{12,14},{14,12},{1,3},{3,1},... | collective-permute-start | bytes 3145736 | tf_op jit(solution)/shard_map/ppermute | solution.py:489
  31.9 54.6 %collective-permute-start.7 = (bf16[4,2,32,2048]{3,2,1,0:T(8,128)(2,1)S(1)}, bf16[4,2,32,2048]{3,2,1,0:T(8,128)(2,1)}, u32[]{:S(2)}, u32[]{:S(2)}) collective-permute-start(bf16[4,2,32,2048]{3,2,1,0:T(8,128)(2,1)S(1)} %bitcast.36), channel_id=1, source_target_pairs={{0,4},{2,6},{4,8},{6,10},{8,12},{10,14},{1,5},{3,7},{5,9},{7,11},{... | collective-permute-start | bytes 3145736 | tf_op jit(solution)/shard_map/ppermute | solution.py:492
  35.2 40.9 %collective-permute-start.2 = (bf16[16,256]{1,0:T(8,128)(2,1)S(1)}, bf16[16,256]{1,0:T(8,128)(2,1)S(1)}, u32[]{:S(2)}, u32[]{:S(2)}) collective-permute-start(bf16[16,256]{1,0:T(8,128)(2,1)S(1)} %get-tuple-element.28), channel_id=1, source_target_pairs={{0,4},{2,6},{4,0},{6,2},{8,12},{10,14},{12,8},{14,10},{1,5},{3,7},... | collective-permute-start | bytes 24584 | tf_op jit(solution)/shard_map/ppermute | solution.py:504
  35.3 45.3 %collective-permute-start.3 = (bf16[16,256]{1,0:T(8,128)(2,1)S(1)}, bf16[16,256]{1,0:T(8,128)(2,1)S(1)}, u32[]{:S(2)}, u32[]{:S(2)}) collective-permute-start(bf16[16,256]{1,0:T(8,128)(2,1)S(1)} %get-tuple-element.28), channel_id=1, source_target_pairs={{0,8},{2,10},{4,12},{6,14},{8,0},{10,2},{12,4},{14,6},{1,9},{3,11}... | collective-permute-start | bytes 24584 | tf_op jit(solution)/shard_map/ppermute | solution.py:504
  51.7 28.9 %collective-permute-start.4 = (bf16[16,256]{1,0:T(8,128)(2,1)S(1)}, bf16[16,256]{1,0:T(8,128)(2,1)S(1)}, u32[]{:S(2)}, u32[]{:S(2)}) collective-permute-start(bf16[16,256]{1,0:T(8,128)(2,1)S(1)} %get-tuple-element.28), channel_id=1, source_target_pairs={{0,12},{2,14},{4,8},{6,10},{8,4},{10,6},{12,0},{14,2},{1,13},{3,15... | collective-permute-start | bytes 24584 | tf_op jit(solution)/shard_map/ppermute | solution.py:504
  76.1 50.2 %collective-permute-start.5 = (bf16[4,2,32,2048]{3,2,1,0:T(8,128)(2,1)}, bf16[4,2,32,2048]{3,2,1,0:T(8,128)(2,1)}, u32[]{:S(2)}, u32[]{:S(2)}) collective-permute-start(bf16[4,2,32,2048]{3,2,1,0:T(8,128)(2,1)} %bitcast.27.other), channel_id=1, source_target_pairs={{0,4},{2,6},{4,8},{6,10},{8,12},{10,14},{1,5},{3,7},{5,9},{7,11},{... | collective-permute-start | bytes 3145736 | tf_op jit(solution)/shard_map/ppermute | solution.py:492
  89.3 31.9 %collective-permute-start.11 = (bf16[7,2,32,1024]{3,2,1,0:T(8,128)(2,1)}, bf16[7,2,32,1024]{3,2,1,0:T(8,128)(2,1)S(1)}, u32[]{:S(2)}, u32[]{:S(2)}) collective-permute-start(bf16[7,2,32,1024]{3,2,1,0:T(8,128)(2,1)} %onward.4.rest_0_), channel_id=1, source_target_pairs={{4,8},{6,10},{8,12},{10,14},{5,9},{7,11},{9,13},{11,15},{20,24},{2... | collective-permute-start | bytes 2752520 | tf_op jit(solution)/shard_map/ppermute | solution.py:492
  95.3 6.9 %collective-permute-start.8 = (bf16[64,256]{1,0:T(8,128)(2,1)}, bf16[64,256]{1,0:T(8,128)(2,1)}, u32[]{:S(2)}, u32[]{:S(2)}) collective-permute-start(bf16[64,256]{1,0:T(8,128)(2,1)} %pad_maximum_fusion), channel_id=1, source_target_pairs={{0,2},{2,0},{4,6},{6,4},{8,10},{10,8},{12,14},{14,12},{1,3},{3,1},... | collective-permute-start | bytes 98312 | tf_op jit(solution)/shard_map/ppermute | solution.py:489
  98.2 45.3 %collective-permute-start.10 = (bf16[7,2,32,1024]{3,2,1,0:T(8,128)(2,1)}, bf16[7,2,32,1024]{3,2,1,0:T(8,128)(2,1)}, u32[]{:S(2)}, u32[]{:S(2)}) collective-permute-start(bf16[7,2,32,1024]{3,2,1,0:T(8,128)(2,1)} %onward.5.rest_1_), channel_id=1, source_target_pairs={{4,8},{6,10},{8,12},{10,14},{5,9},{7,11},{9,13},{11,15},{20,24},{2... | collective-permute-start | bytes 2752520 | tf_op jit(solution)/shard_map/ppermute | solution.py:492
  126.0 17.5 %collective-permute-start.12 = (bf16[4,2,32,1024]{3,2,1,0:T(8,128)(2,1)}, bf16[4,2,32,1024]{3,2,1,0:T(8,128)(2,1)}, u32[]{:S(2)}, u32[]{:S(2)}) collective-permute-start(bf16[4,2,32,1024]{3,2,1,0:T(8,128)(2,1)} %get-tuple-element.19), channel_id=1, source_target_pairs={{0,2},{2,0},{4,6},{6,4},{8,10},{10,8},{12,14},{14,12},{1,3},{3,1},... | collective-permute-start | bytes 1572872 | tf_op jit(solution)/shard_map/ppermute | solution.py:489
  128.9 31.6 %collective-permute-start.9 = (bf16[7,2,32,1024]{3,2,1,0:T(8,128)(2,1)}, bf16[7,2,32,1024]{3,2,1,0:T(8,128)(2,1)}, u32[]{:S(2)}, u32[]{:S(2)}) collective-permute-start(bf16[7,2,32,1024]{3,2,1,0:T(8,128)(2,1)} %onward.6.rest_2_), channel_id=1, source_target_pairs={{4,8},{6,10},{8,12},{10,14},{5,9},{7,11},{9,13},{11,15},{20,24},{2... | collective-permute-start | bytes 2752520 | tf_op jit(solution)/shard_map/ppermute | solution.py:492
  147.6 12.9 %collective-permute-start.13 = (bf16[4,2,32,1024]{3,2,1,0:T(8,128)(2,1)}, bf16[4,2,32,1024]{3,2,1,0:T(8,128)(2,1)}, u32[]{:S(2)}, u32[]{:S(2)}) collective-permute-start(bf16[4,2,32,1024]{3,2,1,0:T(8,128)(2,1)} %get-tuple-element.20), channel_id=1, source_target_pairs={{0,2},{2,0},{4,6},{6,4},{8,10},{10,8},{12,14},{14,12},{1,3},{3,1},... | collective-permute-start | bytes 1572872 | tf_op jit(solution)/shard_map/ppermute | solution.py:489
  148.8 31.3 %collective-permute-start.14 = (bf16[7,2,32,1024]{3,2,1,0:T(8,128)(2,1)S(1)}, bf16[7,2,32,1024]{3,2,1,0:T(8,128)(2,1)}, u32[]{:S(2)}, u32[]{:S(2)}) collective-permute-start(bf16[7,2,32,1024]{3,2,1,0:T(8,128)(2,1)S(1)} %copy-done.3), channel_id=1, source_target_pairs={{4,8},{6,10},{8,12},{10,14},{5,9},{7,11},{9,13},{11,15},{20,24},{2... | collective-permute-start | bytes 2752520 | tf_op jit(solution)/shard_map/ppermute | solution.py:492
  164.4 18.3 %collective-permute-start.15 = (bf16[4,2,32,1024]{3,2,1,0:T(8,128)(2,1)}, bf16[4,2,32,1024]{3,2,1,0:T(8,128)(2,1)}, u32[]{:S(2)}, u32[]{:S(2)}) collective-permute-start(bf16[4,2,32,1024]{3,2,1,0:T(8,128)(2,1)} %get-tuple-element.22), channel_id=1, source_target_pairs={{0,2},{2,0},{4,6},{6,4},{8,10},{10,8},{12,14},{14,12},{1,3},{3,1},... | collective-permute-start | bytes 1572872 | tf_op jit(solution)/shard_map/ppermute | solution.py:489
  164.6 22.3 %collective-permute-start.17 = (bf16[4,2,32,1024]{3,2,1,0:T(8,128)(2,1)}, bf16[4,2,32,1024]{3,2,1,0:T(8,128)(2,1)}, u32[]{:S(2)}, u32[]{:S(2)}) collective-permute-start(bf16[4,2,32,1024]{3,2,1,0:T(8,128)(2,1)} %get-tuple-element.25.refs_0_), channel_id=1, source_target_pairs={{0,1},{1,0},{2,3},{3,2},{4,5},{5,4},{6,7},{7,6},{8,9},{9,8},{10,11... | collective-permute-start | bytes 1572872 | tf_op jit(solution)/shard_map/ppermute | solution.py:495
  169.9 17.3 %collective-permute-start.18 = (bf16[4,2,32,1024]{3,2,1,0:T(8,128)(2,1)}, bf16[4,2,32,1024]{3,2,1,0:T(8,128)(2,1)}, u32[]{:S(2)}, u32[]{:S(2)}) collective-permute-start(bf16[4,2,32,1024]{3,2,1,0:T(8,128)(2,1)} %get-tuple-element.26.refs_1_), channel_id=1, source_target_pairs={{0,1},{1,0},{2,3},{3,2},{4,5},{5,4},{6,7},{7,6},{8,9},{9,8},{10,11... | collective-permute-start | bytes 1572872 | tf_op jit(solution)/shard_map/ppermute | solution.py:495
  169.9 17.5 %collective-permute-start.19 = (bf16[4,2,32,1024]{3,2,1,0:T(8,128)(2,1)}, bf16[4,2,32,1024]{3,2,1,0:T(8,128)(2,1)}, u32[]{:S(2)}, u32[]{:S(2)}) collective-permute-start(bf16[4,2,32,1024]{3,2,1,0:T(8,128)(2,1)} %collective-permute-done.12.rest_0_.refs_2_), channel_id=1, source_target_pairs={{0,1},{1,0},{2,3},{3,2},{4,5},{5,4},{6,7},{7,6},{8,9},{9,8},{10,11... | collective-permute-start | bytes 1572872 | tf_op jit(solution)/shard_map/ppermute | solution.py:495
  180.1 7.6 %collective-permute-start.20 = (bf16[4,2,32,1024]{3,2,1,0:T(8,128)(2,1)}, bf16[4,2,32,1024]{3,2,1,0:T(8,128)(2,1)}, u32[]{:S(2)}, u32[]{:S(2)}) collective-permute-start(bf16[4,2,32,1024]{3,2,1,0:T(8,128)(2,1)} %collective-permute-done.13.rest_0_.refs_3_), channel_id=1, source_target_pairs={{0,1},{1,0},{2,3},{3,2},{4,5},{5,4},{6,7},{7,6},{8,9},{9,8},{10,11... | collective-permute-start | bytes 1572872 | tf_op jit(solution)/shard_map/ppermute | solution.py:495
  186.7 13.8 %collective-permute-start.16 = (bf16[4,2,32,1024]{3,2,1,0:T(8,128)(2,1)}, bf16[4,2,32,1024]{3,2,1,0:T(8,128)(2,1)S(1)}, u32[]{:S(2)}, u32[]{:S(2)}) collective-permute-start(bf16[4,2,32,1024]{3,2,1,0:T(8,128)(2,1)} %get-tuple-element.24), channel_id=1, source_target_pairs={{0,2},{2,0},{4,6},{6,4},{8,10},{10,8},{12,14},{14,12},{1,3},{3,1},... | collective-permute-start | bytes 1572872 | tf_op jit(solution)/shard_map/ppermute | solution.py:489
  186.9 15.1 %collective-permute-start.21 = (bf16[4,2,32,1024]{3,2,1,0:T(8,128)(2,1)}, bf16[4,2,32,1024]{3,2,1,0:T(8,128)(2,1)}, u32[]{:S(2)}, u32[]{:S(2)}) collective-permute-start(bf16[4,2,32,1024]{3,2,1,0:T(8,128)(2,1)} %get-tuple-element.21.refs_0_), channel_id=1, source_target_pairs={{0,1},{1,0},{2,3},{3,2},{4,5},{5,4},{6,7},{7,6},{8,9},{9,8},{10,11... | collective-permute-start | bytes 1572872 | tf_op jit(solution)/shard_map/ppermute | solution.py:495
  187.2 14.9 %collective-permute-start.22 = (bf16[4,2,32,1024]{3,2,1,0:T(8,128)(2,1)}, bf16[4,2,32,1024]{3,2,1,0:T(8,128)(2,1)}, u32[]{:S(2)}, u32[]{:S(2)}) collective-permute-start(bf16[4,2,32,1024]{3,2,1,0:T(8,128)(2,1)} %get-tuple-element.23.refs_10_.refs_1_), channel_id=1, source_target_pairs={{0,1},{1,0},{2,3},{3,2},{4,5},{5,4},{6,7},{7,6},{8,9},{9,8},{10,11... | collective-permute-start | bytes 1572872 | tf_op jit(solution)/shard_map/ppermute | solution.py:495
  187.4 14.6 %collective-permute-start.23 = (bf16[4,2,32,1024]{3,2,1,0:T(8,128)(2,1)}, bf16[4,2,32,1024]{3,2,1,0:T(8,128)(2,1)}, u32[]{:S(2)}, u32[]{:S(2)}) collective-permute-start(bf16[4,2,32,1024]{3,2,1,0:T(8,128)(2,1)} %collective-permute-done.15.rest_0_.refs_2_), channel_id=1, source_target_pairs={{0,1},{1,0},{2,3},{3,2},{4,5},{5,4},{6,7},{7,6},{8,9},{9,8},{10,11... | collective-permute-start | bytes 1572872 | tf_op jit(solution)/shard_map/ppermute | solution.py:495
  (16 other events, 145.4 us)

commit v10 on v9

--- a/solution.py
+++ b/solution.py
@@ -278,7 +278,8 @@
     )(place, taps, partial, far, *earlier)
 
 
-def onward_kernel(place, own_back, other_back, far):
+def onward_kernel(place, own_back, other_back, *rest):
+    far = rest[-1]
     frames = other_back.shape[0]
     own_back = own_back.at[0]
 
@@ -295,7 +296,7 @@
         run(other_back, own_back)
 
 
-def onward(place, own_back, other_back, pol, low, size):
+def onward(place, own_back, other_back, pol, low, size, earlier):
     frames, parts, stations, _ = other_back.shape
     depth = 2 * frames - 1
 
@@ -309,13 +310,13 @@
         grid_spec=pltpu.PrefetchScalarGridSpec(
             num_scalar_prefetch=1,
             grid=(parts,),
-            in_specs=[spec(frames, pol), spec(frames)],
+            in_specs=[spec(frames, pol), spec(frames)] + [pl.BlockSpec(memory_space=pl.ANY)] * len(earlier),
             out_specs=pl.BlockSpec((depth, 1, stations, size), lambda i, place: (0, i, 0, 0)),
         ),
         compiler_params=pltpu.CompilerParams(vmem_limit_bytes=VMEM_LIMIT),
         cost_estimate=cost(3),
         name="onward",
-    )(place, own_back, other_back)
+    )(place, own_back, other_back, *earlier)
 
 
 def weight_kernel(table, index, mask, *rest):
@@ -503,8 +504,7 @@
     shards = [shard] + [
         lax.ppermute(shard, "tm", [(i, i ^ apart) for i in range(time_devices)]) for apart in range(2, time_devices, 2)
     ]
-    own_back = laid(after(hop(own), *shards[1:]))
-    shards = jnp.concatenate(shards)
+    own_back = laid(after(hop(own)))
     own = laid(own)
     other = [laid(after(pair(block))) for block in other]
 
@@ -520,14 +520,19 @@
     table = jnp.asarray(dft_tables(samples))
     taps = jnp.broadcast_to(filter_taps[:, None, :], (history + 1, 8, samples))
 
-    chunks = [(pol, low, samples // 2) for pol in range(pols) for low in (0, samples // 2)]
+    parts_of = [(samples // 2, samples // 2), (5 * samples // 8, 3 * samples // 8)]
+    chunks = [(pol, sum(sizes[:i]), size) for pol, sizes in enumerate(parts_of) for i, size in enumerate(sizes)]
     other_back = [hop(block) for block in other]
-    further = [onward(place, own_back, other_back[pol], pol, low, size) for pol, low, size in chunks]
+    further = []
+    for pol, low, size in chunks:
+        gates = [] if further else shards[1:]
+        further.append(onward(place, own_back, other_back[pol], pol, low, size, gates))
+    shards = jnp.concatenate(shards)
     far = [hop(block, 2) for block in further]
     weights = beam_weights(jnp.concatenate([shards, pair(shards)]), ordered(index), ordered(use_mask), [])
     partial = []
     for pol in range(pols):
-        gates = further[: 2 * pol + 2] + [weights]
+        gates = further[: 2 * pol + 2] + [weights] + other_back[1:]
         partial.append(near_filter(place, taps, own, other[pol], own_back, other_back[pol], pol, gates))
     keeps, sents, power = [], [], None
 
@@ -537,12 +542,12 @@
         return beam_power(place, sources, 2, table, weights, earlier, samples // CORES, later)
 
     for k, (pol, low, size) in enumerate(chunks):
-        gates = {0: [], 1: [*sents[:1], partial[1]], 2: sents[1:2], 3: sents[2:3]}[k]
+        gates = {0: [], 1: [*sents[:1], partial[1]], 2: sents[1:2], 3: [power]}[k]
         keep, send = far_filter(place, taps, partial[pol], far[k], low, size, gates)
         keeps.append(keep)
         sents.append(pair(send))
-    power = power_of(0, None, keeps[-1:])
-    sents[-1] = after(sents[-1], power)
+        if k == 2:
+            power = power_of(0, None, [keep])
     power = power_of(1, power)
     return jnp.moveaxis(power, 1, 2).reshape(power.shape[0], power.shape[2], -1)
 

time: 218 us -> 210 us (0.963)
  waiting for transfers between devices: 80.5 us -> 73.5 us
  starting transfers between devices: 35.9 us -> 38.9 us
  local copies, waits for them, and re-layouts: 24.9 us -> 22.2 us
    ppermute x3, waiting for transfers between devices: 16.7 us -> 8.42 us  [body(): lax.ppermute(shard, 'tm', [(i, i ^ apart) for i in range(time_devices)])]
    ppermute x7, waiting for transfers between devices: 37.6 us -> 44.9 us  [pair(): return lax.ppermute(block, 'tm', [(i, i ^ 1) for i in range(time_devices)])]
    ppermute x7, waiting for transfers between devices: 24.5 us -> 20.1 us  [hop(): lax.ppermute(block, 'tm', [(i, i + 2) for i in range(skip, time_devices -...]
    ppermute x7, starting transfers between devices: 3.68 us -> 6.66 us  [pair(): return lax.ppermute(block, 'tm', [(i, i ^ 1) for i in range(time_devices)])]
    unnamed x34 -> x40, local copies, waits for them, and re-layouts: 8.15 us -> 6.87 us
  transfers between devices with their start and end apart: 25 -> 25, of which waited for: 8 -> 10; matrix products, arithmetic and copies ran while one was open for 10% -> 10% of each run, Pallas kernels for 25% -> 26%
where the time goes in v10:
time: 210 us; the launch traced here: 209 us
  waiting for transfers between devices  73.5 us (35%)
  Pallas kernels  70 us (33%)
  starting transfers between devices  38.9 us (19%)
  local copies, waits for them, and re-layouts  22.2 us (11%)
  other arithmetic  4.21 us (2%)
    ppermute x7, waiting for transfers between devices, pair(): return lax.ppermute(block, 'tm', [(i, i ^ 1) for i in range(time_devices)])  44.9 us
    pallas_call x2, Pallas kernels, beam_power(): pl.pallas_call(functools.partial(beam_kernel, len(sources), ranges, len(l...  20.5 us
    ppermute x7, waiting for transfers between devices, hop(): lax.ppermute(block, 'tm', [(i, i + 2) for i in range(skip, time_devices -...  20.1 us
    ppermute x7, starting transfers between devices, hop(): lax.ppermute(block, 'tm', [(i, i + 2) for i in range(skip, time_devices -...  19.2 us
    pallas_call x4, Pallas kernels, far_filter(): pl.pallas_call(far_kernel, out_shape=(shape, shape), grid_spec=pltpu.Pref...  15.9 us
    pallas_call x2, Pallas kernels, near_filter(): pl.pallas_call(near_kernel, out_shape=jax.ShapeDtypeStruct((2 * frames, p...  15.8 us
    pallas_call x4, Pallas kernels, onward(): pl.pallas_call(onward_kernel, out_shape=jax.ShapeDtypeStruct((depth, part...  11 us
    ppermute x8, starting transfers between devices, swap(): return lax.ppermute(block, 'stn', [(0, 1), (1, 0)])  10.1 us
  transfers between devices with their start and end apart: 25, of which 10 were waited for; matrix products, arithmetic and copies ran while one was open for 10% of the time, Pallas kernels for 26%

profile of v10, /device:TPU:17, one launch (start us, length us, event | category | flops | bytes accessed | tf_op | source)
XLA Modules:
  0.0 209.0 jit_solution(9647074071292351853)
XLA Ops:
  0.6 4.3 %cut.1 = (bf16[32,2,4,2,2048]{4,3,2,1,0:T(2,128)(2,1)}, bf16[32,4,2,2048]{3,2,1,0:T(2,128)(2,1)}, bf16[32,4,2,2048]{3,2,1,0:T(2,128)(2,1)}) custom-call(s32[2]{0:T(128)} %pad_add_fusion.place, bf16[64,2,4,2,2048]{4,3,2,1,0:T(2,128)(2,1)} %voltages.1), custom_call_target="tpu_custom_call" | custom-call | bytes 13200000 | tf_op jit(solution)/shard_map/cut/pallas_call | solution.py:136
  4.9 3.2 %collective-permute-start.1 = (bf16[32,2,4,2,2048]{4,3,2,1,0:T(2,128)(2,1)}, bf16[32,2,4,2,2048]{4,3,2,1,0:T(2,128)(2,1)S(1)}, u32[]{:S(2)}, u32[]{:S(2)}) collective-permute-start(bf16[32,2,4,2,2048]{4,3,2,1,0:T(2,128)(2,1)} %get-tuple-element.16), channel_id=1, source_target_pairs={{0,4},{2,6},{4,8},{6,10},{8,12},{10,14},{1,5},{3,7},{5,9},{7,11},{... | collective-permute-start | bytes 6291464 | tf_op jit(solution)/shard_map/ppermute | solution.py:493
  9.7 22.4 %collective-permute-done.3.refs_0_ = bf16[32,4,2,2048]{3,2,1,0:T(2,128)(2,1)S(1)} collective-permute-done((bf16[32,4,2,2048]{3,2,1,0:T(2,128)(2,1)}, bf16[32,4,2,2048]{3,2,1,0:T(2,128)(2,1)S(1)}, u32[]{:S(2)}, u32[]{:S(2)}) %collective-permute-start.3) | collective-permute-done | bytes 1048608 | tf_op jit(solution)/shard_map/ppermute | solution.py:490
  39.6 15.0 %collective-permute-done.refs_0_ = bf16[32,4,2,2048]{3,2,1,0:T(2,128)(2,1)} collective-permute-done((bf16[32,4,2,2048]{3,2,1,0:T(2,128)(2,1)}, bf16[32,4,2,2048]{3,2,1,0:T(2,128)(2,1)}, u32[]{:S(2)}, u32[]{:S(2)}) %collective-permute-start) | collective-permute-done | bytes 1048608 | tf_op jit(solution)/shard_map/ppermute | solution.py:490
  54.9 2.9 %copy.21 = bf16[32,4,2,2048]{3,0,2,1:T(8,128)(2,1)} copy(bf16[32,4,2,2048]{3,2,1,0:T(2,128)(2,1)} %after.3) | data formatting | bytes 2097152 | tf_op jit(solution)/shard_map/after/pallas_call | solution.py:77
  57.8 3.1 %collective-permute-start.2 = (bf16[4,2,32,2048]{3,2,1,0:T(8,128)(2,1)}, bf16[4,2,32,2048]{3,2,1,0:T(8,128)(2,1)}, u32[]{:S(2)}, u32[]{:S(2)}) collective-permute-start(bf16[4,2,32,2048]{3,2,1,0:T(8,128)(2,1)} %bitcast.27.other), channel_id=1, source_target_pairs={{0,4},{2,6},{4,8},{6,10},{8,12},{10,14},{1,5},{3,7},{5,9},{7,11},{... | collective-permute-start | bytes 3145736 | tf_op jit(solution)/shard_map/ppermute | solution.py:493
  64.1 4.1 %copy.18 = bf16[32,2,4,2,2048]{4,0,3,2,1:T(8,128)(2,1)} copy(bf16[32,2,4,2,2048]{4,3,2,1,0:T(2,128)(2,1)} %after.4) | data formatting | bytes 4194304 | tf_op jit(solution)/shard_map/after/pallas_call | solution.py:77
  68.2 7.0 %collective-permute-done.5.rest_0_ = bf16[16,256]{1,0:T(8,128)(2,1)S(1)} collective-permute-done((bf16[16,256]{1,0:T(8,128)(2,1)S(1)}, bf16[16,256]{1,0:T(8,128)(2,1)S(1)}, u32[]{:S(2)}, u32[]{:S(2)}) %collective-permute-start.5) | collective-permute-done | bytes 8224 | tf_op jit(solution)/shard_map/ppermute | solution.py:505
  79.9 3.0 %collective-permute-start.11 = (bf16[7,2,32,1024]{3,2,1,0:T(8,128)(2,1)}, bf16[7,2,32,1024]{3,2,1,0:T(8,128)(2,1)S(1)}, u32[]{:S(2)}, u32[]{:S(2)}) collective-permute-start(bf16[7,2,32,1024]{3,2,1,0:T(8,128)(2,1)} %onward.4.rest_0_), channel_id=1, source_target_pairs={{4,8},{6,10},{8,12},{10,14},{5,9},{7,11},{9,13},{11,15},{20,24},{2... | collective-permute-start | bytes 2752520 | tf_op jit(solution)/shard_map/ppermute | solution.py:493
  95.0 4.2 %collective-permute-done.2.other_back.rest_5_.rest_3_ = bf16[4,2,32,2048]{3,2,1,0:T(8,128)(2,1)} collective-permute-done((bf16[4,2,32,2048]{3,2,1,0:T(8,128)(2,1)}, bf16[4,2,32,2048]{3,2,1,0:T(8,128)(2,1)}, u32[]{:S(2)}, u32[]{:S(2)}) %collective-permute-start.2) | collective-permute-done | bytes 1048608 | tf_op jit(solution)/shard_map/ppermute | solution.py:493
  99.3 2.9 %onward.6.rest_2_ = bf16[7,2,32,1280]{3,2,1,0:T(8,128)(2,1)} custom-call(s32[2]{0:T(128)} %pad_add_fusion.place, bf16[2,4,2,32,2048]{4,3,2,1,0:T(8,128)(2,1)} %bitcast.30, bf16[4,2,32,2048]{3,2,1,0:T(8,128)(2,1)} %collective-permute-done.2.other_back.rest_5_.rest_3_), custom_call_target="tpu_custom_call" | custom-call | bytes 9900000 | tf_op jit(solution)/shard_map/onward/pallas_call | solution.py:307
  102.1 3.0 %collective-permute-start.9 = (bf16[7,2,32,1280]{3,2,1,0:T(8,128)(2,1)}, bf16[7,2,32,1280]{3,2,1,0:T(8,128)(2,1)}, u32[]{:S(2)}, u32[]{:S(2)}) collective-permute-start(bf16[7,2,32,1280]{3,2,1,0:T(8,128)(2,1)} %onward.6.rest_2_), channel_id=1, source_target_pairs={{4,8},{6,10},{8,12},{10,14},{5,9},{7,11},{9,13},{11,15},{20,24},{2... | collective-permute-start | bytes 3440648 | tf_op jit(solution)/shard_map/ppermute | solution.py:493
  111.2 7.9 %near.3.partial = f32[8,2,32,2048]{3,2,1,0:T(8,128)} custom-call(s32[2]{0:T(128)} %pad_add_fusion.place, f32[16,8,2048]{2,1,0:T(8,128)} %broadcast_in_dim.2.taps, bf16[2,4,2,32,2048]{4,3,2,1,0:T(8,128)(2,1)} %bitcast.34, bf16[4,2,32,2048]{3,2,1,0:T(8,128)(2,1)} %bitcast.37, bf16[2,4,2,32,2048]{4,3,2,1,0:T(8,128)(2,1)} %bitcast.31, ...), custom_call_target="tpu_custom_call" | custom-call | bytes 26400000 | tf_op jit(solution)/shard_map/near/pallas_call | solution.py:233
  120.1 3.9 %far.4 = (bf16[4,2,32,1024]{3,2,1,0:T(8,128)(2,1)}, bf16[4,2,32,1024]{3,2,1,0:T(8,128)(2,1)}) custom-call(s32[2]{0:T(128)} %pad_add_fusion.place, f32[16,8,2048]{2,1,0:T(8,128)} %broadcast_in_dim.2.taps, f32[8,2,32,2048]{3,2,1,0:T(8,128)} %near.3.partial, bf16[7,2,32,1024]{3,2,1,0:T(8,128)(2,1)} %copy-done.6), custom_call_target="tpu_custom_call" | custom-call | bytes 3300000 | tf_op jit(solution)/shard_map/far/pallas_call | solution.py:259
  127.9 7.8 %near.2.rest_1_.partial = f32[8,2,32,2048]{3,2,1,0:T(8,128)} custom-call(s32[2]{0:T(128)} %pad_add_fusion.place, f32[16,8,2048]{2,1,0:T(8,128)} %broadcast_in_dim.2.taps, bf16[2,4,2,32,2048]{4,3,2,1,0:T(8,128)(2,1)} %bitcast.35, bf16[4,2,32,2048]{3,2,1,0:T(8,128)(2,1)} %bitcast.27.other, bf16[2,4,2,32,2048]{4,3,2,1,0:T(8,128)(2,1)} %bitcast.33, ...), custom_call_target="tpu_custom_call" | custom-call | bytes 26400000 | tf_op jit(solution)/shard_map/near/pallas_call | solution.py:233
  138.6 3.9 %far.5 = (bf16[4,2,32,1024]{3,2,1,0:T(8,128)(2,1)}, bf16[4,2,32,1024]{3,2,1,0:T(8,128)(2,1)}) custom-call(s32[2]{0:T(128)} %pad_add_fusion.place, f32[16,8,2048]{2,1,0:T(8,128)} %broadcast_in_dim.2.taps, f32[8,2,32,2048]{3,2,1,0:T(8,128)} %near.3.partial, bf16[7,2,32,1024]{3,2,1,0:T(8,128)(2,1)} %collective-permute-done.10.far, ...), custom_call_target="tpu_custom_call" | custom-call | bytes 3300000 | tf_op jit(solution)/shard_map/far/pallas_call | solution.py:259
  143.7 3.0 %collective-permute-start.15 = (bf16[4,2,32,1024]{3,2,1,0:T(8,128)(2,1)}, bf16[4,2,32,1024]{3,2,1,0:T(8,128)(2,1)}, u32[]{:S(2)}, u32[]{:S(2)}) collective-permute-start(bf16[4,2,32,1024]{3,2,1,0:T(8,128)(2,1)} %get-tuple-element.22.refs_0_), channel_id=1, source_target_pairs={{0,1},{1,0},{2,3},{3,2},{4,5},{5,4},{6,7},{7,6},{8,9},{9,8},{10,11... | collective-permute-start | bytes 1572872 | tf_op jit(solution)/shard_map/ppermute | solution.py:496
  146.7 3.0 %collective-permute-start.14 = (bf16[7,2,32,768]{3,2,1,0:T(8,128)(2,1)S(1)}, bf16[7,2,32,768]{3,2,1,0:T(8,128)(2,1)}, u32[]{:S(2)}, u32[]{:S(2)}) collective-permute-start(bf16[7,2,32,768]{3,2,1,0:T(8,128)(2,1)S(1)} %copy-done.3), channel_id=1, source_target_pairs={{4,8},{6,10},{8,12},{10,14},{5,9},{7,11},{9,13},{11,15},{20,24},{2... | collective-permute-start | bytes 2064392 | tf_op jit(solution)/shard_map/ppermute | solution.py:493
  150.1 13.1 %collective-permute-done.9.far = bf16[7,2,32,1280]{3,2,1,0:T(8,128)(2,1)} collective-permute-done((bf16[7,2,32,1280]{3,2,1,0:T(8,128)(2,1)}, bf16[7,2,32,1280]{3,2,1,0:T(8,128)(2,1)}, u32[]{:S(2)}, u32[]{:S(2)}) %collective-permute-start.9) | collective-permute-done | bytes 1146912 | tf_op jit(solution)/shard_map/ppermute | solution.py:493
  165.9 4.4 %far.6 = (bf16[4,2,32,1280]{3,2,1,0:T(8,128)(2,1)}, bf16[4,2,32,1280]{3,2,1,0:T(8,128)(2,1)}) custom-call(s32[2]{0:T(128)} %pad_add_fusion.place, f32[16,8,2048]{2,1,0:T(8,128)} %broadcast_in_dim.2.taps, f32[8,2,32,2048]{3,2,1,0:T(8,128)} %near.2.rest_1_.partial, bf16[7,2,32,1280]{3,2,1,0:T(8,128)(2,1)} %collective-permute-done.9.far, ...), custom_call_target="tpu_custom_call" | custom-call | bytes 3300000 | tf_op jit(solution)/shard_map/far/pallas_call | solution.py:259
  171.5 9.6 %beams.2.rest_0_.refs_10_ = f32[8,512,256]{2,1,0:T(8,128)} custom-call(s32[2]{0:T(128)} %pad_add_fusion.place, bf16[4,2,32,1024]{3,2,1,0:T(8,128)(2,1)} %get-tuple-element.22.refs_0_, bf16[4,2,32,1024]{3,2,1,0:T(8,128)(2,1)} %get-tuple-element.23.refs_1_, bf16[4,2,32,1024]{3,2,1,0:T(8,128)(2,1)} %collective-permute-done.12.rest_0_.refs_2_, ...), custom_call_target="tpu_custom_call" | custom-call | tf_op jit(solution)/shard_map/beams/pallas_call | solution.py:460
  181.1 3.7 %far.7 = (bf16[4,2,32,768]{3,2,1,0:T(8,128)(2,1)}, bf16[4,2,32,768]{3,2,1,0:T(8,128)(2,1)}) custom-call(s32[2]{0:T(128)} %pad_add_fusion.place, f32[16,8,2048]{2,1,0:T(8,128)} %broadcast_in_dim.2.taps, f32[8,2,32,2048]{3,2,1,0:T(8,128)} %near.2.rest_1_.partial, bf16[7,2,32,768]{3,2,1,0:T(8,128)(2,1)} %collective-permute-done.14.far, ...), custom_call_target="tpu_custom_call" | custom-call | bytes 3300000 | tf_op jit(solution)/shard_map/far/pallas_call | solution.py:259
  187.7 7.1 %collective-permute-done.20.refs_3_ = bf16[4,2,32,768]{3,2,1,0:T(8,128)(2,1)S(1)} collective-permute-done((bf16[4,2,32,768]{3,2,1,0:T(8,128)(2,1)}, bf16[4,2,32,768]{3,2,1,0:T(8,128)(2,1)S(1)}, u32[]{:S(2)}, u32[]{:S(2)}) %collective-permute-start.20) | collective-permute-done | bytes 393248 | tf_op jit(solution)/shard_map/ppermute | solution.py:490
  198.1 10.9 %beams.3 = f32[1024,2,4,128]{3,2,1,0:T(4,128)} custom-call(s32[2]{0:T(128)} %pad_add_fusion.place, bf16[4,2,32,1280]{3,2,1,0:T(8,128)(2,1)} %get-tuple-element.21.refs_10_.refs_0_, bf16[4,2,32,768]{3,2,1,0:T(8,128)(2,1)} %get-tuple-element.24.refs_1_, bf16[4,2,32,1280]{3,2,1,0:T(8,128)(2,1)} %collective-permute-done.19.refs_2_, ...), custom_call_target="tpu_custom_call" | custom-call | tf_op jit(solution)/shard_map/beams/pallas_call | solution.py:460
  (99 shorter events, 55.3 us)
Async XLA Ops:
  4.9 52.9 %collective-permute-start.1 = (bf16[32,2,4,2,2048]{4,3,2,1,0:T(2,128)(2,1)}, bf16[32,2,4,2,2048]{4,3,2,1,0:T(2,128)(2,1)S(1)}, u32[]{:S(2)}, u32[]{:S(2)}) collective-permute-start(bf16[32,2,4,2,2048]{4,3,2,1,0:T(2,128)(2,1)} %get-tuple-element.16), channel_id=1, source_target_pairs={{0,4},{2,6},{4,8},{6,10},{8,12},{10,14},{1,5},{3,7},{5,9},{7,11},{... | collective-permute-start | bytes 6291464 | tf_op jit(solution)/shard_map/ppermute | solution.py:493
  8.1 24.0 %collective-permute-start.3 = (bf16[32,4,2,2048]{3,2,1,0:T(2,128)(2,1)}, bf16[32,4,2,2048]{3,2,1,0:T(2,128)(2,1)S(1)}, u32[]{:S(2)}, u32[]{:S(2)}) collective-permute-start(bf16[32,4,2,2048]{3,2,1,0:T(2,128)(2,1)} %get-tuple-element.18), channel_id=1, source_target_pairs={{0,2},{2,0},{4,6},{6,4},{8,10},{10,8},{12,14},{14,12},{1,3},{3,1},... | collective-permute-start | bytes 3145736 | tf_op jit(solution)/shard_map/ppermute | solution.py:490
  9.4 45.2 %collective-permute-start = (bf16[32,4,2,2048]{3,2,1,0:T(2,128)(2,1)}, bf16[32,4,2,2048]{3,2,1,0:T(2,128)(2,1)}, u32[]{:S(2)}, u32[]{:S(2)}) collective-permute-start(bf16[32,4,2,2048]{3,2,1,0:T(2,128)(2,1)} %get-tuple-element.17), channel_id=1, source_target_pairs={{0,2},{2,0},{4,6},{6,4},{8,10},{10,8},{12,14},{14,12},{1,3},{3,1},... | collective-permute-start | bytes 3145736 | tf_op jit(solution)/shard_map/ppermute | solution.py:490
  34.9 41.7 %collective-permute-start.4 = (bf16[4,2,32,2048]{3,2,1,0:T(8,128)(2,1)S(1)}, bf16[4,2,32,2048]{3,2,1,0:T(8,128)(2,1)}, u32[]{:S(2)}, u32[]{:S(2)}) collective-permute-start(bf16[4,2,32,2048]{3,2,1,0:T(8,128)(2,1)S(1)} %bitcast.36), channel_id=1, source_target_pairs={{0,4},{2,6},{4,8},{6,10},{8,12},{10,14},{1,5},{3,7},{5,9},{7,11},{... | collective-permute-start | bytes 3145736 | tf_op jit(solution)/shard_map/ppermute | solution.py:493
  36.9 38.3 %collective-permute-start.5 = (bf16[16,256]{1,0:T(8,128)(2,1)S(1)}, bf16[16,256]{1,0:T(8,128)(2,1)S(1)}, u32[]{:S(2)}, u32[]{:S(2)}) collective-permute-start(bf16[16,256]{1,0:T(8,128)(2,1)S(1)} %get-tuple-element.28), channel_id=1, source_target_pairs={{0,4},{2,6},{4,0},{6,2},{8,12},{10,14},{12,8},{14,10},{1,5},{3,7},... | collective-permute-start | bytes 24584 | tf_op jit(solution)/shard_map/ppermute | solution.py:505
  36.9 39.0 %collective-permute-start.6 = (bf16[16,256]{1,0:T(8,128)(2,1)S(1)}, bf16[16,256]{1,0:T(8,128)(2,1)S(1)}, u32[]{:S(2)}, u32[]{:S(2)}) collective-permute-start(bf16[16,256]{1,0:T(8,128)(2,1)S(1)} %get-tuple-element.28), channel_id=1, source_target_pairs={{0,8},{2,10},{4,12},{6,14},{8,0},{10,2},{12,4},{14,6},{1,9},{3,11}... | collective-permute-start | bytes 24584 | tf_op jit(solution)/shard_map/ppermute | solution.py:505
  54.7 21.9 %collective-permute-start.7 = (bf16[16,256]{1,0:T(8,128)(2,1)S(1)}, bf16[16,256]{1,0:T(8,128)(2,1)S(1)}, u32[]{:S(2)}, u32[]{:S(2)}) collective-permute-start(bf16[16,256]{1,0:T(8,128)(2,1)S(1)} %get-tuple-element.28), channel_id=1, source_target_pairs={{0,12},{2,14},{4,8},{6,10},{8,4},{10,6},{12,0},{14,2},{1,13},{3,15... | collective-permute-start | bytes 24584 | tf_op jit(solution)/shard_map/ppermute | solution.py:505
  57.8 41.4 %collective-permute-start.2 = (bf16[4,2,32,2048]{3,2,1,0:T(8,128)(2,1)}, bf16[4,2,32,2048]{3,2,1,0:T(8,128)(2,1)}, u32[]{:S(2)}, u32[]{:S(2)}) collective-permute-start(bf16[4,2,32,2048]{3,2,1,0:T(8,128)(2,1)} %bitcast.27.other), channel_id=1, source_target_pairs={{0,4},{2,6},{4,8},{6,10},{8,12},{10,14},{1,5},{3,7},{5,9},{7,11},{... | collective-permute-start | bytes 3145736 | tf_op jit(solution)/shard_map/ppermute | solution.py:493
  79.9 39.3 %collective-permute-start.11 = (bf16[7,2,32,1024]{3,2,1,0:T(8,128)(2,1)}, bf16[7,2,32,1024]{3,2,1,0:T(8,128)(2,1)S(1)}, u32[]{:S(2)}, u32[]{:S(2)}) collective-permute-start(bf16[7,2,32,1024]{3,2,1,0:T(8,128)(2,1)} %onward.4.rest_0_), channel_id=1, source_target_pairs={{4,8},{6,10},{8,12},{10,14},{5,9},{7,11},{9,13},{11,15},{20,24},{2... | collective-permute-start | bytes 2752520 | tf_op jit(solution)/shard_map/ppermute | solution.py:493
  87.1 18.1 %collective-permute-start.8 = (bf16[64,256]{1,0:T(8,128)(2,1)}, bf16[64,256]{1,0:T(8,128)(2,1)}, u32[]{:S(2)}, u32[]{:S(2)}) collective-permute-start(bf16[64,256]{1,0:T(8,128)(2,1)} %pad_maximum_fusion), channel_id=1, source_target_pairs={{0,2},{2,0},{4,6},{6,4},{8,10},{10,8},{12,14},{14,12},{1,3},{3,1},... | collective-permute-start | bytes 98312 | tf_op jit(solution)/shard_map/ppermute | solution.py:490
  91.0 47.6 %collective-permute-start.10 = (bf16[7,2,32,1024]{3,2,1,0:T(8,128)(2,1)}, bf16[7,2,32,1024]{3,2,1,0:T(8,128)(2,1)}, u32[]{:S(2)}, u32[]{:S(2)}) collective-permute-start(bf16[7,2,32,1024]{3,2,1,0:T(8,128)(2,1)} %onward.5.rest_1_), channel_id=1, source_target_pairs={{4,8},{6,10},{8,12},{10,14},{5,9},{7,11},{9,13},{11,15},{20,24},{2... | collective-permute-start | bytes 2752520 | tf_op jit(solution)/shard_map/ppermute | solution.py:493
  102.1 61.0 %collective-permute-start.9 = (bf16[7,2,32,1280]{3,2,1,0:T(8,128)(2,1)}, bf16[7,2,32,1280]{3,2,1,0:T(8,128)(2,1)}, u32[]{:S(2)}, u32[]{:S(2)}) collective-permute-start(bf16[7,2,32,1280]{3,2,1,0:T(8,128)(2,1)} %onward.6.rest_2_), channel_id=1, source_target_pairs={{4,8},{6,10},{8,12},{10,14},{5,9},{7,11},{9,13},{11,15},{20,24},{2... | collective-permute-start | bytes 3440648 | tf_op jit(solution)/shard_map/ppermute | solution.py:493
  124.0 14.6 %collective-permute-start.12 = (bf16[4,2,32,1024]{3,2,1,0:T(8,128)(2,1)}, bf16[4,2,32,1024]{3,2,1,0:T(8,128)(2,1)}, u32[]{:S(2)}, u32[]{:S(2)}) collective-permute-start(bf16[4,2,32,1024]{3,2,1,0:T(8,128)(2,1)} %get-tuple-element.19), channel_id=1, source_target_pairs={{0,2},{2,0},{4,6},{6,4},{8,10},{10,8},{12,14},{14,12},{1,3},{3,1},... | collective-permute-start | bytes 1572872 | tf_op jit(solution)/shard_map/ppermute | solution.py:490
  142.5 23.4 %collective-permute-start.13 = (bf16[4,2,32,1024]{3,2,1,0:T(8,128)(2,1)}, bf16[4,2,32,1024]{3,2,1,0:T(8,128)(2,1)}, u32[]{:S(2)}, u32[]{:S(2)}) collective-permute-start(bf16[4,2,32,1024]{3,2,1,0:T(8,128)(2,1)} %get-tuple-element.20), channel_id=1, source_target_pairs={{0,2},{2,0},{4,6},{6,4},{8,10},{10,8},{12,14},{14,12},{1,3},{3,1},... | collective-permute-start | bytes 1572872 | tf_op jit(solution)/shard_map/ppermute | solution.py:490
  143.7 26.5 %collective-permute-start.15 = (bf16[4,2,32,1024]{3,2,1,0:T(8,128)(2,1)}, bf16[4,2,32,1024]{3,2,1,0:T(8,128)(2,1)}, u32[]{:S(2)}, u32[]{:S(2)}) collective-permute-start(bf16[4,2,32,1024]{3,2,1,0:T(8,128)(2,1)} %get-tuple-element.22.refs_0_), channel_id=1, source_target_pairs={{0,1},{1,0},{2,3},{3,2},{4,5},{5,4},{6,7},{7,6},{8,9},{9,8},{10,11... | collective-permute-start | bytes 1572872 | tf_op jit(solution)/shard_map/ppermute | solution.py:496
  146.7 34.4 %collective-permute-start.14 = (bf16[7,2,32,768]{3,2,1,0:T(8,128)(2,1)S(1)}, bf16[7,2,32,768]{3,2,1,0:T(8,128)(2,1)}, u32[]{:S(2)}, u32[]{:S(2)}) collective-permute-start(bf16[7,2,32,768]{3,2,1,0:T(8,128)(2,1)S(1)} %copy-done.3), channel_id=1, source_target_pairs={{4,8},{6,10},{8,12},{10,14},{5,9},{7,11},{9,13},{11,15},{20,24},{2... | collective-permute-start | bytes 2064392 | tf_op jit(solution)/shard_map/ppermute | solution.py:493
  149.7 21.7 %collective-permute-start.16 = (bf16[4,2,32,1024]{3,2,1,0:T(8,128)(2,1)}, bf16[4,2,32,1024]{3,2,1,0:T(8,128)(2,1)}, u32[]{:S(2)}, u32[]{:S(2)}) collective-permute-start(bf16[4,2,32,1024]{3,2,1,0:T(8,128)(2,1)} %get-tuple-element.23.refs_1_), channel_id=1, source_target_pairs={{0,1},{1,0},{2,3},{3,2},{4,5},{5,4},{6,7},{7,6},{8,9},{9,8},{10,11... | collective-permute-start | bytes 1572872 | tf_op jit(solution)/shard_map/ppermute | solution.py:496
  163.2 8.3 %collective-permute-start.17 = (bf16[4,2,32,1024]{3,2,1,0:T(8,128)(2,1)}, bf16[4,2,32,1024]{3,2,1,0:T(8,128)(2,1)}, u32[]{:S(2)}, u32[]{:S(2)}) collective-permute-start(bf16[4,2,32,1024]{3,2,1,0:T(8,128)(2,1)} %collective-permute-done.12.rest_0_.refs_2_), channel_id=1, source_target_pairs={{0,1},{1,0},{2,3},{3,2},{4,5},{5,4},{6,7},{7,6},{8,9},{9,8},{10,11... | collective-permute-start | bytes 1572872 | tf_op jit(solution)/shard_map/ppermute | solution.py:496
  165.9 5.6 %collective-permute-start.18 = (bf16[4,2,32,1024]{3,2,1,0:T(8,128)(2,1)}, bf16[4,2,32,1024]{3,2,1,0:T(8,128)(2,1)}, u32[]{:S(2)}, u32[]{:S(2)}) collective-permute-start(bf16[4,2,32,1024]{3,2,1,0:T(8,128)(2,1)} %collective-permute-done.13.rest_0_.refs_3_), channel_id=1, source_target_pairs={{0,1},{1,0},{2,3},{3,2},{4,5},{5,4},{6,7},{7,6},{8,9},{9,8},{10,11... | collective-permute-start | bytes 1572872 | tf_op jit(solution)/shard_map/ppermute | solution.py:496
  170.2 16.1 %collective-permute-start.19 = (bf16[4,2,32,1280]{3,2,1,0:T(8,128)(2,1)}, bf16[4,2,32,1280]{3,2,1,0:T(8,128)(2,1)}, u32[]{:S(2)}, u32[]{:S(2)}) collective-permute-start(bf16[4,2,32,1280]{3,2,1,0:T(8,128)(2,1)} %get-tuple-element.25), channel_id=1, source_target_pairs={{0,2},{2,0},{4,6},{6,4},{8,10},{10,8},{12,14},{14,12},{1,3},{3,1},... | collective-permute-start | bytes 1966088 | tf_op jit(solution)/shard_map/ppermute | solution.py:490
  184.8 10.1 %collective-permute-start.20 = (bf16[4,2,32,768]{3,2,1,0:T(8,128)(2,1)}, bf16[4,2,32,768]{3,2,1,0:T(8,128)(2,1)S(1)}, u32[]{:S(2)}, u32[]{:S(2)}) collective-permute-start(bf16[4,2,32,768]{3,2,1,0:T(8,128)(2,1)} %get-tuple-element.26), channel_id=1, source_target_pairs={{0,2},{2,0},{4,6},{6,4},{8,10},{10,8},{12,14},{14,12},{1,3},{3,1},... | collective-permute-start | bytes 1179656 | tf_op jit(solution)/shard_map/ppermute | solution.py:490
  185.0 11.5 %collective-permute-start.21 = (bf16[4,2,32,1280]{3,2,1,0:T(8,128)(2,1)S(1)}, bf16[4,2,32,1280]{3,2,1,0:T(8,128)(2,1)S(1)}, u32[]{:S(2)}, u32[]{:S(2)}) collective-permute-start(bf16[4,2,32,1280]{3,2,1,0:T(8,128)(2,1)S(1)} %copy-done.4), channel_id=1, source_target_pairs={{0,1},{1,0},{2,3},{3,2},{4,5},{5,4},{6,7},{7,6},{8,9},{9,8},{10,11... | collective-permute-start | bytes 1966088 | tf_op jit(solution)/shard_map/ppermute | solution.py:496
  186.4 11.0 %collective-permute-start.23 = (bf16[4,2,32,1280]{3,2,1,0:T(8,128)(2,1)}, bf16[4,2,32,1280]{3,2,1,0:T(8,128)(2,1)}, u32[]{:S(2)}, u32[]{:S(2)}) collective-permute-start(bf16[4,2,32,1280]{3,2,1,0:T(8,128)(2,1)} %collective-permute-done.19.refs_2_), channel_id=1, source_target_pairs={{0,1},{1,0},{2,3},{3,2},{4,5},{5,4},{6,7},{7,6},{8,9},{9,8},{10,11... | collective-permute-start | bytes 1966088 | tf_op jit(solution)/shard_map/ppermute | solution.py:496
  187.7 9.7 %collective-permute-start.22 = (bf16[4,2,32,768]{3,2,1,0:T(8,128)(2,1)}, bf16[4,2,32,768]{3,2,1,0:T(8,128)(2,1)S(1)}, u32[]{:S(2)}, u32[]{:S(2)}) collective-permute-start(bf16[4,2,32,768]{3,2,1,0:T(8,128)(2,1)} %get-tuple-element.24.refs_1_), channel_id=1, source_target_pairs={{0,1},{1,0},{2,3},{3,2},{4,5},{5,4},{6,7},{7,6},{8,9},{9,8},{10,11... | collective-permute-start | bytes 1179656 | tf_op jit(solution)/shard_map/ppermute | solution.py:496
  (19 other events, 172.3 us)

commit v11 on v10

--- a/solution.py
+++ b/solution.py
@@ -85,68 +85,56 @@
     )(block, *earlier)
 
 
-def cut_kernel(cuts, place, voltages, *rest):
-    (own, *outs), (buffer, loads, stores) = rest[-4 - len(cuts) : -3], rest[-3:]
-    half = own.shape[0]
-    pieces = loads.shape[1]
+def cut_kernel(mine, voltages, *rest):
+    count = len(mine)
+    outs, (buffer, loads, stores) = rest[-3 - count : -3], rest[-3:]
+    half = buffer.shape[0]
+    pieces = loads.shape[0]
     size = half // pieces
-    side = place[0]
-
-    def load(h, k):
-        start = jnp.where(side == h, 0, half) + k * size
+    side = lax.rem(lax.axis_index("tm"), 2)
+    start = half * (side if mine[0] is None else 1 - side)
+
+    def load(k):
         return pltpu.make_async_copy(
-            voltages.at[pl.ds(start, size)], buffer.at[h, pl.ds(k * size, size)], loads.at[h, k]
+            voltages.at[pl.ds(start + k * size, size)], buffer.at[pl.ds(k * size, size)], loads.at[k]
         )
 
-    def store(h, k):
-        copies = []
-        if h == 0:
-            copies.append(pltpu.make_async_copy(buffer.at[0, pl.ds(k * size, size)], own.at[pl.ds(k * size, size)], stores.at[0, k]))
-        else:
-            for pol in range(voltages.shape[1]):
-                for out, (which, low, count) in zip(outs, cuts):
-                    if which == pol and low <= k * size < low + count:
-                        copies.append(
-                            pltpu.make_async_copy(
-                                buffer.at[1, pl.ds(k * size, size), pol],
-                                out.at[pl.ds(k * size - low, size)],
-                                stores.at[1 + pol, k],
-                            )
-                        )
-        return copies
-
-    order = [(h, k) for h in range(2) for k in range(pieces)]
-    for h, k in order:
-        load(h, k).start()
-    for h, k in order:
-        load(h, k).wait()
-        for copy in store(h, k):
-            copy.start()
-    for h, k in order:
-        for copy in store(h, k):
-            copy.wait()
-
-
-def cut(place, voltages, cuts, earlier):
+    def store(k, i):
+        block = buffer.at[pl.ds(k * size, size)]
+        block = block if mine[i] is None else block.at[:, mine[i]]
+        return pltpu.make_async_copy(block, outs[i].at[pl.ds(k * size, size)], stores.at[i, k])
+
+    for k in range(pieces):
+        load(k).start()
+    for k in range(pieces):
+        load(k).wait()
+        for i in range(count):
+            store(k, i).start()
+    for k in range(pieces):
+        for i in range(count):
+            store(k, i).wait()
+
+
+def cut(voltages, mine, earlier):
     stations, pols, frames, parts, samples = voltages.shape
-    half = stations // 2
+    whole = (stations // 2, pols, frames, parts, samples)
+    shapes = [whole if pol is None else whole[:1] + whole[2:] for pol in mine]
     pieces = 4
-    shapes = [(half, pols, frames, parts, samples)] + [(size, frames, parts, samples) for _, _, size in cuts]
-    anywhere = pl.BlockSpec(memory_space=pltpu.HBM)
-    return pl.pallas_call(
-        functools.partial(cut_kernel, cuts),
+    there = pl.BlockSpec(memory_space=pltpu.HBM)
+    return pl.pallas_call(
+        functools.partial(cut_kernel, mine),
         out_shape=[jax.ShapeDtypeStruct(shape, BF16) for shape in shapes],
-        in_specs=[pl.BlockSpec(memory_space=pltpu.SMEM), anywhere] + [pl.BlockSpec(memory_space=pl.ANY)] * len(earlier),
-        out_specs=[anywhere] * len(shapes),
+        in_specs=[there] + [pl.BlockSpec(memory_space=pl.ANY)] * len(earlier),
+        out_specs=[there] * len(shapes),
         scratch_shapes=[
-            pltpu.VMEM((2,) + shapes[0], BF16),
-            pltpu.SemaphoreType.DMA((2, pieces)),
-            pltpu.SemaphoreType.DMA((1 + pols, pieces)),
+            pltpu.VMEM(whole, BF16),
+            pltpu.SemaphoreType.DMA((pieces,)),
+            pltpu.SemaphoreType.DMA((len(mine), pieces)),
         ],
         compiler_params=pltpu.CompilerParams(vmem_limit_bytes=VMEM_LIMIT),
-        cost_estimate=cost(4),
+        cost_estimate=cost(2),
         name="cut",
-    )(place, voltages, *earlier)
+    )(voltages, *earlier)
 
 
 def weighted(taps, window, count, lanes, part, rows, sums):
@@ -354,66 +342,94 @@
 
 def beam_kernel(source_count, ranges, later_count, has_earlier, place, *refs):
     refs = list(refs)
-    inputs = [refs.pop(0) for _ in range(source_count + 2 + has_earlier)]
+    sources = [refs.pop(0) for _ in range(source_count)]
+    others = [refs.pop(0) for _ in range(2 + has_earlier)]
+    others[0] = others[0].at[pl.ds(place[1], 1)]
     refs = refs[later_count:]
-    out, mixed, spectra, sems, *held = refs
-    inputs[source_count] = inputs[source_count].at[pl.ds(place[1], 1)]
-    copies = [pltpu.make_async_copy(ref, to, sems.at[k]) for k, (ref, to) in enumerate(zip(inputs, held))]
-    table, weights = held[source_count : source_count + 2]
+    out, spectra, source_sems, other_sems = refs[:4]
+    mixed, held, kept = refs[4:6], refs[6 : 6 + ranges], refs[6 + ranges :]
+    table, weights = kept[:2]
     step = pl.program_id(0)
-    frames, _, stations, _ = held[0].shape
+    members, frames, _, stations, _ = held[0].shape
     tiles = stations // SB
-    station_count = stations * (source_count // ranges)
+    station_count = stations * members
     groups = spectra.shape[0]
     beams = weights.shape[2] // 2
     rows_of = table.shape[2] // 2 // groups
-    pair = 2
+    pair = frames // 2
     lane_tiles = beams // LANES
     at_once = groups // pl.num_programs(0)
 
+    def arrival(p, k):
+        frames_of = pl.ds(p * pair, pair)
+        return pltpu.make_async_copy(
+            sources[k].at[frames_of], held[k % ranges].at[k // ranges, frames_of], source_sems.at[p, k]
+        )
+
+    other_copies = [pltpu.make_async_copy(ref, to, other_sems.at[k]) for k, (ref, to) in enumerate(zip(others, kept))]
+    pieces = []
+    for ref in held:
+        pieces += [(ref, slice(n, n + LANES)) for n in range(0, ref.shape[4], LANES)]
+
+    def radix(p, member, i):
+        f, tile = i // tiles, i % tiles
+        rows = pl.ds(pl.multiple_of(tile * SB, SB), SB)
+        values = [
+            tuple(ref[member, p * pair + f, part, rows, lanes].astype(F32) for part in range(2)) for ref, lanes in pieces
+        ]
+        target = pl.ds(pl.multiple_of(f * station_count + member * stations + tile * SB, SB), SB)
+        for b, (re, im) in enumerate(sixteen_points(values)):
+            mixed[p][b, target, :LANES] = re.astype(BF16)
+            mixed[p][b, target, LANES:] = im.astype(BF16)
+
+    def transform(p, b):
+        product = lax.dot_general(table[0, b], mixed[p][b], (((1,), (1,)), ((), ())), preferred_element_type=F32)
+        product = product.reshape(2, groups, rows_of, pair * station_count)
+        rows = slice(p * pair * rows_of, (p + 1) * pair * rows_of)
+        for part in range(2):
+            value = jnp.concatenate(
+                [product[part, :, :, f * station_count : (f + 1) * station_count] for f in range(pair)], axis=1
+            )
+            columns = slice(part * station_count, (part + 1) * station_count)
+            spectra[:, b, rows, columns] = value.astype(BF16)
+
+    def loop(count, body, unroll):
+        def step(i, carry):
+            body(i)
+            return carry
+
+        lax.fori_loop(0, count, step, 0, unroll=unroll)
+
     @pl.when(step == 0)
     def _():
-        for copy in copies:
+        for k in range(source_count):
+            arrival(0, k).start()
+        other_copies[0].start()
+        for k in range(source_count):
+            arrival(1, k).start()
+        for copy in other_copies[1:]:
             copy.start()
-        for k in range(0, source_count, ranges):
-            for copy in copies[k : k + ranges]:
-                copy.wait()
-            pieces = []
-            for ref in held[k : k + ranges]:
-                pieces += [(ref, slice(n, n + LANES)) for n in range(0, ref.shape[3], LANES)]
-
-            def radix(i, carry, pieces=pieces, low=k // ranges * stations):
-                f, rows = i // tiles, pl.ds(pl.multiple_of(i % tiles * SB, SB), SB)
-                values = [tuple(ref[f, part, rows, lanes].astype(F32) for part in range(2)) for ref, lanes in pieces]
-                target = pl.ds(pl.multiple_of(f * station_count + low + i % tiles * SB, SB), SB)
-                for b, (re, im) in enumerate(sixteen_points(values)):
-                    mixed[b, target, :LANES] = re.astype(BF16)
-                    mixed[b, target, LANES:] = im.astype(BF16)
-                return carry
-
-            lax.fori_loop(0, frames * tiles, radix, 0)
-        copies[source_count].wait()
-
-        def transform(b, carry):
-            for start in range(0, frames, pair):
-                product = lax.dot_general(
-                    table[0, b],
-                    mixed[b, start * station_count : (start + pair) * station_count],
-                    (((1,), (1,)), ((), ())),
-                    preferred_element_type=F32,
-                )
-                product = product.reshape(2, groups, rows_of, pair * station_count)
-                rows = slice(start * rows_of, (start + pair) * rows_of)
-                for part in range(2):
-                    value = jnp.concatenate(
-                        [product[part, :, :, f * station_count : (f + 1) * station_count] for f in range(pair)], axis=1
-                    )
-                    columns = slice(part * station_count, (part + 1) * station_count)
-                    spectra[:, b, rows, columns] = value.astype(BF16)
-            return carry
-
-        lax.fori_loop(0, RADIX, transform, 0, unroll=4)
-        for copy in copies[source_count + 1 :]:
+        for member in range(members):
+            for k in range(ranges):
+                arrival(0, member * ranges + k).wait()
+            loop(pair * tiles, lambda i: radix(0, member, i), 1)
+        for k in range(source_count):
+            arrival(1, k).wait()
+        other_copies[0].wait()
+        each = pair * tiles
+        if members * each == RADIX:
+
+            def both(b):
+                radix(1, b // each, b % each)
+                transform(0, b)
+
+            loop(RADIX, both, 1)
+        else:
+            for member in range(members):
+                loop(each, lambda i: radix(1, member, i), 1)
+            loop(RADIX, lambda b: transform(0, b), 4)
+        loop(RADIX, lambda b: transform(1, b), 4)
+        for copy in other_copies[1:]:
             copy.wait()
 
     for k in range(at_once):
@@ -425,7 +441,7 @@
         if not has_earlier:
             out[k] = power
             continue
-        power = power + held[-1][group]
+        power = power + kept[2][group]
         for b in range(RADIX):
             for f in range(frames):
                 at = (b * frames + f) * rows_of
@@ -444,13 +460,18 @@
     flat_spec = pl.BlockSpec((at_once,) + flat[1:], lambda i, place: (i, 0, 0))
     operands = list(sources) + [table, weights] + ([] if earlier is None else [earlier])
     in_specs = [pl.BlockSpec(memory_space=pltpu.HBM)] * len(operands) + [pl.BlockSpec(memory_space=pl.ANY)] * len(later)
+    members = len(sources) // ranges
+    mixed = pltpu.VMEM((RADIX, frames // 2 * station_count, 2 * LANES), BF16)
     scratch = [
-        pltpu.VMEM((RADIX, frames * station_count, 2 * LANES), BF16),
         pltpu.VMEM((groups, RADIX, frames * channels // groups // RADIX, 2 * station_count), BF16),
-        pltpu.SemaphoreType.DMA((len(operands),)),
+        pltpu.SemaphoreType.DMA((2, len(sources))),
+        pltpu.SemaphoreType.DMA((3,)),
+        mixed,
+        mixed,
     ]
-    for k, block in enumerate(operands):
-        scratch.append(pltpu.VMEM(((1,) if k == len(sources) else block.shape[:1]) + block.shape[1:], block.dtype))
+    scratch += [pltpu.VMEM((members,) + block.shape, BF16) for block in sources[:ranges]]
+    scratch += [pltpu.VMEM((1,) + table.shape[1:], BF16), pltpu.VMEM(weights.shape, BF16)]
+    scratch += [] if earlier is None else [pltpu.VMEM(flat, F32)]
     if earlier is None:
         out_shape = jax.ShapeDtypeStruct(flat, F32)
         out_spec = flat_spec
@@ -498,7 +519,8 @@
     def laid(block):
         return jnp.moveaxis(block, 0, -2)
 
-    own, *other = cut(place, voltages, [(pol, 0, half) for pol in range(pols)], [])
+    (own,) = cut(voltages, [None], [])
+    other = cut(voltages, list(range(pols)), [own, place])
     columns = weight_blocks.shape[1] // CORES
     shard = lax.dynamic_slice_in_dim(weight_blocks, core * columns, columns, 1)
     shards = [shard] + [

time: 210 us -> 212 us (level)
  Pallas kernels: 70 us -> 74.4 us
  waiting for transfers between devices: 73.5 us -> 70.2 us
    ppermute x3, waiting for transfers between devices: 8.42 us -> 4.32 us  [body(): lax.ppermute(shard, 'tm', [(i, i ^ apart) for i in range(time_devices)])]
    pallas_call x2, Pallas kernels: 20.5 us -> 24.3 us  [beam_power(): pl.pallas_call(functools.partial(beam_kernel, len(sources), ranges, len(l...]
    pallas_call x1 -> x2, Pallas kernels: 4.28 us -> 4.89 us  [cut(): pl.pallas_call(functools.partial(cut_kernel, mine), out_shape=[jax.ShapeD...]
    unnamed x40 -> x38, local copies, waits for them, and re-layouts: 6.87 us -> 6.91 us
  transfers between devices with their start and end apart: 25 -> 25, of which waited for: 10 -> 9; matrix products, arithmetic and copies ran while one was open for 10% -> 10% of each run, Pallas kernels for 26% -> 28%
where the time goes in v11:
time: 212 us; the launch traced here: 210 us
  Pallas kernels  74.4 us (35%)
  waiting for transfers between devices  70.2 us (33%)
  starting transfers between devices  39.2 us (18%)
  local copies, waits for them, and re-layouts  22.1 us (10%)
  other arithmetic  4.18 us (2%)
    ppermute x7, waiting for transfers between devices, pair(): return lax.ppermute(block, 'tm', [(i, i ^ 1) for i in range(time_devices)])  45.7 us
    pallas_call x2, Pallas kernels, beam_power(): pl.pallas_call(functools.partial(beam_kernel, len(sources), ranges, len(l...  24.3 us
    ppermute x7, starting transfers between devices, hop(): lax.ppermute(block, 'tm', [(i, i + 2) for i in range(skip, time_devices -...  20.4 us
    ppermute x7, waiting for transfers between devices, hop(): lax.ppermute(block, 'tm', [(i, i + 2) for i in range(skip, time_devices -...  20.1 us
    pallas_call x4, Pallas kernels, far_filter(): pl.pallas_call(far_kernel, out_shape=(shape, shape), grid_spec=pltpu.Pref...  15.9 us
    pallas_call x2, Pallas kernels, near_filter(): pl.pallas_call(near_kernel, out_shape=jax.ShapeDtypeStruct((2 * frames, p...  15.7 us
    pallas_call x4, Pallas kernels, onward(): pl.pallas_call(onward_kernel, out_shape=jax.ShapeDtypeStruct((depth, part...  11 us
    ppermute x8, starting transfers between devices, swap(): return lax.ppermute(block, 'stn', [(0, 1), (1, 0)])  9.27 us
  transfers between devices with their start and end apart: 25, of which 9 were waited for; matrix products, arithmetic and copies ran while one was open for 10% of the time, Pallas kernels for 28%

profile of v11, /device:TPU:17, one launch (start us, length us, event | category | flops | bytes accessed | tf_op | source)
XLA Modules:
  0.0 210.3 jit_solution(9798435030011907761)
XLA Ops:
  2.4 3.2 %collective-permute-start.1 = (bf16[32,2,4,2,2048]{4,3,2,1,0:T(2,128)(2,1)}, bf16[32,2,4,2,2048]{4,3,2,1,0:T(2,128)(2,1)}, u32[]{:S(2)}, u32[]{:S(2)}) collective-permute-start(bf16[32,2,4,2,2048]{4,3,2,1,0:T(2,128)(2,1)} %cut.2.rest_0_), channel_id=1, source_target_pairs={{0,4},{2,6},{4,8},{6,10},{8,12},{10,14},{1,5},{3,7},{5,9},{7,11},{... | collective-permute-start | bytes 6291464 | tf_op jit(solution)/shard_map/ppermute | solution.py:514
  10.3 22.6 %collective-permute-done.3.refs_0_ = bf16[32,4,2,2048]{3,2,1,0:T(2,128)(2,1)S(1)} collective-permute-done((bf16[32,4,2,2048]{3,2,1,0:T(2,128)(2,1)}, bf16[32,4,2,2048]{3,2,1,0:T(2,128)(2,1)S(1)}, u32[]{:S(2)}, u32[]{:S(2)}) %collective-permute-start.3) | collective-permute-done | bytes 1048608 | tf_op jit(solution)/shard_map/ppermute | solution.py:511
  40.4 14.9 %collective-permute-done.refs_0_ = bf16[32,4,2,2048]{3,2,1,0:T(2,128)(2,1)} collective-permute-done((bf16[32,4,2,2048]{3,2,1,0:T(2,128)(2,1)}, bf16[32,4,2,2048]{3,2,1,0:T(2,128)(2,1)}, u32[]{:S(2)}, u32[]{:S(2)}) %collective-permute-start) | collective-permute-done | bytes 1048608 | tf_op jit(solution)/shard_map/ppermute | solution.py:511
  55.5 2.8 %copy.21 = bf16[32,4,2,2048]{3,0,2,1:T(8,128)(2,1)} copy(bf16[32,4,2,2048]{3,2,1,0:T(2,128)(2,1)} %after.3) | data formatting | bytes 2097152 | tf_op jit(solution)/shard_map/after/pallas_call | solution.py:77
  58.3 4.3 %collective-permute-start.2 = (bf16[4,2,32,2048]{3,2,1,0:T(8,128)(2,1)}, bf16[4,2,32,2048]{3,2,1,0:T(8,128)(2,1)}, u32[]{:S(2)}, u32[]{:S(2)}) collective-permute-start(bf16[4,2,32,2048]{3,2,1,0:T(8,128)(2,1)} %bitcast.27.other), channel_id=1, source_target_pairs={{0,4},{2,6},{4,8},{6,10},{8,12},{10,14},{1,5},{3,7},{5,9},{7,11},{... | collective-permute-start | bytes 3145736 | tf_op jit(solution)/shard_map/ppermute | solution.py:514
  65.8 4.1 %copy.18 = bf16[32,2,4,2,2048]{4,0,3,2,1:T(8,128)(2,1)} copy(bf16[32,2,4,2,2048]{4,3,2,1,0:T(2,128)(2,1)} %after.4) | data formatting | bytes 4194304 | tf_op jit(solution)/shard_map/after/pallas_call | solution.py:77
  69.8 2.9 %collective-permute-done.5.rest_0_ = bf16[16,256]{1,0:T(8,128)(2,1)S(1)} collective-permute-done((bf16[16,256]{1,0:T(8,128)(2,1)S(1)}, bf16[16,256]{1,0:T(8,128)(2,1)S(1)}, u32[]{:S(2)}, u32[]{:S(2)}) %collective-permute-start.5) | collective-permute-done | bytes 8224 | tf_op jit(solution)/shard_map/ppermute | solution.py:527
  77.4 3.0 %collective-permute-start.11 = (bf16[7,2,32,1024]{3,2,1,0:T(8,128)(2,1)}, bf16[7,2,32,1024]{3,2,1,0:T(8,128)(2,1)S(1)}, u32[]{:S(2)}, u32[]{:S(2)}) collective-permute-start(bf16[7,2,32,1024]{3,2,1,0:T(8,128)(2,1)} %onward.4.rest_0_), channel_id=1, source_target_pairs={{4,8},{6,10},{8,12},{10,14},{5,9},{7,11},{9,13},{11,15},{20,24},{2... | collective-permute-start | bytes 2752520 | tf_op jit(solution)/shard_map/ppermute | solution.py:514
  92.6 4.2 %collective-permute-done.2.other_back.rest_5_.rest_3_ = bf16[4,2,32,2048]{3,2,1,0:T(8,128)(2,1)} collective-permute-done((bf16[4,2,32,2048]{3,2,1,0:T(8,128)(2,1)}, bf16[4,2,32,2048]{3,2,1,0:T(8,128)(2,1)}, u32[]{:S(2)}, u32[]{:S(2)}) %collective-permute-start.2) | collective-permute-done | bytes 1048608 | tf_op jit(solution)/shard_map/ppermute | solution.py:514
  96.8 2.9 %onward.6.rest_2_ = bf16[7,2,32,1280]{3,2,1,0:T(8,128)(2,1)} custom-call(s32[2]{0:T(128)} %pad_add_fusion.rest_1_.place, bf16[2,4,2,32,2048]{4,3,2,1,0:T(8,128)(2,1)} %bitcast.30, bf16[4,2,32,2048]{3,2,1,0:T(8,128)(2,1)} %collective-permute-done.2.other_back.rest_5_.rest_3_), custom_call_target="tpu_custom_call" | custom-call | bytes 9900000 | tf_op jit(solution)/shard_map/onward/pallas_call | solution.py:295
  99.7 3.0 %collective-permute-start.9 = (bf16[7,2,32,1280]{3,2,1,0:T(8,128)(2,1)}, bf16[7,2,32,1280]{3,2,1,0:T(8,128)(2,1)}, u32[]{:S(2)}, u32[]{:S(2)}) collective-permute-start(bf16[7,2,32,1280]{3,2,1,0:T(8,128)(2,1)} %onward.6.rest_2_), channel_id=1, source_target_pairs={{4,8},{6,10},{8,12},{10,14},{5,9},{7,11},{9,13},{11,15},{20,24},{2... | collective-permute-start | bytes 3440648 | tf_op jit(solution)/shard_map/ppermute | solution.py:514
  108.8 7.9 %near.3.partial = f32[8,2,32,2048]{3,2,1,0:T(8,128)} custom-call(s32[2]{0:T(128)} %pad_add_fusion.rest_1_.place, f32[16,8,2048]{2,1,0:T(8,128)} %broadcast_in_dim.2.taps, bf16[2,4,2,32,2048]{4,3,2,1,0:T(8,128)(2,1)} %bitcast.34, bf16[4,2,32,2048]{3,2,1,0:T(8,128)(2,1)} %bitcast.37, bf16[2,4,2,32,2048]{4,3,2,1,0:T(8,128)(2,1)} %bitcast.31, ...), custom_call_target="tpu_custom_call" | custom-call | bytes 26400000 | tf_op jit(solution)/shard_map/near/pallas_call | solution.py:221
  117.6 3.9 %far.4 = (bf16[4,2,32,1024]{3,2,1,0:T(8,128)(2,1)}, bf16[4,2,32,1024]{3,2,1,0:T(8,128)(2,1)}) custom-call(s32[2]{0:T(128)} %pad_add_fusion.rest_1_.place, f32[16,8,2048]{2,1,0:T(8,128)} %broadcast_in_dim.2.taps, f32[8,2,32,2048]{3,2,1,0:T(8,128)} %near.3.partial, bf16[7,2,32,1024]{3,2,1,0:T(8,128)(2,1)} %copy-done.5), custom_call_target="tpu_custom_call" | custom-call | bytes 3300000 | tf_op jit(solution)/shard_map/far/pallas_call | solution.py:247
  125.4 7.8 %near.2.rest_1_.partial = f32[8,2,32,2048]{3,2,1,0:T(8,128)} custom-call(s32[2]{0:T(128)} %pad_add_fusion.rest_1_.place, f32[16,8,2048]{2,1,0:T(8,128)} %broadcast_in_dim.2.taps, bf16[2,4,2,32,2048]{4,3,2,1,0:T(8,128)(2,1)} %bitcast.35, bf16[4,2,32,2048]{3,2,1,0:T(8,128)(2,1)} %bitcast.27.other, bf16[2,4,2,32,2048]{4,3,2,1,0:T(8,128)(2,1)} %bitcast.33, ...), custom_call_target="tpu_custom_call" | custom-call | bytes 26400000 | tf_op jit(solution)/shard_map/near/pallas_call | solution.py:221
  133.3 2.8 %collective-permute-done.10.far = bf16[7,2,32,1024]{3,2,1,0:T(8,128)(2,1)} collective-permute-done((bf16[7,2,32,1024]{3,2,1,0:T(8,128)(2,1)}, bf16[7,2,32,1024]{3,2,1,0:T(8,128)(2,1)}, u32[]{:S(2)}, u32[]{:S(2)}) %collective-permute-start.10) | collective-permute-done | bytes 917536 | tf_op jit(solution)/shard_map/ppermute | solution.py:514
  136.1 3.9 %far.5 = (bf16[4,2,32,1024]{3,2,1,0:T(8,128)(2,1)}, bf16[4,2,32,1024]{3,2,1,0:T(8,128)(2,1)}) custom-call(s32[2]{0:T(128)} %pad_add_fusion.rest_1_.place, f32[16,8,2048]{2,1,0:T(8,128)} %broadcast_in_dim.2.taps, f32[8,2,32,2048]{3,2,1,0:T(8,128)} %near.3.partial, bf16[7,2,32,1024]{3,2,1,0:T(8,128)(2,1)} %collective-permute-done.10.far, ...), custom_call_target="tpu_custom_call" | custom-call | bytes 3300000 | tf_op jit(solution)/shard_map/far/pallas_call | solution.py:247
  141.3 3.0 %collective-permute-start.15 = (bf16[4,2,32,1024]{3,2,1,0:T(8,128)(2,1)}, bf16[4,2,32,1024]{3,2,1,0:T(8,128)(2,1)}, u32[]{:S(2)}, u32[]{:S(2)}) collective-permute-start(bf16[4,2,32,1024]{3,2,1,0:T(8,128)(2,1)} %get-tuple-element.20.refs_0_), channel_id=1, source_target_pairs={{0,1},{1,0},{2,3},{3,2},{4,5},{5,4},{6,7},{7,6},{8,9},{9,8},{10,11... | collective-permute-start | bytes 1572872 | tf_op jit(solution)/shard_map/ppermute | solution.py:517
  144.2 3.0 %collective-permute-start.14 = (bf16[7,2,32,768]{3,2,1,0:T(8,128)(2,1)S(1)}, bf16[7,2,32,768]{3,2,1,0:T(8,128)(2,1)}, u32[]{:S(2)}, u32[]{:S(2)}) collective-permute-start(bf16[7,2,32,768]{3,2,1,0:T(8,128)(2,1)S(1)} %copy-done.3), channel_id=1, source_target_pairs={{4,8},{6,10},{8,12},{10,14},{5,9},{7,11},{9,13},{11,15},{20,24},{2... | collective-permute-start | bytes 2064392 | tf_op jit(solution)/shard_map/ppermute | solution.py:514
  147.6 13.1 %collective-permute-done.9.far = bf16[7,2,32,1280]{3,2,1,0:T(8,128)(2,1)} collective-permute-done((bf16[7,2,32,1280]{3,2,1,0:T(8,128)(2,1)}, bf16[7,2,32,1280]{3,2,1,0:T(8,128)(2,1)}, u32[]{:S(2)}, u32[]{:S(2)}) %collective-permute-start.9) | collective-permute-done | bytes 1146912 | tf_op jit(solution)/shard_map/ppermute | solution.py:514
  163.4 4.4 %far.6 = (bf16[4,2,32,1280]{3,2,1,0:T(8,128)(2,1)}, bf16[4,2,32,1280]{3,2,1,0:T(8,128)(2,1)}) custom-call(s32[2]{0:T(128)} %pad_add_fusion.rest_1_.place, f32[16,8,2048]{2,1,0:T(8,128)} %broadcast_in_dim.2.taps, f32[8,2,32,2048]{3,2,1,0:T(8,128)} %near.2.rest_1_.partial, bf16[7,2,32,1280]{3,2,1,0:T(8,128)(2,1)} %collective-permute-done.9.far, ...), custom_call_target="tpu_custom_call" | custom-call | bytes 3300000 | tf_op jit(solution)/shard_map/far/pallas_call | solution.py:247
  169.0 11.2 %beams.2.rest_0_.refs_10_ = f32[8,512,256]{2,1,0:T(8,128)} custom-call(s32[2]{0:T(128)} %pad_add_fusion.rest_1_.place, bf16[4,2,32,1024]{3,2,1,0:T(8,128)(2,1)} %get-tuple-element.20.refs_0_, bf16[4,2,32,1024]{3,2,1,0:T(8,128)(2,1)} %get-tuple-element.21.refs_1_, bf16[4,2,32,1024]{3,2,1,0:T(8,128)(2,1)} %collective-permute-done.12.rest_0_.refs_2_, ...), custom_call_target="tpu_custom_call" | custom-call | tf_op jit(solution)/shard_map/beams/pallas_call | solution.py:481
  180.2 3.6 %far.7 = (bf16[4,2,32,768]{3,2,1,0:T(8,128)(2,1)}, bf16[4,2,32,768]{3,2,1,0:T(8,128)(2,1)}) custom-call(s32[2]{0:T(128)} %pad_add_fusion.rest_1_.place, f32[16,8,2048]{2,1,0:T(8,128)} %broadcast_in_dim.2.taps, f32[8,2,32,2048]{3,2,1,0:T(8,128)} %near.2.rest_1_.partial, bf16[7,2,32,768]{3,2,1,0:T(8,128)(2,1)} %collective-permute-done.14.far, ...), custom_call_target="tpu_custom_call" | custom-call | bytes 3300000 | tf_op jit(solution)/shard_map/far/pallas_call | solution.py:247
  185.7 8.3 %collective-permute-done.20.refs_3_ = bf16[4,2,32,768]{3,2,1,0:T(8,128)(2,1)S(1)} collective-permute-done((bf16[4,2,32,768]{3,2,1,0:T(8,128)(2,1)}, bf16[4,2,32,768]{3,2,1,0:T(8,128)(2,1)S(1)}, u32[]{:S(2)}, u32[]{:S(2)}) %collective-permute-start.20) | collective-permute-done | bytes 393248 | tf_op jit(solution)/shard_map/ppermute | solution.py:511
  197.2 13.1 %beams.3 = f32[1024,2,4,128]{3,2,1,0:T(4,128)} custom-call(s32[2]{0:T(128)} %pad_add_fusion.rest_1_.place, bf16[4,2,32,1280]{3,2,1,0:T(8,128)(2,1)} %get-tuple-element.19.refs_10_.refs_0_, bf16[4,2,32,768]{3,2,1,0:T(8,128)(2,1)} %get-tuple-element.22.refs_1_, bf16[4,2,32,1280]{3,2,1,0:T(8,128)(2,1)} %collective-permute-done.19.refs_2_, ...), custom_call_target="tpu_custom_call" | custom-call | tf_op jit(solution)/shard_map/beams/pallas_call | solution.py:481
  (98 shorter events, 56.2 us)
Async XLA Ops:
  2.4 55.8 %collective-permute-start.1 = (bf16[32,2,4,2,2048]{4,3,2,1,0:T(2,128)(2,1)}, bf16[32,2,4,2,2048]{4,3,2,1,0:T(2,128)(2,1)}, u32[]{:S(2)}, u32[]{:S(2)}) collective-permute-start(bf16[32,2,4,2,2048]{4,3,2,1,0:T(2,128)(2,1)} %cut.2.rest_0_), channel_id=1, source_target_pairs={{0,4},{2,6},{4,8},{6,10},{8,12},{10,14},{1,5},{3,7},{5,9},{7,11},{... | collective-permute-start | bytes 6291464 | tf_op jit(solution)/shard_map/ppermute | solution.py:514
  8.7 24.1 %collective-permute-start.3 = (bf16[32,4,2,2048]{3,2,1,0:T(2,128)(2,1)}, bf16[32,4,2,2048]{3,2,1,0:T(2,128)(2,1)S(1)}, u32[]{:S(2)}, u32[]{:S(2)}) collective-permute-start(bf16[32,4,2,2048]{3,2,1,0:T(2,128)(2,1)} %get-tuple-element.16), channel_id=1, source_target_pairs={{0,2},{2,0},{4,6},{6,4},{8,10},{10,8},{12,14},{14,12},{1,3},{3,1},... | collective-permute-start | bytes 3145736 | tf_op jit(solution)/shard_map/ppermute | solution.py:511
  10.1 45.2 %collective-permute-start = (bf16[32,4,2,2048]{3,2,1,0:T(2,128)(2,1)}, bf16[32,4,2,2048]{3,2,1,0:T(2,128)(2,1)}, u32[]{:S(2)}, u32[]{:S(2)}) collective-permute-start(bf16[32,4,2,2048]{3,2,1,0:T(2,128)(2,1)} %get-tuple-element.15), channel_id=1, source_target_pairs={{0,2},{2,0},{4,6},{6,4},{8,10},{10,8},{12,14},{14,12},{1,3},{3,1},... | collective-permute-start | bytes 3145736 | tf_op jit(solution)/shard_map/ppermute | solution.py:511
  35.6 38.5 %collective-permute-start.4 = (bf16[4,2,32,2048]{3,2,1,0:T(8,128)(2,1)S(1)}, bf16[4,2,32,2048]{3,2,1,0:T(8,128)(2,1)}, u32[]{:S(2)}, u32[]{:S(2)}) collective-permute-start(bf16[4,2,32,2048]{3,2,1,0:T(8,128)(2,1)S(1)} %bitcast.36), channel_id=1, source_target_pairs={{0,4},{2,6},{4,8},{6,10},{8,12},{10,14},{1,5},{3,7},{5,9},{7,11},{... | collective-permute-start | bytes 3145736 | tf_op jit(solution)/shard_map/ppermute | solution.py:514
  37.6 35.1 %collective-permute-start.5 = (bf16[16,256]{1,0:T(8,128)(2,1)S(1)}, bf16[16,256]{1,0:T(8,128)(2,1)S(1)}, u32[]{:S(2)}, u32[]{:S(2)}) collective-permute-start(bf16[16,256]{1,0:T(8,128)(2,1)S(1)} %get-tuple-element.26), channel_id=1, source_target_pairs={{0,4},{2,6},{4,0},{6,2},{8,12},{10,14},{12,8},{14,10},{1,5},{3,7},... | collective-permute-start | bytes 24584 | tf_op jit(solution)/shard_map/ppermute | solution.py:527
  37.7 35.8 %collective-permute-start.6 = (bf16[16,256]{1,0:T(8,128)(2,1)S(1)}, bf16[16,256]{1,0:T(8,128)(2,1)S(1)}, u32[]{:S(2)}, u32[]{:S(2)}) collective-permute-start(bf16[16,256]{1,0:T(8,128)(2,1)S(1)} %get-tuple-element.26), channel_id=1, source_target_pairs={{0,8},{2,10},{4,12},{6,14},{8,0},{10,2},{12,4},{14,6},{1,9},{3,11}... | collective-permute-start | bytes 24584 | tf_op jit(solution)/shard_map/ppermute | solution.py:527
  55.3 18.8 %collective-permute-start.7 = (bf16[16,256]{1,0:T(8,128)(2,1)S(1)}, bf16[16,256]{1,0:T(8,128)(2,1)S(1)}, u32[]{:S(2)}, u32[]{:S(2)}) collective-permute-start(bf16[16,256]{1,0:T(8,128)(2,1)S(1)} %get-tuple-element.26), channel_id=1, source_target_pairs={{0,12},{2,14},{4,8},{6,10},{8,4},{10,6},{12,0},{14,2},{1,13},{3,15... | collective-permute-start | bytes 24584 | tf_op jit(solution)/shard_map/ppermute | solution.py:527
  58.3 38.5 %collective-permute-start.2 = (bf16[4,2,32,2048]{3,2,1,0:T(8,128)(2,1)}, bf16[4,2,32,2048]{3,2,1,0:T(8,128)(2,1)}, u32[]{:S(2)}, u32[]{:S(2)}) collective-permute-start(bf16[4,2,32,2048]{3,2,1,0:T(8,128)(2,1)} %bitcast.27.other), channel_id=1, source_target_pairs={{0,4},{2,6},{4,8},{6,10},{8,12},{10,14},{1,5},{3,7},{5,9},{7,11},{... | collective-permute-start | bytes 3145736 | tf_op jit(solution)/shard_map/ppermute | solution.py:514
  77.4 39.2 %collective-permute-start.11 = (bf16[7,2,32,1024]{3,2,1,0:T(8,128)(2,1)}, bf16[7,2,32,1024]{3,2,1,0:T(8,128)(2,1)S(1)}, u32[]{:S(2)}, u32[]{:S(2)}) collective-permute-start(bf16[7,2,32,1024]{3,2,1,0:T(8,128)(2,1)} %onward.4.rest_0_), channel_id=1, source_target_pairs={{4,8},{6,10},{8,12},{10,14},{5,9},{7,11},{9,13},{11,15},{20,24},{2... | collective-permute-start | bytes 2752520 | tf_op jit(solution)/shard_map/ppermute | solution.py:514
  84.6 18.1 %collective-permute-start.8 = (bf16[64,256]{1,0:T(8,128)(2,1)}, bf16[64,256]{1,0:T(8,128)(2,1)}, u32[]{:S(2)}, u32[]{:S(2)}) collective-permute-start(bf16[64,256]{1,0:T(8,128)(2,1)} %pad_maximum_fusion), channel_id=1, source_target_pairs={{0,2},{2,0},{4,6},{6,4},{8,10},{10,8},{12,14},{14,12},{1,3},{3,1},... | collective-permute-start | bytes 98312 | tf_op jit(solution)/shard_map/ppermute | solution.py:511
  88.6 47.5 %collective-permute-start.10 = (bf16[7,2,32,1024]{3,2,1,0:T(8,128)(2,1)}, bf16[7,2,32,1024]{3,2,1,0:T(8,128)(2,1)}, u32[]{:S(2)}, u32[]{:S(2)}) collective-permute-start(bf16[7,2,32,1024]{3,2,1,0:T(8,128)(2,1)} %onward.5.rest_1_), channel_id=1, source_target_pairs={{4,8},{6,10},{8,12},{10,14},{5,9},{7,11},{9,13},{11,15},{20,24},{2... | collective-permute-start | bytes 2752520 | tf_op jit(solution)/shard_map/ppermute | solution.py:514
  99.7 61.0 %collective-permute-start.9 = (bf16[7,2,32,1280]{3,2,1,0:T(8,128)(2,1)}, bf16[7,2,32,1280]{3,2,1,0:T(8,128)(2,1)}, u32[]{:S(2)}, u32[]{:S(2)}) collective-permute-start(bf16[7,2,32,1280]{3,2,1,0:T(8,128)(2,1)} %onward.6.rest_2_), channel_id=1, source_target_pairs={{4,8},{6,10},{8,12},{10,14},{5,9},{7,11},{9,13},{11,15},{20,24},{2... | collective-permute-start | bytes 3440648 | tf_op jit(solution)/shard_map/ppermute | solution.py:514
  121.5 14.6 %collective-permute-start.12 = (bf16[4,2,32,1024]{3,2,1,0:T(8,128)(2,1)}, bf16[4,2,32,1024]{3,2,1,0:T(8,128)(2,1)}, u32[]{:S(2)}, u32[]{:S(2)}) collective-permute-start(bf16[4,2,32,1024]{3,2,1,0:T(8,128)(2,1)} %get-tuple-element.17), channel_id=1, source_target_pairs={{0,2},{2,0},{4,6},{6,4},{8,10},{10,8},{12,14},{14,12},{1,3},{3,1},... | collective-permute-start | bytes 1572872 | tf_op jit(solution)/shard_map/ppermute | solution.py:511
  140.0 23.4 %collective-permute-start.13 = (bf16[4,2,32,1024]{3,2,1,0:T(8,128)(2,1)}, bf16[4,2,32,1024]{3,2,1,0:T(8,128)(2,1)}, u32[]{:S(2)}, u32[]{:S(2)}) collective-permute-start(bf16[4,2,32,1024]{3,2,1,0:T(8,128)(2,1)} %get-tuple-element.18), channel_id=1, source_target_pairs={{0,2},{2,0},{4,6},{6,4},{8,10},{10,8},{12,14},{14,12},{1,3},{3,1},... | collective-permute-start | bytes 1572872 | tf_op jit(solution)/shard_map/ppermute | solution.py:511
  141.3 26.5 %collective-permute-start.15 = (bf16[4,2,32,1024]{3,2,1,0:T(8,128)(2,1)}, bf16[4,2,32,1024]{3,2,1,0:T(8,128)(2,1)}, u32[]{:S(2)}, u32[]{:S(2)}) collective-permute-start(bf16[4,2,32,1024]{3,2,1,0:T(8,128)(2,1)} %get-tuple-element.20.refs_0_), channel_id=1, source_target_pairs={{0,1},{1,0},{2,3},{3,2},{4,5},{5,4},{6,7},{7,6},{8,9},{9,8},{10,11... | collective-permute-start | bytes 1572872 | tf_op jit(solution)/shard_map/ppermute | solution.py:517
  144.2 36.0 %collective-permute-start.14 = (bf16[7,2,32,768]{3,2,1,0:T(8,128)(2,1)S(1)}, bf16[7,2,32,768]{3,2,1,0:T(8,128)(2,1)}, u32[]{:S(2)}, u32[]{:S(2)}) collective-permute-start(bf16[7,2,32,768]{3,2,1,0:T(8,128)(2,1)S(1)} %copy-done.3), channel_id=1, source_target_pairs={{4,8},{6,10},{8,12},{10,14},{5,9},{7,11},{9,13},{11,15},{20,24},{2... | collective-permute-start | bytes 2064392 | tf_op jit(solution)/shard_map/ppermute | solution.py:514
  147.3 21.7 %collective-permute-start.16 = (bf16[4,2,32,1024]{3,2,1,0:T(8,128)(2,1)}, bf16[4,2,32,1024]{3,2,1,0:T(8,128)(2,1)}, u32[]{:S(2)}, u32[]{:S(2)}) collective-permute-start(bf16[4,2,32,1024]{3,2,1,0:T(8,128)(2,1)} %get-tuple-element.21.refs_1_), channel_id=1, source_target_pairs={{0,1},{1,0},{2,3},{3,2},{4,5},{5,4},{6,7},{7,6},{8,9},{9,8},{10,11... | collective-permute-start | bytes 1572872 | tf_op jit(solution)/shard_map/ppermute | solution.py:517
  160.7 8.3 %collective-permute-start.17 = (bf16[4,2,32,1024]{3,2,1,0:T(8,128)(2,1)}, bf16[4,2,32,1024]{3,2,1,0:T(8,128)(2,1)}, u32[]{:S(2)}, u32[]{:S(2)}) collective-permute-start(bf16[4,2,32,1024]{3,2,1,0:T(8,128)(2,1)} %collective-permute-done.12.rest_0_.refs_2_), channel_id=1, source_target_pairs={{0,1},{1,0},{2,3},{3,2},{4,5},{5,4},{6,7},{7,6},{8,9},{9,8},{10,11... | collective-permute-start | bytes 1572872 | tf_op jit(solution)/shard_map/ppermute | solution.py:517
  163.4 5.6 %collective-permute-start.18 = (bf16[4,2,32,1024]{3,2,1,0:T(8,128)(2,1)}, bf16[4,2,32,1024]{3,2,1,0:T(8,128)(2,1)}, u32[]{:S(2)}, u32[]{:S(2)}) collective-permute-start(bf16[4,2,32,1024]{3,2,1,0:T(8,128)(2,1)} %collective-permute-done.13.rest_0_.refs_3_), channel_id=1, source_target_pairs={{0,1},{1,0},{2,3},{3,2},{4,5},{5,4},{6,7},{7,6},{8,9},{9,8},{10,11... | collective-permute-start | bytes 1572872 | tf_op jit(solution)/shard_map/ppermute | solution.py:517
  167.7 17.4 %collective-permute-start.19 = (bf16[4,2,32,1280]{3,2,1,0:T(8,128)(2,1)}, bf16[4,2,32,1280]{3,2,1,0:T(8,128)(2,1)}, u32[]{:S(2)}, u32[]{:S(2)}) collective-permute-start(bf16[4,2,32,1280]{3,2,1,0:T(8,128)(2,1)} %get-tuple-element.23), channel_id=1, source_target_pairs={{0,2},{2,0},{4,6},{6,4},{8,10},{10,8},{12,14},{14,12},{1,3},{3,1},... | collective-permute-start | bytes 1966088 | tf_op jit(solution)/shard_map/ppermute | solution.py:511
  183.8 10.1 %collective-permute-start.20 = (bf16[4,2,32,768]{3,2,1,0:T(8,128)(2,1)}, bf16[4,2,32,768]{3,2,1,0:T(8,128)(2,1)S(1)}, u32[]{:S(2)}, u32[]{:S(2)}) collective-permute-start(bf16[4,2,32,768]{3,2,1,0:T(8,128)(2,1)} %get-tuple-element.24), channel_id=1, source_target_pairs={{0,2},{2,0},{4,6},{6,4},{8,10},{10,8},{12,14},{14,12},{1,3},{3,1},... | collective-permute-start | bytes 1179656 | tf_op jit(solution)/shard_map/ppermute | solution.py:511
  184.1 11.5 %collective-permute-start.21 = (bf16[4,2,32,1280]{3,2,1,0:T(8,128)(2,1)S(1)}, bf16[4,2,32,1280]{3,2,1,0:T(8,128)(2,1)S(1)}, u32[]{:S(2)}, u32[]{:S(2)}) collective-permute-start(bf16[4,2,32,1280]{3,2,1,0:T(8,128)(2,1)S(1)} %copy-done.4), channel_id=1, source_target_pairs={{0,1},{1,0},{2,3},{3,2},{4,5},{5,4},{6,7},{7,6},{8,9},{9,8},{10,11... | collective-permute-start | bytes 1966088 | tf_op jit(solution)/shard_map/ppermute | solution.py:517
  185.1 11.4 %collective-permute-start.23 = (bf16[4,2,32,1280]{3,2,1,0:T(8,128)(2,1)}, bf16[4,2,32,1280]{3,2,1,0:T(8,128)(2,1)}, u32[]{:S(2)}, u32[]{:S(2)}) collective-permute-start(bf16[4,2,32,1280]{3,2,1,0:T(8,128)(2,1)} %collective-permute-done.19.refs_2_), channel_id=1, source_target_pairs={{0,1},{1,0},{2,3},{3,2},{4,5},{5,4},{6,7},{7,6},{8,9},{9,8},{10,11... | collective-permute-start | bytes 1966088 | tf_op jit(solution)/shard_map/ppermute | solution.py:517
  185.2 11.3 %collective-permute-start.22 = (bf16[4,2,32,768]{3,2,1,0:T(8,128)(2,1)}, bf16[4,2,32,768]{3,2,1,0:T(8,128)(2,1)S(1)}, u32[]{:S(2)}, u32[]{:S(2)}) collective-permute-start(bf16[4,2,32,768]{3,2,1,0:T(8,128)(2,1)} %get-tuple-element.22.refs_1_), channel_id=1, source_target_pairs={{0,1},{1,0},{2,3},{3,2},{4,5},{5,4},{6,7},{7,6},{8,9},{9,8},{10,11... | collective-permute-start | bytes 1179656 | tf_op jit(solution)/shard_map/ppermute | solution.py:517
  (18 other events, 181.9 us)

commit v12 on v10

--- a/solution.py
+++ b/solution.py
@@ -85,68 +85,56 @@
     )(block, *earlier)
 
 
-def cut_kernel(cuts, place, voltages, *rest):
-    (own, *outs), (buffer, loads, stores) = rest[-4 - len(cuts) : -3], rest[-3:]
-    half = own.shape[0]
-    pieces = loads.shape[1]
+def cut_kernel(mine, voltages, *rest):
+    count = len(mine)
+    outs, (buffer, loads, stores) = rest[-3 - count : -3], rest[-3:]
+    half = buffer.shape[0]
+    pieces = loads.shape[0]
     size = half // pieces
-    side = place[0]
-
-    def load(h, k):
-        start = jnp.where(side == h, 0, half) + k * size
+    side = lax.rem(lax.axis_index("tm"), 2)
+    start = half * (side if mine[0] is None else 1 - side)
+
+    def load(k):
         return pltpu.make_async_copy(
-            voltages.at[pl.ds(start, size)], buffer.at[h, pl.ds(k * size, size)], loads.at[h, k]
+            voltages.at[pl.ds(start + k * size, size)], buffer.at[pl.ds(k * size, size)], loads.at[k]
         )
 
-    def store(h, k):
-        copies = []
-        if h == 0:
-            copies.append(pltpu.make_async_copy(buffer.at[0, pl.ds(k * size, size)], own.at[pl.ds(k * size, size)], stores.at[0, k]))
-        else:
-            for pol in range(voltages.shape[1]):
-                for out, (which, low, count) in zip(outs, cuts):
-                    if which == pol and low <= k * size < low + count:
-                        copies.append(
-                            pltpu.make_async_copy(
-                                buffer.at[1, pl.ds(k * size, size), pol],
-                                out.at[pl.ds(k * size - low, size)],
-                                stores.at[1 + pol, k],
-                            )
-                        )
-        return copies
-
-    order = [(h, k) for h in range(2) for k in range(pieces)]
-    for h, k in order:
-        load(h, k).start()
-    for h, k in order:
-        load(h, k).wait()
-        for copy in store(h, k):
-            copy.start()
-    for h, k in order:
-        for copy in store(h, k):
-            copy.wait()
-
-
-def cut(place, voltages, cuts, earlier):
+    def store(k, i):
+        block = buffer.at[pl.ds(k * size, size)]
+        block = block if mine[i] is None else block.at[:, mine[i]]
+        return pltpu.make_async_copy(block, outs[i].at[pl.ds(k * size, size)], stores.at[i, k])
+
+    for k in range(pieces):
+        load(k).start()
+    for k in range(pieces):
+        load(k).wait()
+        for i in range(count):
+            store(k, i).start()
+    for k in range(pieces):
+        for i in range(count):
+            store(k, i).wait()
+
+
+def cut(voltages, mine, earlier):
     stations, pols, frames, parts, samples = voltages.shape
-    half = stations // 2
+    whole = (stations // 2, pols, frames, parts, samples)
+    shapes = [whole if pol is None else whole[:1] + whole[2:] for pol in mine]
     pieces = 4
-    shapes = [(half, pols, frames, parts, samples)] + [(size, frames, parts, samples) for _, _, size in cuts]
-    anywhere = pl.BlockSpec(memory_space=pltpu.HBM)
-    return pl.pallas_call(
-        functools.partial(cut_kernel, cuts),
+    there = pl.BlockSpec(memory_space=pltpu.HBM)
+    return pl.pallas_call(
+        functools.partial(cut_kernel, mine),
         out_shape=[jax.ShapeDtypeStruct(shape, BF16) for shape in shapes],
-        in_specs=[pl.BlockSpec(memory_space=pltpu.SMEM), anywhere] + [pl.BlockSpec(memory_space=pl.ANY)] * len(earlier),
-        out_specs=[anywhere] * len(shapes),
+        in_specs=[there] + [pl.BlockSpec(memory_space=pl.ANY)] * len(earlier),
+        out_specs=[there] * len(shapes),
         scratch_shapes=[
-            pltpu.VMEM((2,) + shapes[0], BF16),
-            pltpu.SemaphoreType.DMA((2, pieces)),
-            pltpu.SemaphoreType.DMA((1 + pols, pieces)),
+            pltpu.VMEM(whole, BF16),
+            pltpu.SemaphoreType.DMA((pieces,)),
+            pltpu.SemaphoreType.DMA((len(mine), pieces)),
         ],
         compiler_params=pltpu.CompilerParams(vmem_limit_bytes=VMEM_LIMIT),
-        cost_estimate=cost(4),
+        cost_estimate=cost(2),
         name="cut",
-    )(place, voltages, *earlier)
+    )(voltages, *earlier)
 
 
 def weighted(taps, window, count, lanes, part, rows, sums):
@@ -391,7 +379,7 @@
                     mixed[b, target, LANES:] = im.astype(BF16)
                 return carry
 
-            lax.fori_loop(0, frames * tiles, radix, 0)
+            lax.fori_loop(0, frames * tiles, radix, 0, unroll=2)
         copies[source_count].wait()
 
         def transform(b, carry):
@@ -412,7 +400,7 @@
                     spectra[:, b, rows, columns] = value.astype(BF16)
             return carry
 
-        lax.fori_loop(0, RADIX, transform, 0, unroll=4)
+        lax.fori_loop(0, RADIX, transform, 0, unroll=True)
         for copy in copies[source_count + 1 :]:
             copy.wait()
 
@@ -498,7 +486,8 @@
     def laid(block):
         return jnp.moveaxis(block, 0, -2)
 
-    own, *other = cut(place, voltages, [(pol, 0, half) for pol in range(pols)], [])
+    (own,) = cut(voltages, [None], [])
+    other = cut(voltages, list(range(pols)), [own, place])
     columns = weight_blocks.shape[1] // CORES
     shard = lax.dynamic_slice_in_dim(weight_blocks, core * columns, columns, 1)
     shards = [shard] + [

time: 210 us -> 207 us (0.986)
  waiting for transfers between devices: 73.5 us -> 69.4 us
    ppermute x3, waiting for transfers between devices: 8.42 us -> 4.32 us  [body(): lax.ppermute(shard, 'tm', [(i, i ^ apart) for i in range(time_devices)])]
    pallas_call x1 -> x2, Pallas kernels: 4.28 us -> 4.89 us  [cut(): pl.pallas_call(functools.partial(cut_kernel, mine), out_shape=[jax.ShapeD...]
    unnamed x40 -> x38, local copies, waits for them, and re-layouts: 6.87 us -> 6.91 us
  transfers between devices with their start and end apart: 25 -> 25, of which waited for: 10 -> 10; matrix products, arithmetic and copies ran while one was open for 10% -> 10% of each run, Pallas kernels for 26% -> 28%
where the time goes in v12:
time: 207 us; the launch traced here: 206 us
  Pallas kernels  69.6 us (34%)
  waiting for transfers between devices  69.4 us (34%)
  starting transfers between devices  40.2 us (19%)
  local copies, waits for them, and re-layouts  22.1 us (11%)
  other arithmetic  4.18 us (2%)
    ppermute x7, waiting for transfers between devices, pair(): return lax.ppermute(block, 'tm', [(i, i ^ 1) for i in range(time_devices)])  45.1 us
    ppermute x7, starting transfers between devices, hop(): lax.ppermute(block, 'tm', [(i, i + 2) for i in range(skip, time_devices -...  20.6 us
    ppermute x7, waiting for transfers between devices, hop(): lax.ppermute(block, 'tm', [(i, i + 2) for i in range(skip, time_devices -...  19.9 us
    pallas_call x2, Pallas kernels, beam_power(): pl.pallas_call(functools.partial(beam_kernel, len(sources), ranges, len(l...  19.4 us
    pallas_call x4, Pallas kernels, far_filter(): pl.pallas_call(far_kernel, out_shape=(shape, shape), grid_spec=pltpu.Pref...  15.9 us
    pallas_call x2, Pallas kernels, near_filter(): pl.pallas_call(near_kernel, out_shape=jax.ShapeDtypeStruct((2 * frames, p...  15.7 us
    pallas_call x4, Pallas kernels, onward(): pl.pallas_call(onward_kernel, out_shape=jax.ShapeDtypeStruct((depth, part...  11 us
    ppermute x8, starting transfers between devices, swap(): return lax.ppermute(block, 'stn', [(0, 1), (1, 0)])  10.1 us
  transfers between devices with their start and end apart: 25, of which 10 were waited for; matrix products, arithmetic and copies ran while one was open for 10% of the time, Pallas kernels for 28%

profile of v12, /device:TPU:17, one launch (start us, length us, event | category | flops | bytes accessed | tf_op | source)
XLA Modules:
  0.0 205.8 jit_solution(3724571494919524540)
XLA Ops:
  2.4 3.2 %collective-permute-start.1 = (bf16[32,2,4,2,2048]{4,3,2,1,0:T(2,128)(2,1)}, bf16[32,2,4,2,2048]{4,3,2,1,0:T(2,128)(2,1)}, u32[]{:S(2)}, u32[]{:S(2)}) collective-permute-start(bf16[32,2,4,2,2048]{4,3,2,1,0:T(2,128)(2,1)} %cut.2.rest_0_), channel_id=1, source_target_pairs={{0,4},{2,6},{4,8},{6,10},{8,12},{10,14},{1,5},{3,7},{5,9},{7,11},{... | collective-permute-start | bytes 6291464 | tf_op jit(solution)/shard_map/ppermute | solution.py:481
  10.3 22.6 %collective-permute-done.3.refs_0_ = bf16[32,4,2,2048]{3,2,1,0:T(2,128)(2,1)S(1)} collective-permute-done((bf16[32,4,2,2048]{3,2,1,0:T(2,128)(2,1)}, bf16[32,4,2,2048]{3,2,1,0:T(2,128)(2,1)S(1)}, u32[]{:S(2)}, u32[]{:S(2)}) %collective-permute-start.3) | collective-permute-done | bytes 1048608 | tf_op jit(solution)/shard_map/ppermute | solution.py:478
  40.4 14.9 %collective-permute-done.refs_0_ = bf16[32,4,2,2048]{3,2,1,0:T(2,128)(2,1)} collective-permute-done((bf16[32,4,2,2048]{3,2,1,0:T(2,128)(2,1)}, bf16[32,4,2,2048]{3,2,1,0:T(2,128)(2,1)}, u32[]{:S(2)}, u32[]{:S(2)}) %collective-permute-start) | collective-permute-done | bytes 1048608 | tf_op jit(solution)/shard_map/ppermute | solution.py:478
  55.5 2.8 %copy.21 = bf16[32,4,2,2048]{3,0,2,1:T(8,128)(2,1)} copy(bf16[32,4,2,2048]{3,2,1,0:T(2,128)(2,1)} %after.3) | data formatting | bytes 2097152 | tf_op jit(solution)/shard_map/after/pallas_call | solution.py:77
  58.3 4.3 %collective-permute-start.2 = (bf16[4,2,32,2048]{3,2,1,0:T(8,128)(2,1)}, bf16[4,2,32,2048]{3,2,1,0:T(8,128)(2,1)}, u32[]{:S(2)}, u32[]{:S(2)}) collective-permute-start(bf16[4,2,32,2048]{3,2,1,0:T(8,128)(2,1)} %bitcast.27.other), channel_id=1, source_target_pairs={{0,4},{2,6},{4,8},{6,10},{8,12},{10,14},{1,5},{3,7},{5,9},{7,11},{... | collective-permute-start | bytes 3145736 | tf_op jit(solution)/shard_map/ppermute | solution.py:481
  65.8 4.1 %copy.18 = bf16[32,2,4,2,2048]{4,0,3,2,1:T(8,128)(2,1)} copy(bf16[32,2,4,2,2048]{4,3,2,1,0:T(2,128)(2,1)} %after.4) | data formatting | bytes 4194304 | tf_op jit(solution)/shard_map/after/pallas_call | solution.py:77
  69.8 2.9 %collective-permute-done.5.rest_0_ = bf16[16,256]{1,0:T(8,128)(2,1)S(1)} collective-permute-done((bf16[16,256]{1,0:T(8,128)(2,1)S(1)}, bf16[16,256]{1,0:T(8,128)(2,1)S(1)}, u32[]{:S(2)}, u32[]{:S(2)}) %collective-permute-start.5) | collective-permute-done | bytes 8224 | tf_op jit(solution)/shard_map/ppermute | solution.py:494
  77.4 3.0 %collective-permute-start.11 = (bf16[7,2,32,1024]{3,2,1,0:T(8,128)(2,1)}, bf16[7,2,32,1024]{3,2,1,0:T(8,128)(2,1)S(1)}, u32[]{:S(2)}, u32[]{:S(2)}) collective-permute-start(bf16[7,2,32,1024]{3,2,1,0:T(8,128)(2,1)} %onward.4.rest_0_), channel_id=1, source_target_pairs={{4,8},{6,10},{8,12},{10,14},{5,9},{7,11},{9,13},{11,15},{20,24},{2... | collective-permute-start | bytes 2752520 | tf_op jit(solution)/shard_map/ppermute | solution.py:481
  92.6 4.2 %collective-permute-done.2.other_back.rest_5_.rest_3_ = bf16[4,2,32,2048]{3,2,1,0:T(8,128)(2,1)} collective-permute-done((bf16[4,2,32,2048]{3,2,1,0:T(8,128)(2,1)}, bf16[4,2,32,2048]{3,2,1,0:T(8,128)(2,1)}, u32[]{:S(2)}, u32[]{:S(2)}) %collective-permute-start.2) | collective-permute-done | bytes 1048608 | tf_op jit(solution)/shard_map/ppermute | solution.py:481
  96.8 2.9 %onward.6.rest_2_ = bf16[7,2,32,1280]{3,2,1,0:T(8,128)(2,1)} custom-call(s32[2]{0:T(128)} %pad_add_fusion.rest_1_.place, bf16[2,4,2,32,2048]{4,3,2,1,0:T(8,128)(2,1)} %bitcast.30, bf16[4,2,32,2048]{3,2,1,0:T(8,128)(2,1)} %collective-permute-done.2.other_back.rest_5_.rest_3_), custom_call_target="tpu_custom_call" | custom-call | bytes 9900000 | tf_op jit(solution)/shard_map/onward/pallas_call | solution.py:295
  99.7 3.0 %collective-permute-start.9 = (bf16[7,2,32,1280]{3,2,1,0:T(8,128)(2,1)}, bf16[7,2,32,1280]{3,2,1,0:T(8,128)(2,1)}, u32[]{:S(2)}, u32[]{:S(2)}) collective-permute-start(bf16[7,2,32,1280]{3,2,1,0:T(8,128)(2,1)} %onward.6.rest_2_), channel_id=1, source_target_pairs={{4,8},{6,10},{8,12},{10,14},{5,9},{7,11},{9,13},{11,15},{20,24},{2... | collective-permute-start | bytes 3440648 | tf_op jit(solution)/shard_map/ppermute | solution.py:481
  108.8 7.9 %near.3.partial = f32[8,2,32,2048]{3,2,1,0:T(8,128)} custom-call(s32[2]{0:T(128)} %pad_add_fusion.rest_1_.place, f32[16,8,2048]{2,1,0:T(8,128)} %broadcast_in_dim.2.taps, bf16[2,4,2,32,2048]{4,3,2,1,0:T(8,128)(2,1)} %bitcast.34, bf16[4,2,32,2048]{3,2,1,0:T(8,128)(2,1)} %bitcast.37, bf16[2,4,2,32,2048]{4,3,2,1,0:T(8,128)(2,1)} %bitcast.31, ...), custom_call_target="tpu_custom_call" | custom-call | bytes 26400000 | tf_op jit(solution)/shard_map/near/pallas_call | solution.py:221
  117.6 3.9 %far.4 = (bf16[4,2,32,1024]{3,2,1,0:T(8,128)(2,1)}, bf16[4,2,32,1024]{3,2,1,0:T(8,128)(2,1)}) custom-call(s32[2]{0:T(128)} %pad_add_fusion.rest_1_.place, f32[16,8,2048]{2,1,0:T(8,128)} %broadcast_in_dim.2.taps, f32[8,2,32,2048]{3,2,1,0:T(8,128)} %near.3.partial, bf16[7,2,32,1024]{3,2,1,0:T(8,128)(2,1)} %copy-done.5), custom_call_target="tpu_custom_call" | custom-call | bytes 3300000 | tf_op jit(solution)/shard_map/far/pallas_call | solution.py:247
  125.4 7.8 %near.2.rest_1_.partial = f32[8,2,32,2048]{3,2,1,0:T(8,128)} custom-call(s32[2]{0:T(128)} %pad_add_fusion.rest_1_.place, f32[16,8,2048]{2,1,0:T(8,128)} %broadcast_in_dim.2.taps, bf16[2,4,2,32,2048]{4,3,2,1,0:T(8,128)(2,1)} %bitcast.35, bf16[4,2,32,2048]{3,2,1,0:T(8,128)(2,1)} %bitcast.27.other, bf16[2,4,2,32,2048]{4,3,2,1,0:T(8,128)(2,1)} %bitcast.33, ...), custom_call_target="tpu_custom_call" | custom-call | bytes 26400000 | tf_op jit(solution)/shard_map/near/pallas_call | solution.py:221
  133.3 2.8 %collective-permute-done.10.far = bf16[7,2,32,1024]{3,2,1,0:T(8,128)(2,1)} collective-permute-done((bf16[7,2,32,1024]{3,2,1,0:T(8,128)(2,1)}, bf16[7,2,32,1024]{3,2,1,0:T(8,128)(2,1)}, u32[]{:S(2)}, u32[]{:S(2)}) %collective-permute-start.10) | collective-permute-done | bytes 917536 | tf_op jit(solution)/shard_map/ppermute | solution.py:481
  136.1 3.9 %far.5 = (bf16[4,2,32,1024]{3,2,1,0:T(8,128)(2,1)}, bf16[4,2,32,1024]{3,2,1,0:T(8,128)(2,1)}) custom-call(s32[2]{0:T(128)} %pad_add_fusion.rest_1_.place, f32[16,8,2048]{2,1,0:T(8,128)} %broadcast_in_dim.2.taps, f32[8,2,32,2048]{3,2,1,0:T(8,128)} %near.3.partial, bf16[7,2,32,1024]{3,2,1,0:T(8,128)(2,1)} %collective-permute-done.10.far, ...), custom_call_target="tpu_custom_call" | custom-call | bytes 3300000 | tf_op jit(solution)/shard_map/far/pallas_call | solution.py:247
  141.3 3.0 %collective-permute-start.15 = (bf16[4,2,32,1024]{3,2,1,0:T(8,128)(2,1)}, bf16[4,2,32,1024]{3,2,1,0:T(8,128)(2,1)}, u32[]{:S(2)}, u32[]{:S(2)}) collective-permute-start(bf16[4,2,32,1024]{3,2,1,0:T(8,128)(2,1)} %get-tuple-element.20.refs_0_), channel_id=1, source_target_pairs={{0,1},{1,0},{2,3},{3,2},{4,5},{5,4},{6,7},{7,6},{8,9},{9,8},{10,11... | collective-permute-start | bytes 1572872 | tf_op jit(solution)/shard_map/ppermute | solution.py:484
  144.2 3.2 %collective-permute-start.14 = (bf16[7,2,32,768]{3,2,1,0:T(8,128)(2,1)S(1)}, bf16[7,2,32,768]{3,2,1,0:T(8,128)(2,1)}, u32[]{:S(2)}, u32[]{:S(2)}) collective-permute-start(bf16[7,2,32,768]{3,2,1,0:T(8,128)(2,1)S(1)} %copy-done.3), channel_id=1, source_target_pairs={{4,8},{6,10},{8,12},{10,14},{5,9},{7,11},{9,13},{11,15},{20,24},{2... | collective-permute-start | bytes 2064392 | tf_op jit(solution)/shard_map/ppermute | solution.py:481
  147.8 12.9 %collective-permute-done.9.far = bf16[7,2,32,1280]{3,2,1,0:T(8,128)(2,1)} collective-permute-done((bf16[7,2,32,1280]{3,2,1,0:T(8,128)(2,1)}, bf16[7,2,32,1280]{3,2,1,0:T(8,128)(2,1)}, u32[]{:S(2)}, u32[]{:S(2)}) %collective-permute-start.9) | collective-permute-done | bytes 1146912 | tf_op jit(solution)/shard_map/ppermute | solution.py:481
  163.4 4.4 %far.6 = (bf16[4,2,32,1280]{3,2,1,0:T(8,128)(2,1)}, bf16[4,2,32,1280]{3,2,1,0:T(8,128)(2,1)}) custom-call(s32[2]{0:T(128)} %pad_add_fusion.rest_1_.place, f32[16,8,2048]{2,1,0:T(8,128)} %broadcast_in_dim.2.taps, f32[8,2,32,2048]{3,2,1,0:T(8,128)} %near.2.rest_1_.partial, bf16[7,2,32,1280]{3,2,1,0:T(8,128)(2,1)} %collective-permute-done.9.far, ...), custom_call_target="tpu_custom_call" | custom-call | bytes 3300000 | tf_op jit(solution)/shard_map/far/pallas_call | solution.py:247
  169.0 9.0 %beams.2.rest_0_.refs_10_ = f32[8,512,256]{2,1,0:T(8,128)} custom-call(s32[2]{0:T(128)} %pad_add_fusion.rest_1_.place, bf16[4,2,32,1024]{3,2,1,0:T(8,128)(2,1)} %get-tuple-element.20.refs_0_, bf16[4,2,32,1024]{3,2,1,0:T(8,128)(2,1)} %get-tuple-element.21.refs_1_, bf16[4,2,32,1024]{3,2,1,0:T(8,128)(2,1)} %collective-permute-done.12.rest_0_.refs_2_, ...), custom_call_target="tpu_custom_call" | custom-call | tf_op jit(solution)/shard_map/beams/pallas_call | solution.py:448
  178.0 3.6 %far.7 = (bf16[4,2,32,768]{3,2,1,0:T(8,128)(2,1)}, bf16[4,2,32,768]{3,2,1,0:T(8,128)(2,1)}) custom-call(s32[2]{0:T(128)} %pad_add_fusion.rest_1_.place, f32[16,8,2048]{2,1,0:T(8,128)} %broadcast_in_dim.2.taps, f32[8,2,32,2048]{3,2,1,0:T(8,128)} %near.2.rest_1_.partial, bf16[7,2,32,768]{3,2,1,0:T(8,128)(2,1)} %collective-permute-done.14.far, ...), custom_call_target="tpu_custom_call" | custom-call | bytes 3300000 | tf_op jit(solution)/shard_map/far/pallas_call | solution.py:247
  185.3 6.7 %collective-permute-done.20.refs_3_ = bf16[4,2,32,768]{3,2,1,0:T(8,128)(2,1)S(1)} collective-permute-done((bf16[4,2,32,768]{3,2,1,0:T(8,128)(2,1)}, bf16[4,2,32,768]{3,2,1,0:T(8,128)(2,1)S(1)}, u32[]{:S(2)}, u32[]{:S(2)}) %collective-permute-start.20) | collective-permute-done | bytes 393248 | tf_op jit(solution)/shard_map/ppermute | solution.py:478
  195.2 10.5 %beams.3 = f32[1024,2,4,128]{3,2,1,0:T(4,128)} custom-call(s32[2]{0:T(128)} %pad_add_fusion.rest_1_.place, bf16[4,2,32,1280]{3,2,1,0:T(8,128)(2,1)} %get-tuple-element.19.refs_10_.refs_0_, bf16[4,2,32,768]{3,2,1,0:T(8,128)(2,1)} %get-tuple-element.22.refs_1_, bf16[4,2,32,1280]{3,2,1,0:T(8,128)(2,1)} %collective-permute-done.19.refs_2_, ...), custom_call_target="tpu_custom_call" | custom-call | tf_op jit(solution)/shard_map/beams/pallas_call | solution.py:448
  (98 shorter events, 57.9 us)
Async XLA Ops:
  2.4 55.8 %collective-permute-start.1 = (bf16[32,2,4,2,2048]{4,3,2,1,0:T(2,128)(2,1)}, bf16[32,2,4,2,2048]{4,3,2,1,0:T(2,128)(2,1)}, u32[]{:S(2)}, u32[]{:S(2)}) collective-permute-start(bf16[32,2,4,2,2048]{4,3,2,1,0:T(2,128)(2,1)} %cut.2.rest_0_), channel_id=1, source_target_pairs={{0,4},{2,6},{4,8},{6,10},{8,12},{10,14},{1,5},{3,7},{5,9},{7,11},{... | collective-permute-start | bytes 6291464 | tf_op jit(solution)/shard_map/ppermute | solution.py:481
  8.7 24.1 %collective-permute-start.3 = (bf16[32,4,2,2048]{3,2,1,0:T(2,128)(2,1)}, bf16[32,4,2,2048]{3,2,1,0:T(2,128)(2,1)S(1)}, u32[]{:S(2)}, u32[]{:S(2)}) collective-permute-start(bf16[32,4,2,2048]{3,2,1,0:T(2,128)(2,1)} %get-tuple-element.16), channel_id=1, source_target_pairs={{0,2},{2,0},{4,6},{6,4},{8,10},{10,8},{12,14},{14,12},{1,3},{3,1},... | collective-permute-start | bytes 3145736 | tf_op jit(solution)/shard_map/ppermute | solution.py:478
  10.1 45.2 %collective-permute-start = (bf16[32,4,2,2048]{3,2,1,0:T(2,128)(2,1)}, bf16[32,4,2,2048]{3,2,1,0:T(2,128)(2,1)}, u32[]{:S(2)}, u32[]{:S(2)}) collective-permute-start(bf16[32,4,2,2048]{3,2,1,0:T(2,128)(2,1)} %get-tuple-element.15), channel_id=1, source_target_pairs={{0,2},{2,0},{4,6},{6,4},{8,10},{10,8},{12,14},{14,12},{1,3},{3,1},... | collective-permute-start | bytes 3145736 | tf_op jit(solution)/shard_map/ppermute | solution.py:478
  35.6 38.5 %collective-permute-start.4 = (bf16[4,2,32,2048]{3,2,1,0:T(8,128)(2,1)S(1)}, bf16[4,2,32,2048]{3,2,1,0:T(8,128)(2,1)}, u32[]{:S(2)}, u32[]{:S(2)}) collective-permute-start(bf16[4,2,32,2048]{3,2,1,0:T(8,128)(2,1)S(1)} %bitcast.36), channel_id=1, source_target_pairs={{0,4},{2,6},{4,8},{6,10},{8,12},{10,14},{1,5},{3,7},{5,9},{7,11},{... | collective-permute-start | bytes 3145736 | tf_op jit(solution)/shard_map/ppermute | solution.py:481
  37.6 35.1 %collective-permute-start.5 = (bf16[16,256]{1,0:T(8,128)(2,1)S(1)}, bf16[16,256]{1,0:T(8,128)(2,1)S(1)}, u32[]{:S(2)}, u32[]{:S(2)}) collective-permute-start(bf16[16,256]{1,0:T(8,128)(2,1)S(1)} %get-tuple-element.26), channel_id=1, source_target_pairs={{0,4},{2,6},{4,0},{6,2},{8,12},{10,14},{12,8},{14,10},{1,5},{3,7},... | collective-permute-start | bytes 24584 | tf_op jit(solution)/shard_map/ppermute | solution.py:494
  37.7 35.8 %collective-permute-start.6 = (bf16[16,256]{1,0:T(8,128)(2,1)S(1)}, bf16[16,256]{1,0:T(8,128)(2,1)S(1)}, u32[]{:S(2)}, u32[]{:S(2)}) collective-permute-start(bf16[16,256]{1,0:T(8,128)(2,1)S(1)} %get-tuple-element.26), channel_id=1, source_target_pairs={{0,8},{2,10},{4,12},{6,14},{8,0},{10,2},{12,4},{14,6},{1,9},{3,11}... | collective-permute-start | bytes 24584 | tf_op jit(solution)/shard_map/ppermute | solution.py:494
  55.3 18.8 %collective-permute-start.7 = (bf16[16,256]{1,0:T(8,128)(2,1)S(1)}, bf16[16,256]{1,0:T(8,128)(2,1)S(1)}, u32[]{:S(2)}, u32[]{:S(2)}) collective-permute-start(bf16[16,256]{1,0:T(8,128)(2,1)S(1)} %get-tuple-element.26), channel_id=1, source_target_pairs={{0,12},{2,14},{4,8},{6,10},{8,4},{10,6},{12,0},{14,2},{1,13},{3,15... | collective-permute-start | bytes 24584 | tf_op jit(solution)/shard_map/ppermute | solution.py:494
  58.3 38.5 %collective-permute-start.2 = (bf16[4,2,32,2048]{3,2,1,0:T(8,128)(2,1)}, bf16[4,2,32,2048]{3,2,1,0:T(8,128)(2,1)}, u32[]{:S(2)}, u32[]{:S(2)}) collective-permute-start(bf16[4,2,32,2048]{3,2,1,0:T(8,128)(2,1)} %bitcast.27.other), channel_id=1, source_target_pairs={{0,4},{2,6},{4,8},{6,10},{8,12},{10,14},{1,5},{3,7},{5,9},{7,11},{... | collective-permute-start | bytes 3145736 | tf_op jit(solution)/shard_map/ppermute | solution.py:481
  77.4 39.2 %collective-permute-start.11 = (bf16[7,2,32,1024]{3,2,1,0:T(8,128)(2,1)}, bf16[7,2,32,1024]{3,2,1,0:T(8,128)(2,1)S(1)}, u32[]{:S(2)}, u32[]{:S(2)}) collective-permute-start(bf16[7,2,32,1024]{3,2,1,0:T(8,128)(2,1)} %onward.4.rest_0_), channel_id=1, source_target_pairs={{4,8},{6,10},{8,12},{10,14},{5,9},{7,11},{9,13},{11,15},{20,24},{2... | collective-permute-start | bytes 2752520 | tf_op jit(solution)/shard_map/ppermute | solution.py:481
  84.6 18.1 %collective-permute-start.8 = (bf16[64,256]{1,0:T(8,128)(2,1)}, bf16[64,256]{1,0:T(8,128)(2,1)}, u32[]{:S(2)}, u32[]{:S(2)}) collective-permute-start(bf16[64,256]{1,0:T(8,128)(2,1)} %pad_maximum_fusion), channel_id=1, source_target_pairs={{0,2},{2,0},{4,6},{6,4},{8,10},{10,8},{12,14},{14,12},{1,3},{3,1},... | collective-permute-start | bytes 98312 | tf_op jit(solution)/shard_map/ppermute | solution.py:478
  88.6 47.5 %collective-permute-start.10 = (bf16[7,2,32,1024]{3,2,1,0:T(8,128)(2,1)}, bf16[7,2,32,1024]{3,2,1,0:T(8,128)(2,1)}, u32[]{:S(2)}, u32[]{:S(2)}) collective-permute-start(bf16[7,2,32,1024]{3,2,1,0:T(8,128)(2,1)} %onward.5.rest_1_), channel_id=1, source_target_pairs={{4,8},{6,10},{8,12},{10,14},{5,9},{7,11},{9,13},{11,15},{20,24},{2... | collective-permute-start | bytes 2752520 | tf_op jit(solution)/shard_map/ppermute | solution.py:481
  99.7 61.0 %collective-permute-start.9 = (bf16[7,2,32,1280]{3,2,1,0:T(8,128)(2,1)}, bf16[7,2,32,1280]{3,2,1,0:T(8,128)(2,1)}, u32[]{:S(2)}, u32[]{:S(2)}) collective-permute-start(bf16[7,2,32,1280]{3,2,1,0:T(8,128)(2,1)} %onward.6.rest_2_), channel_id=1, source_target_pairs={{4,8},{6,10},{8,12},{10,14},{5,9},{7,11},{9,13},{11,15},{20,24},{2... | collective-permute-start | bytes 3440648 | tf_op jit(solution)/shard_map/ppermute | solution.py:481
  121.5 14.6 %collective-permute-start.12 = (bf16[4,2,32,1024]{3,2,1,0:T(8,128)(2,1)}, bf16[4,2,32,1024]{3,2,1,0:T(8,128)(2,1)}, u32[]{:S(2)}, u32[]{:S(2)}) collective-permute-start(bf16[4,2,32,1024]{3,2,1,0:T(8,128)(2,1)} %get-tuple-element.17), channel_id=1, source_target_pairs={{0,2},{2,0},{4,6},{6,4},{8,10},{10,8},{12,14},{14,12},{1,3},{3,1},... | collective-permute-start | bytes 1572872 | tf_op jit(solution)/shard_map/ppermute | solution.py:478
  140.0 23.4 %collective-permute-start.13 = (bf16[4,2,32,1024]{3,2,1,0:T(8,128)(2,1)}, bf16[4,2,32,1024]{3,2,1,0:T(8,128)(2,1)}, u32[]{:S(2)}, u32[]{:S(2)}) collective-permute-start(bf16[4,2,32,1024]{3,2,1,0:T(8,128)(2,1)} %get-tuple-element.18), channel_id=1, source_target_pairs={{0,2},{2,0},{4,6},{6,4},{8,10},{10,8},{12,14},{14,12},{1,3},{3,1},... | collective-permute-start | bytes 1572872 | tf_op jit(solution)/shard_map/ppermute | solution.py:478
  141.3 26.5 %collective-permute-start.15 = (bf16[4,2,32,1024]{3,2,1,0:T(8,128)(2,1)}, bf16[4,2,32,1024]{3,2,1,0:T(8,128)(2,1)}, u32[]{:S(2)}, u32[]{:S(2)}) collective-permute-start(bf16[4,2,32,1024]{3,2,1,0:T(8,128)(2,1)} %get-tuple-element.20.refs_0_), channel_id=1, source_target_pairs={{0,1},{1,0},{2,3},{3,2},{4,5},{5,4},{6,7},{7,6},{8,9},{9,8},{10,11... | collective-permute-start | bytes 1572872 | tf_op jit(solution)/shard_map/ppermute | solution.py:484
  144.2 33.8 %collective-permute-start.14 = (bf16[7,2,32,768]{3,2,1,0:T(8,128)(2,1)S(1)}, bf16[7,2,32,768]{3,2,1,0:T(8,128)(2,1)}, u32[]{:S(2)}, u32[]{:S(2)}) collective-permute-start(bf16[7,2,32,768]{3,2,1,0:T(8,128)(2,1)S(1)} %copy-done.3), channel_id=1, source_target_pairs={{4,8},{6,10},{8,12},{10,14},{5,9},{7,11},{9,13},{11,15},{20,24},{2... | collective-permute-start | bytes 2064392 | tf_op jit(solution)/shard_map/ppermute | solution.py:481
  147.4 21.5 %collective-permute-start.16 = (bf16[4,2,32,1024]{3,2,1,0:T(8,128)(2,1)}, bf16[4,2,32,1024]{3,2,1,0:T(8,128)(2,1)}, u32[]{:S(2)}, u32[]{:S(2)}) collective-permute-start(bf16[4,2,32,1024]{3,2,1,0:T(8,128)(2,1)} %get-tuple-element.21.refs_1_), channel_id=1, source_target_pairs={{0,1},{1,0},{2,3},{3,2},{4,5},{5,4},{6,7},{7,6},{8,9},{9,8},{10,11... | collective-permute-start | bytes 1572872 | tf_op jit(solution)/shard_map/ppermute | solution.py:484
  160.7 8.3 %collective-permute-start.17 = (bf16[4,2,32,1024]{3,2,1,0:T(8,128)(2,1)}, bf16[4,2,32,1024]{3,2,1,0:T(8,128)(2,1)}, u32[]{:S(2)}, u32[]{:S(2)}) collective-permute-start(bf16[4,2,32,1024]{3,2,1,0:T(8,128)(2,1)} %collective-permute-done.12.rest_0_.refs_2_), channel_id=1, source_target_pairs={{0,1},{1,0},{2,3},{3,2},{4,5},{5,4},{6,7},{7,6},{8,9},{9,8},{10,11... | collective-permute-start | bytes 1572872 | tf_op jit(solution)/shard_map/ppermute | solution.py:484
  163.4 5.6 %collective-permute-start.18 = (bf16[4,2,32,1024]{3,2,1,0:T(8,128)(2,1)}, bf16[4,2,32,1024]{3,2,1,0:T(8,128)(2,1)}, u32[]{:S(2)}, u32[]{:S(2)}) collective-permute-start(bf16[4,2,32,1024]{3,2,1,0:T(8,128)(2,1)} %collective-permute-done.13.rest_0_.refs_3_), channel_id=1, source_target_pairs={{0,1},{1,0},{2,3},{3,2},{4,5},{5,4},{6,7},{7,6},{8,9},{9,8},{10,11... | collective-permute-start | bytes 1572872 | tf_op jit(solution)/shard_map/ppermute | solution.py:484
  167.7 16.1 %collective-permute-start.19 = (bf16[4,2,32,1280]{3,2,1,0:T(8,128)(2,1)}, bf16[4,2,32,1280]{3,2,1,0:T(8,128)(2,1)}, u32[]{:S(2)}, u32[]{:S(2)}) collective-permute-start(bf16[4,2,32,1280]{3,2,1,0:T(8,128)(2,1)} %get-tuple-element.23), channel_id=1, source_target_pairs={{0,2},{2,0},{4,6},{6,4},{8,10},{10,8},{12,14},{14,12},{1,3},{3,1},... | collective-permute-start | bytes 1966088 | tf_op jit(solution)/shard_map/ppermute | solution.py:478
  181.6 10.4 %collective-permute-start.20 = (bf16[4,2,32,768]{3,2,1,0:T(8,128)(2,1)}, bf16[4,2,32,768]{3,2,1,0:T(8,128)(2,1)S(1)}, u32[]{:S(2)}, u32[]{:S(2)}) collective-permute-start(bf16[4,2,32,768]{3,2,1,0:T(8,128)(2,1)} %get-tuple-element.24), channel_id=1, source_target_pairs={{0,2},{2,0},{4,6},{6,4},{8,10},{10,8},{12,14},{14,12},{1,3},{3,1},... | collective-permute-start | bytes 1179656 | tf_op jit(solution)/shard_map/ppermute | solution.py:478
  181.9 11.7 %collective-permute-start.21 = (bf16[4,2,32,1280]{3,2,1,0:T(8,128)(2,1)S(1)}, bf16[4,2,32,1280]{3,2,1,0:T(8,128)(2,1)S(1)}, u32[]{:S(2)}, u32[]{:S(2)}) collective-permute-start(bf16[4,2,32,1280]{3,2,1,0:T(8,128)(2,1)S(1)} %copy-done.4), channel_id=1, source_target_pairs={{0,1},{1,0},{2,3},{3,2},{4,5},{5,4},{6,7},{7,6},{8,9},{9,8},{10,11... | collective-permute-start | bytes 1966088 | tf_op jit(solution)/shard_map/ppermute | solution.py:484
  183.9 10.6 %collective-permute-start.23 = (bf16[4,2,32,1280]{3,2,1,0:T(8,128)(2,1)}, bf16[4,2,32,1280]{3,2,1,0:T(8,128)(2,1)}, u32[]{:S(2)}, u32[]{:S(2)}) collective-permute-start(bf16[4,2,32,1280]{3,2,1,0:T(8,128)(2,1)} %collective-permute-done.19.refs_2_), channel_id=1, source_target_pairs={{0,1},{1,0},{2,3},{3,2},{4,5},{5,4},{6,7},{7,6},{8,9},{9,8},{10,11... | collective-permute-start | bytes 1966088 | tf_op jit(solution)/shard_map/ppermute | solution.py:484
  185.3 9.2 %collective-permute-start.22 = (bf16[4,2,32,768]{3,2,1,0:T(8,128)(2,1)}, bf16[4,2,32,768]{3,2,1,0:T(8,128)(2,1)S(1)}, u32[]{:S(2)}, u32[]{:S(2)}) collective-permute-start(bf16[4,2,32,768]{3,2,1,0:T(8,128)(2,1)} %get-tuple-element.22.refs_1_), channel_id=1, source_target_pairs={{0,1},{1,0},{2,3},{3,2},{4,5},{5,4},{6,7},{7,6},{8,9},{9,8},{10,11... | collective-permute-start | bytes 1179656 | tf_op jit(solution)/shard_map/ppermute | solution.py:484
  (18 other events, 181.6 us)

commit v13 on v12

--- a/solution.py
+++ b/solution.py
@@ -509,34 +509,34 @@
     table = jnp.asarray(dft_tables(samples))
     taps = jnp.broadcast_to(filter_taps[:, None, :], (history + 1, 8, samples))
 
-    parts_of = [(samples // 2, samples // 2), (5 * samples // 8, 3 * samples // 8)]
-    chunks = [(pol, sum(sizes[:i]), size) for pol, sizes in enumerate(parts_of) for i, size in enumerate(sizes)]
+    large, small = 5 * samples // 8, 3 * samples // 8
+    chunks = [(0, 0, large), (1, 0, large), (0, large, small), (1, large, small)]
     other_back = [hop(block) for block in other]
     further = []
     for pol, low, size in chunks:
-        gates = [] if further else shards[1:]
+        gates = shards[1:] if len(further) == 1 else further[-1:]
         further.append(onward(place, own_back, other_back[pol], pol, low, size, gates))
     shards = jnp.concatenate(shards)
     far = [hop(block, 2) for block in further]
     weights = beam_weights(jnp.concatenate([shards, pair(shards)]), ordered(index), ordered(use_mask), [])
     partial = []
     for pol in range(pols):
-        gates = further[: 2 * pol + 2] + [weights] + other_back[1:]
+        gates = further[: 2 * pol + 2] + [weights]
         partial.append(near_filter(place, taps, own, other[pol], own_back, other_back[pol], pol, gates))
     keeps, sents, power = [], [], None
 
     def power_of(pol, earlier, later=()):
-        mine, pairs = keeps[2 * pol : 2 * pol + 2], sents[2 * pol : 2 * pol + 2]
+        mine, pairs = keeps[pol::2], sents[pol::2]
         sources = mine + pairs + [swap(block) for block in mine + pairs]
         return beam_power(place, sources, 2, table, weights, earlier, samples // CORES, later)
 
     for k, (pol, low, size) in enumerate(chunks):
-        gates = {0: [], 1: [*sents[:1], partial[1]], 2: sents[1:2], 3: [power]}[k]
+        gates = {0: [], 1: [*sents[:1], partial[1]], 2: keeps[1:2], 3: [*keeps[2:3], *sents[1:2]]}[k]
         keep, send = far_filter(place, taps, partial[pol], far[k], low, size, gates)
         keeps.append(keep)
         sents.append(pair(send))
-        if k == 2:
-            power = power_of(0, None, [keep])
+    power = power_of(0, None, keeps[-1:])
+    sents[-1] = after(sents[-1], power)
     power = power_of(1, power)
     return jnp.moveaxis(power, 1, 2).reshape(power.shape[0], power.shape[2], -1)
 

time: 207 us -> 208 us (level)
  waiting for transfers between devices: 69.4 us -> 72.9 us
  other arithmetic: 4.18 us -> 1.37 us
    ppermute x3, waiting for transfers between devices: 4.32 us -> 11.5 us  [body(): lax.ppermute(shard, 'tm', [(i, i ^ apart) for i in range(time_devices)])]
    ppermute x7, waiting for transfers between devices: 45.1 us -> 40.2 us  [pair(): return lax.ppermute(block, 'tm', [(i, i ^ 1) for i in range(time_devices)])]
    transpose x3, other arithmetic: 2.18 us -> 0.02 us  [ordered(): rows = flipped(rows.swapaxes(0, 1), side).swapaxes(0, 1)]
    unnamed x38 -> x34, local copies, waits for them, and re-layouts: 6.91 us -> 6.94 us
  transfers between devices with their start and end apart: 25 -> 25, of which waited for: 10 -> 9; matrix products, arithmetic and copies ran while one was open for 10% -> 9% of each run, Pallas kernels for 28% -> 28%
where the time goes in v13:
time: 208 us; the launch traced here: 206 us
  waiting for transfers between devices  72.9 us (35%)
  Pallas kernels  69.8 us (34%)
  starting transfers between devices  38.9 us (19%)
  local copies, waits for them, and re-layouts  22.1 us (11%)
    ppermute x7, waiting for transfers between devices, pair(): return lax.ppermute(block, 'tm', [(i, i ^ 1) for i in range(time_devices)])  40.2 us
    pallas_call x2, Pallas kernels, beam_power(): pl.pallas_call(functools.partial(beam_kernel, len(sources), ranges, len(l...  19.6 us
    ppermute x7, waiting for transfers between devices, hop(): lax.ppermute(block, 'tm', [(i, i + 2) for i in range(skip, time_devices -...  19.5 us
    ppermute x7, starting transfers between devices, hop(): lax.ppermute(block, 'tm', [(i, i + 2) for i in range(skip, time_devices -...  18.7 us
    pallas_call x4, Pallas kernels, far_filter(): pl.pallas_call(far_kernel, out_shape=(shape, shape), grid_spec=pltpu.Pref...  15.9 us
    pallas_call x2, Pallas kernels, near_filter(): pl.pallas_call(near_kernel, out_shape=jax.ShapeDtypeStruct((2 * frames, p...  15.7 us
    ppermute x3, waiting for transfers between devices, body(): lax.ppermute(shard, 'tm', [(i, i ^ apart) for i in range(time_devices)])  11.5 us
    pallas_call x4, Pallas kernels, onward(): pl.pallas_call(onward_kernel, out_shape=jax.ShapeDtypeStruct((depth, part...  11 us
  transfers between devices with their start and end apart: 25, of which 9 were waited for; matrix products, arithmetic and copies ran while one was open for 9% of the time, Pallas kernels for 28%

profile of v13, /device:TPU:17, one launch (start us, length us, event | category | flops | bytes accessed | tf_op | source)
XLA Modules:
  0.0 205.6 jit_solution(202838909840635622)
XLA Ops:
  2.4 3.2 %collective-permute-start.1 = (bf16[32,2,4,2,2048]{4,3,2,1,0:T(2,128)(2,1)}, bf16[32,2,4,2,2048]{4,3,2,1,0:T(2,128)(2,1)}, u32[]{:S(2)}, u32[]{:S(2)}) collective-permute-start(bf16[32,2,4,2,2048]{4,3,2,1,0:T(2,128)(2,1)} %cut.2.rest_0_), channel_id=1, source_target_pairs={{0,4},{2,6},{4,8},{6,10},{8,12},{10,14},{1,5},{3,7},{5,9},{7,11},{... | collective-permute-start | bytes 6291464 | tf_op jit(solution)/shard_map/ppermute | solution.py:481
  10.2 22.6 %collective-permute-done.3.refs_0_ = bf16[32,4,2,2048]{3,2,1,0:T(2,128)(2,1)S(1)} collective-permute-done((bf16[32,4,2,2048]{3,2,1,0:T(2,128)(2,1)}, bf16[32,4,2,2048]{3,2,1,0:T(2,128)(2,1)S(1)}, u32[]{:S(2)}, u32[]{:S(2)}) %collective-permute-start.3) | collective-permute-done | bytes 1048608 | tf_op jit(solution)/shard_map/ppermute | solution.py:478
  37.7 17.6 %collective-permute-done.refs_0_ = bf16[32,4,2,2048]{3,2,1,0:T(2,128)(2,1)S(1)} collective-permute-done((bf16[32,4,2,2048]{3,2,1,0:T(2,128)(2,1)}, bf16[32,4,2,2048]{3,2,1,0:T(2,128)(2,1)S(1)}, u32[]{:S(2)}, u32[]{:S(2)}) %collective-permute-start) | collective-permute-done | bytes 1048608 | tf_op jit(solution)/shard_map/ppermute | solution.py:478
  56.3 2.8 %copy.22 = bf16[32,4,2,2048]{3,0,2,1:T(8,128)(2,1)} copy(bf16[32,4,2,2048]{3,2,1,0:T(2,128)(2,1)} %after.4) | data formatting | bytes 2097152 | tf_op jit(solution)/shard_map/after/pallas_call | solution.py:77
  64.7 4.1 %copy.19 = bf16[32,2,4,2,2048]{4,0,3,2,1:T(8,128)(2,1)} copy(bf16[32,2,4,2,2048]{4,3,2,1,0:T(2,128)(2,1)} %after.5) | data formatting | bytes 4194304 | tf_op jit(solution)/shard_map/after/pallas_call | solution.py:77
  68.9 4.7 %collective-permute-done.4.other_back = bf16[4,2,32,2048]{3,2,1,0:T(8,128)(2,1)} collective-permute-done((bf16[4,2,32,2048]{3,2,1,0:T(8,128)(2,1)S(1)}, bf16[4,2,32,2048]{3,2,1,0:T(8,128)(2,1)}, u32[]{:S(2)}, u32[]{:S(2)}) %collective-permute-start.4) | collective-permute-done | bytes 1048608 | tf_op jit(solution)/shard_map/ppermute | solution.py:481
  76.4 3.2 %collective-permute-start.10 = (bf16[7,2,32,1280]{3,2,1,0:T(8,128)(2,1)}, bf16[7,2,32,1280]{3,2,1,0:T(8,128)(2,1)}, u32[]{:S(2)}, u32[]{:S(2)}) collective-permute-start(bf16[7,2,32,1280]{3,2,1,0:T(8,128)(2,1)} %onward.4.rest_0_), channel_id=1, source_target_pairs={{4,8},{6,10},{8,12},{10,14},{5,9},{7,11},{9,13},{11,15},{20,24},{2... | collective-permute-start | bytes 3440648 | tf_op jit(solution)/shard_map/ppermute | solution.py:481
  79.7 4.1 %copy.20 = bf16[32,2,4,2,2048]{4,0,3,2,1:T(8,128)(2,1)} copy(bf16[32,2,4,2,2048]{4,3,2,1,0:T(2,128)(2,1)} %cut.2.rest_0_) | data formatting | bytes 4194304 | tf_op jit(solution)/shard_map/cut/pallas_call | solution.py:124
  84.9 11.5 %collective-permute-done.7.rest_2_ = bf16[16,256]{1,0:T(8,128)(2,1)S(1)} collective-permute-done((bf16[16,256]{1,0:T(8,128)(2,1)S(1)}, bf16[16,256]{1,0:T(8,128)(2,1)S(1)}, u32[]{:S(2)}, u32[]{:S(2)}) %collective-permute-start.7) | collective-permute-done | bytes 8224 | tf_op jit(solution)/shard_map/ppermute | solution.py:494
  97.0 2.8 %onward.5.rest_0_.rest_1_ = bf16[7,2,32,1280]{3,2,1,0:T(8,128)(2,1)} custom-call(s32[2]{0:T(128)} %pad_add_fusion.rest_1_.place, bf16[2,4,2,32,2048]{4,3,2,1,0:T(8,128)(2,1)} %bitcast.29, bf16[4,2,32,2048]{3,2,1,0:T(8,128)(2,1)} %collective-permute-done.2.other_back, bf16[16,256]{1,0:T(8,128)(2,1)} %copy-done.11, bf16[16,256]{1,0:T(8,128)(2,1)} %copy-done.10, ...), custom_call_target="tpu_custom_call" | custom-call | bytes 9900000 | tf_op jit(solution)/shard_map/onward/pallas_call | solution.py:295
  99.9 3.2 %collective-permute-start.9 = (bf16[7,2,32,1280]{3,2,1,0:T(8,128)(2,1)}, bf16[7,2,32,1280]{3,2,1,0:T(8,128)(2,1)}, u32[]{:S(2)}, u32[]{:S(2)}) collective-permute-start(bf16[7,2,32,1280]{3,2,1,0:T(8,128)(2,1)} %onward.5.rest_0_.rest_1_), channel_id=1, source_target_pairs={{4,8},{6,10},{8,12},{10,14},{5,9},{7,11},{9,13},{11,15},{20,24},{2... | collective-permute-start | bytes 3440648 | tf_op jit(solution)/shard_map/ppermute | solution.py:481
  111.6 7.9 %near.3.partial = f32[8,2,32,2048]{3,2,1,0:T(8,128)} custom-call(s32[2]{0:T(128)} %pad_add_fusion.rest_1_.place, f32[16,8,2048]{2,1,0:T(8,128)} %broadcast_in_dim.2.taps, bf16[2,4,2,32,2048]{4,3,2,1,0:T(8,128)(2,1)} %bitcast.34, bf16[4,2,32,2048]{3,2,1,0:T(8,128)(2,1)} %bitcast.37, bf16[2,4,2,32,2048]{4,3,2,1,0:T(8,128)(2,1)} %bitcast.30, ...), custom_call_target="tpu_custom_call" | custom-call | bytes 26400000 | tf_op jit(solution)/shard_map/near/pallas_call | solution.py:221
  121.4 4.4 %far.4 = (bf16[4,2,32,1280]{3,2,1,0:T(8,128)(2,1)}, bf16[4,2,32,1280]{3,2,1,0:T(8,128)(2,1)}) custom-call(s32[2]{0:T(128)} %pad_add_fusion.rest_1_.place, f32[16,8,2048]{2,1,0:T(8,128)} %broadcast_in_dim.2.taps, f32[8,2,32,2048]{3,2,1,0:T(8,128)} %near.3.partial, bf16[7,2,32,1280]{3,2,1,0:T(8,128)(2,1)} %collective-permute-done.10.far), custom_call_target="tpu_custom_call" | custom-call | bytes 3300000 | tf_op jit(solution)/shard_map/far/pallas_call | solution.py:247
  129.7 3.0 %collective-permute-start.13 = (bf16[7,2,32,768]{3,2,1,0:T(8,128)(2,1)}, bf16[7,2,32,768]{3,2,1,0:T(8,128)(2,1)}, u32[]{:S(2)}, u32[]{:S(2)}) collective-permute-start(bf16[7,2,32,768]{3,2,1,0:T(8,128)(2,1)} %onward.6.rest_0_.rest_2_), channel_id=1, source_target_pairs={{4,8},{6,10},{8,12},{10,14},{5,9},{7,11},{9,13},{11,15},{20,24},{2... | collective-permute-start | bytes 2064392 | tf_op jit(solution)/shard_map/ppermute | solution.py:481
  137.5 7.8 %near.2.partial.rest_1_ = f32[8,2,32,2048]{3,2,1,0:T(8,128)} custom-call(s32[2]{0:T(128)} %pad_add_fusion.rest_1_.place, f32[16,8,2048]{2,1,0:T(8,128)} %broadcast_in_dim.2.taps, bf16[2,4,2,32,2048]{4,3,2,1,0:T(8,128)(2,1)} %bitcast.35, bf16[4,2,32,2048]{3,2,1,0:T(8,128)(2,1)} %bitcast.27.other, bf16[2,4,2,32,2048]{4,3,2,1,0:T(8,128)(2,1)} %bitcast.33, ...), custom_call_target="tpu_custom_call" | custom-call | bytes 26400000 | tf_op jit(solution)/shard_map/near/pallas_call | solution.py:221
  146.8 4.4 %far.5 = (bf16[4,2,32,1280]{3,2,1,0:T(8,128)(2,1)}, bf16[4,2,32,1280]{3,2,1,0:T(8,128)(2,1)}) custom-call(s32[2]{0:T(128)} %pad_add_fusion.rest_1_.place, f32[16,8,2048]{2,1,0:T(8,128)} %broadcast_in_dim.2.taps, f32[8,2,32,2048]{3,2,1,0:T(8,128)} %near.2.partial.rest_1_, bf16[7,2,32,1280]{3,2,1,0:T(8,128)(2,1)} %collective-permute-done.9.far, ...), custom_call_target="tpu_custom_call" | custom-call | bytes 3300000 | tf_op jit(solution)/shard_map/far/pallas_call | solution.py:247
  152.4 3.0 %collective-permute-start.17 = (bf16[4,2,32,1280]{3,2,1,0:T(8,128)(2,1)}, bf16[4,2,32,1280]{3,2,1,0:T(8,128)(2,1)}, u32[]{:S(2)}, u32[]{:S(2)}) collective-permute-start(bf16[4,2,32,1280]{3,2,1,0:T(8,128)(2,1)} %get-tuple-element.23.refs_0_), channel_id=1, source_target_pairs={{0,1},{1,0},{2,3},{3,2},{4,5},{5,4},{6,7},{7,6},{8,9},{9,8},{10,11... | collective-permute-start | bytes 1966088 | tf_op jit(solution)/shard_map/ppermute | solution.py:484
  155.4 5.3 %collective-permute-done.13.far = bf16[7,2,32,768]{3,2,1,0:T(8,128)(2,1)} collective-permute-done((bf16[7,2,32,768]{3,2,1,0:T(8,128)(2,1)}, bf16[7,2,32,768]{3,2,1,0:T(8,128)(2,1)}, u32[]{:S(2)}, u32[]{:S(2)}) %collective-permute-start.13) | collective-permute-done | bytes 688160 | tf_op jit(solution)/shard_map/ppermute | solution.py:481
  160.7 3.6 %far.6 = (bf16[4,2,32,768]{3,2,1,0:T(8,128)(2,1)}, bf16[4,2,32,768]{3,2,1,0:T(8,128)(2,1)}) custom-call(s32[2]{0:T(128)} %pad_add_fusion.rest_1_.place, f32[16,8,2048]{2,1,0:T(8,128)} %broadcast_in_dim.2.taps, f32[8,2,32,2048]{3,2,1,0:T(8,128)} %near.3.partial, bf16[7,2,32,768]{3,2,1,0:T(8,128)(2,1)} %collective-permute-done.13.far, ...), custom_call_target="tpu_custom_call" | custom-call | bytes 3300000 | tf_op jit(solution)/shard_map/far/pallas_call | solution.py:247
  165.6 3.0 %collective-permute-start.19 = (bf16[4,2,32,1280]{3,2,1,0:T(8,128)(2,1)S(1)}, bf16[4,2,32,1280]{3,2,1,0:T(8,128)(2,1)}, u32[]{:S(2)}, u32[]{:S(2)}) collective-permute-start(bf16[4,2,32,1280]{3,2,1,0:T(8,128)(2,1)S(1)} %copy-done.4), channel_id=1, source_target_pairs={{0,1},{1,0},{2,3},{3,2},{4,5},{5,4},{6,7},{7,6},{8,9},{9,8},{10,11... | collective-permute-start | bytes 1966088 | tf_op jit(solution)/shard_map/ppermute | solution.py:484
  168.5 6.9 %collective-permute-done.12.far = bf16[7,2,32,768]{3,2,1,0:T(8,128)(2,1)} collective-permute-done((bf16[7,2,32,768]{3,2,1,0:T(8,128)(2,1)}, bf16[7,2,32,768]{3,2,1,0:T(8,128)(2,1)}, u32[]{:S(2)}, u32[]{:S(2)}) %collective-permute-start.12) | collective-permute-done | bytes 688160 | tf_op jit(solution)/shard_map/ppermute | solution.py:481
  177.1 3.5 %far.7 = (bf16[4,2,32,768]{3,2,1,0:T(8,128)(2,1)}, bf16[4,2,32,768]{3,2,1,0:T(8,128)(2,1)}) custom-call(s32[2]{0:T(128)} %pad_add_fusion.rest_1_.place, f32[16,8,2048]{2,1,0:T(8,128)} %broadcast_in_dim.2.taps, f32[8,2,32,2048]{3,2,1,0:T(8,128)} %near.2.partial.rest_1_, bf16[7,2,32,768]{3,2,1,0:T(8,128)(2,1)} %collective-permute-done.12.far, ...), custom_call_target="tpu_custom_call" | custom-call | bytes 3300000 | tf_op jit(solution)/shard_map/far/pallas_call | solution.py:247
  183.0 9.2 %beams.2.refs_1_.refs_10_ = f32[8,512,256]{2,1,0:T(8,128)} custom-call(s32[2]{0:T(128)} %pad_add_fusion.rest_1_.place, bf16[4,2,32,1280]{3,2,1,0:T(8,128)(2,1)} %get-tuple-element.23.refs_0_, bf16[4,2,32,768]{3,2,1,0:T(8,128)(2,1)} %get-tuple-element.19.rest_0_.refs_1_, bf16[4,2,32,1280]{3,2,1,0:T(8,128)(2,1)} %copy-done.3, ...), custom_call_target="tpu_custom_call" | custom-call | tf_op jit(solution)/shard_map/beams/pallas_call | solution.py:448
  195.0 10.5 %beams.3 = f32[1024,2,4,128]{3,2,1,0:T(4,128)} custom-call(s32[2]{0:T(128)} %pad_add_fusion.rest_1_.place, bf16[4,2,32,1280]{3,2,1,0:T(8,128)(2,1)} %get-tuple-element.18.rest_0_.refs_0_, bf16[4,2,32,768]{3,2,1,0:T(8,128)(2,1)} %get-tuple-element.21.refs_10_.refs_1_, bf16[4,2,32,1280]{3,2,1,0:T(8,128)(2,1)} %collective-permute-done.14.rest_1_.refs_2_, ...), custom_call_target="tpu_custom_call" | custom-call | tf_op jit(solution)/shard_map/beams/pallas_call | solution.py:448
  (95 shorter events, 52.9 us)
Async XLA Ops:
  2.4 61.1 %collective-permute-start.1 = (bf16[32,2,4,2,2048]{4,3,2,1,0:T(2,128)(2,1)}, bf16[32,2,4,2,2048]{4,3,2,1,0:T(2,128)(2,1)}, u32[]{:S(2)}, u32[]{:S(2)}) collective-permute-start(bf16[32,2,4,2,2048]{4,3,2,1,0:T(2,128)(2,1)} %cut.2.rest_0_), channel_id=1, source_target_pairs={{0,4},{2,6},{4,8},{6,10},{8,12},{10,14},{1,5},{3,7},{5,9},{7,11},{... | collective-permute-start | bytes 6291464 | tf_op jit(solution)/shard_map/ppermute | solution.py:481
  8.7 24.1 %collective-permute-start.3 = (bf16[32,4,2,2048]{3,2,1,0:T(2,128)(2,1)}, bf16[32,4,2,2048]{3,2,1,0:T(2,128)(2,1)S(1)}, u32[]{:S(2)}, u32[]{:S(2)}) collective-permute-start(bf16[32,4,2,2048]{3,2,1,0:T(2,128)(2,1)} %get-tuple-element.16), channel_id=1, source_target_pairs={{0,2},{2,0},{4,6},{6,4},{8,10},{10,8},{12,14},{14,12},{1,3},{3,1},... | collective-permute-start | bytes 3145736 | tf_op jit(solution)/shard_map/ppermute | solution.py:478
  10.0 45.3 %collective-permute-start = (bf16[32,4,2,2048]{3,2,1,0:T(2,128)(2,1)}, bf16[32,4,2,2048]{3,2,1,0:T(2,128)(2,1)S(1)}, u32[]{:S(2)}, u32[]{:S(2)}) collective-permute-start(bf16[32,4,2,2048]{3,2,1,0:T(2,128)(2,1)} %get-tuple-element.15), channel_id=1, source_target_pairs={{0,2},{2,0},{4,6},{6,4},{8,10},{10,8},{12,14},{14,12},{1,3},{3,1},... | collective-permute-start | bytes 3145736 | tf_op jit(solution)/shard_map/ppermute | solution.py:478
  35.6 38.0 %collective-permute-start.4 = (bf16[4,2,32,2048]{3,2,1,0:T(8,128)(2,1)S(1)}, bf16[4,2,32,2048]{3,2,1,0:T(8,128)(2,1)}, u32[]{:S(2)}, u32[]{:S(2)}) collective-permute-start(bf16[4,2,32,2048]{3,2,1,0:T(8,128)(2,1)S(1)} %bitcast.36), channel_id=1, source_target_pairs={{0,4},{2,6},{4,8},{6,10},{8,12},{10,14},{1,5},{3,7},{5,9},{7,11},{... | collective-permute-start | bytes 3145736 | tf_op jit(solution)/shard_map/ppermute | solution.py:481
  59.1 37.3 %collective-permute-start.2 = (bf16[4,2,32,2048]{3,2,1,0:T(8,128)(2,1)}, bf16[4,2,32,2048]{3,2,1,0:T(8,128)(2,1)}, u32[]{:S(2)}, u32[]{:S(2)}) collective-permute-start(bf16[4,2,32,2048]{3,2,1,0:T(8,128)(2,1)} %bitcast.27.other), channel_id=1, source_target_pairs={{0,4},{2,6},{4,8},{6,10},{8,12},{10,14},{1,5},{3,7},{5,9},{7,11},{... | collective-permute-start | bytes 3145736 | tf_op jit(solution)/shard_map/ppermute | solution.py:481
  61.1 35.4 %collective-permute-start.7 = (bf16[16,256]{1,0:T(8,128)(2,1)S(1)}, bf16[16,256]{1,0:T(8,128)(2,1)S(1)}, u32[]{:S(2)}, u32[]{:S(2)}) collective-permute-start(bf16[16,256]{1,0:T(8,128)(2,1)S(1)} %get-tuple-element.26), channel_id=1, source_target_pairs={{0,12},{2,14},{4,8},{6,10},{8,4},{10,6},{12,0},{14,2},{1,13},{3,15... | collective-permute-start | bytes 24584 | tf_op jit(solution)/shard_map/ppermute | solution.py:494
  62.6 33.8 %collective-permute-start.6 = (bf16[16,256]{1,0:T(8,128)(2,1)S(1)}, bf16[16,256]{1,0:T(8,128)(2,1)S(1)}, u32[]{:S(2)}, u32[]{:S(2)}) collective-permute-start(bf16[16,256]{1,0:T(8,128)(2,1)S(1)} %get-tuple-element.26), channel_id=1, source_target_pairs={{0,8},{2,10},{4,12},{6,14},{8,0},{10,2},{12,4},{14,6},{1,9},{3,11}... | collective-permute-start | bytes 24584 | tf_op jit(solution)/shard_map/ppermute | solution.py:494
  63.5 32.9 %collective-permute-start.5 = (bf16[16,256]{1,0:T(8,128)(2,1)S(1)}, bf16[16,256]{1,0:T(8,128)(2,1)S(1)}, u32[]{:S(2)}, u32[]{:S(2)}) collective-permute-start(bf16[16,256]{1,0:T(8,128)(2,1)S(1)} %get-tuple-element.26), channel_id=1, source_target_pairs={{0,4},{2,6},{4,0},{6,2},{8,12},{10,14},{12,8},{14,10},{1,5},{3,7},... | collective-permute-start | bytes 24584 | tf_op jit(solution)/shard_map/ppermute | solution.py:494
  76.4 44.9 %collective-permute-start.10 = (bf16[7,2,32,1280]{3,2,1,0:T(8,128)(2,1)}, bf16[7,2,32,1280]{3,2,1,0:T(8,128)(2,1)}, u32[]{:S(2)}, u32[]{:S(2)}) collective-permute-start(bf16[7,2,32,1280]{3,2,1,0:T(8,128)(2,1)} %onward.4.rest_0_), channel_id=1, source_target_pairs={{4,8},{6,10},{8,12},{10,14},{5,9},{7,11},{9,13},{11,15},{20,24},{2... | collective-permute-start | bytes 3440648 | tf_op jit(solution)/shard_map/ppermute | solution.py:481
  99.9 46.1 %collective-permute-start.9 = (bf16[7,2,32,1280]{3,2,1,0:T(8,128)(2,1)}, bf16[7,2,32,1280]{3,2,1,0:T(8,128)(2,1)}, u32[]{:S(2)}, u32[]{:S(2)}) collective-permute-start(bf16[7,2,32,1280]{3,2,1,0:T(8,128)(2,1)} %onward.5.rest_0_.rest_1_), channel_id=1, source_target_pairs={{4,8},{6,10},{8,12},{10,14},{5,9},{7,11},{9,13},{11,15},{20,24},{2... | collective-permute-start | bytes 3440648 | tf_op jit(solution)/shard_map/ppermute | solution.py:481
  103.9 3.3 %collective-permute-start.8 = (bf16[64,256]{1,0:T(8,128)(2,1)S(1)}, bf16[64,256]{1,0:T(8,128)(2,1)S(1)}, u32[]{:S(2)}, u32[]{:S(2)}) collective-permute-start(bf16[64,256]{1,0:T(8,128)(2,1)S(1)} %pad_maximum_fusion), channel_id=1, source_target_pairs={{0,2},{2,0},{4,6},{6,4},{8,10},{10,8},{12,14},{14,12},{1,3},{3,1},... | collective-permute-start | bytes 98312 | tf_op jit(solution)/shard_map/ppermute | solution.py:478
  125.7 20.2 %collective-permute-start.11 = (bf16[4,2,32,1280]{3,2,1,0:T(8,128)(2,1)}, bf16[4,2,32,1280]{3,2,1,0:T(8,128)(2,1)S(1)}, u32[]{:S(2)}, u32[]{:S(2)}) collective-permute-start(bf16[4,2,32,1280]{3,2,1,0:T(8,128)(2,1)} %get-tuple-element.17), channel_id=1, source_target_pairs={{0,2},{2,0},{4,6},{6,4},{8,10},{10,8},{12,14},{14,12},{1,3},{3,1},... | collective-permute-start | bytes 1966088 | tf_op jit(solution)/shard_map/ppermute | solution.py:478
  129.7 31.0 %collective-permute-start.13 = (bf16[7,2,32,768]{3,2,1,0:T(8,128)(2,1)}, bf16[7,2,32,768]{3,2,1,0:T(8,128)(2,1)}, u32[]{:S(2)}, u32[]{:S(2)}) collective-permute-start(bf16[7,2,32,768]{3,2,1,0:T(8,128)(2,1)} %onward.6.rest_0_.rest_2_), channel_id=1, source_target_pairs={{4,8},{6,10},{8,12},{10,14},{5,9},{7,11},{9,13},{11,15},{20,24},{2... | collective-permute-start | bytes 2064392 | tf_op jit(solution)/shard_map/ppermute | solution.py:481
  135.4 40.1 %collective-permute-start.12 = (bf16[7,2,32,768]{3,2,1,0:T(8,128)(2,1)}, bf16[7,2,32,768]{3,2,1,0:T(8,128)(2,1)}, u32[]{:S(2)}, u32[]{:S(2)}) collective-permute-start(bf16[7,2,32,768]{3,2,1,0:T(8,128)(2,1)} %onward.7.rest_3_), channel_id=1, source_target_pairs={{4,8},{6,10},{8,12},{10,14},{5,9},{7,11},{9,13},{11,15},{20,24},{2... | collective-permute-start | bytes 2064392 | tf_op jit(solution)/shard_map/ppermute | solution.py:481
  151.2 25.9 %collective-permute-start.14 = (bf16[4,2,32,1280]{3,2,1,0:T(8,128)(2,1)}, bf16[4,2,32,1280]{3,2,1,0:T(8,128)(2,1)}, u32[]{:S(2)}, u32[]{:S(2)}) collective-permute-start(bf16[4,2,32,1280]{3,2,1,0:T(8,128)(2,1)} %get-tuple-element.20), channel_id=1, source_target_pairs={{0,2},{2,0},{4,6},{6,4},{8,10},{10,8},{12,14},{14,12},{1,3},{3,1},... | collective-permute-start | bytes 1966088 | tf_op jit(solution)/shard_map/ppermute | solution.py:478
  152.4 29.4 %collective-permute-start.17 = (bf16[4,2,32,1280]{3,2,1,0:T(8,128)(2,1)}, bf16[4,2,32,1280]{3,2,1,0:T(8,128)(2,1)}, u32[]{:S(2)}, u32[]{:S(2)}) collective-permute-start(bf16[4,2,32,1280]{3,2,1,0:T(8,128)(2,1)} %get-tuple-element.23.refs_0_), channel_id=1, source_target_pairs={{0,1},{1,0},{2,3},{3,2},{4,5},{5,4},{6,7},{7,6},{8,9},{9,8},{10,11... | collective-permute-start | bytes 1966088 | tf_op jit(solution)/shard_map/ppermute | solution.py:484
  164.3 12.6 %collective-permute-start.16 = (bf16[4,2,32,768]{3,2,1,0:T(8,128)(2,1)}, bf16[4,2,32,768]{3,2,1,0:T(8,128)(2,1)}, u32[]{:S(2)}, u32[]{:S(2)}) collective-permute-start(bf16[4,2,32,768]{3,2,1,0:T(8,128)(2,1)} %get-tuple-element.24), channel_id=1, source_target_pairs={{0,2},{2,0},{4,6},{6,4},{8,10},{10,8},{12,14},{14,12},{1,3},{3,1},... | collective-permute-start | bytes 1179656 | tf_op jit(solution)/shard_map/ppermute | solution.py:478
  165.6 17.0 %collective-permute-start.19 = (bf16[4,2,32,1280]{3,2,1,0:T(8,128)(2,1)S(1)}, bf16[4,2,32,1280]{3,2,1,0:T(8,128)(2,1)}, u32[]{:S(2)}, u32[]{:S(2)}) collective-permute-start(bf16[4,2,32,1280]{3,2,1,0:T(8,128)(2,1)S(1)} %copy-done.4), channel_id=1, source_target_pairs={{0,1},{1,0},{2,3},{3,2},{4,5},{5,4},{6,7},{7,6},{8,9},{9,8},{10,11... | collective-permute-start | bytes 1966088 | tf_op jit(solution)/shard_map/ppermute | solution.py:484
  175.4 7.1 %collective-permute-start.18 = (bf16[4,2,32,768]{3,2,1,0:T(8,128)(2,1)}, bf16[4,2,32,768]{3,2,1,0:T(8,128)(2,1)}, u32[]{:S(2)}, u32[]{:S(2)}) collective-permute-start(bf16[4,2,32,768]{3,2,1,0:T(8,128)(2,1)} %get-tuple-element.19.rest_0_.refs_1_), channel_id=1, source_target_pairs={{0,1},{1,0},{2,3},{3,2},{4,5},{5,4},{6,7},{7,6},{8,9},{9,8},{10,11... | collective-permute-start | bytes 1179656 | tf_op jit(solution)/shard_map/ppermute | solution.py:484
  177.0 6.0 %collective-permute-start.20 = (bf16[4,2,32,768]{3,2,1,0:T(8,128)(2,1)}, bf16[4,2,32,768]{3,2,1,0:T(8,128)(2,1)}, u32[]{:S(2)}, u32[]{:S(2)}) collective-permute-start(bf16[4,2,32,768]{3,2,1,0:T(8,128)(2,1)} %collective-permute-done.16.refs_3_), channel_id=1, source_target_pairs={{0,1},{1,0},{2,3},{3,2},{4,5},{5,4},{6,7},{7,6},{8,9},{9,8},{10,11... | collective-permute-start | bytes 1179656 | tf_op jit(solution)/shard_map/ppermute | solution.py:484
  180.6 11.6 %collective-permute-start.15 = (bf16[4,2,32,768]{3,2,1,0:T(8,128)(2,1)}, bf16[4,2,32,768]{3,2,1,0:T(8,128)(2,1)}, u32[]{:S(2)}, u32[]{:S(2)}) collective-permute-start(bf16[4,2,32,768]{3,2,1,0:T(8,128)(2,1)} %get-tuple-element.22), channel_id=1, source_target_pairs={{0,2},{2,0},{4,6},{6,4},{8,10},{10,8},{12,14},{14,12},{1,3},{3,1},... | collective-permute-start | bytes 1179656 | tf_op jit(solution)/shard_map/ppermute | solution.py:478
  181.8 10.6 %collective-permute-start.21 = (bf16[4,2,32,1280]{3,2,1,0:T(8,128)(2,1)}, bf16[4,2,32,1280]{3,2,1,0:T(8,128)(2,1)}, u32[]{:S(2)}, u32[]{:S(2)}) collective-permute-start(bf16[4,2,32,1280]{3,2,1,0:T(8,128)(2,1)} %get-tuple-element.18.rest_0_.refs_0_), channel_id=1, source_target_pairs={{0,1},{1,0},{2,3},{3,2},{4,5},{5,4},{6,7},{7,6},{8,9},{9,8},{10,11... | collective-permute-start | bytes 1966088 | tf_op jit(solution)/shard_map/ppermute | solution.py:484
  182.5 9.9 %collective-permute-start.23 = (bf16[4,2,32,1280]{3,2,1,0:T(8,128)(2,1)}, bf16[4,2,32,1280]{3,2,1,0:T(8,128)(2,1)}, u32[]{:S(2)}, u32[]{:S(2)}) collective-permute-start(bf16[4,2,32,1280]{3,2,1,0:T(8,128)(2,1)} %collective-permute-done.14.rest_1_.refs_2_), channel_id=1, source_target_pairs={{0,1},{1,0},{2,3},{3,2},{4,5},{5,4},{6,7},{7,6},{8,9},{9,8},{10,11... | collective-permute-start | bytes 1966088 | tf_op jit(solution)/shard_map/ppermute | solution.py:484
  182.6 9.8 %collective-permute-start.22 = (bf16[4,2,32,768]{3,2,1,0:T(8,128)(2,1)}, bf16[4,2,32,768]{3,2,1,0:T(8,128)(2,1)S(1)}, u32[]{:S(2)}, u32[]{:S(2)}) collective-permute-start(bf16[4,2,32,768]{3,2,1,0:T(8,128)(2,1)} %get-tuple-element.21.refs_10_.refs_1_), channel_id=1, source_target_pairs={{0,1},{1,0},{2,3},{3,2},{4,5},{5,4},{6,7},{7,6},{8,9},{9,8},{10,11... | collective-permute-start | bytes 1179656 | tf_op jit(solution)/shard_map/ppermute | solution.py:484
  (16 other events, 130.1 us)

commit v14 on v12

--- a/solution.py
+++ b/solution.py
@@ -237,7 +237,7 @@
 def far_filter(place, taps, partial, far, low, size, earlier):
     count, parts, stations, _ = partial.shape
     frames = count // 2
-    block = size // 2
+    block = next(size // n for n in (2, 3, 1) if size // n % LANES == 0)
 
     def spec(depth, start):
         shape = (pl.Element(depth), pl.Element(parts), pl.Element(stations), pl.Element(block))
@@ -379,7 +379,7 @@
                     mixed[b, target, LANES:] = im.astype(BF16)
                 return carry
 
-            lax.fori_loop(0, frames * tiles, radix, 0, unroll=2)
+            lax.fori_loop(0, frames * tiles, radix, 0, unroll=4 if has_earlier else 2)
         copies[source_count].wait()
 
         def transform(b, carry):
@@ -427,7 +427,7 @@
     groups, depth, width = weights.shape
     beams = width // 2
     station_count = sum(s.shape[2] for s in sources) // ranges
-    at_once = 2
+    at_once = 4 if earlier is None else 2
     flat = (groups, channels // groups * frames, beams)
     flat_spec = pl.BlockSpec((at_once,) + flat[1:], lambda i, place: (i, 0, 0))
     operands = list(sources) + [table, weights] + ([] if earlier is None else [earlier])
@@ -509,7 +509,7 @@
     table = jnp.asarray(dft_tables(samples))
     taps = jnp.broadcast_to(filter_taps[:, None, :], (history + 1, 8, samples))
 
-    parts_of = [(samples // 2, samples // 2), (5 * samples // 8, 3 * samples // 8)]
+    parts_of = [(samples // 2, samples // 2), (9 * samples // 16, 7 * samples // 16)]
     chunks = [(pol, sum(sizes[:i]), size) for pol, sizes in enumerate(parts_of) for i, size in enumerate(sizes)]
     other_back = [hop(block) for block in other]
     further = []

time: 207 us -> 207 us (level)
  transfers between devices with their start and end apart: 25 -> 25, of which waited for: 10 -> 9; matrix products, arithmetic and copies ran while one was open for 10% -> 10% of each run, Pallas kernels for 28% -> 28%
where the time goes in v14:
time: 207 us; the launch traced here: 206 us
  Pallas kernels  70.5 us (34%)
  waiting for transfers between devices  69.1 us (33%)
  starting transfers between devices  39.5 us (19%)
  local copies, waits for them, and re-layouts  22 us (11%)
  other arithmetic  4.12 us (2%)
    ppermute x7, waiting for transfers between devices, pair(): return lax.ppermute(block, 'tm', [(i, i ^ 1) for i in range(time_devices)])  45.1 us
    ppermute x7, waiting for transfers between devices, hop(): lax.ppermute(block, 'tm', [(i, i + 2) for i in range(skip, time_devices -...  19.5 us
    ppermute x7, starting transfers between devices, hop(): lax.ppermute(block, 'tm', [(i, i + 2) for i in range(skip, time_devices -...  19.3 us
    pallas_call x2, Pallas kernels, beam_power(): pl.pallas_call(functools.partial(beam_kernel, len(sources), ranges, len(l...  18.8 us
    pallas_call x4, Pallas kernels, far_filter(): pl.pallas_call(far_kernel, out_shape=(shape, shape), grid_spec=pltpu.Pref...  17.5 us
    pallas_call x2, Pallas kernels, near_filter(): pl.pallas_call(near_kernel, out_shape=jax.ShapeDtypeStruct((2 * frames, p...  15.7 us
    pallas_call x4, Pallas kernels, onward(): pl.pallas_call(onward_kernel, out_shape=jax.ShapeDtypeStruct((depth, part...  10.9 us
    ppermute x8, starting transfers between devices, swap(): return lax.ppermute(block, 'stn', [(0, 1), (1, 0)])  10.9 us
  transfers between devices with their start and end apart: 25, of which 9 were waited for; matrix products, arithmetic and copies ran while one was open for 10% of the time, Pallas kernels for 28%

profile of v14, /device:TPU:17, one launch (start us, length us, event | category | flops | bytes accessed | tf_op | source)
XLA Modules:
  0.0 205.6 jit_solution(1439584312029978731)
XLA Ops:
  2.4 3.2 %collective-permute-start.1 = (bf16[32,2,4,2,2048]{4,3,2,1,0:T(2,128)(2,1)}, bf16[32,2,4,2,2048]{4,3,2,1,0:T(2,128)(2,1)}, u32[]{:S(2)}, u32[]{:S(2)}) collective-permute-start(bf16[32,2,4,2,2048]{4,3,2,1,0:T(2,128)(2,1)} %cut.2.rest_0_), channel_id=1, source_target_pairs={{0,4},{2,6},{4,8},{6,10},{8,12},{10,14},{1,5},{3,7},{5,9},{7,11},{... | collective-permute-start | bytes 6291464 | tf_op jit(solution)/shard_map/ppermute | solution.py:481
  10.2 22.6 %collective-permute-done.3.refs_0_ = bf16[32,4,2,2048]{3,2,1,0:T(2,128)(2,1)S(1)} collective-permute-done((bf16[32,4,2,2048]{3,2,1,0:T(2,128)(2,1)}, bf16[32,4,2,2048]{3,2,1,0:T(2,128)(2,1)S(1)}, u32[]{:S(2)}, u32[]{:S(2)}) %collective-permute-start.3) | collective-permute-done | bytes 1048608 | tf_op jit(solution)/shard_map/ppermute | solution.py:478
  40.3 14.9 %collective-permute-done.refs_0_ = bf16[32,4,2,2048]{3,2,1,0:T(2,128)(2,1)} collective-permute-done((bf16[32,4,2,2048]{3,2,1,0:T(2,128)(2,1)}, bf16[32,4,2,2048]{3,2,1,0:T(2,128)(2,1)}, u32[]{:S(2)}, u32[]{:S(2)}) %collective-permute-start) | collective-permute-done | bytes 1048608 | tf_op jit(solution)/shard_map/ppermute | solution.py:478
  55.4 2.8 %copy.21 = bf16[32,4,2,2048]{3,0,2,1:T(8,128)(2,1)} copy(bf16[32,4,2,2048]{3,2,1,0:T(2,128)(2,1)} %after.3) | data formatting | bytes 2097152 | tf_op jit(solution)/shard_map/after/pallas_call | solution.py:77
  58.2 4.3 %collective-permute-start.2 = (bf16[4,2,32,2048]{3,2,1,0:T(8,128)(2,1)}, bf16[4,2,32,2048]{3,2,1,0:T(8,128)(2,1)}, u32[]{:S(2)}, u32[]{:S(2)}) collective-permute-start(bf16[4,2,32,2048]{3,2,1,0:T(8,128)(2,1)} %bitcast.27.other), channel_id=1, source_target_pairs={{0,4},{2,6},{4,8},{6,10},{8,12},{10,14},{1,5},{3,7},{5,9},{7,11},{... | collective-permute-start | bytes 3145736 | tf_op jit(solution)/shard_map/ppermute | solution.py:481
  65.7 4.1 %copy.18 = bf16[32,2,4,2,2048]{4,0,3,2,1:T(8,128)(2,1)} copy(bf16[32,2,4,2,2048]{4,3,2,1,0:T(2,128)(2,1)} %after.4) | data formatting | bytes 4194304 | tf_op jit(solution)/shard_map/after/pallas_call | solution.py:77
  69.7 3.0 %collective-permute-done.5.rest_0_ = bf16[16,256]{1,0:T(8,128)(2,1)S(1)} collective-permute-done((bf16[16,256]{1,0:T(8,128)(2,1)S(1)}, bf16[16,256]{1,0:T(8,128)(2,1)S(1)}, u32[]{:S(2)}, u32[]{:S(2)}) %collective-permute-start.5) | collective-permute-done | bytes 8224 | tf_op jit(solution)/shard_map/ppermute | solution.py:494
  74.7 2.7 %onward.4.rest_0_ = bf16[7,2,32,1024]{3,2,1,0:T(8,128)(2,1)} custom-call(s32[2]{0:T(128)} %pad_add_fusion.rest_1_.place, bf16[2,4,2,32,2048]{4,3,2,1,0:T(8,128)(2,1)} %bitcast.28, bf16[4,2,32,2048]{3,2,1,0:T(8,128)(2,1)} %collective-permute-done.4.other_back, bf16[16,256]{1,0:T(8,128)(2,1)} %copy-done.10, bf16[16,256]{1,0:T(8,128)(2,1)} %copy-done.11, ...), custom_call_target="tpu_custom_call" | custom-call | bytes 9900000 | tf_op jit(solution)/shard_map/onward/pallas_call | solution.py:295
  77.4 3.0 %collective-permute-start.11 = (bf16[7,2,32,1024]{3,2,1,0:T(8,128)(2,1)}, bf16[7,2,32,1024]{3,2,1,0:T(8,128)(2,1)S(1)}, u32[]{:S(2)}, u32[]{:S(2)}) collective-permute-start(bf16[7,2,32,1024]{3,2,1,0:T(8,128)(2,1)} %onward.4.rest_0_), channel_id=1, source_target_pairs={{4,8},{6,10},{8,12},{10,14},{5,9},{7,11},{9,13},{11,15},{20,24},{2... | collective-permute-start | bytes 2752520 | tf_op jit(solution)/shard_map/ppermute | solution.py:481
  98.8 7.8 %near.3.partial = f32[8,2,32,2048]{3,2,1,0:T(8,128)} custom-call(s32[2]{0:T(128)} %pad_add_fusion.rest_1_.place, f32[16,8,2048]{2,1,0:T(8,128)} %broadcast_in_dim.2.taps, bf16[2,4,2,32,2048]{4,3,2,1,0:T(8,128)(2,1)} %bitcast.34, bf16[4,2,32,2048]{3,2,1,0:T(8,128)(2,1)} %bitcast.37, bf16[2,4,2,32,2048]{4,3,2,1,0:T(8,128)(2,1)} %bitcast.30, ...), custom_call_target="tpu_custom_call" | custom-call | bytes 26400000 | tf_op jit(solution)/shard_map/near/pallas_call | solution.py:221
  106.6 9.7 %collective-permute-done.11.far = bf16[7,2,32,1024]{3,2,1,0:T(8,128)(2,1)S(1)} collective-permute-done((bf16[7,2,32,1024]{3,2,1,0:T(8,128)(2,1)}, bf16[7,2,32,1024]{3,2,1,0:T(8,128)(2,1)S(1)}, u32[]{:S(2)}, u32[]{:S(2)}) %collective-permute-start.11) | collective-permute-done | bytes 917536 | tf_op jit(solution)/shard_map/ppermute | solution.py:481
  117.3 3.9 %far.4 = (bf16[4,2,32,1024]{3,2,1,0:T(8,128)(2,1)}, bf16[4,2,32,1024]{3,2,1,0:T(8,128)(2,1)}) custom-call(s32[2]{0:T(128)} %pad_add_fusion.rest_1_.place, f32[16,8,2048]{2,1,0:T(8,128)} %broadcast_in_dim.2.taps, f32[8,2,32,2048]{3,2,1,0:T(8,128)} %near.3.partial, bf16[7,2,32,1024]{3,2,1,0:T(8,128)(2,1)} %copy-done.5), custom_call_target="tpu_custom_call" | custom-call | bytes 3300000 | tf_op jit(solution)/shard_map/far/pallas_call | solution.py:247
  122.4 2.8 %onward.6.rest_2_ = bf16[7,2,32,1152]{3,2,1,0:T(8,128)(2,1)} custom-call(s32[2]{0:T(128)} %pad_add_fusion.rest_1_.place, bf16[2,4,2,32,2048]{4,3,2,1,0:T(8,128)(2,1)} %bitcast.31, bf16[4,2,32,2048]{3,2,1,0:T(8,128)(2,1)} %collective-permute-done.2.other_back.rest_5_.rest_3_), custom_call_target="tpu_custom_call" | custom-call | bytes 9900000 | tf_op jit(solution)/shard_map/onward/pallas_call | solution.py:295
  125.2 3.0 %collective-permute-start.9 = (bf16[7,2,32,1152]{3,2,1,0:T(8,128)(2,1)}, bf16[7,2,32,1152]{3,2,1,0:T(8,128)(2,1)}, u32[]{:S(2)}, u32[]{:S(2)}) collective-permute-start(bf16[7,2,32,1152]{3,2,1,0:T(8,128)(2,1)} %onward.6.rest_2_), channel_id=1, source_target_pairs={{4,8},{6,10},{8,12},{10,14},{5,9},{7,11},{9,13},{11,15},{20,24},{2... | collective-permute-start | bytes 3096584 | tf_op jit(solution)/shard_map/ppermute | solution.py:481
  128.2 2.8 %onward.7.rest_3_ = bf16[7,2,32,896]{3,2,1,0:T(8,128)(2,1)} custom-call(s32[2]{0:T(128)} %pad_add_fusion.rest_1_.place, bf16[2,4,2,32,2048]{4,3,2,1,0:T(8,128)(2,1)} %bitcast.32, bf16[4,2,32,2048]{3,2,1,0:T(8,128)(2,1)} %collective-permute-done.2.other_back.rest_5_.rest_3_), custom_call_target="tpu_custom_call" | custom-call | bytes 9900000 | tf_op jit(solution)/shard_map/onward/pallas_call | solution.py:295
  131.0 7.8 %near.2.rest_1_.partial = f32[8,2,32,2048]{3,2,1,0:T(8,128)} custom-call(s32[2]{0:T(128)} %pad_add_fusion.rest_1_.place, f32[16,8,2048]{2,1,0:T(8,128)} %broadcast_in_dim.2.taps, bf16[2,4,2,32,2048]{4,3,2,1,0:T(8,128)(2,1)} %bitcast.35, bf16[4,2,32,2048]{3,2,1,0:T(8,128)(2,1)} %bitcast.27.other, bf16[2,4,2,32,2048]{4,3,2,1,0:T(8,128)(2,1)} %bitcast.33, ...), custom_call_target="tpu_custom_call" | custom-call | bytes 26400000 | tf_op jit(solution)/shard_map/near/pallas_call | solution.py:221
  138.8 4.0 %far.5 = (bf16[4,2,32,1024]{3,2,1,0:T(8,128)(2,1)}, bf16[4,2,32,1024]{3,2,1,0:T(8,128)(2,1)}) custom-call(s32[2]{0:T(128)} %pad_add_fusion.rest_1_.place, f32[16,8,2048]{2,1,0:T(8,128)} %broadcast_in_dim.2.taps, f32[8,2,32,2048]{3,2,1,0:T(8,128)} %near.3.partial, bf16[7,2,32,1024]{3,2,1,0:T(8,128)(2,1)} %collective-permute-done.10.far, ...), custom_call_target="tpu_custom_call" | custom-call | bytes 3300000 | tf_op jit(solution)/shard_map/far/pallas_call | solution.py:247
  144.9 3.6 %collective-permute-start.15 = (bf16[4,2,32,1024]{3,2,1,0:T(8,128)(2,1)}, bf16[4,2,32,1024]{3,2,1,0:T(8,128)(2,1)}, u32[]{:S(2)}, u32[]{:S(2)}) collective-permute-start(bf16[4,2,32,1024]{3,2,1,0:T(8,128)(2,1)} %get-tuple-element.20.refs_0_), channel_id=1, source_target_pairs={{0,1},{1,0},{2,3},{3,2},{4,5},{5,4},{6,7},{7,6},{8,9},{9,8},{10,11... | collective-permute-start | bytes 1572872 | tf_op jit(solution)/shard_map/ppermute | solution.py:484
  148.6 9.6 %collective-permute-done.9.far = bf16[7,2,32,1152]{3,2,1,0:T(8,128)(2,1)} collective-permute-done((bf16[7,2,32,1152]{3,2,1,0:T(8,128)(2,1)}, bf16[7,2,32,1152]{3,2,1,0:T(8,128)(2,1)}, u32[]{:S(2)}, u32[]{:S(2)}) %collective-permute-start.9) | collective-permute-done | bytes 1032224 | tf_op jit(solution)/shard_map/ppermute | solution.py:481
  160.9 5.0 %far.6 = (bf16[4,2,32,1152]{3,2,1,0:T(8,128)(2,1)}, bf16[4,2,32,1152]{3,2,1,0:T(8,128)(2,1)}) custom-call(s32[2]{0:T(128)} %pad_add_fusion.rest_1_.place, f32[16,8,2048]{2,1,0:T(8,128)} %broadcast_in_dim.2.taps, f32[8,2,32,2048]{3,2,1,0:T(8,128)} %near.2.rest_1_.partial, bf16[7,2,32,1152]{3,2,1,0:T(8,128)(2,1)} %collective-permute-done.9.far, ...), custom_call_target="tpu_custom_call" | custom-call | bytes 3300000 | tf_op jit(solution)/shard_map/far/pallas_call | solution.py:247
  167.2 8.5 %beams.2.rest_0_.refs_10_ = f32[8,512,256]{2,1,0:T(8,128)} custom-call(s32[2]{0:T(128)} %pad_add_fusion.rest_1_.place, bf16[4,2,32,1024]{3,2,1,0:T(8,128)(2,1)} %get-tuple-element.20.refs_0_, bf16[4,2,32,1024]{3,2,1,0:T(8,128)(2,1)} %get-tuple-element.21.refs_1_, bf16[4,2,32,1024]{3,2,1,0:T(8,128)(2,1)} %collective-permute-done.12.rest_0_.refs_2_, ...), custom_call_target="tpu_custom_call" | custom-call | tf_op jit(solution)/shard_map/beams/pallas_call | solution.py:448
  175.7 4.6 %far.7 = (bf16[4,2,32,896]{3,2,1,0:T(8,128)(2,1)}, bf16[4,2,32,896]{3,2,1,0:T(8,128)(2,1)}) custom-call(s32[2]{0:T(128)} %pad_add_fusion.rest_1_.place, f32[16,8,2048]{2,1,0:T(8,128)} %broadcast_in_dim.2.taps, f32[8,2,32,2048]{3,2,1,0:T(8,128)} %near.2.rest_1_.partial, bf16[7,2,32,896]{3,2,1,0:T(8,128)(2,1)} %collective-permute-done.14.far, ...), custom_call_target="tpu_custom_call" | custom-call | bytes 3300000 | tf_op jit(solution)/shard_map/far/pallas_call | solution.py:247
  183.6 7.6 %collective-permute-done.20.refs_3_ = bf16[4,2,32,896]{3,2,1,0:T(8,128)(2,1)S(1)} collective-permute-done((bf16[4,2,32,896]{3,2,1,0:T(8,128)(2,1)}, bf16[4,2,32,896]{3,2,1,0:T(8,128)(2,1)S(1)}, u32[]{:S(2)}, u32[]{:S(2)}) %collective-permute-start.20) | collective-permute-done | bytes 458784 | tf_op jit(solution)/shard_map/ppermute | solution.py:478
  195.0 10.4 %beams.3 = f32[1024,2,4,128]{3,2,1,0:T(4,128)} custom-call(s32[2]{0:T(128)} %pad_add_fusion.rest_1_.place, bf16[4,2,32,1152]{3,2,1,0:T(8,128)(2,1)} %get-tuple-element.19.refs_10_.refs_0_, bf16[4,2,32,896]{3,2,1,0:T(8,128)(2,1)} %get-tuple-element.22.refs_1_, bf16[4,2,32,1152]{3,2,1,0:T(8,128)(2,1)} %collective-permute-done.19.refs_2_, ...), custom_call_target="tpu_custom_call" | custom-call | tf_op jit(solution)/shard_map/beams/pallas_call | solution.py:448
  (98 shorter events, 53.5 us)
Async XLA Ops:
  2.4 55.8 %collective-permute-start.1 = (bf16[32,2,4,2,2048]{4,3,2,1,0:T(2,128)(2,1)}, bf16[32,2,4,2,2048]{4,3,2,1,0:T(2,128)(2,1)}, u32[]{:S(2)}, u32[]{:S(2)}) collective-permute-start(bf16[32,2,4,2,2048]{4,3,2,1,0:T(2,128)(2,1)} %cut.2.rest_0_), channel_id=1, source_target_pairs={{0,4},{2,6},{4,8},{6,10},{8,12},{10,14},{1,5},{3,7},{5,9},{7,11},{... | collective-permute-start | bytes 6291464 | tf_op jit(solution)/shard_map/ppermute | solution.py:481
  8.7 24.1 %collective-permute-start.3 = (bf16[32,4,2,2048]{3,2,1,0:T(2,128)(2,1)}, bf16[32,4,2,2048]{3,2,1,0:T(2,128)(2,1)S(1)}, u32[]{:S(2)}, u32[]{:S(2)}) collective-permute-start(bf16[32,4,2,2048]{3,2,1,0:T(2,128)(2,1)} %get-tuple-element.16), channel_id=1, source_target_pairs={{0,2},{2,0},{4,6},{6,4},{8,10},{10,8},{12,14},{14,12},{1,3},{3,1},... | collective-permute-start | bytes 3145736 | tf_op jit(solution)/shard_map/ppermute | solution.py:478
  10.0 45.2 %collective-permute-start = (bf16[32,4,2,2048]{3,2,1,0:T(2,128)(2,1)}, bf16[32,4,2,2048]{3,2,1,0:T(2,128)(2,1)}, u32[]{:S(2)}, u32[]{:S(2)}) collective-permute-start(bf16[32,4,2,2048]{3,2,1,0:T(2,128)(2,1)} %get-tuple-element.15), channel_id=1, source_target_pairs={{0,2},{2,0},{4,6},{6,4},{8,10},{10,8},{12,14},{14,12},{1,3},{3,1},... | collective-permute-start | bytes 3145736 | tf_op jit(solution)/shard_map/ppermute | solution.py:478
  35.6 38.5 %collective-permute-start.4 = (bf16[4,2,32,2048]{3,2,1,0:T(8,128)(2,1)S(1)}, bf16[4,2,32,2048]{3,2,1,0:T(8,128)(2,1)}, u32[]{:S(2)}, u32[]{:S(2)}) collective-permute-start(bf16[4,2,32,2048]{3,2,1,0:T(8,128)(2,1)S(1)} %bitcast.36), channel_id=1, source_target_pairs={{0,4},{2,6},{4,8},{6,10},{8,12},{10,14},{1,5},{3,7},{5,9},{7,11},{... | collective-permute-start | bytes 3145736 | tf_op jit(solution)/shard_map/ppermute | solution.py:481
  37.6 35.1 %collective-permute-start.5 = (bf16[16,256]{1,0:T(8,128)(2,1)S(1)}, bf16[16,256]{1,0:T(8,128)(2,1)S(1)}, u32[]{:S(2)}, u32[]{:S(2)}) collective-permute-start(bf16[16,256]{1,0:T(8,128)(2,1)S(1)} %get-tuple-element.26), channel_id=1, source_target_pairs={{0,4},{2,6},{4,0},{6,2},{8,12},{10,14},{12,8},{14,10},{1,5},{3,7},... | collective-permute-start | bytes 24584 | tf_op jit(solution)/shard_map/ppermute | solution.py:494
  37.6 35.8 %collective-permute-start.6 = (bf16[16,256]{1,0:T(8,128)(2,1)S(1)}, bf16[16,256]{1,0:T(8,128)(2,1)S(1)}, u32[]{:S(2)}, u32[]{:S(2)}) collective-permute-start(bf16[16,256]{1,0:T(8,128)(2,1)S(1)} %get-tuple-element.26), channel_id=1, source_target_pairs={{0,8},{2,10},{4,12},{6,14},{8,0},{10,2},{12,4},{14,6},{1,9},{3,11}... | collective-permute-start | bytes 24584 | tf_op jit(solution)/shard_map/ppermute | solution.py:494
  55.3 18.9 %collective-permute-start.7 = (bf16[16,256]{1,0:T(8,128)(2,1)S(1)}, bf16[16,256]{1,0:T(8,128)(2,1)S(1)}, u32[]{:S(2)}, u32[]{:S(2)}) collective-permute-start(bf16[16,256]{1,0:T(8,128)(2,1)S(1)} %get-tuple-element.26), channel_id=1, source_target_pairs={{0,12},{2,14},{4,8},{6,10},{8,4},{10,6},{12,0},{14,2},{1,13},{3,15... | collective-permute-start | bytes 24584 | tf_op jit(solution)/shard_map/ppermute | solution.py:494
  58.2 38.6 %collective-permute-start.2 = (bf16[4,2,32,2048]{3,2,1,0:T(8,128)(2,1)}, bf16[4,2,32,2048]{3,2,1,0:T(8,128)(2,1)}, u32[]{:S(2)}, u32[]{:S(2)}) collective-permute-start(bf16[4,2,32,2048]{3,2,1,0:T(8,128)(2,1)} %bitcast.27.other), channel_id=1, source_target_pairs={{0,4},{2,6},{4,8},{6,10},{8,12},{10,14},{1,5},{3,7},{5,9},{7,11},{... | collective-permute-start | bytes 3145736 | tf_op jit(solution)/shard_map/ppermute | solution.py:481
  77.4 38.9 %collective-permute-start.11 = (bf16[7,2,32,1024]{3,2,1,0:T(8,128)(2,1)}, bf16[7,2,32,1024]{3,2,1,0:T(8,128)(2,1)S(1)}, u32[]{:S(2)}, u32[]{:S(2)}) collective-permute-start(bf16[7,2,32,1024]{3,2,1,0:T(8,128)(2,1)} %onward.4.rest_0_), channel_id=1, source_target_pairs={{4,8},{6,10},{8,12},{10,14},{5,9},{7,11},{9,13},{11,15},{20,24},{2... | collective-permute-start | bytes 2752520 | tf_op jit(solution)/shard_map/ppermute | solution.py:481
  84.6 7.9 %collective-permute-start.8 = (bf16[64,256]{1,0:T(8,128)(2,1)}, bf16[64,256]{1,0:T(8,128)(2,1)}, u32[]{:S(2)}, u32[]{:S(2)}) collective-permute-start(bf16[64,256]{1,0:T(8,128)(2,1)} %pad_maximum_fusion), channel_id=1, source_target_pairs={{0,2},{2,0},{4,6},{6,4},{8,10},{10,8},{12,14},{14,12},{1,3},{3,1},... | collective-permute-start | bytes 98312 | tf_op jit(solution)/shard_map/ppermute | solution.py:478
  88.5 50.3 %collective-permute-start.10 = (bf16[7,2,32,1024]{3,2,1,0:T(8,128)(2,1)}, bf16[7,2,32,1024]{3,2,1,0:T(8,128)(2,1)}, u32[]{:S(2)}, u32[]{:S(2)}) collective-permute-start(bf16[7,2,32,1024]{3,2,1,0:T(8,128)(2,1)} %onward.5.rest_1_), channel_id=1, source_target_pairs={{4,8},{6,10},{8,12},{10,14},{5,9},{7,11},{9,13},{11,15},{20,24},{2... | collective-permute-start | bytes 2752520 | tf_op jit(solution)/shard_map/ppermute | solution.py:481
  121.2 17.6 %collective-permute-start.12 = (bf16[4,2,32,1024]{3,2,1,0:T(8,128)(2,1)}, bf16[4,2,32,1024]{3,2,1,0:T(8,128)(2,1)}, u32[]{:S(2)}, u32[]{:S(2)}) collective-permute-start(bf16[4,2,32,1024]{3,2,1,0:T(8,128)(2,1)} %get-tuple-element.17), channel_id=1, source_target_pairs={{0,2},{2,0},{4,6},{6,4},{8,10},{10,8},{12,14},{14,12},{1,3},{3,1},... | collective-permute-start | bytes 1572872 | tf_op jit(solution)/shard_map/ppermute | solution.py:478
  125.2 33.0 %collective-permute-start.9 = (bf16[7,2,32,1152]{3,2,1,0:T(8,128)(2,1)}, bf16[7,2,32,1152]{3,2,1,0:T(8,128)(2,1)}, u32[]{:S(2)}, u32[]{:S(2)}) collective-permute-start(bf16[7,2,32,1152]{3,2,1,0:T(8,128)(2,1)} %onward.6.rest_2_), channel_id=1, source_target_pairs={{4,8},{6,10},{8,12},{10,14},{5,9},{7,11},{9,13},{11,15},{20,24},{2... | collective-permute-start | bytes 3096584 | tf_op jit(solution)/shard_map/ppermute | solution.py:481
  142.8 18.1 %collective-permute-start.13 = (bf16[4,2,32,1024]{3,2,1,0:T(8,128)(2,1)}, bf16[4,2,32,1024]{3,2,1,0:T(8,128)(2,1)}, u32[]{:S(2)}, u32[]{:S(2)}) collective-permute-start(bf16[4,2,32,1024]{3,2,1,0:T(8,128)(2,1)} %get-tuple-element.18), channel_id=1, source_target_pairs={{0,2},{2,0},{4,6},{6,4},{8,10},{10,8},{12,14},{14,12},{1,3},{3,1},... | collective-permute-start | bytes 1572872 | tf_op jit(solution)/shard_map/ppermute | solution.py:478
  143.0 32.7 %collective-permute-start.14 = (bf16[7,2,32,896]{3,2,1,0:T(8,128)(2,1)S(1)}, bf16[7,2,32,896]{3,2,1,0:T(8,128)(2,1)}, u32[]{:S(2)}, u32[]{:S(2)}) collective-permute-start(bf16[7,2,32,896]{3,2,1,0:T(8,128)(2,1)S(1)} %copy-done.3), channel_id=1, source_target_pairs={{4,8},{6,10},{8,12},{10,14},{5,9},{7,11},{9,13},{11,15},{20,24},{2... | collective-permute-start | bytes 2408456 | tf_op jit(solution)/shard_map/ppermute | solution.py:481
  144.9 21.0 %collective-permute-start.15 = (bf16[4,2,32,1024]{3,2,1,0:T(8,128)(2,1)}, bf16[4,2,32,1024]{3,2,1,0:T(8,128)(2,1)}, u32[]{:S(2)}, u32[]{:S(2)}) collective-permute-start(bf16[4,2,32,1024]{3,2,1,0:T(8,128)(2,1)} %get-tuple-element.20.refs_0_), channel_id=1, source_target_pairs={{0,1},{1,0},{2,3},{3,2},{4,5},{5,4},{6,7},{7,6},{8,9},{9,8},{10,11... | collective-permute-start | bytes 1572872 | tf_op jit(solution)/shard_map/ppermute | solution.py:484
  148.5 18.7 %collective-permute-start.16 = (bf16[4,2,32,1024]{3,2,1,0:T(8,128)(2,1)}, bf16[4,2,32,1024]{3,2,1,0:T(8,128)(2,1)}, u32[]{:S(2)}, u32[]{:S(2)}) collective-permute-start(bf16[4,2,32,1024]{3,2,1,0:T(8,128)(2,1)} %get-tuple-element.21.refs_1_), channel_id=1, source_target_pairs={{0,1},{1,0},{2,3},{3,2},{4,5},{5,4},{6,7},{7,6},{8,9},{9,8},{10,11... | collective-permute-start | bytes 1572872 | tf_op jit(solution)/shard_map/ppermute | solution.py:484
  158.2 9.0 %collective-permute-start.17 = (bf16[4,2,32,1024]{3,2,1,0:T(8,128)(2,1)}, bf16[4,2,32,1024]{3,2,1,0:T(8,128)(2,1)}, u32[]{:S(2)}, u32[]{:S(2)}) collective-permute-start(bf16[4,2,32,1024]{3,2,1,0:T(8,128)(2,1)} %collective-permute-done.12.rest_0_.refs_2_), channel_id=1, source_target_pairs={{0,1},{1,0},{2,3},{3,2},{4,5},{5,4},{6,7},{7,6},{8,9},{9,8},{10,11... | collective-permute-start | bytes 1572872 | tf_op jit(solution)/shard_map/ppermute | solution.py:484
  160.9 6.3 %collective-permute-start.18 = (bf16[4,2,32,1024]{3,2,1,0:T(8,128)(2,1)}, bf16[4,2,32,1024]{3,2,1,0:T(8,128)(2,1)}, u32[]{:S(2)}, u32[]{:S(2)}) collective-permute-start(bf16[4,2,32,1024]{3,2,1,0:T(8,128)(2,1)} %collective-permute-done.13.rest_0_.refs_3_), channel_id=1, source_target_pairs={{0,1},{1,0},{2,3},{3,2},{4,5},{5,4},{6,7},{7,6},{8,9},{9,8},{10,11... | collective-permute-start | bytes 1572872 | tf_op jit(solution)/shard_map/ppermute | solution.py:484
  165.9 17.1 %collective-permute-start.19 = (bf16[4,2,32,1152]{3,2,1,0:T(8,128)(2,1)}, bf16[4,2,32,1152]{3,2,1,0:T(8,128)(2,1)}, u32[]{:S(2)}, u32[]{:S(2)}) collective-permute-start(bf16[4,2,32,1152]{3,2,1,0:T(8,128)(2,1)} %get-tuple-element.23), channel_id=1, source_target_pairs={{0,2},{2,0},{4,6},{6,4},{8,10},{10,8},{12,14},{14,12},{1,3},{3,1},... | collective-permute-start | bytes 1769480 | tf_op jit(solution)/shard_map/ppermute | solution.py:478
  180.3 10.9 %collective-permute-start.20 = (bf16[4,2,32,896]{3,2,1,0:T(8,128)(2,1)}, bf16[4,2,32,896]{3,2,1,0:T(8,128)(2,1)S(1)}, u32[]{:S(2)}, u32[]{:S(2)}) collective-permute-start(bf16[4,2,32,896]{3,2,1,0:T(8,128)(2,1)} %get-tuple-element.24), channel_id=1, source_target_pairs={{0,2},{2,0},{4,6},{6,4},{8,10},{10,8},{12,14},{14,12},{1,3},{3,1},... | collective-permute-start | bytes 1376264 | tf_op jit(solution)/shard_map/ppermute | solution.py:478
  181.2 12.2 %collective-permute-start.21 = (bf16[4,2,32,1152]{3,2,1,0:T(8,128)(2,1)S(1)}, bf16[4,2,32,1152]{3,2,1,0:T(8,128)(2,1)S(1)}, u32[]{:S(2)}, u32[]{:S(2)}) collective-permute-start(bf16[4,2,32,1152]{3,2,1,0:T(8,128)(2,1)S(1)} %copy-done.4), channel_id=1, source_target_pairs={{0,1},{1,0},{2,3},{3,2},{4,5},{5,4},{6,7},{7,6},{8,9},{9,8},{10,11... | collective-permute-start | bytes 1769480 | tf_op jit(solution)/shard_map/ppermute | solution.py:484
  183.1 11.2 %collective-permute-start.23 = (bf16[4,2,32,1152]{3,2,1,0:T(8,128)(2,1)}, bf16[4,2,32,1152]{3,2,1,0:T(8,128)(2,1)}, u32[]{:S(2)}, u32[]{:S(2)}) collective-permute-start(bf16[4,2,32,1152]{3,2,1,0:T(8,128)(2,1)} %collective-permute-done.19.refs_2_), channel_id=1, source_target_pairs={{0,1},{1,0},{2,3},{3,2},{4,5},{5,4},{6,7},{7,6},{8,9},{9,8},{10,11... | collective-permute-start | bytes 1769480 | tf_op jit(solution)/shard_map/ppermute | solution.py:484
  183.1 11.1 %collective-permute-start.22 = (bf16[4,2,32,896]{3,2,1,0:T(8,128)(2,1)}, bf16[4,2,32,896]{3,2,1,0:T(8,128)(2,1)S(1)}, u32[]{:S(2)}, u32[]{:S(2)}) collective-permute-start(bf16[4,2,32,896]{3,2,1,0:T(8,128)(2,1)} %get-tuple-element.22.refs_1_), channel_id=1, source_target_pairs={{0,1},{1,0},{2,3},{3,2},{4,5},{5,4},{6,7},{7,6},{8,9},{9,8},{10,11... | collective-permute-start | bytes 1376264 | tf_op jit(solution)/shard_map/ppermute | solution.py:484
  (18 other events, 177.7 us)

commit v15 on v14

--- a/solution.py
+++ b/solution.py
@@ -137,13 +137,13 @@
     )(voltages, *earlier)
 
 
-def weighted(taps, window, count, lanes, part, rows, sums):
+def weighted(taps, first_tap, window, count, lanes, part, rows, sums):
     tap_count = taps.shape[0]
     tap_rows = [taps[k, :, lanes][None] for k in range(tap_count)]
     for j, ref, index in window:
         value = ref[index, part, rows, lanes].astype(F32).reshape(SB // 8, 8, LANES)
         for f in range(count):
-            k = f - j
+            k = f - j - first_tap
             if 0 <= k < tap_count:
                 term = tap_rows[k] * value
                 sums[f] = term if sums[f] is None else sums[f] + term
@@ -173,7 +173,7 @@
             window += [(start + i, ref, i) for i in range(frames)]
 
         def step(lanes, part, rows):
-            sums = weighted(taps, window, count, lanes, part, rows, [None] * count)
+            sums = weighted(taps, 0, window, count, lanes, part, rows, [None] * count)
             for f in range(count):
                 partial[f, part, rows, lanes] = sums[f].reshape(SB, LANES)
 
@@ -197,7 +197,7 @@
     def run(first_out, second_out):
         def step(lanes, part, rows):
             sums = [partial[f, part, rows, lanes].reshape(SB // 8, 8, LANES) for f in range(count)]
-            sums = weighted(taps, window, count, lanes, part, rows, sums)
+            sums = weighted(taps, count, window, count, lanes, part, rows, sums)
             for f in range(count):
                 out = first_out if f < frames else second_out
                 out[f % frames, part, rows, lanes] = sums[f].reshape(SB, LANES).astype(BF16)
@@ -252,8 +252,8 @@
             grid=(size // block,),
             in_specs=[
                 pl.BlockSpec(
-                    (pl.Element(taps.shape[0]), pl.Element(8), pl.Element(block)),
-                    lambda i, place: (0, 0, pl.multiple_of(low + i * block, LANES)),
+                    (pl.Element(taps.shape[0] - count), pl.Element(8), pl.Element(block)),
+                    lambda i, place: (count, 0, pl.multiple_of(low + i * block, LANES)),
                 )
             ]
             + [spec(count, low), spec(far.shape[0], 0)]
@@ -379,7 +379,7 @@
                     mixed[b, target, LANES:] = im.astype(BF16)
                 return carry
 
-            lax.fori_loop(0, frames * tiles, radix, 0, unroll=4 if has_earlier else 2)
+            lax.fori_loop(0, frames * tiles, radix, 0, unroll=2)
         copies[source_count].wait()
 
         def transform(b, carry):
@@ -427,7 +427,7 @@
     groups, depth, width = weights.shape
     beams = width // 2
     station_count = sum(s.shape[2] for s in sources) // ranges
-    at_once = 4 if earlier is None else 2
+    at_once = 4
     flat = (groups, channels // groups * frames, beams)
     flat_spec = pl.BlockSpec((at_once,) + flat[1:], lambda i, place: (i, 0, 0))
     operands = list(sources) + [table, weights] + ([] if earlier is None else [earlier])

time: 207 us -> 207 us (level)
  no operation moved by 1% of the time
where the time goes in v15:
time: 207 us; the launch traced here: 205 us
  Pallas kernels  70.3 us (34%)
  waiting for transfers between devices  69.1 us (33%)
  starting transfers between devices  39.6 us (19%)
  local copies, waits for them, and re-layouts  22 us (11%)
  other arithmetic  4.12 us (2%)
    ppermute x7, waiting for transfers between devices, pair(): return lax.ppermute(block, 'tm', [(i, i ^ 1) for i in range(time_devices)])  45 us
    ppermute x7, waiting for transfers between devices, hop(): lax.ppermute(block, 'tm', [(i, i + 2) for i in range(skip, time_devices -...  19.7 us
    ppermute x7, starting transfers between devices, hop(): lax.ppermute(block, 'tm', [(i, i + 2) for i in range(skip, time_devices -...  19.3 us
    pallas_call x2, Pallas kernels, beam_power(): pl.pallas_call(functools.partial(beam_kernel, len(sources), ranges, len(l...  18.9 us
    pallas_call x4, Pallas kernels, far_filter(): pl.pallas_call(far_kernel, out_shape=(shape, shape), grid_spec=pltpu.Pref...  17.3 us
    pallas_call x2, Pallas kernels, near_filter(): pl.pallas_call(near_kernel, out_shape=jax.ShapeDtypeStruct((2 * frames, p...  15.7 us
    ppermute x8, starting transfers between devices, swap(): return lax.ppermute(block, 'stn', [(0, 1), (1, 0)])  11 us
    pallas_call x4, Pallas kernels, onward(): pl.pallas_call(onward_kernel, out_shape=jax.ShapeDtypeStruct((depth, part...  10.9 us
  transfers between devices with their start and end apart: 25, of which 9 were waited for; matrix products, arithmetic and copies ran while one was open for 10% of the time, Pallas kernels for 28%

profile of v15, /device:TPU:17, one launch (start us, length us, event | category | flops | bytes accessed | tf_op | source)
XLA Modules:
  0.0 205.5 jit_solution(8946610222314567818)
XLA Ops:
  2.4 3.2 %collective-permute-start.1 = (bf16[32,2,4,2,2048]{4,3,2,1,0:T(2,128)(2,1)}, bf16[32,2,4,2,2048]{4,3,2,1,0:T(2,128)(2,1)}, u32[]{:S(2)}, u32[]{:S(2)}) collective-permute-start(bf16[32,2,4,2,2048]{4,3,2,1,0:T(2,128)(2,1)} %cut.2.rest_0_), channel_id=1, source_target_pairs={{0,4},{2,6},{4,8},{6,10},{8,12},{10,14},{1,5},{3,7},{5,9},{7,11},{... | collective-permute-start | bytes 6291464 | tf_op jit(solution)/shard_map/ppermute | solution.py:481
  10.2 22.6 %collective-permute-done.3.refs_0_ = bf16[32,4,2,2048]{3,2,1,0:T(2,128)(2,1)S(1)} collective-permute-done((bf16[32,4,2,2048]{3,2,1,0:T(2,128)(2,1)}, bf16[32,4,2,2048]{3,2,1,0:T(2,128)(2,1)S(1)}, u32[]{:S(2)}, u32[]{:S(2)}) %collective-permute-start.3) | collective-permute-done | bytes 1048608 | tf_op jit(solution)/shard_map/ppermute | solution.py:478
  40.3 14.9 %collective-permute-done.refs_0_ = bf16[32,4,2,2048]{3,2,1,0:T(2,128)(2,1)} collective-permute-done((bf16[32,4,2,2048]{3,2,1,0:T(2,128)(2,1)}, bf16[32,4,2,2048]{3,2,1,0:T(2,128)(2,1)}, u32[]{:S(2)}, u32[]{:S(2)}) %collective-permute-start) | collective-permute-done | bytes 1048608 | tf_op jit(solution)/shard_map/ppermute | solution.py:478
  55.4 2.8 %copy.21 = bf16[32,4,2,2048]{3,0,2,1:T(8,128)(2,1)} copy(bf16[32,4,2,2048]{3,2,1,0:T(2,128)(2,1)} %after.3) | data formatting | bytes 2097152 | tf_op jit(solution)/shard_map/after/pallas_call | solution.py:77
  58.2 4.3 %collective-permute-start.2 = (bf16[4,2,32,2048]{3,2,1,0:T(8,128)(2,1)}, bf16[4,2,32,2048]{3,2,1,0:T(8,128)(2,1)}, u32[]{:S(2)}, u32[]{:S(2)}) collective-permute-start(bf16[4,2,32,2048]{3,2,1,0:T(8,128)(2,1)} %bitcast.27.other), channel_id=1, source_target_pairs={{0,4},{2,6},{4,8},{6,10},{8,12},{10,14},{1,5},{3,7},{5,9},{7,11},{... | collective-permute-start | bytes 3145736 | tf_op jit(solution)/shard_map/ppermute | solution.py:481
  65.7 4.1 %copy.18 = bf16[32,2,4,2,2048]{4,0,3,2,1:T(8,128)(2,1)} copy(bf16[32,2,4,2,2048]{4,3,2,1,0:T(2,128)(2,1)} %after.4) | data formatting | bytes 4194304 | tf_op jit(solution)/shard_map/after/pallas_call | solution.py:77
  69.7 3.0 %collective-permute-done.5.rest_0_ = bf16[16,256]{1,0:T(8,128)(2,1)S(1)} collective-permute-done((bf16[16,256]{1,0:T(8,128)(2,1)S(1)}, bf16[16,256]{1,0:T(8,128)(2,1)S(1)}, u32[]{:S(2)}, u32[]{:S(2)}) %collective-permute-start.5) | collective-permute-done | bytes 8224 | tf_op jit(solution)/shard_map/ppermute | solution.py:494
  74.7 2.7 %onward.4.rest_0_ = bf16[7,2,32,1024]{3,2,1,0:T(8,128)(2,1)} custom-call(s32[2]{0:T(128)} %pad_add_fusion.rest_1_.place, bf16[2,4,2,32,2048]{4,3,2,1,0:T(8,128)(2,1)} %bitcast.28, bf16[4,2,32,2048]{3,2,1,0:T(8,128)(2,1)} %collective-permute-done.4.other_back, bf16[16,256]{1,0:T(8,128)(2,1)} %copy-done.10, bf16[16,256]{1,0:T(8,128)(2,1)} %copy-done.11, ...), custom_call_target="tpu_custom_call" | custom-call | bytes 9900000 | tf_op jit(solution)/shard_map/onward/pallas_call | solution.py:295
  77.4 3.0 %collective-permute-start.11 = (bf16[7,2,32,1024]{3,2,1,0:T(8,128)(2,1)}, bf16[7,2,32,1024]{3,2,1,0:T(8,128)(2,1)S(1)}, u32[]{:S(2)}, u32[]{:S(2)}) collective-permute-start(bf16[7,2,32,1024]{3,2,1,0:T(8,128)(2,1)} %onward.4.rest_0_), channel_id=1, source_target_pairs={{4,8},{6,10},{8,12},{10,14},{5,9},{7,11},{9,13},{11,15},{20,24},{2... | collective-permute-start | bytes 2752520 | tf_op jit(solution)/shard_map/ppermute | solution.py:481
  98.8 7.8 %near.3.partial = f32[8,2,32,2048]{3,2,1,0:T(8,128)} custom-call(s32[2]{0:T(128)} %pad_add_fusion.rest_1_.place, f32[16,8,2048]{2,1,0:T(8,128)} %broadcast_in_dim.2.taps, bf16[2,4,2,32,2048]{4,3,2,1,0:T(8,128)(2,1)} %bitcast.34, bf16[4,2,32,2048]{3,2,1,0:T(8,128)(2,1)} %bitcast.37, bf16[2,4,2,32,2048]{4,3,2,1,0:T(8,128)(2,1)} %bitcast.30, ...), custom_call_target="tpu_custom_call" | custom-call | bytes 26400000 | tf_op jit(solution)/shard_map/near/pallas_call | solution.py:221
  106.6 9.7 %collective-permute-done.11.far = bf16[7,2,32,1024]{3,2,1,0:T(8,128)(2,1)S(1)} collective-permute-done((bf16[7,2,32,1024]{3,2,1,0:T(8,128)(2,1)}, bf16[7,2,32,1024]{3,2,1,0:T(8,128)(2,1)S(1)}, u32[]{:S(2)}, u32[]{:S(2)}) %collective-permute-start.11) | collective-permute-done | bytes 917536 | tf_op jit(solution)/shard_map/ppermute | solution.py:481
  117.3 3.9 %far.4 = (bf16[4,2,32,1024]{3,2,1,0:T(8,128)(2,1)}, bf16[4,2,32,1024]{3,2,1,0:T(8,128)(2,1)}) custom-call(s32[2]{0:T(128)} %pad_add_fusion.rest_1_.place, f32[16,8,2048]{2,1,0:T(8,128)} %broadcast_in_dim.2.taps, f32[8,2,32,2048]{3,2,1,0:T(8,128)} %near.3.partial, bf16[7,2,32,1024]{3,2,1,0:T(8,128)(2,1)} %copy-done.5), custom_call_target="tpu_custom_call" | custom-call | bytes 3300000 | tf_op jit(solution)/shard_map/far/pallas_call | solution.py:247
  122.3 2.8 %onward.6.rest_2_ = bf16[7,2,32,1152]{3,2,1,0:T(8,128)(2,1)} custom-call(s32[2]{0:T(128)} %pad_add_fusion.rest_1_.place, bf16[2,4,2,32,2048]{4,3,2,1,0:T(8,128)(2,1)} %bitcast.31, bf16[4,2,32,2048]{3,2,1,0:T(8,128)(2,1)} %collective-permute-done.2.other_back.rest_5_.rest_3_), custom_call_target="tpu_custom_call" | custom-call | bytes 9900000 | tf_op jit(solution)/shard_map/onward/pallas_call | solution.py:295
  125.1 3.0 %collective-permute-start.9 = (bf16[7,2,32,1152]{3,2,1,0:T(8,128)(2,1)}, bf16[7,2,32,1152]{3,2,1,0:T(8,128)(2,1)}, u32[]{:S(2)}, u32[]{:S(2)}) collective-permute-start(bf16[7,2,32,1152]{3,2,1,0:T(8,128)(2,1)} %onward.6.rest_2_), channel_id=1, source_target_pairs={{4,8},{6,10},{8,12},{10,14},{5,9},{7,11},{9,13},{11,15},{20,24},{2... | collective-permute-start | bytes 3096584 | tf_op jit(solution)/shard_map/ppermute | solution.py:481
  128.1 2.8 %onward.7.rest_3_ = bf16[7,2,32,896]{3,2,1,0:T(8,128)(2,1)} custom-call(s32[2]{0:T(128)} %pad_add_fusion.rest_1_.place, bf16[2,4,2,32,2048]{4,3,2,1,0:T(8,128)(2,1)} %bitcast.32, bf16[4,2,32,2048]{3,2,1,0:T(8,128)(2,1)} %collective-permute-done.2.other_back.rest_5_.rest_3_), custom_call_target="tpu_custom_call" | custom-call | bytes 9900000 | tf_op jit(solution)/shard_map/onward/pallas_call | solution.py:295
  130.9 7.8 %near.2.rest_1_.partial = f32[8,2,32,2048]{3,2,1,0:T(8,128)} custom-call(s32[2]{0:T(128)} %pad_add_fusion.rest_1_.place, f32[16,8,2048]{2,1,0:T(8,128)} %broadcast_in_dim.2.taps, bf16[2,4,2,32,2048]{4,3,2,1,0:T(8,128)(2,1)} %bitcast.35, bf16[4,2,32,2048]{3,2,1,0:T(8,128)(2,1)} %bitcast.27.other, bf16[2,4,2,32,2048]{4,3,2,1,0:T(8,128)(2,1)} %bitcast.33, ...), custom_call_target="tpu_custom_call" | custom-call | bytes 26400000 | tf_op jit(solution)/shard_map/near/pallas_call | solution.py:221
  138.7 4.0 %far.5 = (bf16[4,2,32,1024]{3,2,1,0:T(8,128)(2,1)}, bf16[4,2,32,1024]{3,2,1,0:T(8,128)(2,1)}) custom-call(s32[2]{0:T(128)} %pad_add_fusion.rest_1_.place, f32[16,8,2048]{2,1,0:T(8,128)} %broadcast_in_dim.2.taps, f32[8,2,32,2048]{3,2,1,0:T(8,128)} %near.3.partial, bf16[7,2,32,1024]{3,2,1,0:T(8,128)(2,1)} %collective-permute-done.10.far, ...), custom_call_target="tpu_custom_call" | custom-call | bytes 3300000 | tf_op jit(solution)/shard_map/far/pallas_call | solution.py:247
  144.8 3.6 %collective-permute-start.15 = (bf16[4,2,32,1024]{3,2,1,0:T(8,128)(2,1)}, bf16[4,2,32,1024]{3,2,1,0:T(8,128)(2,1)}, u32[]{:S(2)}, u32[]{:S(2)}) collective-permute-start(bf16[4,2,32,1024]{3,2,1,0:T(8,128)(2,1)} %get-tuple-element.20.refs_0_), channel_id=1, source_target_pairs={{0,1},{1,0},{2,3},{3,2},{4,5},{5,4},{6,7},{7,6},{8,9},{9,8},{10,11... | collective-permute-start | bytes 1572872 | tf_op jit(solution)/shard_map/ppermute | solution.py:484
  148.5 9.7 %collective-permute-done.9.far = bf16[7,2,32,1152]{3,2,1,0:T(8,128)(2,1)} collective-permute-done((bf16[7,2,32,1152]{3,2,1,0:T(8,128)(2,1)}, bf16[7,2,32,1152]{3,2,1,0:T(8,128)(2,1)}, u32[]{:S(2)}, u32[]{:S(2)}) %collective-permute-start.9) | collective-permute-done | bytes 1032224 | tf_op jit(solution)/shard_map/ppermute | solution.py:481
  160.9 4.9 %far.6 = (bf16[4,2,32,1152]{3,2,1,0:T(8,128)(2,1)}, bf16[4,2,32,1152]{3,2,1,0:T(8,128)(2,1)}) custom-call(s32[2]{0:T(128)} %pad_add_fusion.rest_1_.place, f32[16,8,2048]{2,1,0:T(8,128)} %broadcast_in_dim.2.taps, f32[8,2,32,2048]{3,2,1,0:T(8,128)} %near.2.rest_1_.partial, bf16[7,2,32,1152]{3,2,1,0:T(8,128)(2,1)} %collective-permute-done.9.far, ...), custom_call_target="tpu_custom_call" | custom-call | bytes 3300000 | tf_op jit(solution)/shard_map/far/pallas_call | solution.py:247
  167.1 8.5 %beams.2.rest_0_.refs_10_ = f32[8,512,256]{2,1,0:T(8,128)} custom-call(s32[2]{0:T(128)} %pad_add_fusion.rest_1_.place, bf16[4,2,32,1024]{3,2,1,0:T(8,128)(2,1)} %get-tuple-element.20.refs_0_, bf16[4,2,32,1024]{3,2,1,0:T(8,128)(2,1)} %get-tuple-element.21.refs_1_, bf16[4,2,32,1024]{3,2,1,0:T(8,128)(2,1)} %collective-permute-done.12.rest_0_.refs_2_, ...), custom_call_target="tpu_custom_call" | custom-call | tf_op jit(solution)/shard_map/beams/pallas_call | solution.py:448
  175.6 4.5 %far.7 = (bf16[4,2,32,896]{3,2,1,0:T(8,128)(2,1)}, bf16[4,2,32,896]{3,2,1,0:T(8,128)(2,1)}) custom-call(s32[2]{0:T(128)} %pad_add_fusion.rest_1_.place, f32[16,8,2048]{2,1,0:T(8,128)} %broadcast_in_dim.2.taps, f32[8,2,32,2048]{3,2,1,0:T(8,128)} %near.2.rest_1_.partial, bf16[7,2,32,896]{3,2,1,0:T(8,128)(2,1)} %collective-permute-done.14.far, ...), custom_call_target="tpu_custom_call" | custom-call | bytes 3300000 | tf_op jit(solution)/shard_map/far/pallas_call | solution.py:247
  183.5 7.5 %collective-permute-done.20.refs_3_ = bf16[4,2,32,896]{3,2,1,0:T(8,128)(2,1)S(1)} collective-permute-done((bf16[4,2,32,896]{3,2,1,0:T(8,128)(2,1)}, bf16[4,2,32,896]{3,2,1,0:T(8,128)(2,1)S(1)}, u32[]{:S(2)}, u32[]{:S(2)}) %collective-permute-start.20) | collective-permute-done | bytes 458784 | tf_op jit(solution)/shard_map/ppermute | solution.py:478
  194.9 10.4 %beams.3 = f32[1024,2,4,128]{3,2,1,0:T(4,128)} custom-call(s32[2]{0:T(128)} %pad_add_fusion.rest_1_.place, bf16[4,2,32,1152]{3,2,1,0:T(8,128)(2,1)} %get-tuple-element.19.refs_10_.refs_0_, bf16[4,2,32,896]{3,2,1,0:T(8,128)(2,1)} %get-tuple-element.22.refs_1_, bf16[4,2,32,1152]{3,2,1,0:T(8,128)(2,1)} %collective-permute-done.19.refs_2_, ...), custom_call_target="tpu_custom_call" | custom-call | tf_op jit(solution)/shard_map/beams/pallas_call | solution.py:448
  (98 shorter events, 53.7 us)
Async XLA Ops:
  2.4 55.8 %collective-permute-start.1 = (bf16[32,2,4,2,2048]{4,3,2,1,0:T(2,128)(2,1)}, bf16[32,2,4,2,2048]{4,3,2,1,0:T(2,128)(2,1)}, u32[]{:S(2)}, u32[]{:S(2)}) collective-permute-start(bf16[32,2,4,2,2048]{4,3,2,1,0:T(2,128)(2,1)} %cut.2.rest_0_), channel_id=1, source_target_pairs={{0,4},{2,6},{4,8},{6,10},{8,12},{10,14},{1,5},{3,7},{5,9},{7,11},{... | collective-permute-start | bytes 6291464 | tf_op jit(solution)/shard_map/ppermute | solution.py:481
  8.7 24.1 %collective-permute-start.3 = (bf16[32,4,2,2048]{3,2,1,0:T(2,128)(2,1)}, bf16[32,4,2,2048]{3,2,1,0:T(2,128)(2,1)S(1)}, u32[]{:S(2)}, u32[]{:S(2)}) collective-permute-start(bf16[32,4,2,2048]{3,2,1,0:T(2,128)(2,1)} %get-tuple-element.16), channel_id=1, source_target_pairs={{0,2},{2,0},{4,6},{6,4},{8,10},{10,8},{12,14},{14,12},{1,3},{3,1},... | collective-permute-start | bytes 3145736 | tf_op jit(solution)/shard_map/ppermute | solution.py:478
  10.0 45.2 %collective-permute-start = (bf16[32,4,2,2048]{3,2,1,0:T(2,128)(2,1)}, bf16[32,4,2,2048]{3,2,1,0:T(2,128)(2,1)}, u32[]{:S(2)}, u32[]{:S(2)}) collective-permute-start(bf16[32,4,2,2048]{3,2,1,0:T(2,128)(2,1)} %get-tuple-element.15), channel_id=1, source_target_pairs={{0,2},{2,0},{4,6},{6,4},{8,10},{10,8},{12,14},{14,12},{1,3},{3,1},... | collective-permute-start | bytes 3145736 | tf_op jit(solution)/shard_map/ppermute | solution.py:478
  35.6 38.5 %collective-permute-start.4 = (bf16[4,2,32,2048]{3,2,1,0:T(8,128)(2,1)S(1)}, bf16[4,2,32,2048]{3,2,1,0:T(8,128)(2,1)}, u32[]{:S(2)}, u32[]{:S(2)}) collective-permute-start(bf16[4,2,32,2048]{3,2,1,0:T(8,128)(2,1)S(1)} %bitcast.36), channel_id=1, source_target_pairs={{0,4},{2,6},{4,8},{6,10},{8,12},{10,14},{1,5},{3,7},{5,9},{7,11},{... | collective-permute-start | bytes 3145736 | tf_op jit(solution)/shard_map/ppermute | solution.py:481
  37.6 35.1 %collective-permute-start.5 = (bf16[16,256]{1,0:T(8,128)(2,1)S(1)}, bf16[16,256]{1,0:T(8,128)(2,1)S(1)}, u32[]{:S(2)}, u32[]{:S(2)}) collective-permute-start(bf16[16,256]{1,0:T(8,128)(2,1)S(1)} %get-tuple-element.26), channel_id=1, source_target_pairs={{0,4},{2,6},{4,0},{6,2},{8,12},{10,14},{12,8},{14,10},{1,5},{3,7},... | collective-permute-start | bytes 24584 | tf_op jit(solution)/shard_map/ppermute | solution.py:494
  37.6 35.8 %collective-permute-start.6 = (bf16[16,256]{1,0:T(8,128)(2,1)S(1)}, bf16[16,256]{1,0:T(8,128)(2,1)S(1)}, u32[]{:S(2)}, u32[]{:S(2)}) collective-permute-start(bf16[16,256]{1,0:T(8,128)(2,1)S(1)} %get-tuple-element.26), channel_id=1, source_target_pairs={{0,8},{2,10},{4,12},{6,14},{8,0},{10,2},{12,4},{14,6},{1,9},{3,11}... | collective-permute-start | bytes 24584 | tf_op jit(solution)/shard_map/ppermute | solution.py:494
  55.3 18.9 %collective-permute-start.7 = (bf16[16,256]{1,0:T(8,128)(2,1)S(1)}, bf16[16,256]{1,0:T(8,128)(2,1)S(1)}, u32[]{:S(2)}, u32[]{:S(2)}) collective-permute-start(bf16[16,256]{1,0:T(8,128)(2,1)S(1)} %get-tuple-element.26), channel_id=1, source_target_pairs={{0,12},{2,14},{4,8},{6,10},{8,4},{10,6},{12,0},{14,2},{1,13},{3,15... | collective-permute-start | bytes 24584 | tf_op jit(solution)/shard_map/ppermute | solution.py:494
  58.2 38.6 %collective-permute-start.2 = (bf16[4,2,32,2048]{3,2,1,0:T(8,128)(2,1)}, bf16[4,2,32,2048]{3,2,1,0:T(8,128)(2,1)}, u32[]{:S(2)}, u32[]{:S(2)}) collective-permute-start(bf16[4,2,32,2048]{3,2,1,0:T(8,128)(2,1)} %bitcast.27.other), channel_id=1, source_target_pairs={{0,4},{2,6},{4,8},{6,10},{8,12},{10,14},{1,5},{3,7},{5,9},{7,11},{... | collective-permute-start | bytes 3145736 | tf_op jit(solution)/shard_map/ppermute | solution.py:481
  77.4 38.9 %collective-permute-start.11 = (bf16[7,2,32,1024]{3,2,1,0:T(8,128)(2,1)}, bf16[7,2,32,1024]{3,2,1,0:T(8,128)(2,1)S(1)}, u32[]{:S(2)}, u32[]{:S(2)}) collective-permute-start(bf16[7,2,32,1024]{3,2,1,0:T(8,128)(2,1)} %onward.4.rest_0_), channel_id=1, source_target_pairs={{4,8},{6,10},{8,12},{10,14},{5,9},{7,11},{9,13},{11,15},{20,24},{2... | collective-permute-start | bytes 2752520 | tf_op jit(solution)/shard_map/ppermute | solution.py:481
  84.6 7.9 %collective-permute-start.8 = (bf16[64,256]{1,0:T(8,128)(2,1)}, bf16[64,256]{1,0:T(8,128)(2,1)}, u32[]{:S(2)}, u32[]{:S(2)}) collective-permute-start(bf16[64,256]{1,0:T(8,128)(2,1)} %pad_maximum_fusion), channel_id=1, source_target_pairs={{0,2},{2,0},{4,6},{6,4},{8,10},{10,8},{12,14},{14,12},{1,3},{3,1},... | collective-permute-start | bytes 98312 | tf_op jit(solution)/shard_map/ppermute | solution.py:478
  88.5 50.2 %collective-permute-start.10 = (bf16[7,2,32,1024]{3,2,1,0:T(8,128)(2,1)}, bf16[7,2,32,1024]{3,2,1,0:T(8,128)(2,1)}, u32[]{:S(2)}, u32[]{:S(2)}) collective-permute-start(bf16[7,2,32,1024]{3,2,1,0:T(8,128)(2,1)} %onward.5.rest_1_), channel_id=1, source_target_pairs={{4,8},{6,10},{8,12},{10,14},{5,9},{7,11},{9,13},{11,15},{20,24},{2... | collective-permute-start | bytes 2752520 | tf_op jit(solution)/shard_map/ppermute | solution.py:481
  121.1 17.6 %collective-permute-start.12 = (bf16[4,2,32,1024]{3,2,1,0:T(8,128)(2,1)}, bf16[4,2,32,1024]{3,2,1,0:T(8,128)(2,1)}, u32[]{:S(2)}, u32[]{:S(2)}) collective-permute-start(bf16[4,2,32,1024]{3,2,1,0:T(8,128)(2,1)} %get-tuple-element.17), channel_id=1, source_target_pairs={{0,2},{2,0},{4,6},{6,4},{8,10},{10,8},{12,14},{14,12},{1,3},{3,1},... | collective-permute-start | bytes 1572872 | tf_op jit(solution)/shard_map/ppermute | solution.py:478
  125.1 33.1 %collective-permute-start.9 = (bf16[7,2,32,1152]{3,2,1,0:T(8,128)(2,1)}, bf16[7,2,32,1152]{3,2,1,0:T(8,128)(2,1)}, u32[]{:S(2)}, u32[]{:S(2)}) collective-permute-start(bf16[7,2,32,1152]{3,2,1,0:T(8,128)(2,1)} %onward.6.rest_2_), channel_id=1, source_target_pairs={{4,8},{6,10},{8,12},{10,14},{5,9},{7,11},{9,13},{11,15},{20,24},{2... | collective-permute-start | bytes 3096584 | tf_op jit(solution)/shard_map/ppermute | solution.py:481
  142.7 18.2 %collective-permute-start.13 = (bf16[4,2,32,1024]{3,2,1,0:T(8,128)(2,1)}, bf16[4,2,32,1024]{3,2,1,0:T(8,128)(2,1)}, u32[]{:S(2)}, u32[]{:S(2)}) collective-permute-start(bf16[4,2,32,1024]{3,2,1,0:T(8,128)(2,1)} %get-tuple-element.18), channel_id=1, source_target_pairs={{0,2},{2,0},{4,6},{6,4},{8,10},{10,8},{12,14},{14,12},{1,3},{3,1},... | collective-permute-start | bytes 1572872 | tf_op jit(solution)/shard_map/ppermute | solution.py:478
  142.9 32.7 %collective-permute-start.14 = (bf16[7,2,32,896]{3,2,1,0:T(8,128)(2,1)S(1)}, bf16[7,2,32,896]{3,2,1,0:T(8,128)(2,1)}, u32[]{:S(2)}, u32[]{:S(2)}) collective-permute-start(bf16[7,2,32,896]{3,2,1,0:T(8,128)(2,1)S(1)} %copy-done.3), channel_id=1, source_target_pairs={{4,8},{6,10},{8,12},{10,14},{5,9},{7,11},{9,13},{11,15},{20,24},{2... | collective-permute-start | bytes 2408456 | tf_op jit(solution)/shard_map/ppermute | solution.py:481
  144.8 21.1 %collective-permute-start.15 = (bf16[4,2,32,1024]{3,2,1,0:T(8,128)(2,1)}, bf16[4,2,32,1024]{3,2,1,0:T(8,128)(2,1)}, u32[]{:S(2)}, u32[]{:S(2)}) collective-permute-start(bf16[4,2,32,1024]{3,2,1,0:T(8,128)(2,1)} %get-tuple-element.20.refs_0_), channel_id=1, source_target_pairs={{0,1},{1,0},{2,3},{3,2},{4,5},{5,4},{6,7},{7,6},{8,9},{9,8},{10,11... | collective-permute-start | bytes 1572872 | tf_op jit(solution)/shard_map/ppermute | solution.py:484
  148.4 18.7 %collective-permute-start.16 = (bf16[4,2,32,1024]{3,2,1,0:T(8,128)(2,1)}, bf16[4,2,32,1024]{3,2,1,0:T(8,128)(2,1)}, u32[]{:S(2)}, u32[]{:S(2)}) collective-permute-start(bf16[4,2,32,1024]{3,2,1,0:T(8,128)(2,1)} %get-tuple-element.21.refs_1_), channel_id=1, source_target_pairs={{0,1},{1,0},{2,3},{3,2},{4,5},{5,4},{6,7},{7,6},{8,9},{9,8},{10,11... | collective-permute-start | bytes 1572872 | tf_op jit(solution)/shard_map/ppermute | solution.py:484
  158.2 8.9 %collective-permute-start.17 = (bf16[4,2,32,1024]{3,2,1,0:T(8,128)(2,1)}, bf16[4,2,32,1024]{3,2,1,0:T(8,128)(2,1)}, u32[]{:S(2)}, u32[]{:S(2)}) collective-permute-start(bf16[4,2,32,1024]{3,2,1,0:T(8,128)(2,1)} %collective-permute-done.12.rest_0_.refs_2_), channel_id=1, source_target_pairs={{0,1},{1,0},{2,3},{3,2},{4,5},{5,4},{6,7},{7,6},{8,9},{9,8},{10,11... | collective-permute-start | bytes 1572872 | tf_op jit(solution)/shard_map/ppermute | solution.py:484
  160.9 6.2 %collective-permute-start.18 = (bf16[4,2,32,1024]{3,2,1,0:T(8,128)(2,1)}, bf16[4,2,32,1024]{3,2,1,0:T(8,128)(2,1)}, u32[]{:S(2)}, u32[]{:S(2)}) collective-permute-start(bf16[4,2,32,1024]{3,2,1,0:T(8,128)(2,1)} %collective-permute-done.13.rest_0_.refs_3_), channel_id=1, source_target_pairs={{0,1},{1,0},{2,3},{3,2},{4,5},{5,4},{6,7},{7,6},{8,9},{9,8},{10,11... | collective-permute-start | bytes 1572872 | tf_op jit(solution)/shard_map/ppermute | solution.py:484
  165.9 17.1 %collective-permute-start.19 = (bf16[4,2,32,1152]{3,2,1,0:T(8,128)(2,1)}, bf16[4,2,32,1152]{3,2,1,0:T(8,128)(2,1)}, u32[]{:S(2)}, u32[]{:S(2)}) collective-permute-start(bf16[4,2,32,1152]{3,2,1,0:T(8,128)(2,1)} %get-tuple-element.23), channel_id=1, source_target_pairs={{0,2},{2,0},{4,6},{6,4},{8,10},{10,8},{12,14},{14,12},{1,3},{3,1},... | collective-permute-start | bytes 1769480 | tf_op jit(solution)/shard_map/ppermute | solution.py:478
  180.1 10.9 %collective-permute-start.20 = (bf16[4,2,32,896]{3,2,1,0:T(8,128)(2,1)}, bf16[4,2,32,896]{3,2,1,0:T(8,128)(2,1)S(1)}, u32[]{:S(2)}, u32[]{:S(2)}) collective-permute-start(bf16[4,2,32,896]{3,2,1,0:T(8,128)(2,1)} %get-tuple-element.24), channel_id=1, source_target_pairs={{0,2},{2,0},{4,6},{6,4},{8,10},{10,8},{12,14},{14,12},{1,3},{3,1},... | collective-permute-start | bytes 1376264 | tf_op jit(solution)/shard_map/ppermute | solution.py:478
  181.2 12.1 %collective-permute-start.21 = (bf16[4,2,32,1152]{3,2,1,0:T(8,128)(2,1)S(1)}, bf16[4,2,32,1152]{3,2,1,0:T(8,128)(2,1)S(1)}, u32[]{:S(2)}, u32[]{:S(2)}) collective-permute-start(bf16[4,2,32,1152]{3,2,1,0:T(8,128)(2,1)S(1)} %copy-done.4), channel_id=1, source_target_pairs={{0,1},{1,0},{2,3},{3,2},{4,5},{5,4},{6,7},{7,6},{8,9},{9,8},{10,11... | collective-permute-start | bytes 1769480 | tf_op jit(solution)/shard_map/ppermute | solution.py:484
  183.0 11.1 %collective-permute-start.23 = (bf16[4,2,32,1152]{3,2,1,0:T(8,128)(2,1)}, bf16[4,2,32,1152]{3,2,1,0:T(8,128)(2,1)}, u32[]{:S(2)}, u32[]{:S(2)}) collective-permute-start(bf16[4,2,32,1152]{3,2,1,0:T(8,128)(2,1)} %collective-permute-done.19.refs_2_), channel_id=1, source_target_pairs={{0,1},{1,0},{2,3},{3,2},{4,5},{5,4},{6,7},{7,6},{8,9},{9,8},{10,11... | collective-permute-start | bytes 1769480 | tf_op jit(solution)/shard_map/ppermute | solution.py:484
  183.1 11.1 %collective-permute-start.22 = (bf16[4,2,32,896]{3,2,1,0:T(8,128)(2,1)}, bf16[4,2,32,896]{3,2,1,0:T(8,128)(2,1)S(1)}, u32[]{:S(2)}, u32[]{:S(2)}) collective-permute-start(bf16[4,2,32,896]{3,2,1,0:T(8,128)(2,1)} %get-tuple-element.22.refs_1_), channel_id=1, source_target_pairs={{0,1},{1,0},{2,3},{3,2},{4,5},{5,4},{6,7},{7,6},{8,9},{9,8},{10,11... | collective-permute-start | bytes 1376264 | tf_op jit(solution)/shard_map/ppermute | solution.py:484
  (18 other events, 177.7 us)

commit v16 on v15

--- a/solution.py
+++ b/solution.py
@@ -237,7 +237,7 @@
 def far_filter(place, taps, partial, far, low, size, earlier):
     count, parts, stations, _ = partial.shape
     frames = count // 2
-    block = next(size // n for n in (2, 3, 1) if size // n % LANES == 0)
+    block = next(size // n for n in (2, 1) if size // n % LANES == 0)
 
     def spec(depth, start):
         shape = (pl.Element(depth), pl.Element(parts), pl.Element(stations), pl.Element(block))
@@ -509,7 +509,7 @@
     table = jnp.asarray(dft_tables(samples))
     taps = jnp.broadcast_to(filter_taps[:, None, :], (history + 1, 8, samples))
 
-    parts_of = [(samples // 2, samples // 2), (9 * samples // 16, 7 * samples // 16)]
+    parts_of = [tuple(n * samples // 16 for n in sizes) for sizes in ((10,6), (8,5,3))]
     chunks = [(pol, sum(sizes[:i]), size) for pol, sizes in enumerate(parts_of) for i, size in enumerate(sizes)]
     other_back = [hop(block) for block in other]
     further = []
@@ -521,17 +521,18 @@
     weights = beam_weights(jnp.concatenate([shards, pair(shards)]), ordered(index), ordered(use_mask), [])
     partial = []
     for pol in range(pols):
-        gates = further[: 2 * pol + 2] + [weights] + other_back[1:]
+        gates = (further if pol else further[:2]) + [weights] + other_back[1:]
         partial.append(near_filter(place, taps, own, other[pol], own_back, other_back[pol], pol, gates))
     keeps, sents, power = [], [], None
 
     def power_of(pol, earlier, later=()):
-        mine, pairs = keeps[2 * pol : 2 * pol + 2], sents[2 * pol : 2 * pol + 2]
+        here = slice(2 * pol, 2 + len(chunks) * pol)
+        mine, pairs = keeps[here], sents[here]
         sources = mine + pairs + [swap(block) for block in mine + pairs]
-        return beam_power(place, sources, 2, table, weights, earlier, samples // CORES, later)
+        return beam_power(place, sources, len(mine), table, weights, earlier, samples // CORES, later)
 
     for k, (pol, low, size) in enumerate(chunks):
-        gates = {0: [], 1: [*sents[:1], partial[1]], 2: sents[1:2], 3: [power]}[k]
+        gates = {0: [], 1: [*sents[:1], partial[1]], 2: sents[1:2], 3: [power], 4: keeps[3:4]}[k]
         keep, send = far_filter(place, taps, partial[pol], far[k], low, size, gates)
         keeps.append(keep)
         sents.append(pair(send))

time: 207 us -> 215 us (1.039)
  waiting for transfers between devices: 69.1 us -> 77.1 us
  Pallas kernels: 70.3 us -> 74.2 us
  other arithmetic: 4.12 us -> 0.7 us
    ppermute x7 -> x8, waiting for transfers between devices: 45 us -> 51.4 us  [pair(): return lax.ppermute(block, 'tm', [(i, i ^ 1) for i in range(time_devices)])]
    ppermute x3, waiting for transfers between devices: 4.38 us -> 7.37 us  [body(): lax.ppermute(shard, 'tm', [(i, i ^ apart) for i in range(time_devices)])]
    pallas_call x4 -> x5, Pallas kernels: 10.9 us -> 13.4 us  [onward(): pl.pallas_call(onward_kernel, out_shape=jax.ShapeDtypeStruct((depth, part...]
    ppermute x7 -> x8, waiting for transfers between devices: 19.7 us -> 17.3 us  [hop(): lax.ppermute(block, 'tm', [(i, i + 2) for i in range(skip, time_devices -...]
    transpose x3, other arithmetic: 2.18 us -> 0.02 us  [ordered(): rows = flipped(rows.swapaxes(0, 1), side).swapaxes(0, 1)]
    unnamed x38 -> x50, local copies, waits for them, and re-layouts: 6.86 us -> 5.37 us
    pallas_call x4 -> x5, Pallas kernels: 17.3 us -> 18.6 us  [far_filter(): pl.pallas_call(far_kernel, out_shape=(shape, shape), grid_spec=pltpu.Pref...]
    ppermute x8 -> x10, starting transfers between devices: 11 us -> 9.7 us  [swap(): return lax.ppermute(block, 'stn', [(0, 1), (1, 0)])]
  transfers between devices with their start and end apart: 25 -> 29, of which waited for: 9 -> 12; matrix products, arithmetic and copies ran while one was open for 10% -> 7% of each run, Pallas kernels for 28% -> 29%
where the time goes in v16:
time: 215 us; the launch traced here: 212 us
  waiting for transfers between devices  77.1 us (36%)
  Pallas kernels  74.2 us (35%)
  starting transfers between devices  38.8 us (18%)
  local copies, waits for them, and re-layouts  20.5 us (10%)
    ppermute x8, waiting for transfers between devices, pair(): return lax.ppermute(block, 'tm', [(i, i ^ 1) for i in range(time_devices)])  51.4 us
    ppermute x8, starting transfers between devices, hop(): lax.ppermute(block, 'tm', [(i, i + 2) for i in range(skip, time_devices -...  20.4 us
    pallas_call x2, Pallas kernels, beam_power(): pl.pallas_call(functools.partial(beam_kernel, len(sources), ranges, len(l...  19.1 us
    pallas_call x5, Pallas kernels, far_filter(): pl.pallas_call(far_kernel, out_shape=(shape, shape), grid_spec=pltpu.Pref...  18.6 us
    ppermute x8, waiting for transfers between devices, hop(): lax.ppermute(block, 'tm', [(i, i + 2) for i in range(skip, time_devices -...  17.3 us
    pallas_call x2, Pallas kernels, near_filter(): pl.pallas_call(near_kernel, out_shape=jax.ShapeDtypeStruct((2 * frames, p...  15.7 us
    pallas_call x5, Pallas kernels, onward(): pl.pallas_call(onward_kernel, out_shape=jax.ShapeDtypeStruct((depth, part...  13.4 us
    ppermute x10, starting transfers between devices, swap(): return lax.ppermute(block, 'stn', [(0, 1), (1, 0)])  9.7 us
  transfers between devices with their start and end apart: 29, of which 12 were waited for; matrix products, arithmetic and copies ran while one was open for 7% of the time, Pallas kernels for 29%

profile of v16, /device:TPU:17, one launch (start us, length us, event | category | flops | bytes accessed | tf_op | source)
XLA Modules:
  0.0 211.9 jit_solution(4121936860411844179)
XLA Ops:
  2.4 3.2 %collective-permute-start.1 = (bf16[32,2,4,2,2048]{4,3,2,1,0:T(2,128)(2,1)}, bf16[32,2,4,2,2048]{4,3,2,1,0:T(2,128)(2,1)}, u32[]{:S(2)}, u32[]{:S(2)}) collective-permute-start(bf16[32,2,4,2,2048]{4,3,2,1,0:T(2,128)(2,1)} %cut.2.rest_0_), channel_id=1, source_target_pairs={{0,4},{2,6},{4,8},{6,10},{8,12},{10,14},{1,5},{3,7},{5,9},{7,11},{... | collective-permute-start | bytes 6291464 | tf_op jit(solution)/shard_map/ppermute | solution.py:481
  10.3 22.6 %collective-permute-done.3.refs_0_ = bf16[32,4,2,2048]{3,2,1,0:T(2,128)(2,1)S(1)} collective-permute-done((bf16[32,4,2,2048]{3,2,1,0:T(2,128)(2,1)}, bf16[32,4,2,2048]{3,2,1,0:T(2,128)(2,1)S(1)}, u32[]{:S(2)}, u32[]{:S(2)}) %collective-permute-start.3) | collective-permute-done | bytes 1048608 | tf_op jit(solution)/shard_map/ppermute | solution.py:478
  40.3 15.0 %collective-permute-done.refs_0_ = bf16[32,4,2,2048]{3,2,1,0:T(2,128)(2,1)S(1)} collective-permute-done((bf16[32,4,2,2048]{3,2,1,0:T(2,128)(2,1)}, bf16[32,4,2,2048]{3,2,1,0:T(2,128)(2,1)S(1)}, u32[]{:S(2)}, u32[]{:S(2)}) %collective-permute-start) | collective-permute-done | bytes 1048608 | tf_op jit(solution)/shard_map/ppermute | solution.py:478
  59.1 3.5 %collective-permute-start.2 = (bf16[4,2,32,2048]{3,2,1,0:T(8,128)(2,1)}, bf16[4,2,32,2048]{3,2,1,0:T(8,128)(2,1)}, u32[]{:S(2)}, u32[]{:S(2)}) collective-permute-start(bf16[4,2,32,2048]{3,2,1,0:T(8,128)(2,1)} %bitcast.27.other), channel_id=1, source_target_pairs={{0,4},{2,6},{4,8},{6,10},{8,12},{10,14},{1,5},{3,7},{5,9},{7,11},{... | collective-permute-start | bytes 3145736 | tf_op jit(solution)/shard_map/ppermute | solution.py:481
  62.6 4.1 %copy.18 = bf16[32,2,4,2,2048]{4,0,3,2,1:T(8,128)(2,1)} copy(bf16[32,2,4,2,2048]{4,3,2,1,0:T(2,128)(2,1)} %after.4) | data formatting | bytes 4194304 | tf_op jit(solution)/shard_map/after/pallas_call | solution.py:77
  66.8 5.9 %collective-permute-done.5.rest_0_ = bf16[16,256]{1,0:T(8,128)(2,1)S(1)} collective-permute-done((bf16[16,256]{1,0:T(8,128)(2,1)S(1)}, bf16[16,256]{1,0:T(8,128)(2,1)S(1)}, u32[]{:S(2)}, u32[]{:S(2)}) %collective-permute-start.5) | collective-permute-done | bytes 8224 | tf_op jit(solution)/shard_map/ppermute | solution.py:494
  74.7 2.9 %onward.5.rest_0_ = bf16[7,2,32,1280]{3,2,1,0:T(8,128)(2,1)} custom-call(s32[2]{0:T(128)} %pad_add_fusion.rest_1_.place, bf16[2,4,2,32,2048]{4,3,2,1,0:T(8,128)(2,1)} %bitcast.28, bf16[4,2,32,2048]{3,2,1,0:T(8,128)(2,1)} %collective-permute-done.4.other_back, bf16[16,256]{1,0:T(8,128)(2,1)} %copy-done.14, bf16[16,256]{1,0:T(8,128)(2,1)} %copy-done.16, ...), custom_call_target="tpu_custom_call" | custom-call | bytes 9900000 | tf_op jit(solution)/shard_map/onward/pallas_call | solution.py:295
  77.6 3.0 %collective-permute-start.11 = (bf16[7,2,32,1280]{3,2,1,0:T(8,128)(2,1)}, bf16[7,2,32,1280]{3,2,1,0:T(8,128)(2,1)}, u32[]{:S(2)}, u32[]{:S(2)}) collective-permute-start(bf16[7,2,32,1280]{3,2,1,0:T(8,128)(2,1)} %onward.5.rest_0_), channel_id=1, source_target_pairs={{4,8},{6,10},{8,12},{10,14},{5,9},{7,11},{9,13},{11,15},{20,24},{2... | collective-permute-start | bytes 3440648 | tf_op jit(solution)/shard_map/ppermute | solution.py:481
  80.7 4.1 %copy.19 = bf16[32,2,4,2,2048]{4,0,3,2,1:T(8,128)(2,1)} copy(bf16[32,2,4,2,2048]{4,3,2,1,0:T(2,128)(2,1)} %cut.2.rest_0_) | data formatting | bytes 4194304 | tf_op jit(solution)/shard_map/cut/pallas_call | solution.py:124
  97.9 7.8 %near.3.partial = f32[8,2,32,2048]{3,2,1,0:T(8,128)} custom-call(s32[2]{0:T(128)} %pad_add_fusion.rest_1_.place, f32[16,8,2048]{2,1,0:T(8,128)} %broadcast_in_dim.2.taps, bf16[2,4,2,32,2048]{4,3,2,1,0:T(8,128)(2,1)} %bitcast.35, bf16[4,2,32,2048]{3,2,1,0:T(8,128)(2,1)} %bitcast.38, bf16[2,4,2,32,2048]{4,3,2,1,0:T(8,128)(2,1)} %bitcast.30, ...), custom_call_target="tpu_custom_call" | custom-call | bytes 26400000 | tf_op jit(solution)/shard_map/near/pallas_call | solution.py:221
  105.7 15.6 %collective-permute-done.11.far = bf16[7,2,32,1280]{3,2,1,0:T(8,128)(2,1)} collective-permute-done((bf16[7,2,32,1280]{3,2,1,0:T(8,128)(2,1)}, bf16[7,2,32,1280]{3,2,1,0:T(8,128)(2,1)}, u32[]{:S(2)}, u32[]{:S(2)}) %collective-permute-start.11) | collective-permute-done | bytes 1146912 | tf_op jit(solution)/shard_map/ppermute | solution.py:481
  121.4 4.3 %far.5 = (bf16[4,2,32,1280]{3,2,1,0:T(8,128)(2,1)}, bf16[4,2,32,1280]{3,2,1,0:T(8,128)(2,1)}) custom-call(s32[2]{0:T(128)} %pad_add_fusion.rest_1_.place, f32[16,8,2048]{2,1,0:T(8,128)} %broadcast_in_dim.2.taps, f32[8,2,32,2048]{3,2,1,0:T(8,128)} %near.3.partial, bf16[7,2,32,1280]{3,2,1,0:T(8,128)(2,1)} %collective-permute-done.11.far), custom_call_target="tpu_custom_call" | custom-call | bytes 3300000 | tf_op jit(solution)/shard_map/far/pallas_call | solution.py:247
  129.6 3.0 %collective-permute-start.9 = (bf16[7,2,32,1024]{3,2,1,0:T(8,128)(2,1)}, bf16[7,2,32,1024]{3,2,1,0:T(8,128)(2,1)}, u32[]{:S(2)}, u32[]{:S(2)}) collective-permute-start(bf16[7,2,32,1024]{3,2,1,0:T(8,128)(2,1)} %onward.7.rest_2_), channel_id=1, source_target_pairs={{4,8},{6,10},{8,12},{10,14},{5,9},{7,11},{9,13},{11,15},{20,24},{2... | collective-permute-start | bytes 2752520 | tf_op jit(solution)/shard_map/ppermute | solution.py:481
  132.6 3.3 %collective-permute-start.15 = (bf16[4,2,32,1280]{3,2,1,0:T(8,128)(2,1)}, bf16[4,2,32,1280]{3,2,1,0:T(8,128)(2,1)}, u32[]{:S(2)}, u32[]{:S(2)}) collective-permute-start(bf16[4,2,32,1280]{3,2,1,0:T(8,128)(2,1)} %get-tuple-element.22.refs_0_), channel_id=1, source_target_pairs={{0,1},{1,0},{2,3},{3,2},{4,5},{5,4},{6,7},{7,6},{8,9},{9,8},{10,11... | collective-permute-start | bytes 1966088 | tf_op jit(solution)/shard_map/ppermute | solution.py:484
  141.0 7.8 %near.2.rest_1_.partial = f32[8,2,32,2048]{3,2,1,0:T(8,128)} custom-call(s32[2]{0:T(128)} %pad_add_fusion.rest_1_.place, f32[16,8,2048]{2,1,0:T(8,128)} %broadcast_in_dim.2.taps, bf16[2,4,2,32,2048]{4,3,2,1,0:T(8,128)(2,1)} %bitcast.36, bf16[4,2,32,2048]{3,2,1,0:T(8,128)(2,1)} %bitcast.27.other, bf16[2,4,2,32,2048]{4,3,2,1,0:T(8,128)(2,1)} %bitcast.34, ...), custom_call_target="tpu_custom_call" | custom-call | bytes 26400000 | tf_op jit(solution)/shard_map/near/pallas_call | solution.py:221
  149.7 3.5 %far.6 = (bf16[4,2,32,768]{3,2,1,0:T(8,128)(2,1)}, bf16[4,2,32,768]{3,2,1,0:T(8,128)(2,1)}) custom-call(s32[2]{0:T(128)} %pad_add_fusion.rest_1_.place, f32[16,8,2048]{2,1,0:T(8,128)} %broadcast_in_dim.2.taps, f32[8,2,32,2048]{3,2,1,0:T(8,128)} %near.3.partial, bf16[7,2,32,768]{3,2,1,0:T(8,128)(2,1)} %collective-permute-done.10.far, ...), custom_call_target="tpu_custom_call" | custom-call | bytes 3300000 | tf_op jit(solution)/shard_map/far/pallas_call | solution.py:247
  157.3 6.9 %collective-permute-done.13.rest_0_.refs_3_ = bf16[4,2,32,768]{3,2,1,0:T(8,128)(2,1)S(1)} collective-permute-done((bf16[4,2,32,768]{3,2,1,0:T(8,128)(2,1)}, bf16[4,2,32,768]{3,2,1,0:T(8,128)(2,1)S(1)}, u32[]{:S(2)}, u32[]{:S(2)}) %collective-permute-start.13) | collective-permute-done | bytes 393248 | tf_op jit(solution)/shard_map/ppermute | solution.py:478
  165.0 3.9 %far.7 = (bf16[4,2,32,1024]{3,2,1,0:T(8,128)(2,1)}, bf16[4,2,32,1024]{3,2,1,0:T(8,128)(2,1)}) custom-call(s32[2]{0:T(128)} %pad_add_fusion.rest_1_.place, f32[16,8,2048]{2,1,0:T(8,128)} %broadcast_in_dim.2.taps, f32[8,2,32,2048]{3,2,1,0:T(8,128)} %near.2.rest_1_.partial, bf16[7,2,32,1024]{3,2,1,0:T(8,128)(2,1)} %collective-permute-done.9.far, ...), custom_call_target="tpu_custom_call" | custom-call | bytes 3300000 | tf_op jit(solution)/shard_map/far/pallas_call | solution.py:247
  172.0 8.6 %beams.2.rest_0_.refs_14_ = f32[8,512,256]{2,1,0:T(8,128)} custom-call(s32[2]{0:T(128)} %pad_add_fusion.rest_1_.place, bf16[4,2,32,1280]{3,2,1,0:T(8,128)(2,1)} %get-tuple-element.22.refs_0_, bf16[4,2,32,768]{3,2,1,0:T(8,128)(2,1)} %get-tuple-element.23.refs_1_, bf16[4,2,32,1280]{3,2,1,0:T(8,128)(2,1)} %copy-done.3, bf16[4,2,32,768]{3,2,1,0:T(8,128)(2,1)} %copy-done.4, ...), custom_call_target="tpu_custom_call" | custom-call | tf_op jit(solution)/shard_map/beams/pallas_call | solution.py:448
  180.6 3.6 %far.8 = (bf16[4,2,32,640]{3,2,1,0:T(8,128)(2,1)}, bf16[4,2,32,640]{3,2,1,0:T(8,128)(2,1)}) custom-call(s32[2]{0:T(128)} %pad_add_fusion.rest_1_.place, f32[16,8,2048]{2,1,0:T(8,128)} %broadcast_in_dim.2.taps, f32[8,2,32,2048]{3,2,1,0:T(8,128)} %near.2.rest_1_.partial, bf16[7,2,32,640]{3,2,1,0:T(8,128)(2,1)} %collective-permute-done.14.far, ...), custom_call_target="tpu_custom_call" | custom-call | bytes 3300000 | tf_op jit(solution)/shard_map/far/pallas_call | solution.py:247
  185.8 3.3 %far.9 = (bf16[4,2,32,384]{3,2,1,0:T(8,128)(2,1)}, bf16[4,2,32,384]{3,2,1,0:T(8,128)(2,1)}) custom-call(s32[2]{0:T(128)} %pad_add_fusion.rest_1_.place, f32[16,8,2048]{2,1,0:T(8,128)} %broadcast_in_dim.2.taps, f32[8,2,32,2048]{3,2,1,0:T(8,128)} %near.2.rest_1_.partial, bf16[7,2,32,384]{3,2,1,0:T(8,128)(2,1)} %collective-permute-done.19.far, ...), custom_call_target="tpu_custom_call" | custom-call | bytes 3300000 | tf_op jit(solution)/shard_map/far/pallas_call | solution.py:247
  189.8 4.1 %collective-permute-done.21.refs_4_ = bf16[4,2,32,640]{3,2,1,0:T(8,128)(2,1)} collective-permute-done((bf16[4,2,32,640]{3,2,1,0:T(8,128)(2,1)}, bf16[4,2,32,640]{3,2,1,0:T(8,128)(2,1)}, u32[]{:S(2)}, u32[]{:S(2)}) %collective-permute-start.21) | collective-permute-done | bytes 327712 | tf_op jit(solution)/shard_map/ppermute | solution.py:478
  195.1 2.9 %collective-permute-done.22.refs_5_ = bf16[4,2,32,384]{3,2,1,0:T(8,128)(2,1)S(1)} collective-permute-done((bf16[4,2,32,384]{3,2,1,0:T(8,128)(2,1)}, bf16[4,2,32,384]{3,2,1,0:T(8,128)(2,1)S(1)}, u32[]{:S(2)}, u32[]{:S(2)}) %collective-permute-start.22) | collective-permute-done | bytes 196640 | tf_op jit(solution)/shard_map/ppermute | solution.py:478
  201.3 10.5 %beams.3 = f32[1024,2,4,128]{3,2,1,0:T(4,128)} custom-call(s32[2]{0:T(128)} %pad_add_fusion.rest_1_.place, bf16[4,2,32,1024]{3,2,1,0:T(8,128)(2,1)} %get-tuple-element.21.refs_10_.refs_0_, bf16[4,2,32,640]{3,2,1,0:T(8,128)(2,1)} %get-tuple-element.24.rest_0_.refs_1_, bf16[4,2,32,384]{3,2,1,0:T(8,128)(2,1)} %get-tuple-element.25.refs_2_, ...), custom_call_target="tpu_custom_call" | custom-call | tf_op jit(solution)/shard_map/beams/pallas_call | solution.py:448
  (120 shorter events, 58.0 us)
Async XLA Ops:
  2.4 56.7 %collective-permute-start.1 = (bf16[32,2,4,2,2048]{4,3,2,1,0:T(2,128)(2,1)}, bf16[32,2,4,2,2048]{4,3,2,1,0:T(2,128)(2,1)}, u32[]{:S(2)}, u32[]{:S(2)}) collective-permute-start(bf16[32,2,4,2,2048]{4,3,2,1,0:T(2,128)(2,1)} %cut.2.rest_0_), channel_id=1, source_target_pairs={{0,4},{2,6},{4,8},{6,10},{8,12},{10,14},{1,5},{3,7},{5,9},{7,11},{... | collective-permute-start | bytes 6291464 | tf_op jit(solution)/shard_map/ppermute | solution.py:481
  8.8 24.1 %collective-permute-start.3 = (bf16[32,4,2,2048]{3,2,1,0:T(2,128)(2,1)}, bf16[32,4,2,2048]{3,2,1,0:T(2,128)(2,1)S(1)}, u32[]{:S(2)}, u32[]{:S(2)}) collective-permute-start(bf16[32,4,2,2048]{3,2,1,0:T(2,128)(2,1)} %get-tuple-element.18), channel_id=1, source_target_pairs={{0,2},{2,0},{4,6},{6,4},{8,10},{10,8},{12,14},{14,12},{1,3},{3,1},... | collective-permute-start | bytes 3145736 | tf_op jit(solution)/shard_map/ppermute | solution.py:478
  10.1 45.2 %collective-permute-start = (bf16[32,4,2,2048]{3,2,1,0:T(2,128)(2,1)}, bf16[32,4,2,2048]{3,2,1,0:T(2,128)(2,1)S(1)}, u32[]{:S(2)}, u32[]{:S(2)}) collective-permute-start(bf16[32,4,2,2048]{3,2,1,0:T(2,128)(2,1)} %get-tuple-element.17), channel_id=1, source_target_pairs={{0,2},{2,0},{4,6},{6,4},{8,10},{10,8},{12,14},{14,12},{1,3},{3,1},... | collective-permute-start | bytes 3145736 | tf_op jit(solution)/shard_map/ppermute | solution.py:478
  35.7 38.5 %collective-permute-start.4 = (bf16[4,2,32,2048]{3,2,1,0:T(8,128)(2,1)S(1)}, bf16[4,2,32,2048]{3,2,1,0:T(8,128)(2,1)}, u32[]{:S(2)}, u32[]{:S(2)}) collective-permute-start(bf16[4,2,32,2048]{3,2,1,0:T(8,128)(2,1)S(1)} %bitcast.37), channel_id=1, source_target_pairs={{0,4},{2,6},{4,8},{6,10},{8,12},{10,14},{1,5},{3,7},{5,9},{7,11},{... | collective-permute-start | bytes 3145736 | tf_op jit(solution)/shard_map/ppermute | solution.py:481
  37.6 35.1 %collective-permute-start.5 = (bf16[16,256]{1,0:T(8,128)(2,1)S(1)}, bf16[16,256]{1,0:T(8,128)(2,1)S(1)}, u32[]{:S(2)}, u32[]{:S(2)}) collective-permute-start(bf16[16,256]{1,0:T(8,128)(2,1)S(1)} %get-tuple-element.30), channel_id=1, source_target_pairs={{0,4},{2,6},{4,0},{6,2},{8,12},{10,14},{12,8},{14,10},{1,5},{3,7},... | collective-permute-start | bytes 24584 | tf_op jit(solution)/shard_map/ppermute | solution.py:494
  37.7 35.8 %collective-permute-start.6 = (bf16[16,256]{1,0:T(8,128)(2,1)S(1)}, bf16[16,256]{1,0:T(8,128)(2,1)S(1)}, u32[]{:S(2)}, u32[]{:S(2)}) collective-permute-start(bf16[16,256]{1,0:T(8,128)(2,1)S(1)} %get-tuple-element.30), channel_id=1, source_target_pairs={{0,8},{2,10},{4,12},{6,14},{8,0},{10,2},{12,4},{14,6},{1,9},{3,11}... | collective-permute-start | bytes 24584 | tf_op jit(solution)/shard_map/ppermute | solution.py:494
  55.3 18.8 %collective-permute-start.7 = (bf16[16,256]{1,0:T(8,128)(2,1)S(1)}, bf16[16,256]{1,0:T(8,128)(2,1)S(1)}, u32[]{:S(2)}, u32[]{:S(2)}) collective-permute-start(bf16[16,256]{1,0:T(8,128)(2,1)S(1)} %get-tuple-element.30), channel_id=1, source_target_pairs={{0,12},{2,14},{4,8},{6,10},{8,4},{10,6},{12,0},{14,2},{1,13},{3,15... | collective-permute-start | bytes 24584 | tf_op jit(solution)/shard_map/ppermute | solution.py:494
  59.1 37.6 %collective-permute-start.2 = (bf16[4,2,32,2048]{3,2,1,0:T(8,128)(2,1)}, bf16[4,2,32,2048]{3,2,1,0:T(8,128)(2,1)}, u32[]{:S(2)}, u32[]{:S(2)}) collective-permute-start(bf16[4,2,32,2048]{3,2,1,0:T(8,128)(2,1)} %bitcast.27.other), channel_id=1, source_target_pairs={{0,4},{2,6},{4,8},{6,10},{8,12},{10,14},{1,5},{3,7},{5,9},{7,11},{... | collective-permute-start | bytes 3145736 | tf_op jit(solution)/shard_map/ppermute | solution.py:481
  77.6 43.8 %collective-permute-start.11 = (bf16[7,2,32,1280]{3,2,1,0:T(8,128)(2,1)}, bf16[7,2,32,1280]{3,2,1,0:T(8,128)(2,1)}, u32[]{:S(2)}, u32[]{:S(2)}) collective-permute-start(bf16[7,2,32,1280]{3,2,1,0:T(8,128)(2,1)} %onward.5.rest_0_), channel_id=1, source_target_pairs={{4,8},{6,10},{8,12},{10,14},{5,9},{7,11},{9,13},{11,15},{20,24},{2... | collective-permute-start | bytes 3440648 | tf_op jit(solution)/shard_map/ppermute | solution.py:481
  90.1 58.7 %collective-permute-start.10 = (bf16[7,2,32,768]{3,2,1,0:T(8,128)(2,1)}, bf16[7,2,32,768]{3,2,1,0:T(8,128)(2,1)}, u32[]{:S(2)}, u32[]{:S(2)}) collective-permute-start(bf16[7,2,32,768]{3,2,1,0:T(8,128)(2,1)} %onward.6.rest_1_), channel_id=1, source_target_pairs={{4,8},{6,10},{8,12},{10,14},{5,9},{7,11},{9,13},{11,15},{20,24},{2... | collective-permute-start | bytes 2064392 | tf_op jit(solution)/shard_map/ppermute | solution.py:481
  125.7 23.1 %collective-permute-start.12 = (bf16[4,2,32,1280]{3,2,1,0:T(8,128)(2,1)}, bf16[4,2,32,1280]{3,2,1,0:T(8,128)(2,1)S(1)}, u32[]{:S(2)}, u32[]{:S(2)}) collective-permute-start(bf16[4,2,32,1280]{3,2,1,0:T(8,128)(2,1)} %get-tuple-element.19), channel_id=1, source_target_pairs={{0,2},{2,0},{4,6},{6,4},{8,10},{10,8},{12,14},{14,12},{1,3},{3,1},... | collective-permute-start | bytes 1966088 | tf_op jit(solution)/shard_map/ppermute | solution.py:478
  129.6 26.2 %collective-permute-start.9 = (bf16[7,2,32,1024]{3,2,1,0:T(8,128)(2,1)}, bf16[7,2,32,1024]{3,2,1,0:T(8,128)(2,1)}, u32[]{:S(2)}, u32[]{:S(2)}) collective-permute-start(bf16[7,2,32,1024]{3,2,1,0:T(8,128)(2,1)} %onward.7.rest_2_), channel_id=1, source_target_pairs={{4,8},{6,10},{8,12},{10,14},{5,9},{7,11},{9,13},{11,15},{20,24},{2... | collective-permute-start | bytes 2752520 | tf_op jit(solution)/shard_map/ppermute | solution.py:481
  132.6 36.2 %collective-permute-start.15 = (bf16[4,2,32,1280]{3,2,1,0:T(8,128)(2,1)}, bf16[4,2,32,1280]{3,2,1,0:T(8,128)(2,1)}, u32[]{:S(2)}, u32[]{:S(2)}) collective-permute-start(bf16[4,2,32,1280]{3,2,1,0:T(8,128)(2,1)} %get-tuple-element.22.refs_0_), channel_id=1, source_target_pairs={{0,1},{1,0},{2,3},{3,2},{4,5},{5,4},{6,7},{7,6},{8,9},{9,8},{10,11... | collective-permute-start | bytes 1966088 | tf_op jit(solution)/shard_map/ppermute | solution.py:484
  153.2 11.1 %collective-permute-start.13 = (bf16[4,2,32,768]{3,2,1,0:T(8,128)(2,1)}, bf16[4,2,32,768]{3,2,1,0:T(8,128)(2,1)S(1)}, u32[]{:S(2)}, u32[]{:S(2)}) collective-permute-start(bf16[4,2,32,768]{3,2,1,0:T(8,128)(2,1)} %get-tuple-element.20), channel_id=1, source_target_pairs={{0,2},{2,0},{4,6},{6,4},{8,10},{10,8},{12,14},{14,12},{1,3},{3,1},... | collective-permute-start | bytes 1179656 | tf_op jit(solution)/shard_map/ppermute | solution.py:478
  153.3 17.6 %collective-permute-start.17 = (bf16[4,2,32,1280]{3,2,1,0:T(8,128)(2,1)}, bf16[4,2,32,1280]{3,2,1,0:T(8,128)(2,1)}, u32[]{:S(2)}, u32[]{:S(2)}) collective-permute-start(bf16[4,2,32,1280]{3,2,1,0:T(8,128)(2,1)} %copy-done.3), channel_id=1, source_target_pairs={{0,1},{1,0},{2,3},{3,2},{4,5},{5,4},{6,7},{7,6},{8,9},{9,8},{10,11... | collective-permute-start | bytes 1966088 | tf_op jit(solution)/shard_map/ppermute | solution.py:484
  153.6 27.0 %collective-permute-start.14 = (bf16[7,2,32,640]{3,2,1,0:T(8,128)(2,1)}, bf16[7,2,32,640]{3,2,1,0:T(8,128)(2,1)}, u32[]{:S(2)}, u32[]{:S(2)}) collective-permute-start(bf16[7,2,32,640]{3,2,1,0:T(8,128)(2,1)} %onward.8.rest_3_), channel_id=1, source_target_pairs={{4,8},{6,10},{8,12},{10,14},{5,9},{7,11},{9,13},{11,15},{20,24},{2... | collective-permute-start | bytes 1720328 | tf_op jit(solution)/shard_map/ppermute | solution.py:481
  155.8 13.2 %collective-permute-start.16 = (bf16[4,2,32,768]{3,2,1,0:T(8,128)(2,1)}, bf16[4,2,32,768]{3,2,1,0:T(8,128)(2,1)}, u32[]{:S(2)}, u32[]{:S(2)}) collective-permute-start(bf16[4,2,32,768]{3,2,1,0:T(8,128)(2,1)} %get-tuple-element.23.refs_1_), channel_id=1, source_target_pairs={{0,1},{1,0},{2,3},{3,2},{4,5},{5,4},{6,7},{7,6},{8,9},{9,8},{10,11... | collective-permute-start | bytes 1179656 | tf_op jit(solution)/shard_map/ppermute | solution.py:484
  168.8 16.7 %collective-permute-start.20 = (bf16[4,2,32,1024]{3,2,1,0:T(8,128)(2,1)}, bf16[4,2,32,1024]{3,2,1,0:T(8,128)(2,1)}, u32[]{:S(2)}, u32[]{:S(2)}) collective-permute-start(bf16[4,2,32,1024]{3,2,1,0:T(8,128)(2,1)} %get-tuple-element.26), channel_id=1, source_target_pairs={{0,2},{2,0},{4,6},{6,4},{8,10},{10,8},{12,14},{14,12},{1,3},{3,1},... | collective-permute-start | bytes 1572872 | tf_op jit(solution)/shard_map/ppermute | solution.py:478
  169.0 16.8 %collective-permute-start.19 = (bf16[7,2,32,384]{3,2,1,0:T(8,128)(2,1)S(1)}, bf16[7,2,32,384]{3,2,1,0:T(8,128)(2,1)}, u32[]{:S(2)}, u32[]{:S(2)}) collective-permute-start(bf16[7,2,32,384]{3,2,1,0:T(8,128)(2,1)S(1)} %copy-done.5), channel_id=1, source_target_pairs={{4,8},{6,10},{8,12},{10,14},{5,9},{7,11},{9,13},{11,15},{20,24},{2... | collective-permute-start | bytes 1032200 | tf_op jit(solution)/shard_map/ppermute | solution.py:481
  170.9 24.1 %collective-permute-start.23 = (bf16[4,2,32,1024]{3,2,1,0:T(8,128)(2,1)}, bf16[4,2,32,1024]{3,2,1,0:T(8,128)(2,1)}, u32[]{:S(2)}, u32[]{:S(2)}) collective-permute-start(bf16[4,2,32,1024]{3,2,1,0:T(8,128)(2,1)} %get-tuple-element.21.refs_10_.refs_0_), channel_id=1, source_target_pairs={{0,1},{1,0},{2,3},{3,2},{4,5},{5,4},{6,7},{7,6},{8,9},{9,8},{10,11... | collective-permute-start | bytes 1572872 | tf_op jit(solution)/shard_map/ppermute | solution.py:484
  184.2 9.6 %collective-permute-start.21 = (bf16[4,2,32,640]{3,2,1,0:T(8,128)(2,1)}, bf16[4,2,32,640]{3,2,1,0:T(8,128)(2,1)}, u32[]{:S(2)}, u32[]{:S(2)}) collective-permute-start(bf16[4,2,32,640]{3,2,1,0:T(8,128)(2,1)} %get-tuple-element.27), channel_id=1, source_target_pairs={{0,2},{2,0},{4,6},{6,4},{8,10},{10,8},{12,14},{14,12},{1,3},{3,1},... | collective-permute-start | bytes 983048 | tf_op jit(solution)/shard_map/ppermute | solution.py:478
  185.5 14.3 %collective-permute-start.26 = (bf16[4,2,32,1024]{3,2,1,0:T(8,128)(2,1)}, bf16[4,2,32,1024]{3,2,1,0:T(8,128)(2,1)}, u32[]{:S(2)}, u32[]{:S(2)}) collective-permute-start(bf16[4,2,32,1024]{3,2,1,0:T(8,128)(2,1)} %collective-permute-done.20.refs_3_), channel_id=1, source_target_pairs={{0,1},{1,0},{2,3},{3,2},{4,5},{5,4},{6,7},{7,6},{8,9},{9,8},{10,11... | collective-permute-start | bytes 1572872 | tf_op jit(solution)/shard_map/ppermute | solution.py:484
  189.1 8.8 %collective-permute-start.22 = (bf16[4,2,32,384]{3,2,1,0:T(8,128)(2,1)}, bf16[4,2,32,384]{3,2,1,0:T(8,128)(2,1)S(1)}, u32[]{:S(2)}, u32[]{:S(2)}) collective-permute-start(bf16[4,2,32,384]{3,2,1,0:T(8,128)(2,1)} %get-tuple-element.28), channel_id=1, source_target_pairs={{0,2},{2,0},{4,6},{6,4},{8,10},{10,8},{12,14},{14,12},{1,3},{3,1},... | collective-permute-start | bytes 589832 | tf_op jit(solution)/shard_map/ppermute | solution.py:478
  189.3 9.5 %collective-permute-start.24 = (bf16[4,2,32,640]{3,2,1,0:T(8,128)(2,1)S(1)}, bf16[4,2,32,640]{3,2,1,0:T(8,128)(2,1)S(1)}, u32[]{:S(2)}, u32[]{:S(2)}) collective-permute-start(bf16[4,2,32,640]{3,2,1,0:T(8,128)(2,1)S(1)} %copy-done.6), channel_id=1, source_target_pairs={{0,1},{1,0},{2,3},{3,2},{4,5},{5,4},{6,7},{7,6},{8,9},{9,8},{10,11... | collective-permute-start | bytes 983048 | tf_op jit(solution)/shard_map/ppermute | solution.py:484
  (28 other events, 223.2 us)

commit v17 on v15

--- a/solution.py
+++ b/solution.py
@@ -355,7 +355,7 @@
     groups = spectra.shape[0]
     beams = weights.shape[2] // 2
     rows_of = table.shape[2] // 2 // groups
-    pair = 2
+    pair = frames if has_earlier else 2
     lane_tiles = beams // LANES
     at_once = groups // pl.num_programs(0)
 

time: 207 us -> 207 us (level)
  no operation moved by 1% of the time
where the time goes in v17:
time: 207 us; the launch traced here: 205 us
  Pallas kernels  70.3 us (34%)
  waiting for transfers between devices  69.1 us (33%)
  starting transfers between devices  39.6 us (19%)
  local copies, waits for them, and re-layouts  22 us (11%)
  other arithmetic  4.12 us (2%)
    ppermute x7, waiting for transfers between devices, pair(): return lax.ppermute(block, 'tm', [(i, i ^ 1) for i in range(time_devices)])  45 us
    ppermute x7, waiting for transfers between devices, hop(): lax.ppermute(block, 'tm', [(i, i + 2) for i in range(skip, time_devices -...  19.7 us
    ppermute x7, starting transfers between devices, hop(): lax.ppermute(block, 'tm', [(i, i + 2) for i in range(skip, time_devices -...  19.3 us
    pallas_call x2, Pallas kernels, beam_power(): pl.pallas_call(functools.partial(beam_kernel, len(sources), ranges, len(l...  18.9 us
    pallas_call x4, Pallas kernels, far_filter(): pl.pallas_call(far_kernel, out_shape=(shape, shape), grid_spec=pltpu.Pref...  17.3 us
    pallas_call x2, Pallas kernels, near_filter(): pl.pallas_call(near_kernel, out_shape=jax.ShapeDtypeStruct((2 * frames, p...  15.7 us
    ppermute x8, starting transfers between devices, swap(): return lax.ppermute(block, 'stn', [(0, 1), (1, 0)])  11 us
    pallas_call x4, Pallas kernels, onward(): pl.pallas_call(onward_kernel, out_shape=jax.ShapeDtypeStruct((depth, part...  10.9 us
  transfers between devices with their start and end apart: 25, of which 9 were waited for; matrix products, arithmetic and copies ran while one was open for 10% of the time, Pallas kernels for 28%

profile of v17, /device:TPU:17, one launch (start us, length us, event | category | flops | bytes accessed | tf_op | source)
XLA Modules:
  0.0 205.5 jit_solution(8946610222314567818)
XLA Ops:
  2.4 3.2 %collective-permute-start.1 = (bf16[32,2,4,2,2048]{4,3,2,1,0:T(2,128)(2,1)}, bf16[32,2,4,2,2048]{4,3,2,1,0:T(2,128)(2,1)}, u32[]{:S(2)}, u32[]{:S(2)}) collective-permute-start(bf16[32,2,4,2,2048]{4,3,2,1,0:T(2,128)(2,1)} %cut.2.rest_0_), channel_id=1, source_target_pairs={{0,4},{2,6},{4,8},{6,10},{8,12},{10,14},{1,5},{3,7},{5,9},{7,11},{... | collective-permute-start | bytes 6291464 | tf_op jit(solution)/shard_map/ppermute | solution.py:481
  10.2 22.6 %collective-permute-done.3.refs_0_ = bf16[32,4,2,2048]{3,2,1,0:T(2,128)(2,1)S(1)} collective-permute-done((bf16[32,4,2,2048]{3,2,1,0:T(2,128)(2,1)}, bf16[32,4,2,2048]{3,2,1,0:T(2,128)(2,1)S(1)}, u32[]{:S(2)}, u32[]{:S(2)}) %collective-permute-start.3) | collective-permute-done | bytes 1048608 | tf_op jit(solution)/shard_map/ppermute | solution.py:478
  40.3 14.9 %collective-permute-done.refs_0_ = bf16[32,4,2,2048]{3,2,1,0:T(2,128)(2,1)} collective-permute-done((bf16[32,4,2,2048]{3,2,1,0:T(2,128)(2,1)}, bf16[32,4,2,2048]{3,2,1,0:T(2,128)(2,1)}, u32[]{:S(2)}, u32[]{:S(2)}) %collective-permute-start) | collective-permute-done | bytes 1048608 | tf_op jit(solution)/shard_map/ppermute | solution.py:478
  55.4 2.8 %copy.21 = bf16[32,4,2,2048]{3,0,2,1:T(8,128)(2,1)} copy(bf16[32,4,2,2048]{3,2,1,0:T(2,128)(2,1)} %after.3) | data formatting | bytes 2097152 | tf_op jit(solution)/shard_map/after/pallas_call | solution.py:77
  58.2 4.3 %collective-permute-start.2 = (bf16[4,2,32,2048]{3,2,1,0:T(8,128)(2,1)}, bf16[4,2,32,2048]{3,2,1,0:T(8,128)(2,1)}, u32[]{:S(2)}, u32[]{:S(2)}) collective-permute-start(bf16[4,2,32,2048]{3,2,1,0:T(8,128)(2,1)} %bitcast.27.other), channel_id=1, source_target_pairs={{0,4},{2,6},{4,8},{6,10},{8,12},{10,14},{1,5},{3,7},{5,9},{7,11},{... | collective-permute-start | bytes 3145736 | tf_op jit(solution)/shard_map/ppermute | solution.py:481
  65.7 4.1 %copy.18 = bf16[32,2,4,2,2048]{4,0,3,2,1:T(8,128)(2,1)} copy(bf16[32,2,4,2,2048]{4,3,2,1,0:T(2,128)(2,1)} %after.4) | data formatting | bytes 4194304 | tf_op jit(solution)/shard_map/after/pallas_call | solution.py:77
  69.7 3.0 %collective-permute-done.5.rest_0_ = bf16[16,256]{1,0:T(8,128)(2,1)S(1)} collective-permute-done((bf16[16,256]{1,0:T(8,128)(2,1)S(1)}, bf16[16,256]{1,0:T(8,128)(2,1)S(1)}, u32[]{:S(2)}, u32[]{:S(2)}) %collective-permute-start.5) | collective-permute-done | bytes 8224 | tf_op jit(solution)/shard_map/ppermute | solution.py:494
  74.7 2.7 %onward.4.rest_0_ = bf16[7,2,32,1024]{3,2,1,0:T(8,128)(2,1)} custom-call(s32[2]{0:T(128)} %pad_add_fusion.rest_1_.place, bf16[2,4,2,32,2048]{4,3,2,1,0:T(8,128)(2,1)} %bitcast.28, bf16[4,2,32,2048]{3,2,1,0:T(8,128)(2,1)} %collective-permute-done.4.other_back, bf16[16,256]{1,0:T(8,128)(2,1)} %copy-done.10, bf16[16,256]{1,0:T(8,128)(2,1)} %copy-done.11, ...), custom_call_target="tpu_custom_call" | custom-call | bytes 9900000 | tf_op jit(solution)/shard_map/onward/pallas_call | solution.py:295
  77.4 3.0 %collective-permute-start.11 = (bf16[7,2,32,1024]{3,2,1,0:T(8,128)(2,1)}, bf16[7,2,32,1024]{3,2,1,0:T(8,128)(2,1)S(1)}, u32[]{:S(2)}, u32[]{:S(2)}) collective-permute-start(bf16[7,2,32,1024]{3,2,1,0:T(8,128)(2,1)} %onward.4.rest_0_), channel_id=1, source_target_pairs={{4,8},{6,10},{8,12},{10,14},{5,9},{7,11},{9,13},{11,15},{20,24},{2... | collective-permute-start | bytes 2752520 | tf_op jit(solution)/shard_map/ppermute | solution.py:481
  98.8 7.8 %near.3.partial = f32[8,2,32,2048]{3,2,1,0:T(8,128)} custom-call(s32[2]{0:T(128)} %pad_add_fusion.rest_1_.place, f32[16,8,2048]{2,1,0:T(8,128)} %broadcast_in_dim.2.taps, bf16[2,4,2,32,2048]{4,3,2,1,0:T(8,128)(2,1)} %bitcast.34, bf16[4,2,32,2048]{3,2,1,0:T(8,128)(2,1)} %bitcast.37, bf16[2,4,2,32,2048]{4,3,2,1,0:T(8,128)(2,1)} %bitcast.30, ...), custom_call_target="tpu_custom_call" | custom-call | bytes 26400000 | tf_op jit(solution)/shard_map/near/pallas_call | solution.py:221
  106.6 9.7 %collective-permute-done.11.far = bf16[7,2,32,1024]{3,2,1,0:T(8,128)(2,1)S(1)} collective-permute-done((bf16[7,2,32,1024]{3,2,1,0:T(8,128)(2,1)}, bf16[7,2,32,1024]{3,2,1,0:T(8,128)(2,1)S(1)}, u32[]{:S(2)}, u32[]{:S(2)}) %collective-permute-start.11) | collective-permute-done | bytes 917536 | tf_op jit(solution)/shard_map/ppermute | solution.py:481
  117.3 3.9 %far.4 = (bf16[4,2,32,1024]{3,2,1,0:T(8,128)(2,1)}, bf16[4,2,32,1024]{3,2,1,0:T(8,128)(2,1)}) custom-call(s32[2]{0:T(128)} %pad_add_fusion.rest_1_.place, f32[16,8,2048]{2,1,0:T(8,128)} %broadcast_in_dim.2.taps, f32[8,2,32,2048]{3,2,1,0:T(8,128)} %near.3.partial, bf16[7,2,32,1024]{3,2,1,0:T(8,128)(2,1)} %copy-done.5), custom_call_target="tpu_custom_call" | custom-call | bytes 3300000 | tf_op jit(solution)/shard_map/far/pallas_call | solution.py:247
  122.3 2.8 %onward.6.rest_2_ = bf16[7,2,32,1152]{3,2,1,0:T(8,128)(2,1)} custom-call(s32[2]{0:T(128)} %pad_add_fusion.rest_1_.place, bf16[2,4,2,32,2048]{4,3,2,1,0:T(8,128)(2,1)} %bitcast.31, bf16[4,2,32,2048]{3,2,1,0:T(8,128)(2,1)} %collective-permute-done.2.other_back.rest_5_.rest_3_), custom_call_target="tpu_custom_call" | custom-call | bytes 9900000 | tf_op jit(solution)/shard_map/onward/pallas_call | solution.py:295
  125.1 3.0 %collective-permute-start.9 = (bf16[7,2,32,1152]{3,2,1,0:T(8,128)(2,1)}, bf16[7,2,32,1152]{3,2,1,0:T(8,128)(2,1)}, u32[]{:S(2)}, u32[]{:S(2)}) collective-permute-start(bf16[7,2,32,1152]{3,2,1,0:T(8,128)(2,1)} %onward.6.rest_2_), channel_id=1, source_target_pairs={{4,8},{6,10},{8,12},{10,14},{5,9},{7,11},{9,13},{11,15},{20,24},{2... | collective-permute-start | bytes 3096584 | tf_op jit(solution)/shard_map/ppermute | solution.py:481
  128.1 2.8 %onward.7.rest_3_ = bf16[7,2,32,896]{3,2,1,0:T(8,128)(2,1)} custom-call(s32[2]{0:T(128)} %pad_add_fusion.rest_1_.place, bf16[2,4,2,32,2048]{4,3,2,1,0:T(8,128)(2,1)} %bitcast.32, bf16[4,2,32,2048]{3,2,1,0:T(8,128)(2,1)} %collective-permute-done.2.other_back.rest_5_.rest_3_), custom_call_target="tpu_custom_call" | custom-call | bytes 9900000 | tf_op jit(solution)/shard_map/onward/pallas_call | solution.py:295
  130.9 7.8 %near.2.rest_1_.partial = f32[8,2,32,2048]{3,2,1,0:T(8,128)} custom-call(s32[2]{0:T(128)} %pad_add_fusion.rest_1_.place, f32[16,8,2048]{2,1,0:T(8,128)} %broadcast_in_dim.2.taps, bf16[2,4,2,32,2048]{4,3,2,1,0:T(8,128)(2,1)} %bitcast.35, bf16[4,2,32,2048]{3,2,1,0:T(8,128)(2,1)} %bitcast.27.other, bf16[2,4,2,32,2048]{4,3,2,1,0:T(8,128)(2,1)} %bitcast.33, ...), custom_call_target="tpu_custom_call" | custom-call | bytes 26400000 | tf_op jit(solution)/shard_map/near/pallas_call | solution.py:221
  138.7 4.0 %far.5 = (bf16[4,2,32,1024]{3,2,1,0:T(8,128)(2,1)}, bf16[4,2,32,1024]{3,2,1,0:T(8,128)(2,1)}) custom-call(s32[2]{0:T(128)} %pad_add_fusion.rest_1_.place, f32[16,8,2048]{2,1,0:T(8,128)} %broadcast_in_dim.2.taps, f32[8,2,32,2048]{3,2,1,0:T(8,128)} %near.3.partial, bf16[7,2,32,1024]{3,2,1,0:T(8,128)(2,1)} %collective-permute-done.10.far, ...), custom_call_target="tpu_custom_call" | custom-call | bytes 3300000 | tf_op jit(solution)/shard_map/far/pallas_call | solution.py:247
  144.8 3.6 %collective-permute-start.15 = (bf16[4,2,32,1024]{3,2,1,0:T(8,128)(2,1)}, bf16[4,2,32,1024]{3,2,1,0:T(8,128)(2,1)}, u32[]{:S(2)}, u32[]{:S(2)}) collective-permute-start(bf16[4,2,32,1024]{3,2,1,0:T(8,128)(2,1)} %get-tuple-element.20.refs_0_), channel_id=1, source_target_pairs={{0,1},{1,0},{2,3},{3,2},{4,5},{5,4},{6,7},{7,6},{8,9},{9,8},{10,11... | collective-permute-start | bytes 1572872 | tf_op jit(solution)/shard_map/ppermute | solution.py:484
  148.5 9.7 %collective-permute-done.9.far = bf16[7,2,32,1152]{3,2,1,0:T(8,128)(2,1)} collective-permute-done((bf16[7,2,32,1152]{3,2,1,0:T(8,128)(2,1)}, bf16[7,2,32,1152]{3,2,1,0:T(8,128)(2,1)}, u32[]{:S(2)}, u32[]{:S(2)}) %collective-permute-start.9) | collective-permute-done | bytes 1032224 | tf_op jit(solution)/shard_map/ppermute | solution.py:481
  160.9 4.9 %far.6 = (bf16[4,2,32,1152]{3,2,1,0:T(8,128)(2,1)}, bf16[4,2,32,1152]{3,2,1,0:T(8,128)(2,1)}) custom-call(s32[2]{0:T(128)} %pad_add_fusion.rest_1_.place, f32[16,8,2048]{2,1,0:T(8,128)} %broadcast_in_dim.2.taps, f32[8,2,32,2048]{3,2,1,0:T(8,128)} %near.2.rest_1_.partial, bf16[7,2,32,1152]{3,2,1,0:T(8,128)(2,1)} %collective-permute-done.9.far, ...), custom_call_target="tpu_custom_call" | custom-call | bytes 3300000 | tf_op jit(solution)/shard_map/far/pallas_call | solution.py:247
  167.1 8.5 %beams.2.rest_0_.refs_10_ = f32[8,512,256]{2,1,0:T(8,128)} custom-call(s32[2]{0:T(128)} %pad_add_fusion.rest_1_.place, bf16[4,2,32,1024]{3,2,1,0:T(8,128)(2,1)} %get-tuple-element.20.refs_0_, bf16[4,2,32,1024]{3,2,1,0:T(8,128)(2,1)} %get-tuple-element.21.refs_1_, bf16[4,2,32,1024]{3,2,1,0:T(8,128)(2,1)} %collective-permute-done.12.rest_0_.refs_2_, ...), custom_call_target="tpu_custom_call" | custom-call | tf_op jit(solution)/shard_map/beams/pallas_call | solution.py:448
  175.6 4.5 %far.7 = (bf16[4,2,32,896]{3,2,1,0:T(8,128)(2,1)}, bf16[4,2,32,896]{3,2,1,0:T(8,128)(2,1)}) custom-call(s32[2]{0:T(128)} %pad_add_fusion.rest_1_.place, f32[16,8,2048]{2,1,0:T(8,128)} %broadcast_in_dim.2.taps, f32[8,2,32,2048]{3,2,1,0:T(8,128)} %near.2.rest_1_.partial, bf16[7,2,32,896]{3,2,1,0:T(8,128)(2,1)} %collective-permute-done.14.far, ...), custom_call_target="tpu_custom_call" | custom-call | bytes 3300000 | tf_op jit(solution)/shard_map/far/pallas_call | solution.py:247
  183.5 7.5 %collective-permute-done.20.refs_3_ = bf16[4,2,32,896]{3,2,1,0:T(8,128)(2,1)S(1)} collective-permute-done((bf16[4,2,32,896]{3,2,1,0:T(8,128)(2,1)}, bf16[4,2,32,896]{3,2,1,0:T(8,128)(2,1)S(1)}, u32[]{:S(2)}, u32[]{:S(2)}) %collective-permute-start.20) | collective-permute-done | bytes 458784 | tf_op jit(solution)/shard_map/ppermute | solution.py:478
  194.9 10.4 %beams.3 = f32[1024,2,4,128]{3,2,1,0:T(4,128)} custom-call(s32[2]{0:T(128)} %pad_add_fusion.rest_1_.place, bf16[4,2,32,1152]{3,2,1,0:T(8,128)(2,1)} %get-tuple-element.19.refs_10_.refs_0_, bf16[4,2,32,896]{3,2,1,0:T(8,128)(2,1)} %get-tuple-element.22.refs_1_, bf16[4,2,32,1152]{3,2,1,0:T(8,128)(2,1)} %collective-permute-done.19.refs_2_, ...), custom_call_target="tpu_custom_call" | custom-call | tf_op jit(solution)/shard_map/beams/pallas_call | solution.py:448
  (98 shorter events, 53.7 us)
Async XLA Ops:
  2.4 55.8 %collective-permute-start.1 = (bf16[32,2,4,2,2048]{4,3,2,1,0:T(2,128)(2,1)}, bf16[32,2,4,2,2048]{4,3,2,1,0:T(2,128)(2,1)}, u32[]{:S(2)}, u32[]{:S(2)}) collective-permute-start(bf16[32,2,4,2,2048]{4,3,2,1,0:T(2,128)(2,1)} %cut.2.rest_0_), channel_id=1, source_target_pairs={{0,4},{2,6},{4,8},{6,10},{8,12},{10,14},{1,5},{3,7},{5,9},{7,11},{... | collective-permute-start | bytes 6291464 | tf_op jit(solution)/shard_map/ppermute | solution.py:481
  8.7 24.1 %collective-permute-start.3 = (bf16[32,4,2,2048]{3,2,1,0:T(2,128)(2,1)}, bf16[32,4,2,2048]{3,2,1,0:T(2,128)(2,1)S(1)}, u32[]{:S(2)}, u32[]{:S(2)}) collective-permute-start(bf16[32,4,2,2048]{3,2,1,0:T(2,128)(2,1)} %get-tuple-element.16), channel_id=1, source_target_pairs={{0,2},{2,0},{4,6},{6,4},{8,10},{10,8},{12,14},{14,12},{1,3},{3,1},... | collective-permute-start | bytes 3145736 | tf_op jit(solution)/shard_map/ppermute | solution.py:478
  10.0 45.2 %collective-permute-start = (bf16[32,4,2,2048]{3,2,1,0:T(2,128)(2,1)}, bf16[32,4,2,2048]{3,2,1,0:T(2,128)(2,1)}, u32[]{:S(2)}, u32[]{:S(2)}) collective-permute-start(bf16[32,4,2,2048]{3,2,1,0:T(2,128)(2,1)} %get-tuple-element.15), channel_id=1, source_target_pairs={{0,2},{2,0},{4,6},{6,4},{8,10},{10,8},{12,14},{14,12},{1,3},{3,1},... | collective-permute-start | bytes 3145736 | tf_op jit(solution)/shard_map/ppermute | solution.py:478
  35.6 38.5 %collective-permute-start.4 = (bf16[4,2,32,2048]{3,2,1,0:T(8,128)(2,1)S(1)}, bf16[4,2,32,2048]{3,2,1,0:T(8,128)(2,1)}, u32[]{:S(2)}, u32[]{:S(2)}) collective-permute-start(bf16[4,2,32,2048]{3,2,1,0:T(8,128)(2,1)S(1)} %bitcast.36), channel_id=1, source_target_pairs={{0,4},{2,6},{4,8},{6,10},{8,12},{10,14},{1,5},{3,7},{5,9},{7,11},{... | collective-permute-start | bytes 3145736 | tf_op jit(solution)/shard_map/ppermute | solution.py:481
  37.6 35.1 %collective-permute-start.5 = (bf16[16,256]{1,0:T(8,128)(2,1)S(1)}, bf16[16,256]{1,0:T(8,128)(2,1)S(1)}, u32[]{:S(2)}, u32[]{:S(2)}) collective-permute-start(bf16[16,256]{1,0:T(8,128)(2,1)S(1)} %get-tuple-element.26), channel_id=1, source_target_pairs={{0,4},{2,6},{4,0},{6,2},{8,12},{10,14},{12,8},{14,10},{1,5},{3,7},... | collective-permute-start | bytes 24584 | tf_op jit(solution)/shard_map/ppermute | solution.py:494
  37.6 35.8 %collective-permute-start.6 = (bf16[16,256]{1,0:T(8,128)(2,1)S(1)}, bf16[16,256]{1,0:T(8,128)(2,1)S(1)}, u32[]{:S(2)}, u32[]{:S(2)}) collective-permute-start(bf16[16,256]{1,0:T(8,128)(2,1)S(1)} %get-tuple-element.26), channel_id=1, source_target_pairs={{0,8},{2,10},{4,12},{6,14},{8,0},{10,2},{12,4},{14,6},{1,9},{3,11}... | collective-permute-start | bytes 24584 | tf_op jit(solution)/shard_map/ppermute | solution.py:494
  55.3 18.9 %collective-permute-start.7 = (bf16[16,256]{1,0:T(8,128)(2,1)S(1)}, bf16[16,256]{1,0:T(8,128)(2,1)S(1)}, u32[]{:S(2)}, u32[]{:S(2)}) collective-permute-start(bf16[16,256]{1,0:T(8,128)(2,1)S(1)} %get-tuple-element.26), channel_id=1, source_target_pairs={{0,12},{2,14},{4,8},{6,10},{8,4},{10,6},{12,0},{14,2},{1,13},{3,15... | collective-permute-start | bytes 24584 | tf_op jit(solution)/shard_map/ppermute | solution.py:494
  58.2 38.6 %collective-permute-start.2 = (bf16[4,2,32,2048]{3,2,1,0:T(8,128)(2,1)}, bf16[4,2,32,2048]{3,2,1,0:T(8,128)(2,1)}, u32[]{:S(2)}, u32[]{:S(2)}) collective-permute-start(bf16[4,2,32,2048]{3,2,1,0:T(8,128)(2,1)} %bitcast.27.other), channel_id=1, source_target_pairs={{0,4},{2,6},{4,8},{6,10},{8,12},{10,14},{1,5},{3,7},{5,9},{7,11},{... | collective-permute-start | bytes 3145736 | tf_op jit(solution)/shard_map/ppermute | solution.py:481
  77.4 38.9 %collective-permute-start.11 = (bf16[7,2,32,1024]{3,2,1,0:T(8,128)(2,1)}, bf16[7,2,32,1024]{3,2,1,0:T(8,128)(2,1)S(1)}, u32[]{:S(2)}, u32[]{:S(2)}) collective-permute-start(bf16[7,2,32,1024]{3,2,1,0:T(8,128)(2,1)} %onward.4.rest_0_), channel_id=1, source_target_pairs={{4,8},{6,10},{8,12},{10,14},{5,9},{7,11},{9,13},{11,15},{20,24},{2... | collective-permute-start | bytes 2752520 | tf_op jit(solution)/shard_map/ppermute | solution.py:481
  84.6 7.9 %collective-permute-start.8 = (bf16[64,256]{1,0:T(8,128)(2,1)}, bf16[64,256]{1,0:T(8,128)(2,1)}, u32[]{:S(2)}, u32[]{:S(2)}) collective-permute-start(bf16[64,256]{1,0:T(8,128)(2,1)} %pad_maximum_fusion), channel_id=1, source_target_pairs={{0,2},{2,0},{4,6},{6,4},{8,10},{10,8},{12,14},{14,12},{1,3},{3,1},... | collective-permute-start | bytes 98312 | tf_op jit(solution)/shard_map/ppermute | solution.py:478
  88.5 50.2 %collective-permute-start.10 = (bf16[7,2,32,1024]{3,2,1,0:T(8,128)(2,1)}, bf16[7,2,32,1024]{3,2,1,0:T(8,128)(2,1)}, u32[]{:S(2)}, u32[]{:S(2)}) collective-permute-start(bf16[7,2,32,1024]{3,2,1,0:T(8,128)(2,1)} %onward.5.rest_1_), channel_id=1, source_target_pairs={{4,8},{6,10},{8,12},{10,14},{5,9},{7,11},{9,13},{11,15},{20,24},{2... | collective-permute-start | bytes 2752520 | tf_op jit(solution)/shard_map/ppermute | solution.py:481
  121.1 17.6 %collective-permute-start.12 = (bf16[4,2,32,1024]{3,2,1,0:T(8,128)(2,1)}, bf16[4,2,32,1024]{3,2,1,0:T(8,128)(2,1)}, u32[]{:S(2)}, u32[]{:S(2)}) collective-permute-start(bf16[4,2,32,1024]{3,2,1,0:T(8,128)(2,1)} %get-tuple-element.17), channel_id=1, source_target_pairs={{0,2},{2,0},{4,6},{6,4},{8,10},{10,8},{12,14},{14,12},{1,3},{3,1},... | collective-permute-start | bytes 1572872 | tf_op jit(solution)/shard_map/ppermute | solution.py:478
  125.1 33.1 %collective-permute-start.9 = (bf16[7,2,32,1152]{3,2,1,0:T(8,128)(2,1)}, bf16[7,2,32,1152]{3,2,1,0:T(8,128)(2,1)}, u32[]{:S(2)}, u32[]{:S(2)}) collective-permute-start(bf16[7,2,32,1152]{3,2,1,0:T(8,128)(2,1)} %onward.6.rest_2_), channel_id=1, source_target_pairs={{4,8},{6,10},{8,12},{10,14},{5,9},{7,11},{9,13},{11,15},{20,24},{2... | collective-permute-start | bytes 3096584 | tf_op jit(solution)/shard_map/ppermute | solution.py:481
  142.7 18.2 %collective-permute-start.13 = (bf16[4,2,32,1024]{3,2,1,0:T(8,128)(2,1)}, bf16[4,2,32,1024]{3,2,1,0:T(8,128)(2,1)}, u32[]{:S(2)}, u32[]{:S(2)}) collective-permute-start(bf16[4,2,32,1024]{3,2,1,0:T(8,128)(2,1)} %get-tuple-element.18), channel_id=1, source_target_pairs={{0,2},{2,0},{4,6},{6,4},{8,10},{10,8},{12,14},{14,12},{1,3},{3,1},... | collective-permute-start | bytes 1572872 | tf_op jit(solution)/shard_map/ppermute | solution.py:478
  142.9 32.7 %collective-permute-start.14 = (bf16[7,2,32,896]{3,2,1,0:T(8,128)(2,1)S(1)}, bf16[7,2,32,896]{3,2,1,0:T(8,128)(2,1)}, u32[]{:S(2)}, u32[]{:S(2)}) collective-permute-start(bf16[7,2,32,896]{3,2,1,0:T(8,128)(2,1)S(1)} %copy-done.3), channel_id=1, source_target_pairs={{4,8},{6,10},{8,12},{10,14},{5,9},{7,11},{9,13},{11,15},{20,24},{2... | collective-permute-start | bytes 2408456 | tf_op jit(solution)/shard_map/ppermute | solution.py:481
  144.8 21.1 %collective-permute-start.15 = (bf16[4,2,32,1024]{3,2,1,0:T(8,128)(2,1)}, bf16[4,2,32,1024]{3,2,1,0:T(8,128)(2,1)}, u32[]{:S(2)}, u32[]{:S(2)}) collective-permute-start(bf16[4,2,32,1024]{3,2,1,0:T(8,128)(2,1)} %get-tuple-element.20.refs_0_), channel_id=1, source_target_pairs={{0,1},{1,0},{2,3},{3,2},{4,5},{5,4},{6,7},{7,6},{8,9},{9,8},{10,11... | collective-permute-start | bytes 1572872 | tf_op jit(solution)/shard_map/ppermute | solution.py:484
  148.4 18.7 %collective-permute-start.16 = (bf16[4,2,32,1024]{3,2,1,0:T(8,128)(2,1)}, bf16[4,2,32,1024]{3,2,1,0:T(8,128)(2,1)}, u32[]{:S(2)}, u32[]{:S(2)}) collective-permute-start(bf16[4,2,32,1024]{3,2,1,0:T(8,128)(2,1)} %get-tuple-element.21.refs_1_), channel_id=1, source_target_pairs={{0,1},{1,0},{2,3},{3,2},{4,5},{5,4},{6,7},{7,6},{8,9},{9,8},{10,11... | collective-permute-start | bytes 1572872 | tf_op jit(solution)/shard_map/ppermute | solution.py:484
  158.2 8.9 %collective-permute-start.17 = (bf16[4,2,32,1024]{3,2,1,0:T(8,128)(2,1)}, bf16[4,2,32,1024]{3,2,1,0:T(8,128)(2,1)}, u32[]{:S(2)}, u32[]{:S(2)}) collective-permute-start(bf16[4,2,32,1024]{3,2,1,0:T(8,128)(2,1)} %collective-permute-done.12.rest_0_.refs_2_), channel_id=1, source_target_pairs={{0,1},{1,0},{2,3},{3,2},{4,5},{5,4},{6,7},{7,6},{8,9},{9,8},{10,11... | collective-permute-start | bytes 1572872 | tf_op jit(solution)/shard_map/ppermute | solution.py:484
  160.9 6.2 %collective-permute-start.18 = (bf16[4,2,32,1024]{3,2,1,0:T(8,128)(2,1)}, bf16[4,2,32,1024]{3,2,1,0:T(8,128)(2,1)}, u32[]{:S(2)}, u32[]{:S(2)}) collective-permute-start(bf16[4,2,32,1024]{3,2,1,0:T(8,128)(2,1)} %collective-permute-done.13.rest_0_.refs_3_), channel_id=1, source_target_pairs={{0,1},{1,0},{2,3},{3,2},{4,5},{5,4},{6,7},{7,6},{8,9},{9,8},{10,11... | collective-permute-start | bytes 1572872 | tf_op jit(solution)/shard_map/ppermute | solution.py:484
  165.9 17.1 %collective-permute-start.19 = (bf16[4,2,32,1152]{3,2,1,0:T(8,128)(2,1)}, bf16[4,2,32,1152]{3,2,1,0:T(8,128)(2,1)}, u32[]{:S(2)}, u32[]{:S(2)}) collective-permute-start(bf16[4,2,32,1152]{3,2,1,0:T(8,128)(2,1)} %get-tuple-element.23), channel_id=1, source_target_pairs={{0,2},{2,0},{4,6},{6,4},{8,10},{10,8},{12,14},{14,12},{1,3},{3,1},... | collective-permute-start | bytes 1769480 | tf_op jit(solution)/shard_map/ppermute | solution.py:478
  180.1 10.9 %collective-permute-start.20 = (bf16[4,2,32,896]{3,2,1,0:T(8,128)(2,1)}, bf16[4,2,32,896]{3,2,1,0:T(8,128)(2,1)S(1)}, u32[]{:S(2)}, u32[]{:S(2)}) collective-permute-start(bf16[4,2,32,896]{3,2,1,0:T(8,128)(2,1)} %get-tuple-element.24), channel_id=1, source_target_pairs={{0,2},{2,0},{4,6},{6,4},{8,10},{10,8},{12,14},{14,12},{1,3},{3,1},... | collective-permute-start | bytes 1376264 | tf_op jit(solution)/shard_map/ppermute | solution.py:478
  181.2 12.1 %collective-permute-start.21 = (bf16[4,2,32,1152]{3,2,1,0:T(8,128)(2,1)S(1)}, bf16[4,2,32,1152]{3,2,1,0:T(8,128)(2,1)S(1)}, u32[]{:S(2)}, u32[]{:S(2)}) collective-permute-start(bf16[4,2,32,1152]{3,2,1,0:T(8,128)(2,1)S(1)} %copy-done.4), channel_id=1, source_target_pairs={{0,1},{1,0},{2,3},{3,2},{4,5},{5,4},{6,7},{7,6},{8,9},{9,8},{10,11... | collective-permute-start | bytes 1769480 | tf_op jit(solution)/shard_map/ppermute | solution.py:484
  183.0 11.1 %collective-permute-start.23 = (bf16[4,2,32,1152]{3,2,1,0:T(8,128)(2,1)}, bf16[4,2,32,1152]{3,2,1,0:T(8,128)(2,1)}, u32[]{:S(2)}, u32[]{:S(2)}) collective-permute-start(bf16[4,2,32,1152]{3,2,1,0:T(8,128)(2,1)} %collective-permute-done.19.refs_2_), channel_id=1, source_target_pairs={{0,1},{1,0},{2,3},{3,2},{4,5},{5,4},{6,7},{7,6},{8,9},{9,8},{10,11... | collective-permute-start | bytes 1769480 | tf_op jit(solution)/shard_map/ppermute | solution.py:484
  183.1 11.1 %collective-permute-start.22 = (bf16[4,2,32,896]{3,2,1,0:T(8,128)(2,1)}, bf16[4,2,32,896]{3,2,1,0:T(8,128)(2,1)S(1)}, u32[]{:S(2)}, u32[]{:S(2)}) collective-permute-start(bf16[4,2,32,896]{3,2,1,0:T(8,128)(2,1)} %get-tuple-element.22.refs_1_), channel_id=1, source_target_pairs={{0,1},{1,0},{2,3},{3,2},{4,5},{5,4},{6,7},{7,6},{8,9},{9,8},{10,11... | collective-permute-start | bytes 1376264 | tf_op jit(solution)/shard_map/ppermute | solution.py:484
  (18 other events, 177.7 us)
